TPU v7x, 256 devices: a whole 4x4x8 slice. The times are simulated.
256 devices in a mesh: sub: 64 (over y, z, core), rhs: 4 (over x).
Axes of the slice: x: 4, y: 4, z: 8, core: 2. Of those that a mesh axis runs over, the one named last changes fastest.
Arguments:
- right_side: float32 [256, 252, 512], P('sub', None, 'rhs'), parts along dimension 2, may hold values from -70 to 70
- coupling: bfloat16 [256, 508032], P('sub'), may hold values from -0.0625 to 0.0625
- neighbours: int32 [256, 8], P('sub'), may hold values from 0 to 255, as said below
- inverse: bfloat16 [64, 1512, 1512], P('sub'), may hold values from -1 to 1
- margin: int32 [64, 2], P('sub'), may hold values from 0 to 255, as said below
- counts: int32 [64], P('sub'), may hold values from 1 to 4, as said below
Outputs:
- solution: float32 [256, 252, 512], P('sub', None, 'rhs'), parts along dimension 2
There are 4 independent parts, one for each index of `rhs`. A program takes and returns all parts, laid end to end along the dimension named above; an argument that names none is the same for every part. Nothing has to cross between parts.
Inputs may be any that keep to these rules, and one draw needn't show every extreme that they name: `counts`: every subdomain holds 1 to 4 live spheres, and some subdomain holds exactly 4. `neighbours`: every entry of row i is a live sphere slot of the subdomain of i or of a subdomain adjacent to it (index one lower or one higher). `margin`: for subdomain d the first 1 entries are live slots of subdomain d - 1 (of subdomain 0 itself for d = 0), the last 1 live slots of subdomain d + 1 (of the last subdomain itself for the last one).
All inputs are finite; a program needn't handle non-finite values.
Results may differ from a plain program's by a relative error of at most 0.0055.
Values may be sent and summed in bfloat16 or wider, within the bound.
No kernel may reach another device: no remote copies, remote signals or barrier semaphores. Data moves between devices by JAX's collectives and lax.ppermute only.
A program may use at most 64 MiB of HBM per device.

v0:
```python
import jax
import jax.numpy as jnp
from jax import lax
from jax.sharding import PartitionSpec as P

epsilon = 1e-06


def extended_2(block, sides, width):
    for axis, dim in sides:
        count = lax.axis_size(axis)
        forward = [(i, i + 1) for i in range(count - 1)]
        backward = [(target, source) for source, target in forward]
        low = lax.ppermute(
            lax.slice_in_dim(block, block.shape[dim] - width, None, axis=dim), axis, forward
        )
        high = lax.ppermute(lax.slice_in_dim(block, 0, width, axis=dim), axis, backward)
        block = jnp.concatenate([low, block, high], axis=dim)
    return block


def passed_along(x, axis, by):
    size = lax.axis_size(axis)
    pairs = [(i, i + by) for i in range(size) if 0 <= i + by < size]
    return lax.ppermute(x, axis, pairs)


def inner(left, right):
    return jnp.sum(left * right, axis=(0, 1))


def global_norm(vector):
    return jnp.sqrt(lax.psum(inner(vector, vector), "sub") + epsilon)


def body(right_side, coupling, neighbours, inverse, margin, counts):
    rows = right_side.shape[0]
    width = right_side.shape[1]
    fields = right_side.shape[2]
    blocks = neighbours.shape[1]
    matrices = coupling.reshape(rows, blocks, width, width)
    here = lax.axis_index("sub")
    slots = jnp.arange(rows, dtype=jnp.int32)
    alive = (slots < counts[0]).astype(jnp.float32)[:, None, None]
    offset = (here - 1) * rows
    frame_slots = jnp.arange(3 * rows, dtype=jnp.int32)
    extra_slots = margin[0]
    picker = (extra_slots[:, None] - offset == frame_slots[None, :]).astype(jnp.float32)
    picker_low = picker.astype(jnp.bfloat16)
    near_local = (neighbours - offset).reshape(-1)

    def precondition(vector):
        rounded = vector.astype(jnp.bfloat16)
        frame = extended_2(rounded, (("sub", 0),), rows)
        extra = jnp.einsum(
            "hq,qwr->hwr", picker_low, frame, preferred_element_type=jnp.float32
        ).astype(jnp.bfloat16)
        extended = jnp.concatenate([rounded, extra], axis=0).reshape(-1, fields)
        output = jnp.dot(inverse[0], extended, preferred_element_type=jnp.float32)
        output = output.reshape(-1, width, fields)
        spill = output[rows:]
        framed = jnp.einsum("hq,hwr->qwr", picker, spill, precision=lax.Precision.HIGHEST)
        from_right = passed_along(framed[:rows].astype(jnp.bfloat16), "sub", -1).astype(jnp.float32)
        from_left = passed_along(framed[2 * rows :].astype(jnp.bfloat16), "sub", 1).astype(
            jnp.float32
        )
        result = output[:rows] + framed[rows : 2 * rows] + from_right + from_left
        return result * alive

    def apply_system(vector):
        rounded = vector.astype(jnp.bfloat16)
        frame = extended_2(rounded, (("sub", 0),), rows)
        nearby = jnp.take(frame, near_local, axis=0).reshape(rows, blocks, width, fields)
        product = jnp.einsum("pkvw,pkwr->pvr", matrices, nearby, preferred_element_type=jnp.float32)
        return (vector + product) * alive

    start = right_side * alive
    initial = global_norm(start)
    basis_one = start / initial[None, None, :]
    pre_one = precondition(basis_one)
    image = apply_system(pre_one)
    h_one_one = lax.psum(inner(basis_one, image), "sub")
    image = image - h_one_one[None, None, :] * basis_one
    h_two_one = global_norm(image)
    basis_two = image / h_two_one[None, None, :]
    pre_two = precondition(basis_two)
    image = apply_system(pre_two)
    h_one_two = lax.psum(inner(basis_one, image), "sub")
    image = image - h_one_two[None, None, :] * basis_one
    h_two_two = lax.psum(inner(basis_two, image), "sub")
    image = image - h_two_two[None, None, :] * basis_two
    h_three_two = global_norm(image)
    gram_aa = h_one_one * h_one_one + h_two_one * h_two_one
    gram_ab = h_one_one * h_one_two + h_two_one * h_two_two
    gram_bb = h_one_two * h_one_two + h_two_two * h_two_two + h_three_two * h_three_two
    determinant = gram_aa * gram_bb - gram_ab * gram_ab
    weight_one = initial * (gram_bb * h_one_one - gram_ab * h_one_two) / determinant
    weight_two = initial * (gram_aa * h_one_two - gram_ab * h_one_one) / determinant
    return weight_one[None, None, :] * pre_one + weight_two[None, None, :] * pre_two


def solution(mesh):
    placed = (
        P("sub", None, "rhs"),
        P("sub", None),
        P("sub", None),
        P("sub", None, None),
        P("sub", None),
        P("sub"),
    )
    return jax.shard_map(
        body, mesh=mesh, in_specs=placed, out_specs=P("sub", None, "rhs"), check_vma=False
    )
```

profile of v0, /device:TPU:2, one launch (start us, length us, event | category | flops | bytes accessed | tf_op | source)
XLA Modules:
  0.0 863.7 jit_solution(13683966303049429386)
XLA Ops:
  0.7 1.4 multiply_reduce_fusion.5
  2.1 131.8 %psum.42 = f32[128]{0:T(128)S(1)} all-reduce(f32[128]{0:T(128)S(1)} %multiply_reduce_fusion.5), channel_id=1, replica_groups=mesh['sub'=64,'rhs'=4] {'sub'}, use_global_device_ids=true, to_apply=%region_1.0 | all-reduce | flops 128 | bytes 1024 | tf_op jit(solution)/shard_map/psum | solution.py:33
  133.8 1.2 fusion.48
  135.1 1.3 collective-permute-start.1
  136.4 3.0 collective-permute-start
  141.6 3.7 fusion.4
  146.0 2.2 fusion.51
  149.1 1.3 collective-permute-start.2
  150.4 5.4 collective-permute-start.3
  157.8 2.4 fusion.46
  160.2 1.3 collective-permute-start.5
  161.5 6.1 collective-permute-start.4
  167.6 6.9 reshape.82
  174.5 13.2 %reshape.53 = bf16[4,8,252,252]{3,2,1,0:T(8,128)(2,1)} reshape(bf16[2032128]{0:T(1024)(128)(2,1)} %reshape.82) | data formatting | bytes 8128512 | tf_op jit(solution)/shard_map/reshape | solution.py:41
  189.7 1.9 copy-done
  191.6 1.2 convolution_bitcast_fusion.1
  193.4 126.5 %psum.43 = f32[128]{0:T(128)S(1)} all-reduce(f32[128]{0:T(128)S(1)} %get-tuple-element.12), channel_id=1, replica_groups=mesh['sub'=64,'rhs'=4] {'sub'}, use_global_device_ids=true, to_apply=%region_3.5 | all-reduce | flops 128 | bytes 1024 | tf_op jit(solution)/shard_map/psum | solution.py:82
  320.2 124.0 %psum.44 = f32[128]{0:T(128)S(1)} all-reduce(f32[128]{0:T(128)S(1)} %multiply_reduce_fusion.3), channel_id=1, replica_groups=mesh['sub'=64,'rhs'=4] {'sub'}, use_global_device_ids=true, to_apply=%region_5.7 | all-reduce | flops 128 | bytes 1024 | tf_op jit(solution)/shard_map/psum | solution.py:33
  445.2 1.3 collective-permute-start.7
  446.5 3.0 collective-permute-start.6
  451.7 3.7 fusion.7
  456.2 2.2 fusion.52
  459.3 1.3 collective-permute-start.8
  460.6 6.5 collective-permute-start.9
  469.0 2.5 fusion.42
  471.4 1.3 collective-permute-start.11
  472.7 5.9 collective-permute-start.10
  481.8 1.9 copy-done.1
  483.7 1.2 convolution_bitcast_fusion
  485.5 128.6 %psum.45 = f32[128]{0:T(128)S(1)} all-reduce(f32[128]{0:T(128)S(1)} %get-tuple-element.6), channel_id=1, replica_groups=mesh['sub'=64,'rhs'=4] {'sub'}, use_global_device_ids=true, to_apply=%region_7.9 | all-reduce | flops 128 | bytes 1024 | tf_op jit(solution)/shard_map/psum | solution.py:88
  614.4 124.0 %psum.46 = f32[128]{0:T(128)S(1)} all-reduce(f32[128]{0:T(128)S(1)} %multiply_reduce_fusion.1), channel_id=1, replica_groups=mesh['sub'=64,'rhs'=4] {'sub'}, use_global_device_ids=true, to_apply=%region_9.11 | all-reduce | flops 128 | bytes 1024 | tf_op jit(solution)/shard_map/psum | solution.py:90
  738.7 124.0 %psum.47 = f32[128]{0:T(128)S(1)} all-reduce(f32[128]{0:T(128)S(1)} %multiply_reduce_fusion), channel_id=1, replica_groups=mesh['sub'=64,'rhs'=4] {'sub'}, use_global_device_ids=true, to_apply=%region_11.13 | all-reduce | flops 128 | bytes 1024 | tf_op jit(solution)/shard_map/psum | solution.py:33
  (67 shorter events, 20.3 us)
Async XLA Ops:
  135.1 5.0 collective-permute-start.1
  136.4 4.2 collective-permute-start
  146.0 9.8 %copy-start.6 = (s32[4,8]{1,0:T(4,128)S(1)}, s32[4,8]{1,0:T(4,128)}, u32[]{:S(2)}) copy-start(s32[4,8]{1,0:T(4,128)} %param.10) | copy-start | bytes 388
  149.1 8.7 %collective-permute-start.2 = (bf16[4,252,128]{2,0,1:T(4,128)(2,1)}, bf16[4,252,128]{2,0,1:T(4,128)(2,1)}, u32[]{:S(2)}, u32[]{:S(2)}) collective-permute-start(bf16[4,252,128]{2,0,1:T(4,128)(2,1)} %get-tuple-element.20), channel_id=1, source_target_pairs={{4,0},{8,4},{12,8},{16,12},{20,16},{24,20},{28,24},{32,28},{36,32}... | collective-permute-start | bytes 774152 | tf_op jit(solution)/shard_map/ppermute | solution.py:25
  150.4 7.4 collective-permute-start.3
  160.2 27.5 %collective-permute-start.5 = (bf16[4,252,128]{2,0,1:T(4,128)(2,1)S(1)}, bf16[4,252,128]{2,0,1:T(4,128)(2,1)S(1)}, u32[]{:S(2)}, u32[]{:S(2)}) collective-permute-start(bf16[4,252,128]{2,0,1:T(4,128)(2,1)S(1)} %get-tuple-element.14), channel_id=1, source_target_pairs={{4,0},{8,4},{12,8},{16,12},{20,16},{24,20},{28,24},{32,28},{36,32}... | collective-permute-start | bytes 774152 | tf_op jit(solution)/shard_map/ppermute | solution.py:17
  161.5 26.2 %collective-permute-start.4 = (bf16[4,252,128]{2,0,1:T(4,128)(2,1)S(1)}, bf16[4,252,128]{2,0,1:T(4,128)(2,1)S(1)}, u32[]{:S(2)}, u32[]{:S(2)}) collective-permute-start(bf16[4,252,128]{2,0,1:T(4,128)(2,1)S(1)} %get-tuple-element.14), channel_id=1, source_target_pairs={{0,4},{4,8},{8,12},{12,16},{16,20},{20,24},{24,28},{28,32},{32,36}... | collective-permute-start | bytes 774152 | tf_op jit(solution)/shard_map/ppermute | solution.py:14
  189.4 2.2 copy-start
  191.6 1.3 copy-start.2
  445.2 4.3 collective-permute-start.7
  446.5 4.2 collective-permute-start.6
  459.3 9.7 %collective-permute-start.8 = (bf16[4,252,128]{2,0,1:T(4,128)(2,1)}, bf16[4,252,128]{2,0,1:T(4,128)(2,1)}, u32[]{:S(2)}, u32[]{:S(2)}) collective-permute-start(bf16[4,252,128]{2,0,1:T(4,128)(2,1)} %get-tuple-element.18), channel_id=1, source_target_pairs={{4,0},{8,4},{12,8},{16,12},{20,16},{24,20},{28,24},{32,28},{36,32}... | collective-permute-start | bytes 774152 | tf_op jit(solution)/shard_map/ppermute | solution.py:25
  460.6 8.4 collective-permute-start.9
  471.4 7.2 collective-permute-start.11
  472.7 7.1 collective-permute-start.10
  481.5 2.2 copy-start.1
  483.7 1.3 copy-start.4
  484.9 129.2 %copy-start.5 = (f32[4,252,128]{2,0,1:T(4,128)S(1)}, f32[4,252,128]{2,0,1:T(4,128)}, u32[]{:S(2)}) copy-start(f32[4,252,128]{2,0,1:T(4,128)} %get-tuple-element.11) | copy-start | bytes 1548292
  484.9 377.9 %copy-start.3 = (f32[4,252,128]{2,0,1:T(4,128)S(1)}, f32[4,252,128]{2,0,1:T(4,128)}, u32[]{:S(2)}) copy-start(f32[4,252,128]{2,0,1:T(4,128)} %get-tuple-element.15) | copy-start | bytes 1548292
where the time goes:
time: 866 us; the launch traced here: 864 us
  blocking collectives  759 us (88%)
  starting transfers between devices  37.6 us (4%)
  local copies, waits for them, and re-layouts  33.8 us (4%)
  matrix products  15.4 us (2%)
  other arithmetic  14.1 us (2%)
    psum x3, blocking collectives, global_norm(): return jnp.sqrt(lax.psum(inner(vector, vector), 'sub') + epsilon)  380 us
    psum x1, blocking collectives, body(): h_one_two = lax.psum(inner(basis_one, image), 'sub')  129 us
    psum x1, blocking collectives, body(): h_one_one = lax.psum(inner(basis_one, image), 'sub')  127 us
    psum x1, blocking collectives, body(): h_two_two = lax.psum(inner(basis_two, image), 'sub')  124 us
    ppermute x4, starting transfers between devices, extended_2(): lax.ppermute(lax.slice_in_dim(block, block.shape[dim] - width, None, axis...  18.1 us
  transfers between devices with their start and end apart: 12, of which 3 were waited for; matrix products, arithmetic and copies ran while one was open for 3% of the time, Pallas kernels for 0%

commit v1 on v0

v1 whole, which is shorter than its diff:
```python
import functools
import jax
import jax.numpy as jnp
from jax import lax
from jax.experimental import pallas as pl
from jax.experimental.pallas import tpu as pltpu
from jax.sharding import PartitionSpec as P

EPS = 1e-06
W = 252
WP = 256
NS = 4
NB = 8
R = 128
NSUB = 64
SHIFT = 1.0
ROWS = NB * W
GROUP = 32
F32 = jnp.float32
BF16 = jnp.bfloat16
VM = pl.BlockSpec(memory_space=pltpu.VMEM)
SM = pl.BlockSpec(memory_space=pltpu.SMEM)


def call(kernel, outs, ins, scratch=(), limit=24, **cost):
    return pl.pallas_call(
        kernel,
        out_shape=[jax.ShapeDtypeStruct(s, d) for s, d in outs],
        in_specs=ins,
        out_specs=[VM] * len(outs),
        scratch_shapes=list(scratch),
        compiler_params=pltpu.CompilerParams(vmem_limit_bytes=limit << 20),
    )


def start_kernel(counts, right, v0_ref, v0b_ref):
    for s in range(NS):
        alive = jnp.where(counts[0] > s, 1.0, 0.0)
        v0_ref[s, :W, :] = right[pl.ds(s, W, stride=NS), :] * alive
        v0_ref[s, W:, :] = jnp.zeros((WP - W, R), F32)
        v0b_ref[s] = v0_ref[s].astype(BF16)


def coupling_kernel(flat, c_ref, lo, hi):
    lanes = GROUP * W

    def group(g, carry):
        x = flat[:, pl.ds(pl.multiple_of(g * lanes, 128), lanes)].astype(F32)
        base = pl.multiple_of(g * GROUP * NS, 8)
        for s in range(0, GROUP, 2):
            a = x[:, s * W : (s + 1) * W]
            b = x[:, (s + 1) * W : (s + 2) * W]
            lo[pl.ds(base + s * NS, 2 * NS), :] = jnp.concatenate([a[:, :128], b[:, :128]], axis=0)
            hi[pl.ds(base + s * NS, 2 * NS), : W - 128] = jnp.concatenate([a[:, 128:], b[:, 128:]], axis=0)
        return carry

    lax.fori_loop(0, ROWS // GROUP, group, 0)
    keep = lax.broadcasted_iota(jnp.int32, (WP, 128), 1) < W - 128
    pad = jnp.zeros((WP - W, 128), F32)

    def place(k, carry):
        for p in range(NS):
            first = k * (W * NS) + p
            left = lo[pl.ds(first, W, stride=NS), :]
            right = hi[pl.ds(first, W, stride=NS), :]
            left = jnp.concatenate([left, pad], axis=0)
            right = jnp.where(keep, jnp.concatenate([right, pad], axis=0), 0.0)
            c_ref[p * NB + k, :, :128] = left.astype(BF16)
            c_ref[p * NB + k, :, 128:] = right.astype(BF16)
        return carry

    lax.fori_loop(0, NB, place, 0)


def solve_kernel(
    place, margin, inverse, own, left, right,
    out_ref, up_ref, down_ref, ext, res,
):
    here = place[0]
    low = jnp.clip(margin[0, 0] - NS * jnp.maximum(here - 1, 0), 0, NS - 1)
    high = jnp.clip(margin[0, 1] - NS * jnp.minimum(here + 1, NSUB - 1), 0, NS - 1)
    for s in range(NS):
        ext[s * W : (s + 1) * W, :] = own[s, :W, :]
    some = left.shape[0] > 1

    def put(first, from_own, got, index):
        @pl.when(from_own)
        def _():
            ext[first : first + W, :] = own[index][:W]

        @pl.when(jnp.logical_not(from_own))
        def _():
            ext[first : first + W, :] = got[index if some else 0].astype(F32)[:W]

    put(NS * W, here == 0, left, low)
    put((NS + 1) * W, here == NSUB - 1, right, high)
    res[...] = jnp.dot(inverse[0], ext[...].astype(BF16), preferred_element_type=F32)
    pad = jnp.zeros((WP - W, R), F32)
    for s in range(NS):
        out_ref[s] = jnp.concatenate([res[s * W : (s + 1) * W, :], pad], axis=0)
    spill_low = res[NS * W : (NS + 1) * W, :]
    spill_high = res[(NS + 1) * W : (NS + 2) * W, :]

    @pl.when(here == 0)
    def _():
        out_ref[low] += jnp.concatenate([spill_low, pad], axis=0)

    @pl.when(here == NSUB - 1)
    def _():
        out_ref[high] += jnp.concatenate([spill_high, pad], axis=0)

    for s in range(NS):
        block = out_ref[s].astype(BF16)
        up_ref[s] = block
        down_ref[s] = block
    mark = jnp.ones((WP - W, R), F32)
    up_ref[NS] = jnp.concatenate([spill_high, mark * high.astype(F32)], axis=0).astype(BF16)
    down_ref[NS] = jnp.concatenate([spill_low, mark * low.astype(F32)], axis=0).astype(BF16)


def opened(block):
    x = block.astype(F32)
    rows = lax.broadcasted_iota(jnp.int32, x.shape, 0)
    return jnp.where(rows < W, x, 0.0), x[W : W + 1, :]


def system_kernel(
    first, place, counts, neighbours, c_ref, out, up, down, low, high, low2, high2, v0, *rest
):
    if first:
        p_ref, w_ref, wup_ref, wdown_ref, sums_ref, u = rest
    else:
        w, p_ref, sums_ref, u = rest
    here = place[0]
    spill_low = opened(low[NS])
    spill_high = opened(high[NS])
    mine_low = opened(down[NS])
    mine_high = opened(up[NS])
    far_low = opened(low2[0])
    far_high = opened(high2[0])
    rows = lax.broadcasted_iota(jnp.int32, (WP, R), 0) < W

    def added(x, spill, s):
        return x + jnp.where(spill[1] == s, spill[0], 0.0)

    for s in range(NS):
        u[s] = added(added(low[s].astype(F32), mine_low, s), far_low, s).astype(BF16)
        u[2 * NS + s] = added(added(high[s].astype(F32), mine_high, s), far_high, s).astype(BF16)
        alive = jnp.where(counts[0] > s, 1.0, 0.0)
        mine = added(added(out[s], spill_low, s), spill_high, s) * alive
        p_ref[s] = mine
        u[NS + s] = mine.astype(BF16)
    del rows
    zero = jnp.zeros((1, R), F32)
    sums = [zero] * 3
    for s in range(NS):
        acc = jnp.zeros((WP, R), F32)
        for k in range(NB):
            slot = jnp.clip(neighbours[s, k] - NS * (here - 1), 0, 3 * NS - 1)
            acc += jnp.dot(c_ref[s * NB + k], u[slot], preferred_element_type=F32)
        alive = jnp.where(counts[0] > s, 1.0, 0.0)
        image = (p_ref[s] + acc) * alive
        start = v0[s]
        if first:
            image = image - SHIFT * start
            w_ref[s] = image
            terms = (start * start, start * image, image * image)
        else:
            terms = (start * image, w[s] * image, image * image)
        sums = [t + jnp.sum(x, axis=0, keepdims=True) for t, x in zip(sums, terms)]
    if first:
        for ref, index in ((wup_ref, spill_high[1]), (wdown_ref, spill_low[1])):
            chosen = jnp.zeros((WP, R), F32)
            for s in range(NS):
                chosen = chosen + jnp.where(index == s, w_ref[s], 0.0)
            ref[0] = chosen.astype(BF16)
    sums_ref[...] = jnp.concatenate(sums + [zero] * 5, axis=0)


def finish_kernel(gathered, p0, q, out):
    total = jnp.sum(gathered[...], axis=0)
    s00, s01, s11, s02, s12, s22 = (total[i : i + 1, :] for i in range(6))
    c = SHIFT
    bb = s00 + EPS
    beta = jnp.sqrt(bb)
    h11 = (s01 + c * s00) / bb
    a = c - h11
    n2 = (s11 + 2 * a * s01 + a * a * s00) / bb
    h21s = jnp.maximum(n2, 0.0) + EPS
    h21 = jnp.sqrt(h21s)
    full = bb * h21s
    v0i = s01 + c * s00
    h12 = (s02 + a * v0i) / (bb * h21)
    cross = (s01 + a * s00) / (bb * h21)
    b2i = (s12 + a * s02 + a * (s11 + c * s01) + a * a * v0i) / full
    h22 = b2i - h12 * cross
    ii = (s22 + 2 * a * (s12 + c * s02) + a * a * (s11 + 2 * c * s01 + c * c * s00)) / full
    rest = (
        ii + h12 * h12 * (s00 / bb) + h22 * h22 * (n2 / h21s)
        - 2 * h12 * h12 - 2 * h22 * b2i + 2 * h12 * h22 * cross
    )
    h32s = jnp.maximum(rest, 0.0) + EPS
    g00 = h11 * h11 + h21s
    g01 = h11 * h12 + h21 * h22
    g11 = h12 * h12 + h22 * h22 + h32s
    det = g00 * g11 - g01 * g01
    y1 = beta * (g11 * h11 - g01 * h12) / det
    y2 = beta * (g00 * h12 - g01 * h11) / det
    two = y2 / (beta * h21)
    one = y1 / beta + a * two
    for s in range(NS):
        out[pl.ds(s, W, stride=NS), :] = one * p0[s, :W, :] + two * q[s, :W, :]


def shifted(x, by):
    pairs = [(i, i + by) for i in range(NSUB) if 0 <= i + by < NSUB]
    return lax.ppermute(x, "sub", pairs)


def body(right_side, coupling, neighbours, inverse, margin, counts):
    here = lax.axis_index("sub").astype(jnp.int32).reshape(1)
    flat_right = right_side.transpose(1, 0, 2).reshape(W * NS, R)
    block = (NS, WP, R)
    v0, v0b = call(start_kernel, [(block, F32), (block, BF16)], [SM, VM])(counts, flat_right)
    (mats,) = call(
        coupling_kernel,
        [((NS * NB, WP, WP), BF16)],
        [VM],
        [pltpu.VMEM((ROWS * NS, 128), F32)] * 2,
        limit=32,
    )(coupling)

    def solve(own, left, right):
        return call(
            solve_kernel,
            [(block, F32), ((NS + 1, WP, R), BF16), ((NS + 1, WP, R), BF16)],
            [SM, SM, VM, VM, VM, VM],
            [pltpu.VMEM((6 * W, R), F32)] * 2,
        )(here, margin, inverse, own, left, right)

    def system(first, out, up, down, *more):
        low, high = shifted(up, 1), shifted(down, -1)
        low2, high2 = shifted(up[NS:], 2), shifted(down[NS:], -2)
        if first:
            outs = [(block, F32)] * 2 + [((1, WP, R), BF16)] * 2 + [((8, R), F32)]
        else:
            outs = [(block, F32), ((8, R), F32)]
        return call(
            functools.partial(system_kernel, first),
            outs,
            [SM, SM, SM] + [VM] * (8 + len(more)),
            [pltpu.VMEM((3 * NS, WP, R), BF16)],
        )(here, counts, neighbours, mats, out, up, down, low, high, low2, high2, *more)

    out, up, down = solve(v0, shifted(v0b, 1), shifted(v0b, -1))
    p0, w, wup, wdown, sums_one = system(True, out, up, down, v0)
    out, up, down = solve(w, shifted(wup, 1), shifted(wdown, -1))
    q, sums_two = system(False, out, up, down, v0, w)
    sums = jnp.concatenate([sums_one[:3], sums_two[:3]], axis=0)
    gathered = lax.all_to_all(jnp.broadcast_to(sums[None], (NSUB, 6, R)), "sub", 0, 0)
    (flat,) = call(finish_kernel, [((W * NS, R), F32)], [VM] * 3)(gathered, p0, q)
    return flat.reshape(W, NS, R).transpose(1, 0, 2)


def solution(mesh):
    placed = (
        P("sub", None, "rhs"),
        P("sub", None),
        P("sub", None),
        P("sub", None, None),
        P("sub", None),
        P("sub"),
    )
    return jax.shard_map(
        body, mesh=mesh, in_specs=placed, out_specs=P("sub", None, "rhs"), check_vma=False
    )
```

time: 866 us -> 105 us (0.12)
  blocking collectives: 759 us -> 32.4 us
  local copies, waits for them, and re-layouts: 33.8 us -> 4.08 us
  Pallas kernels: 0 us -> 22.6 us
  matrix products: 15.4 us -> 0 us
  other arithmetic: 14.1 us -> 0.01 us
    psum x6 -> x0, blocking collectives: 759 us -> none  [the longest x3 380 us: global_norm(): return jnp.sqrt(lax.psum(inner(vector, vector), 'sub') + epsilon)]
    all_to_all x0 -> x1, blocking collectives: none -> 32.4 us  [body(): lax.all_to_all(jnp.broadcast_to(sums[None], (NSUB, 6, R)), 'sub', 0, 0)]
    pallas_call x0 -> x7, Pallas kernels: none -> 22.6 us  [the longest x1 12.7 us: body(): call(coupling_kernel, [((NS * NB, WP, WP), BF16)], [VM], [pltpu.VMEM((ROW...]
    dot_general x8 -> x0, matrix products: 15.4 us -> none  [the longest x2 7.41 us: precondition(): output = jnp.dot(inverse[0], extended, preferred_element_type=jnp.float32)]
    reshape x4 -> x0, local copies, waits for them, and re-layouts: 13.5 us -> none  [the longest x1 13.2 us: body(): matrices = coupling.reshape(rows, blocks, width, width)]
  transfers between devices with their start and end apart: 12 -> 12, of which waited for: 3 -> 3; matrix products, arithmetic and copies ran while one was open for 3% -> 0% of each run, Pallas kernels for 0% -> 12%
where the time goes in v1:
time: 105 us; the launch traced here: 104 us
  starting transfers between devices  36.4 us (35%)
  blocking collectives  32.4 us (31%)
  Pallas kernels  22.6 us (22%)
  waiting for transfers between devices  7.14 us (7%)
  local copies, waits for them, and re-layouts  4.08 us (4%)
    ppermute x12, starting transfers between devices, shifted(): return lax.ppermute(x, 'sub', pairs)  36.4 us
    all_to_all x1, blocking collectives, body(): lax.all_to_all(jnp.broadcast_to(sums[None], (NSUB, 6, R)), 'sub', 0, 0)  32.4 us
    pallas_call x1, Pallas kernels, body(): call(coupling_kernel, [((NS * NB, WP, WP), BF16)], [VM], [pltpu.VMEM((ROW...  12.7 us
    ppermute x12, waiting for transfers between devices, shifted(): return lax.ppermute(x, 'sub', pairs)  7.14 us
    pallas_call x2, Pallas kernels, system(): call(functools.partial(system_kernel, first), outs, [SM, SM, SM] + [VM] *...  4.63 us
    pallas_call x2, Pallas kernels, solve(): call(solve_kernel, [(block, F32), ((NS + 1, WP, R), BF16), ((NS + 1, WP,...  4.23 us
    unnamed x16, local copies, waits for them, and re-layouts  4.03 us
  transfers between devices with their start and end apart: 12, of which 3 were waited for; matrix products, arithmetic and copies ran while one was open for 0% of the time, Pallas kernels for 12%

profile of v1, /device:TPU:2, one launch (start us, length us, event | category | flops | bytes accessed | tf_op | source)
XLA Modules:
  0.0 103.5 jit_solution(11174334068715163302)
XLA Ops:
  0.7 1.0 copy-done.2
  1.7 0.1 shard_map.65
  1.8 1.3 %collective-permute-start.1 = (bf16[4,256,128]{2,1,0:T(8,128)(2,1)S(1)}, bf16[4,256,128]{2,1,0:T(8,128)(2,1)S(1)}, u32[]{:S(2)}, u32[]{:S(2)}) collective-permute-start(bf16[4,256,128]{2,1,0:T(8,128)(2,1)S(1)} %get-tuple-element.21), channel_id=1, source_target_pairs={{4,0},{8,4},{12,8},{16,12},{20,16},{24,20},{28,24},{32,28},{36,32}... | collective-permute-start | bytes 786440 | tf_op jit(solution)/shard_map/ppermute | solution.py:217
  3.1 3.0 %collective-permute-start = (bf16[4,256,128]{2,1,0:T(8,128)(2,1)S(1)}, bf16[4,256,128]{2,1,0:T(8,128)(2,1)S(1)}, u32[]{:S(2)}, u32[]{:S(2)}) collective-permute-start(bf16[4,256,128]{2,1,0:T(8,128)(2,1)S(1)} %get-tuple-element.21), channel_id=1, source_target_pairs={{0,4},{4,8},{8,12},{12,16},{16,20},{20,24},{24,28},{28,32},{32,36}... | collective-permute-start | bytes 786440 | tf_op jit(solution)/shard_map/ppermute | solution.py:217
  6.1 1.1 %collective-permute-done.left = bf16[4,256,128]{2,1,0:T(8,128)(2,1)S(1)} collective-permute-done((bf16[4,256,128]{2,1,0:T(8,128)(2,1)S(1)}, bf16[4,256,128]{2,1,0:T(8,128)(2,1)S(1)}, u32[]{:S(2)}, u32[]{:S(2)}) %collective-permute-start) | collective-permute-done | bytes 262176 | tf_op jit(solution)/shard_map/ppermute | solution.py:217
  7.2 2.3 %copy-done = bf16[1,1512,1512]{2,1,0:T(8,128)(2,1)S(1)} copy-done((bf16[1,1512,1512]{2,1,0:T(8,128)(2,1)S(1)}, bf16[1,1512,1512]{2,1,0:T(8,128)(2,1)}, u32[]{:S(2)}) %copy-start) | copy-done | bytes 4572312
  9.6 0.7 copy-done.4
  10.2 2.1 %shard_map.66 = (f32[4,256,128]{2,1,0:T(8,128)S(1)}, bf16[5,256,128]{2,1,0:T(8,128)(2,1)S(1)}, bf16[5,256,128]{2,1,0:T(8,128)(2,1)S(1)}) custom-call(s32[1]{0:T(128)} %bitcast.place, s32[1,2]{1,0:T(1,128)S(1)} %copy-done.4, bf16[1,1512,1512]{2,1,0:T(8,128)(2,1)S(1)} %copy-done, f32[4,256,128]{2,1,0:T(8,128)S(1)} %get-tuple-element.20.own.v0, ...), custom_call_target="tpu_custom_call" | custom-call | tf_op jit(solution)/shard_map/pallas_call | solution.py:234
  12.3 5.6 %collective-permute-start.2 = (bf16[5,256,128]{2,1,0:T(8,128)(2,1)S(1)}, bf16[5,256,128]{2,1,0:T(8,128)(2,1)S(1)}, u32[]{:S(2)}, u32[]{:S(2)}) collective-permute-start(bf16[5,256,128]{2,1,0:T(8,128)(2,1)S(1)} %get-tuple-element.23.up), channel_id=1, source_target_pairs={{0,4},{4,8},{8,12},{12,16},{16,20},{20,24},{24,28},{28,32},{32,36}... | collective-permute-start | bytes 983048 | tf_op jit(solution)/shard_map/ppermute | solution.py:217
  17.9 1.3 %collective-permute-start.3 = (bf16[5,256,128]{2,1,0:T(8,128)(2,1)S(1)}, bf16[5,256,128]{2,1,0:T(8,128)(2,1)S(1)}, u32[]{:S(2)}, u32[]{:S(2)}) collective-permute-start(bf16[5,256,128]{2,1,0:T(8,128)(2,1)S(1)} %get-tuple-element.24.down), channel_id=1, source_target_pairs={{4,0},{8,4},{12,8},{16,12},{20,16},{24,20},{28,24},{32,28},{36,32}... | collective-permute-start | bytes 983048 | tf_op jit(solution)/shard_map/ppermute | solution.py:217
  19.3 0.0 copy-start.3
  19.3 0.0 slice-start
  19.3 0.0 slice-start.1
  19.3 1.6 %collective-permute-start.5 = (bf16[1,256,128]{2,1,0:T(8,128)(2,1)S(1)}, bf16[1,256,128]{2,1,0:T(8,128)(2,1)S(1)}, u32[]{:S(2)}, u32[]{:S(2)}) collective-permute-start(bf16[1,256,128]{2,1,0:T(8,128)(2,1)S(1)} %slice.19), channel_id=1, source_target_pairs={{8,0},{12,4},{16,8},{20,12},{24,16},{28,20},{32,24},{36,28},{40,32... | collective-permute-start | bytes 196616 | tf_op jit(solution)/shard_map/ppermute | solution.py:217
  20.9 7.2 %collective-permute-start.4 = (bf16[1,256,128]{2,1,0:T(8,128)(2,1)S(1)}, bf16[1,256,128]{2,1,0:T(8,128)(2,1)S(1)}, u32[]{:S(2)}, u32[]{:S(2)}) collective-permute-start(bf16[1,256,128]{2,1,0:T(8,128)(2,1)S(1)} %slice.18), channel_id=1, source_target_pairs={{0,8},{4,12},{8,16},{12,20},{16,24},{20,28},{24,32},{28,36},{32,40... | collective-permute-start | bytes 196616 | tf_op jit(solution)/shard_map/ppermute | solution.py:217
  28.1 12.7 %shard_map.64.c_ref = bf16[32,256,256]{2,1,0:T(8,128)(2,1)S(1)} custom-call(bf16[4,508032]{1,0:T(4,128)(2,1)S(1)} %copy-done.1), custom_call_target="tpu_custom_call" | custom-call | tf_op jit(solution)/shard_map/pallas_call | solution.py:225
  40.8 0.0 copy-start.5
  40.8 0.0 collective-permute-done.5.high2
  40.8 0.0 collective-permute-done.2.low
  40.9 2.3 %shard_map.67 = (f32[4,256,128]{2,1,0:T(8,128)S(1)}, f32[4,256,128]{2,1,0:T(8,128)S(1)}, bf16[1,256,128]{2,1,0:T(8,128)(2,1)S(1)}, bf16[1,256,128]{2,1,0:T(8,128)(2,1)S(1)}, f32[8,128]{1,0:T(8,128)S(1)}) custom-call(s32[1]{0:T(128)} %bitcast.place, s32[1]{0:T(128)S(6)} %copy.7.counts, s32[4,8]{1,0:T(4,128)S(1)} %copy-done.3, ...), custom_call_target="tpu_custom_call" | custom-call | tf_op jit(solution)/shard_map/pallas_call | solution.py:248
  43.2 1.9 %collective-permute-start.6 = (bf16[1,256,128]{2,1,0:T(8,128)(2,1)S(1)}, bf16[1,256,128]{2,1,0:T(8,128)(2,1)S(1)}, u32[]{:S(2)}, u32[]{:S(2)}) collective-permute-start(bf16[1,256,128]{2,1,0:T(8,128)(2,1)S(1)} %get-tuple-element.27), channel_id=1, source_target_pairs={{0,4},{4,8},{8,12},{12,16},{16,20},{20,24},{24,28},{28,32},{32,36}... | collective-permute-start | bytes 196616 | tf_op jit(solution)/shard_map/ppermute | solution.py:217
  45.1 1.3 %collective-permute-start.7 = (bf16[1,256,128]{2,1,0:T(8,128)(2,1)S(1)}, bf16[1,256,128]{2,1,0:T(8,128)(2,1)S(1)}, u32[]{:S(2)}, u32[]{:S(2)}) collective-permute-start(bf16[1,256,128]{2,1,0:T(8,128)(2,1)S(1)} %get-tuple-element.28), channel_id=1, source_target_pairs={{4,0},{8,4},{12,8},{16,12},{20,16},{24,20},{28,24},{32,28},{36,32}... | collective-permute-start | bytes 196616 | tf_op jit(solution)/shard_map/ppermute | solution.py:217
  46.4 3.5 %collective-permute-done.7.right = bf16[1,256,128]{2,1,0:T(8,128)(2,1)S(1)} collective-permute-done((bf16[1,256,128]{2,1,0:T(8,128)(2,1)S(1)}, bf16[1,256,128]{2,1,0:T(8,128)(2,1)S(1)}, u32[]{:S(2)}, u32[]{:S(2)}) %collective-permute-start.7) | collective-permute-done | bytes 65568 | tf_op jit(solution)/shard_map/ppermute | solution.py:217
  49.9 2.1 %shard_map.68 = (f32[4,256,128]{2,1,0:T(8,128)S(1)}, bf16[5,256,128]{2,1,0:T(8,128)(2,1)S(1)}, bf16[5,256,128]{2,1,0:T(8,128)(2,1)S(1)}) custom-call(s32[1]{0:T(128)} %bitcast.place, s32[1,2]{1,0:T(1,128)S(1)} %copy-done.5, bf16[1,1512,1512]{2,1,0:T(8,128)(2,1)S(1)} %bitcast.8, f32[4,256,128]{2,1,0:T(8,128)S(1)} %get-tuple-element.26.own.rest_0_, ...), custom_call_target="tpu_custom_call" | custom-call | tf_op jit(solution)/shard_map/pallas_call | solution.py:234
  52.0 4.9 %collective-permute-start.8 = (bf16[5,256,128]{2,1,0:T(8,128)(2,1)S(1)}, bf16[5,256,128]{2,1,0:T(8,128)(2,1)S(1)}, u32[]{:S(2)}, u32[]{:S(2)}) collective-permute-start(bf16[5,256,128]{2,1,0:T(8,128)(2,1)S(1)} %get-tuple-element.30.up), channel_id=1, source_target_pairs={{0,4},{4,8},{8,12},{12,16},{16,20},{20,24},{24,28},{28,32},{32,36}... | collective-permute-start | bytes 983048 | tf_op jit(solution)/shard_map/ppermute | solution.py:217
  56.9 1.3 %collective-permute-start.9 = (bf16[5,256,128]{2,1,0:T(8,128)(2,1)S(1)}, bf16[5,256,128]{2,1,0:T(8,128)(2,1)S(1)}, u32[]{:S(2)}, u32[]{:S(2)}) collective-permute-start(bf16[5,256,128]{2,1,0:T(8,128)(2,1)S(1)} %get-tuple-element.31.down), channel_id=1, source_target_pairs={{4,0},{8,4},{12,8},{16,12},{20,16},{24,20},{28,24},{32,28},{36,32}... | collective-permute-start | bytes 983048 | tf_op jit(solution)/shard_map/ppermute | solution.py:217
  58.2 1.3 %collective-permute-start.11 = (bf16[1,256,128]{2,1,0:T(8,128)(2,1)S(1)}, bf16[1,256,128]{2,1,0:T(8,128)(2,1)S(1)}, u32[]{:S(2)}, u32[]{:S(2)}) collective-permute-start(bf16[1,256,128]{2,1,0:T(8,128)(2,1)S(1)} %slice.22), channel_id=1, source_target_pairs={{8,0},{12,4},{16,8},{20,12},{24,16},{28,20},{32,24},{36,28},{40,32... | collective-permute-start | bytes 196616 | tf_op jit(solution)/shard_map/ppermute | solution.py:217
  59.5 5.7 %collective-permute-start.10 = (bf16[1,256,128]{2,1,0:T(8,128)(2,1)S(1)}, bf16[1,256,128]{2,1,0:T(8,128)(2,1)S(1)}, u32[]{:S(2)}, u32[]{:S(2)}) collective-permute-start(bf16[1,256,128]{2,1,0:T(8,128)(2,1)S(1)} %slice.21), channel_id=1, source_target_pairs={{0,8},{4,12},{8,16},{12,20},{16,24},{20,28},{24,32},{28,36},{32,40... | collective-permute-start | bytes 196616 | tf_op jit(solution)/shard_map/ppermute | solution.py:217
  65.2 2.5 %collective-permute-done.11.high2 = bf16[1,256,128]{2,1,0:T(8,128)(2,1)S(1)} collective-permute-done((bf16[1,256,128]{2,1,0:T(8,128)(2,1)S(1)}, bf16[1,256,128]{2,1,0:T(8,128)(2,1)S(1)}, u32[]{:S(2)}, u32[]{:S(2)}) %collective-permute-start.11) | collective-permute-done | bytes 65568 | tf_op jit(solution)/shard_map/ppermute | solution.py:217
  67.8 2.3 %shard_map.69 = (f32[4,256,128]{2,1,0:T(8,128)S(1)}, f32[8,128]{1,0:T(8,128)S(1)}) custom-call(s32[1]{0:T(128)} %bitcast.place, s32[1]{0:T(128)S(6)} %copy.7.counts, s32[4,8]{1,0:T(4,128)S(1)} %copy-done.3, bf16[32,256,256]{2,1,0:T(8,128)(2,1)S(1)} %shard_map.64.c_ref, f32[4,256,128]{2,1,0:T(8,128)S(1)} %get-tuple-element.29.out, ...), custom_call_target="tpu_custom_call" | custom-call | tf_op jit(solution)/shard_map/pallas_call | solution.py:248
  70.2 32.4 %all_to_all.5.gathered = f32[64,6,128]{2,1,0:T(8,128)S(1)} all-to-all(f32[64,6,128]{2,1,0:T(8,128)S(1)} %broadcast_in_dim.2), channel_id=1, replica_groups=mesh['sub'=64,'rhs'=4] {'sub'}, dimensions={0} | all-to-all | bytes 393216 | tf_op jit(solution)/shard_map/all_to_all | solution.py:260
  102.5 1.0 shard_map.70
  (25 shorter events, 0.1 us)
Async XLA Ops:
  0.7 1.0 %copy-start.2 = (f32[4,252,128]{2,0,1:T(4,128)S(1)}, f32[4,252,128]{2,0,1:T(4,128)}, u32[]{:S(2)}) copy-start(f32[4,252,128]{2,0,1:T(4,128)} %param.6) | copy-start | bytes 1548292
  1.8 4.4 %collective-permute-start.1 = (bf16[4,256,128]{2,1,0:T(8,128)(2,1)S(1)}, bf16[4,256,128]{2,1,0:T(8,128)(2,1)S(1)}, u32[]{:S(2)}, u32[]{:S(2)}) collective-permute-start(bf16[4,256,128]{2,1,0:T(8,128)(2,1)S(1)} %get-tuple-element.21), channel_id=1, source_target_pairs={{4,0},{8,4},{12,8},{16,12},{20,16},{24,20},{28,24},{32,28},{36,32}... | collective-permute-start | bytes 786440 | tf_op jit(solution)/shard_map/ppermute | solution.py:217
  3.1 4.2 %collective-permute-start = (bf16[4,256,128]{2,1,0:T(8,128)(2,1)S(1)}, bf16[4,256,128]{2,1,0:T(8,128)(2,1)S(1)}, u32[]{:S(2)}, u32[]{:S(2)}) collective-permute-start(bf16[4,256,128]{2,1,0:T(8,128)(2,1)S(1)} %get-tuple-element.21), channel_id=1, source_target_pairs={{0,4},{4,8},{8,12},{12,16},{16,20},{20,24},{24,28},{28,32},{32,36}... | collective-permute-start | bytes 786440 | tf_op jit(solution)/shard_map/ppermute | solution.py:217
  7.2 2.3 %copy-start = (bf16[1,1512,1512]{2,1,0:T(8,128)(2,1)S(1)}, bf16[1,1512,1512]{2,1,0:T(8,128)(2,1)}, u32[]{:S(2)}) copy-start(bf16[1,1512,1512]{2,1,0:T(8,128)(2,1)} %inverse.3) | copy-start | bytes 13716868
  9.6 0.7 copy-start.4
  10.2 17.9 %copy-start.1 = (bf16[4,508032]{1,0:T(4,128)(2,1)S(1)}, bf16[4,508032]{1,0:T(4,128)(2,1)}, u32[]{:S(2)}) copy-start(bf16[4,508032]{1,0:T(4,128)(2,1)} %flat.1) | copy-start | bytes 12192772
  12.3 28.5 %collective-permute-start.2 = (bf16[5,256,128]{2,1,0:T(8,128)(2,1)S(1)}, bf16[5,256,128]{2,1,0:T(8,128)(2,1)S(1)}, u32[]{:S(2)}, u32[]{:S(2)}) collective-permute-start(bf16[5,256,128]{2,1,0:T(8,128)(2,1)S(1)} %get-tuple-element.23.up), channel_id=1, source_target_pairs={{0,4},{4,8},{8,12},{12,16},{16,20},{20,24},{24,28},{28,32},{32,36}... | collective-permute-start | bytes 983048 | tf_op jit(solution)/shard_map/ppermute | solution.py:217
  17.9 22.9 %collective-permute-start.3 = (bf16[5,256,128]{2,1,0:T(8,128)(2,1)S(1)}, bf16[5,256,128]{2,1,0:T(8,128)(2,1)S(1)}, u32[]{:S(2)}, u32[]{:S(2)}) collective-permute-start(bf16[5,256,128]{2,1,0:T(8,128)(2,1)S(1)} %get-tuple-element.24.down), channel_id=1, source_target_pairs={{4,0},{8,4},{12,8},{16,12},{20,16},{24,20},{28,24},{32,28},{36,32}... | collective-permute-start | bytes 983048 | tf_op jit(solution)/shard_map/ppermute | solution.py:217
  19.3 21.6 %copy-start.3 = (s32[4,8]{1,0:T(4,128)S(1)}, s32[4,8]{1,0:T(4,128)}, u32[]{:S(2)}) copy-start(s32[4,8]{1,0:T(4,128)} %neighbours.3) | copy-start | bytes 388
  19.3 30.6 %slice-start = ((s8[4644864]{0:T(1024)(128)(4,1)}), s8[4194304]{0:T(1024)(128)(4,1)S(1)}, s32[]{:S(2)}) async-start(s8[4644864]{0:T(1024)(128)(4,1)} %bitcast.7), calls=%async_computation.1 | async-start | bytes 8388608
  19.3 30.6 %slice-start.1 = ((s8[4644864]{0:T(1024)(128)(4,1)}), s8[450560]{0:T(1024)(128)(4,1)S(1)}, s32[]{:S(2)}) async-start(s8[4644864]{0:T(1024)(128)(4,1)} %bitcast.7), calls=%async_computation.2 | async-start | bytes 901120
  19.3 21.5 %collective-permute-start.5 = (bf16[1,256,128]{2,1,0:T(8,128)(2,1)S(1)}, bf16[1,256,128]{2,1,0:T(8,128)(2,1)S(1)}, u32[]{:S(2)}, u32[]{:S(2)}) collective-permute-start(bf16[1,256,128]{2,1,0:T(8,128)(2,1)S(1)} %slice.19), channel_id=1, source_target_pairs={{8,0},{12,4},{16,8},{20,12},{24,16},{28,20},{32,24},{36,28},{40,32... | collective-permute-start | bytes 196616 | tf_op jit(solution)/shard_map/ppermute | solution.py:217
  20.9 20.0 %collective-permute-start.4 = (bf16[1,256,128]{2,1,0:T(8,128)(2,1)S(1)}, bf16[1,256,128]{2,1,0:T(8,128)(2,1)S(1)}, u32[]{:S(2)}, u32[]{:S(2)}) collective-permute-start(bf16[1,256,128]{2,1,0:T(8,128)(2,1)S(1)} %slice.18), channel_id=1, source_target_pairs={{0,8},{4,12},{8,16},{12,20},{16,24},{20,28},{24,32},{28,36},{32,40... | collective-permute-start | bytes 196616 | tf_op jit(solution)/shard_map/ppermute | solution.py:217
  40.8 9.1 %copy-start.5 = (s32[1,2]{1,0:T(1,128)S(1)}, s32[1,2]{1,0:T(1,128)}, u32[]{:S(2)}) copy-start(s32[1,2]{1,0:T(1,128)} %margin.3) | copy-start | bytes 28
  43.2 3.2 %collective-permute-start.6 = (bf16[1,256,128]{2,1,0:T(8,128)(2,1)S(1)}, bf16[1,256,128]{2,1,0:T(8,128)(2,1)S(1)}, u32[]{:S(2)}, u32[]{:S(2)}) collective-permute-start(bf16[1,256,128]{2,1,0:T(8,128)(2,1)S(1)} %get-tuple-element.27), channel_id=1, source_target_pairs={{0,4},{4,8},{8,12},{12,16},{16,20},{20,24},{24,28},{28,32},{32,36}... | collective-permute-start | bytes 196616 | tf_op jit(solution)/shard_map/ppermute | solution.py:217
  45.1 4.8 %collective-permute-start.7 = (bf16[1,256,128]{2,1,0:T(8,128)(2,1)S(1)}, bf16[1,256,128]{2,1,0:T(8,128)(2,1)S(1)}, u32[]{:S(2)}, u32[]{:S(2)}) collective-permute-start(bf16[1,256,128]{2,1,0:T(8,128)(2,1)S(1)} %get-tuple-element.28), channel_id=1, source_target_pairs={{4,0},{8,4},{12,8},{16,12},{20,16},{24,20},{28,24},{32,28},{36,32}... | collective-permute-start | bytes 196616 | tf_op jit(solution)/shard_map/ppermute | solution.py:217
  52.0 15.7 %collective-permute-start.8 = (bf16[5,256,128]{2,1,0:T(8,128)(2,1)S(1)}, bf16[5,256,128]{2,1,0:T(8,128)(2,1)S(1)}, u32[]{:S(2)}, u32[]{:S(2)}) collective-permute-start(bf16[5,256,128]{2,1,0:T(8,128)(2,1)S(1)} %get-tuple-element.30.up), channel_id=1, source_target_pairs={{0,4},{4,8},{8,12},{12,16},{16,20},{20,24},{24,28},{28,32},{32,36}... | collective-permute-start | bytes 983048 | tf_op jit(solution)/shard_map/ppermute | solution.py:217
  56.9 10.9 %collective-permute-start.9 = (bf16[5,256,128]{2,1,0:T(8,128)(2,1)S(1)}, bf16[5,256,128]{2,1,0:T(8,128)(2,1)S(1)}, u32[]{:S(2)}, u32[]{:S(2)}) collective-permute-start(bf16[5,256,128]{2,1,0:T(8,128)(2,1)S(1)} %get-tuple-element.31.down), channel_id=1, source_target_pairs={{4,0},{8,4},{12,8},{16,12},{20,16},{24,20},{28,24},{32,28},{36,32}... | collective-permute-start | bytes 983048 | tf_op jit(solution)/shard_map/ppermute | solution.py:217
  58.2 9.5 %collective-permute-start.11 = (bf16[1,256,128]{2,1,0:T(8,128)(2,1)S(1)}, bf16[1,256,128]{2,1,0:T(8,128)(2,1)S(1)}, u32[]{:S(2)}, u32[]{:S(2)}) collective-permute-start(bf16[1,256,128]{2,1,0:T(8,128)(2,1)S(1)} %slice.22), channel_id=1, source_target_pairs={{8,0},{12,4},{16,8},{20,12},{24,16},{28,20},{32,24},{36,28},{40,32... | collective-permute-start | bytes 196616 | tf_op jit(solution)/shard_map/ppermute | solution.py:217
  59.5 8.3 %collective-permute-start.10 = (bf16[1,256,128]{2,1,0:T(8,128)(2,1)S(1)}, bf16[1,256,128]{2,1,0:T(8,128)(2,1)S(1)}, u32[]{:S(2)}, u32[]{:S(2)}) collective-permute-start(bf16[1,256,128]{2,1,0:T(8,128)(2,1)S(1)} %slice.21), channel_id=1, source_target_pairs={{0,8},{4,12},{8,16},{12,20},{16,24},{20,28},{24,32},{28,36},{32,40... | collective-permute-start | bytes 196616 | tf_op jit(solution)/shard_map/ppermute | solution.py:217

commit v2 on v1

v2 whole, which is shorter than its diff:
```python
import functools
import jax
import jax.numpy as jnp
from jax import lax
from jax.experimental import pallas as pl
from jax.experimental.pallas import tpu as pltpu
from jax.sharding import PartitionSpec as P

EPS = 1e-06
W = 252
WP = 256
NS = 4
NB = 8
R = 128
NSUB = 64
SHIFT = 1.0
ROWS = NB * W
GROUP = 32
F32 = jnp.float32
BF16 = jnp.bfloat16
GROUPS = 32
CHUNKS = 4
ANY = pl.BlockSpec(memory_space=pl.ANY)
VM = pl.BlockSpec(memory_space=pltpu.VMEM)
SM = pl.BlockSpec(memory_space=pltpu.SMEM)


def call(kernel, outs, ins, scratch=(), limit=24, cost=None):
    return pl.pallas_call(
        kernel,
        out_shape=[pltpu.VMEM(s, d) if keep else jax.ShapeDtypeStruct(s, d) for s, d, *keep in outs],
        in_specs=ins,
        out_specs=[VM] * len(outs),
        scratch_shapes=list(scratch),
        compiler_params=pltpu.CompilerParams(vmem_limit_bytes=limit << 20),
        cost_estimate=cost,
    )


def start_kernel(counts, right, v0_ref, v0b_ref):
    for s in range(NS):
        alive = jnp.where(counts[0] > s, 1.0, 0.0)
        v0_ref[s, :W, :] = right[pl.ds(s, W, stride=NS), :] * alive
        v0_ref[s, W:, :] = jnp.zeros((WP - W, R), F32)
        v0b_ref[s] = v0_ref[s].astype(BF16)


def coupling_kernel(half, flat, *rest):
    if half == 0:
        inverse, c_ref, inverse_ref, raw, x, lo, hi, sems = rest
    else:
        _, c_ref, raw, x, lo, hi, sems = rest
    lanes = GROUP * W
    offset = half * (ROWS // GROUP // 2) * lanes
    step = GROUPS // CHUNKS * lanes
    copies = [
        pltpu.make_async_copy(
            flat.at[:, pl.ds(offset + c * step, step)], raw.at[:, pl.ds(c * step, step)], sems.at[c]
        )
        for c in range(CHUNKS)
    ]
    if half == 0:
        copies.append(pltpu.make_async_copy(inverse.at[0], inverse_ref, sems.at[CHUNKS]))
    for copy in copies:
        copy.start()
    lane = lax.broadcasted_iota(jnp.int32, (8, 128), 1)

    def pair(i, carry):
        for h in range(2):
            at = pl.multiple_of((2 * i + h) * lanes, 128)
            x[4 * h : 4 * h + 4, :] = raw[:, pl.ds(at, lanes)].astype(F32)
        base = pl.multiple_of(2 * i * (GROUP * NS), 8)
        for s in range(GROUP):
            def rolled(t):
                piece = x[:, 128 * t : 128 * t + 128]
                return pltpu.roll(piece, 4 * s, 1) if s else piece

            middle = rolled(2 * s)
            if s == 0:
                left, right = middle, rolled(1)
            else:
                early = lane < 4 * s
                left = jnp.where(early, rolled(2 * s - 1), middle)
                right = jnp.where(early, middle, rolled(2 * s + 1)) if s < GROUP - 1 else middle
            for h in range(2):
                at = base + (h * GROUP + s) * NS
                lo[pl.ds(at, NS), :] = left[4 * h : 4 * h + 4]
                hi[pl.ds(at, NS), :] = right[4 * h : 4 * h + 4]
        return carry

    for c in range(CHUNKS):
        copies[c].wait()
        pairs = GROUPS // CHUNKS // 2
        lax.fori_loop(c * pairs, (c + 1) * pairs, pair, 0)
    keep = lax.broadcasted_iota(jnp.int32, (WP, 128), 1) < W - 128
    pad = jnp.zeros((WP - W, 128), F32)
    skip = half * (NB // 2 * W - (ROWS // GROUP // 2) * GROUP) * NS

    def place(k, carry):
        for p in range(NS):
            first = skip + k * (W * NS) + p
            left = lo[pl.ds(first, W, stride=NS), :]
            right = hi[pl.ds(first, W, stride=NS), :]
            right = jnp.where(keep, jnp.concatenate([right, pad], axis=0), 0.0)
            c_ref[p * (NB // 2) + k, :, :128] = jnp.concatenate([left, pad], axis=0).astype(BF16)
            c_ref[p * (NB // 2) + k, :, 128:] = right.astype(BF16)
        return carry

    lax.fori_loop(0, NB // 2, place, 0)
    if half == 0:
        copies[CHUNKS].wait()


def solve_kernel(
    place, margin, inverse, own, inner, outer,
    out_ref, in_ref, out2_ref, ext, res,
):
    here = place[0]
    even = here % 2 == 0
    low = jnp.clip(margin[0, 0] - NS * jnp.maximum(here - 1, 0), 0, NS - 1)
    high = jnp.clip(margin[0, 1] - NS * jnp.minimum(here + 1, NSUB - 1), 0, NS - 1)
    first, last = here == 0, here == NSUB - 1
    for s in range(NS):
        ext[s * W : (s + 1) * W, :] = own[s, :W, :]
    some = inner.shape[0] > 1

    def put(when, block, source, index):
        @pl.when(when)
        def _():
            ext[block * W : (block + 1) * W, :] = source[index].astype(F32)[:W]

    put(first, NS, own, low)
    put(jnp.logical_and(even, jnp.logical_not(first)), NS, outer, low if some else 0)
    put(jnp.logical_not(even), NS, inner, low if some else 0)
    put(last, NS + 1, own, high)
    put(jnp.logical_not(jnp.logical_or(even, last)), NS + 1, outer, high if some else 0)
    put(even, NS + 1, inner, high if some else 0)
    res[...] = jnp.dot(inverse[...], ext[...].astype(BF16), preferred_element_type=F32)
    pad = jnp.zeros((WP - W, R), F32)
    mark = jnp.ones((WP - W, R), F32)
    for s in range(NS):
        out_ref[s] = jnp.concatenate([res[s * W : (s + 1) * W, :], pad], axis=0)

    def spill(block):
        return res[block * W : (block + 1) * W, :]

    def marked(block, index):
        return jnp.concatenate([spill(block), mark * index.astype(F32)], axis=0).astype(BF16)

    @pl.when(first)
    def _():
        out_ref[low] += jnp.concatenate([spill(NS), pad], axis=0)

    @pl.when(last)
    def _():
        out_ref[high] += jnp.concatenate([spill(NS + 1), pad], axis=0)

    @pl.when(even)
    def _():
        in_ref[0] = marked(NS + 1, high)
        out2_ref[0] = marked(NS, low)

    @pl.when(jnp.logical_not(even))
    def _():
        in_ref[0] = marked(NS, low)
        out2_ref[0] = marked(NS + 1, high)


def opened(block):
    x = block.astype(F32)
    rows = lax.broadcasted_iota(jnp.int32, x.shape, 0)
    return jnp.where(rows < W, x, 0.0), x[W : W + 1, :]


def inner_kernel(out, spill_in, spill_out, part_ref, sent_ref):
    values, index = opened(spill_in[0])
    for s in range(NS):
        part = out[s] + jnp.where(index == s, values, 0.0)
        part_ref[s] = part
        sent_ref[s] = part.astype(BF16)
    sent_ref[NS] = spill_out[0]


def outer_kernel(place, counts, part, got, spill_in, spill_out, p_ref, own_ref, outer_ref, marks_ref):
    here = place[0]
    ends = jnp.logical_or(here == 0, here == NSUB - 1)
    got_values, got_index = opened(got[NS])
    got_index = jnp.where(ends, -1.0, got_index)
    values, index = opened(spill_out[0])
    for s in range(NS):
        alive = jnp.where(counts[0] > s, 1.0, 0.0)
        p = (part[s] + jnp.where(got_index == s, got_values, 0.0)) * alive
        p_ref[s] = p
        own_ref[s] = p.astype(BF16)
        outer_ref[s] = (got[s].astype(F32) + jnp.where(index == s, values, 0.0)).astype(BF16)
    marks_ref[...] = jnp.concatenate([spill_in[0][WP - 8 :].astype(F32)[4:5]] * 4 + [got_index] * 4, axis=0)


def system_kernel(first, place, counts, neighbours, ca, cb, p, own, outer, inner, marks, v0, *rest):
    if first:
        w_ref, win_ref, wout_ref, sums_ref, u = rest
    else:
        w, sums_ref, u = rest
    here = place[0]
    odd = here % 2 == 1
    for s in range(NS):
        u[s] = outer[s]
        u[NS + s] = own[s]
        u[2 * NS + s] = inner[s]
    zero = jnp.zeros((1, R), F32)
    sums = [zero] * 3
    for s in range(NS):
        acc = jnp.zeros((WP, R), F32)
        for k in range(NB):
            slot = jnp.clip(neighbours[s, k] - NS * (here - 1), 0, 3 * NS - 1)
            slot = jnp.where(odd, slot + 2 * NS * (1 - slot // NS), slot)
            c_ref = ca if k < NB // 2 else cb
            acc += jnp.dot(c_ref[s * (NB // 2) + k % (NB // 2)], u[slot], preferred_element_type=F32)
        alive = jnp.where(counts[0] > s, 1.0, 0.0)
        image = (p[s] + acc) * alive
        start = v0[s]
        if first:
            image = image - SHIFT * start
            w_ref[s] = image
            terms = (start * start, start * image, image * image)
        else:
            terms = (start * image, w[s] * image, image * image)
        sums = [t + jnp.sum(x, axis=0, keepdims=True) for t, x in zip(sums, terms)]
    if first:
        for ref, index in ((win_ref, marks[0:1, :]), (wout_ref, marks[4:5, :])):
            chosen = jnp.zeros((WP, R), F32)
            for s in range(NS):
                chosen = chosen + jnp.where(index == s, w_ref[s], 0.0)
            ref[0] = chosen.astype(BF16)
    sums_ref[...] = jnp.concatenate(sums + [zero] * 5, axis=0)


def finish_kernel(gathered, p0, q, out):
    total = jnp.sum(gathered[...], axis=0)
    s00, s01, s11, s02, s12, s22 = (total[i : i + 1, :] for i in range(6))
    c = SHIFT
    bb = s00 + EPS
    beta = jnp.sqrt(bb)
    h11 = (s01 + c * s00) / bb
    a = c - h11
    n2 = (s11 + 2 * a * s01 + a * a * s00) / bb
    h21s = jnp.maximum(n2, 0.0) + EPS
    h21 = jnp.sqrt(h21s)
    full = bb * h21s
    v0i = s01 + c * s00
    h12 = (s02 + a * v0i) / (bb * h21)
    cross = (s01 + a * s00) / (bb * h21)
    b2i = (s12 + a * s02 + a * (s11 + c * s01) + a * a * v0i) / full
    h22 = b2i - h12 * cross
    ii = (s22 + 2 * a * (s12 + c * s02) + a * a * (s11 + 2 * c * s01 + c * c * s00)) / full
    rest = (
        ii + h12 * h12 * (s00 / bb) + h22 * h22 * (n2 / h21s)
        - 2 * h12 * h12 - 2 * h22 * b2i + 2 * h12 * h22 * cross
    )
    h32s = jnp.maximum(rest, 0.0) + EPS
    g00 = h11 * h11 + h21s
    g01 = h11 * h12 + h21 * h22
    g11 = h12 * h12 + h22 * h22 + h32s
    det = g00 * g11 - g01 * g01
    y1 = beta * (g11 * h11 - g01 * h12) / det
    y2 = beta * (g00 * h12 - g01 * h11) / det
    two = y2 / (beta * h21)
    one = y1 / beta + a * two
    for s in range(NS):
        out[pl.ds(s, W, stride=NS), :] = one * p0[s, :W, :] + two * q[s, :W, :]


def to_inner(x):
    return lax.ppermute(x, "sub", [(i, i ^ 1) for i in range(NSUB)])


def to_outer(x):
    return lax.ppermute(x, "sub", [(i, (((i + 1) ^ 1) - 1) % NSUB) for i in range(NSUB)])


def body(right_side, coupling, neighbours, inverse, margin, counts):
    here = lax.axis_index("sub").astype(jnp.int32).reshape(1)
    flat_right = right_side.transpose(1, 0, 2).reshape(W * NS, R)
    block, one = (NS, WP, R), (1, WP, R)
    v0, v0b = call(start_kernel, [(block, F32), (block, BF16)], [SM, VM])(counts, flat_right)
    outer, inner = to_outer(v0b), to_inner(v0b)

    def matrices(half, *more):
        lanes = GROUP * W
        outs = [((NS * NB // 2, WP, WP), BF16, True)]
        if half == 0:
            outs.append(((6 * W, 6 * W), BF16, True))
        return call(
            functools.partial(coupling_kernel, half),
            outs,
            [ANY, ANY],
            [
                pltpu.VMEM((NS, GROUPS * lanes), BF16),
                pltpu.VMEM((2 * NS, lanes), F32),
                pltpu.VMEM((GROUPS * GROUP * NS, 128), F32),
                pltpu.VMEM((GROUPS * GROUP * NS, 128), F32),
                pltpu.SemaphoreType.DMA((CHUNKS + 1,)),
            ],
            limit=24,
            cost=pl.CostEstimate(flops=1 << 20, bytes_accessed=12 << 20, transcendentals=0),
        )(coupling, *more)

    first_half, held = matrices(0, inverse)
    held = pltpu.with_memory_space_constraint(held, pltpu.VMEM)
    first_half = pltpu.with_memory_space_constraint(first_half, pltpu.VMEM)

    def solve(own, inner, outer):
        return call(
            solve_kernel,
            [(block, F32), (one, BF16), (one, BF16)],
            [SM, SM, VM, VM, VM, VM],
            [pltpu.VMEM((6 * W, R), F32)] * 2,
        )(here, margin, held, own, inner, outer)

    def joined(out, spill_in, spill_out):
        got_in = to_inner(spill_in)
        part, sent = call(inner_kernel, [(block, F32), ((NS + 1, WP, R), BF16)], [VM] * 3)(
            out, got_in, spill_out
        )
        got = to_outer(sent)
        p, own, outer, marks = call(
            outer_kernel,
            [(block, F32), (block, BF16), (block, BF16), ((8, R), F32)],
            [SM, SM] + [VM] * 4,
        )(here, counts, part, got, got_in, spill_out)
        return sent, p, own, outer, to_inner(own), marks

    def system(first, halves, p, own, outer, inner, marks, *more):
        outs = [(block, F32), (one, BF16), (one, BF16)] if first else []
        return call(
            functools.partial(system_kernel, first),
            outs + [((8, R), F32)],
            [SM, SM, SM] + [VM] * (7 + len(more)),
            [pltpu.VMEM((3 * NS, WP, R), BF16)],
        )(here, counts, neighbours, *halves, p, own, outer, inner, marks, *more)

    sent, p0, *rest = joined(*solve(v0, inner, outer))
    (second_half,) = matrices(1, sent)
    second_half = pltpu.with_memory_space_constraint(second_half, pltpu.VMEM)
    halves = first_half, second_half
    w, w_in, w_out, sums_one = system(True, halves, p0, *rest, v0)
    _, q, *rest = joined(*solve(w, to_inner(w_in), to_outer(w_out)))
    (sums_two,) = system(False, halves, q, *rest, v0, w)
    sums = jnp.concatenate([sums_one[:3], sums_two[:3]], axis=0)
    sums = sums + to_inner(sums)
    gathered = lax.all_to_all(
        jnp.broadcast_to(sums[None], (NSUB // 2, 6, R)), "sub", 0, 0,
        axis_index_groups=[list(range(c, NSUB, 2)) for c in range(2)],
    )
    (flat,) = call(finish_kernel, [((W * NS, R), F32)], [VM] * 3)(gathered, p0, q)
    return flat.reshape(W, NS, R).transpose(1, 0, 2)


def solution(mesh):
    placed = (
        P("sub", None, "rhs"),
        P("sub", None),
        P("sub", None),
        P("sub", None, None),
        P("sub", None),
        P("sub"),
    )
    return jax.shard_map(
        body, mesh=mesh, in_specs=placed, out_specs=P("sub", None, "rhs"), check_vma=False
    )
```

time: 105 us -> 80.7 us (0.77); the launches traced: 104 us -> 80.5 us
  starting transfers between devices: 36.4 us -> 12.8 us
  waiting for transfers between devices: 7.14 us -> 28.4 us
  blocking collectives: 32.4 us -> 13.9 us
  Pallas kernels: 22.6 us -> 19 us
  local copies, waits for them, and re-layouts: 4.08 us -> 5.53 us
    ppermute x12 -> x11, starting transfers between devices: 36.4 us -> 12.8 us  [the longest x4 10.9 us: to_outer(): lax.ppermute(x, 'sub', [(i, ((i + 1 ^ 1) - 1) % NSUB) for i in range(NSUB)])]
    ppermute x12 -> x11, waiting for transfers between devices: 7.14 us -> 28.4 us  [the longest x4 23.7 us: to_outer(): lax.ppermute(x, 'sub', [(i, ((i + 1 ^ 1) - 1) % NSUB) for i in range(NSUB)])]
    all_to_all x1, blocking collectives: 32.4 us -> 13.9 us  [body(): lax.all_to_all(jnp.broadcast_to(sums[None], (NSUB // 2, 6, R)), 'sub', 0,...]
    pallas_call x5 -> x10, Pallas kernels: 21.5 us -> 17.9 us  [the longest x2 9.48 us: matrices(): call(functools.partial(coupling_kernel, half), outs, [ANY, ANY], [pltpu.V...]
    unnamed x16 -> x12, local copies, waits for them, and re-layouts: 4.03 us -> 5.51 us
  transfers between devices with their start and end apart: 12 -> 11, of which waited for: 3 -> 7; matrix products, arithmetic and copies ran while one was open for 0% -> 0% of each run, Pallas kernels for 12% -> 12%
where the time goes in v2:
time: 80.7 us; the launch traced here: 80.5 us
  waiting for transfers between devices  28.4 us (35%)
  Pallas kernels  19 us (24%)
  blocking collectives  13.9 us (17%)
  starting transfers between devices  12.8 us (16%)
  local copies, waits for them, and re-layouts  5.53 us (7%)
  between operations  0.84 us (1%)
    ppermute x4, waiting for transfers between devices, to_outer(): lax.ppermute(x, 'sub', [(i, ((i + 1 ^ 1) - 1) % NSUB) for i in range(NSUB)])  23.7 us
    all_to_all x1, blocking collectives, body(): lax.all_to_all(jnp.broadcast_to(sums[None], (NSUB // 2, 6, R)), 'sub', 0,...  13.9 us
    ppermute x4, starting transfers between devices, to_outer(): lax.ppermute(x, 'sub', [(i, ((i + 1 ^ 1) - 1) % NSUB) for i in range(NSUB)])  10.9 us
    pallas_call x2, Pallas kernels, matrices(): call(functools.partial(coupling_kernel, half), outs, [ANY, ANY], [pltpu.V...  9.48 us
    unnamed x12, local copies, waits for them, and re-layouts  5.51 us
    ppermute x7, waiting for transfers between devices, to_inner(): return lax.ppermute(x, 'sub', [(i, i ^ 1) for i in range(NSUB)])  4.7 us
    pallas_call x2, Pallas kernels, solve(): call(solve_kernel, [(block, F32), (one, BF16), (one, BF16)], [SM, SM, VM,...  4.16 us
    pallas_call x2, Pallas kernels, system(): call(functools.partial(system_kernel, first), outs + [((8, R), F32)], [SM...  3.87 us
  transfers between devices with their start and end apart: 11, of which 7 were waited for; matrix products, arithmetic and copies ran while one was open for 0% of the time, Pallas kernels for 12%

profile of v2, /device:TPU:2, one launch (start us, length us, event | category | flops | bytes accessed | tf_op | source)
XLA Modules:
  0.0 80.5 jit_solution(9002971353973145506)
XLA Ops:
  0.7 1.0 %copy-done.3 = f32[4,252,128]{2,0,1:T(4,128)S(1)} copy-done((f32[4,252,128]{2,0,1:T(4,128)S(1)}, f32[4,252,128]{2,0,1:T(4,128)}, u32[]{:S(2)}) %copy-start.3) | copy-done | bytes 516120
  1.8 7.8 %collective-permute-start.1 = (bf16[4,256,128]{2,1,0:T(8,128)(2,1)S(1)}, bf16[4,256,128]{2,1,0:T(8,128)(2,1)S(1)}, u32[]{:S(2)}, u32[]{:S(2)}) collective-permute-start(bf16[4,256,128]{2,1,0:T(8,128)(2,1)S(1)} %get-tuple-element.34), channel_id=1, source_target_pairs={{0,252},{4,8},{8,4},{12,16},{16,12},{20,24},{24,20},{28,32},{32,28... | collective-permute-start | bytes 786440 | tf_op jit(solution)/shard_map/ppermute | solution.py:278
  9.6 2.1 %copy-done = bf16[4,508032]{1,0:T(4,128)(2,1)S(1)} copy-done((bf16[4,508032]{1,0:T(4,128)(2,1)S(1)}, bf16[4,508032]{1,0:T(4,128)(2,1)}, u32[]{:S(2)}) %copy-start) | copy-done | bytes 4064280
  11.7 2.3 %copy-done.2 = bf16[1,1512,1512]{2,1,0:T(8,128)(2,1)S(1)} copy-done((bf16[1,1512,1512]{2,1,0:T(8,128)(2,1)S(1)}, bf16[1,1512,1512]{2,1,0:T(8,128)(2,1)}, u32[]{:S(2)}) %copy-start.2) | copy-done | bytes 4572312
  14.1 5.0 %shard_map.64 = (bf16[16,256,256]{2,1,0:T(8,128)(2,1)S(1)}, bf16[1512,1512]{1,0:T(8,128)(2,1)S(1)}) custom-call(bf16[4,508032]{1,0:T(4,128)(2,1)S(1)} %copy-done, bf16[1,1512,1512]{2,1,0:T(8,128)(2,1)S(1)} %copy-done.2), custom_call_target="tpu_custom_call" | custom-call | flops 1048576 | bytes 12582912 | tf_op jit(solution)/shard_map/pallas_call | solution.py:293
  19.1 2.1 %shard_map.66 = (f32[4,256,128]{2,1,0:T(8,128)S(1)}, bf16[1,256,128]{2,1,0:T(8,128)(2,1)S(1)}, bf16[1,256,128]{2,1,0:T(8,128)(2,1)S(1)}) custom-call(s32[1]{0:T(128)} %bitcast.place, s32[1,2]{1,0:T(1,128)S(1)} %copy-done.5, bf16[1512,1512]{1,0:T(8,128)(2,1)S(1)} %get-tuple-element.32.inverse, f32[4,256,128]{2,1,0:T(8,128)S(1)} %get-tuple-element.33.own.v0, ...), custom_call_target="tpu_custom_call" | custom-call | tf_op jit(solution)/shard_map/pallas_call | solution.py:313
  21.2 0.6 collective-permute-start.2
  21.8 0.9 %collective-permute-done.2.spill_in = bf16[1,256,128]{2,1,0:T(8,128)(2,1)S(1)} collective-permute-done((bf16[1,256,128]{2,1,0:T(8,128)(2,1)S(1)}, bf16[1,256,128]{2,1,0:T(8,128)(2,1)S(1)}, u32[]{:S(2)}, u32[]{:S(2)}) %collective-permute-start.2) | collective-permute-done | bytes 65568 | tf_op jit(solution)/shard_map/ppermute | solution.py:274
  22.7 0.1 shard_map.67
  22.8 1.1 %collective-permute-start.3 = (bf16[5,256,128]{2,1,0:T(8,128)(2,1)S(1)}, bf16[5,256,128]{2,1,0:T(8,128)(2,1)S(1)}, u32[]{:S(2)}, u32[]{:S(2)}) collective-permute-start(bf16[5,256,128]{2,1,0:T(8,128)(2,1)S(1)} %get-tuple-element.38.rest_0_), channel_id=1, source_target_pairs={{0,252},{4,8},{8,4},{12,16},{16,12},{20,24},{24,20},{28,32},{32,28... | collective-permute-start | bytes 983048 | tf_op jit(solution)/shard_map/ppermute | solution.py:278
  23.8 8.8 %collective-permute-done.3.got = bf16[5,256,128]{2,1,0:T(8,128)(2,1)S(1)} collective-permute-done((bf16[5,256,128]{2,1,0:T(8,128)(2,1)S(1)}, bf16[5,256,128]{2,1,0:T(8,128)(2,1)S(1)}, u32[]{:S(2)}, u32[]{:S(2)}) %collective-permute-start.3) | collective-permute-done | bytes 327712 | tf_op jit(solution)/shard_map/ppermute | solution.py:278
  32.7 0.2 shard_map.69
  32.8 0.1 collective-permute-start.4
  33.0 4.5 %shard_map.68.cb = bf16[16,256,256]{2,1,0:T(8,128)(2,1)S(1)} custom-call(bf16[4,508032]{1,0:T(4,128)(2,1)S(1)} %copy-done.1, bf16[5,256,128]{2,1,0:T(8,128)(2,1)S(1)} %get-tuple-element.38.rest_0_), custom_call_target="tpu_custom_call" | custom-call | flops 1048576 | bytes 12582912 | tf_op jit(solution)/shard_map/pallas_call | solution.py:293
  37.5 1.9 %shard_map.70 = (f32[4,256,128]{2,1,0:T(8,128)S(1)}, bf16[1,256,128]{2,1,0:T(8,128)(2,1)S(1)}, bf16[1,256,128]{2,1,0:T(8,128)(2,1)S(1)}, f32[8,128]{1,0:T(8,128)S(1)}) custom-call(s32[1]{0:T(128)} %bitcast.place, s32[1]{0:T(128)S(6)} %copy.7.counts, s32[4,8]{1,0:T(4,128)S(1)} %copy-done.4, bf16[16,256,256]{2,1,0:T(8,128)(2,1)S(1)} %get-tuple-element.31.ca, ...), custom_call_target="tpu_custom_call" | custom-call | tf_op jit(solution)/shard_map/pallas_call | solution.py:335
  39.4 0.6 collective-permute-start.5
  40.0 1.0 %collective-permute-start.6 = (bf16[1,256,128]{2,1,0:T(8,128)(2,1)S(1)}, bf16[1,256,128]{2,1,0:T(8,128)(2,1)S(1)}, u32[]{:S(2)}, u32[]{:S(2)}) collective-permute-start(bf16[1,256,128]{2,1,0:T(8,128)(2,1)S(1)} %get-tuple-element.47), channel_id=1, source_target_pairs={{0,252},{4,8},{8,4},{12,16},{16,12},{20,24},{24,20},{28,32},{32,28... | collective-permute-start | bytes 196616 | tf_op jit(solution)/shard_map/ppermute | solution.py:278
  40.9 6.0 %collective-permute-done.6.outer = bf16[1,256,128]{2,1,0:T(8,128)(2,1)S(1)} collective-permute-done((bf16[1,256,128]{2,1,0:T(8,128)(2,1)S(1)}, bf16[1,256,128]{2,1,0:T(8,128)(2,1)S(1)}, u32[]{:S(2)}, u32[]{:S(2)}) %collective-permute-start.6) | collective-permute-done | bytes 65568 | tf_op jit(solution)/shard_map/ppermute | solution.py:278
  47.0 2.1 %shard_map.71 = (f32[4,256,128]{2,1,0:T(8,128)S(1)}, bf16[1,256,128]{2,1,0:T(8,128)(2,1)S(1)}, bf16[1,256,128]{2,1,0:T(8,128)(2,1)S(1)}) custom-call(s32[1]{0:T(128)} %bitcast.place, s32[1,2]{1,0:T(1,128)S(1)} %copy-done.5, bf16[1512,1512]{1,0:T(8,128)(2,1)S(1)} %get-tuple-element.32.inverse, f32[4,256,128]{2,1,0:T(8,128)S(1)} %get-tuple-element.45.own.rest_0_, ...), custom_call_target="tpu_custom_call" | custom-call | tf_op jit(solution)/shard_map/pallas_call | solution.py:313
  49.1 0.1 collective-permute-start.7
  49.2 1.2 %collective-permute-done.7.spill_in = bf16[1,256,128]{2,1,0:T(8,128)(2,1)S(1)} collective-permute-done((bf16[1,256,128]{2,1,0:T(8,128)(2,1)S(1)}, bf16[1,256,128]{2,1,0:T(8,128)(2,1)S(1)}, u32[]{:S(2)}, u32[]{:S(2)}) %collective-permute-start.7) | collective-permute-done | bytes 65568 | tf_op jit(solution)/shard_map/ppermute | solution.py:274
  50.4 0.1 shard_map.72
  50.5 1.1 %collective-permute-start.8 = (bf16[5,256,128]{2,1,0:T(8,128)(2,1)S(1)}, bf16[5,256,128]{2,1,0:T(8,128)(2,1)S(1)}, u32[]{:S(2)}, u32[]{:S(2)}) collective-permute-start(bf16[5,256,128]{2,1,0:T(8,128)(2,1)S(1)} %get-tuple-element.52), channel_id=1, source_target_pairs={{0,252},{4,8},{8,4},{12,16},{16,12},{20,24},{24,20},{28,32},{32,28... | collective-permute-start | bytes 983048 | tf_op jit(solution)/shard_map/ppermute | solution.py:278
  51.5 8.8 %collective-permute-done.8.got = bf16[5,256,128]{2,1,0:T(8,128)(2,1)S(1)} collective-permute-done((bf16[5,256,128]{2,1,0:T(8,128)(2,1)S(1)}, bf16[5,256,128]{2,1,0:T(8,128)(2,1)S(1)}, u32[]{:S(2)}, u32[]{:S(2)}) %collective-permute-start.8) | collective-permute-done | bytes 327712 | tf_op jit(solution)/shard_map/ppermute | solution.py:278
  60.4 0.2 shard_map.73
  60.5 0.3 collective-permute-start.9
  60.8 1.5 %collective-permute-done.9.inner = bf16[4,256,128]{2,1,0:T(8,128)(2,1)S(1)} collective-permute-done((bf16[4,256,128]{2,1,0:T(8,128)(2,1)S(1)}, bf16[4,256,128]{2,1,0:T(8,128)(2,1)S(1)}, u32[]{:S(2)}, u32[]{:S(2)}) %collective-permute-start.9) | collective-permute-done | bytes 262176 | tf_op jit(solution)/shard_map/ppermute | solution.py:274
  62.3 1.9 %shard_map.74 = f32[8,128]{1,0:T(8,128)S(1)} custom-call(s32[1]{0:T(128)} %bitcast.place, s32[1]{0:T(128)S(6)} %copy.7.counts, s32[4,8]{1,0:T(4,128)S(1)} %copy-done.4, bf16[16,256,256]{2,1,0:T(8,128)(2,1)S(1)} %get-tuple-element.31.ca, bf16[16,256,256]{2,1,0:T(8,128)(2,1)S(1)} %shard_map.68.cb, f32[4,256,128]{2,1,0:T(8,128)S(1)} %get-tuple-element.53.p.q, ...), custom_call_target="tpu_custom_call" | custom-call | tf_op jit(solution)/shard_map/pallas_call | solution.py:335
  64.3 0.2 collective-permute-start.10
  64.5 1.0 %collective-permute-done.10 = f32[6,128]{1,0:T(8,128)S(1)} collective-permute-done((f32[6,128]{1,0:T(8,128)S(1)}, f32[6,128]{1,0:T(8,128)S(1)}, u32[]{:S(2)}, u32[]{:S(2)}) %collective-permute-start.10) | collective-permute-done | bytes 3104 | tf_op jit(solution)/shard_map/ppermute | solution.py:274
  65.6 13.9 %all_to_all.5.gathered = f32[32,6,128]{2,1,0:T(8,128)S(1)} all-to-all(f32[32,6,128]{2,1,0:T(8,128)S(1)} %broadcast_in_dim.2), channel_id=1, replica_groups={{0,8,16,24,32,40,48,56,64,72,80,88,96,104,112,120,128,136,144,152,160,1..., dimensions={0} | all-to-all | bytes 196608 | tf_op jit(solution)/shard_map/all_to_all | solution.py:351
  79.5 1.0 %shard_map.75 = f32[1008,128]{1,0:T(8,128)} custom-call(f32[32,6,128]{2,1,0:T(8,128)S(1)} %all_to_all.5.gathered, f32[4,256,128]{2,1,0:T(8,128)S(1)} %get-tuple-element.40.p.p0, f32[4,256,128]{2,1,0:T(8,128)S(1)} %get-tuple-element.53.p.q), custom_call_target="tpu_custom_call" | custom-call | tf_op jit(solution)/shard_map/pallas_call | solution.py:355
  (20 shorter events, 0.1 us)
Async XLA Ops:
  0.7 1.0 %copy-start.3 = (f32[4,252,128]{2,0,1:T(4,128)S(1)}, f32[4,252,128]{2,0,1:T(4,128)}, u32[]{:S(2)}) copy-start(f32[4,252,128]{2,0,1:T(4,128)} %param.6) | copy-start | bytes 1548292
  1.8 17.3 %collective-permute-start.1 = (bf16[4,256,128]{2,1,0:T(8,128)(2,1)S(1)}, bf16[4,256,128]{2,1,0:T(8,128)(2,1)S(1)}, u32[]{:S(2)}, u32[]{:S(2)}) collective-permute-start(bf16[4,256,128]{2,1,0:T(8,128)(2,1)S(1)} %get-tuple-element.34), channel_id=1, source_target_pairs={{0,252},{4,8},{8,4},{12,16},{16,12},{20,24},{24,20},{28,32},{32,28... | collective-permute-start | bytes 786440 | tf_op jit(solution)/shard_map/ppermute | solution.py:278
  9.6 9.5 %collective-permute-start = (bf16[4,256,128]{2,1,0:T(8,128)(2,1)S(1)}, bf16[4,256,128]{2,1,0:T(8,128)(2,1)S(1)}, u32[]{:S(2)}, u32[]{:S(2)}) collective-permute-start(bf16[4,256,128]{2,1,0:T(8,128)(2,1)S(1)} %get-tuple-element.34), channel_id=1, source_target_pairs={{0,4},{4,0},{8,12},{12,8},{16,20},{20,16},{24,28},{28,24},{32,36},... | collective-permute-start | bytes 786440 | tf_op jit(solution)/shard_map/ppermute | solution.py:274
  9.6 2.2 %copy-start = (bf16[4,508032]{1,0:T(4,128)(2,1)S(1)}, bf16[4,508032]{1,0:T(4,128)(2,1)}, u32[]{:S(2)}) copy-start(bf16[4,508032]{1,0:T(4,128)(2,1)} %flat.3) | copy-start | bytes 12192772
  11.7 2.3 %copy-start.2 = (bf16[1,1512,1512]{2,1,0:T(8,128)(2,1)S(1)}, bf16[1,1512,1512]{2,1,0:T(8,128)(2,1)}, u32[]{:S(2)}) copy-start(bf16[1,1512,1512]{2,1,0:T(8,128)(2,1)} %rest_0_.1) | copy-start | bytes 13716868
  14.1 5.1 %copy-start.5 = (s32[1,2]{1,0:T(1,128)S(1)}, s32[1,2]{1,0:T(1,128)}, u32[]{:S(2)}) copy-start(s32[1,2]{1,0:T(1,128)} %margin.3) | copy-start | bytes 28
  19.1 13.9 %copy-start.1 = (bf16[4,508032]{1,0:T(4,128)(2,1)S(1)}, bf16[4,508032]{1,0:T(4,128)(2,1)}, u32[]{:S(2)}) copy-start(bf16[4,508032]{1,0:T(4,128)(2,1)} %flat.3) | copy-start | bytes 12192772
  21.2 1.5 %collective-permute-start.2 = (bf16[1,256,128]{2,1,0:T(8,128)(2,1)S(1)}, bf16[1,256,128]{2,1,0:T(8,128)(2,1)S(1)}, u32[]{:S(2)}, u32[]{:S(2)}) collective-permute-start(bf16[1,256,128]{2,1,0:T(8,128)(2,1)S(1)} %get-tuple-element.36), channel_id=1, source_target_pairs={{0,4},{4,0},{8,12},{12,8},{16,20},{20,16},{24,28},{28,24},{32,36},... | collective-permute-start | bytes 196616 | tf_op jit(solution)/shard_map/ppermute | solution.py:274
  22.7 14.7 %copy-start.4 = (s32[4,8]{1,0:T(4,128)S(1)}, s32[4,8]{1,0:T(4,128)}, u32[]{:S(2)}) copy-start(s32[4,8]{1,0:T(4,128)} %neighbours.3) | copy-start | bytes 388
  22.8 9.9 %collective-permute-start.3 = (bf16[5,256,128]{2,1,0:T(8,128)(2,1)S(1)}, bf16[5,256,128]{2,1,0:T(8,128)(2,1)S(1)}, u32[]{:S(2)}, u32[]{:S(2)}) collective-permute-start(bf16[5,256,128]{2,1,0:T(8,128)(2,1)S(1)} %get-tuple-element.38.rest_0_), channel_id=1, source_target_pairs={{0,252},{4,8},{8,4},{12,16},{16,12},{20,24},{24,20},{28,32},{32,28... | collective-permute-start | bytes 983048 | tf_op jit(solution)/shard_map/ppermute | solution.py:278
  32.8 4.6 %collective-permute-start.4 = (bf16[4,256,128]{2,1,0:T(8,128)(2,1)S(1)}, bf16[4,256,128]{2,1,0:T(8,128)(2,1)S(1)}, u32[]{:S(2)}, u32[]{:S(2)}) collective-permute-start(bf16[4,256,128]{2,1,0:T(8,128)(2,1)S(1)} %get-tuple-element.41.own), channel_id=1, source_target_pairs={{0,4},{4,0},{8,12},{12,8},{16,20},{20,16},{24,28},{28,24},{32,36},... | collective-permute-start | bytes 786440 | tf_op jit(solution)/shard_map/ppermute | solution.py:274
  39.4 1.5 %collective-permute-start.5 = (bf16[1,256,128]{2,1,0:T(8,128)(2,1)S(1)}, bf16[1,256,128]{2,1,0:T(8,128)(2,1)S(1)}, u32[]{:S(2)}, u32[]{:S(2)}) collective-permute-start(bf16[1,256,128]{2,1,0:T(8,128)(2,1)S(1)} %get-tuple-element.46), channel_id=1, source_target_pairs={{0,4},{4,0},{8,12},{12,8},{16,20},{20,16},{24,28},{28,24},{32,36},... | collective-permute-start | bytes 196616 | tf_op jit(solution)/shard_map/ppermute | solution.py:274
  40.0 7.0 %collective-permute-start.6 = (bf16[1,256,128]{2,1,0:T(8,128)(2,1)S(1)}, bf16[1,256,128]{2,1,0:T(8,128)(2,1)S(1)}, u32[]{:S(2)}, u32[]{:S(2)}) collective-permute-start(bf16[1,256,128]{2,1,0:T(8,128)(2,1)S(1)} %get-tuple-element.47), channel_id=1, source_target_pairs={{0,252},{4,8},{8,4},{12,16},{16,12},{20,24},{24,20},{28,32},{32,28... | collective-permute-start | bytes 196616 | tf_op jit(solution)/shard_map/ppermute | solution.py:278
  49.1 1.3 %collective-permute-start.7 = (bf16[1,256,128]{2,1,0:T(8,128)(2,1)S(1)}, bf16[1,256,128]{2,1,0:T(8,128)(2,1)S(1)}, u32[]{:S(2)}, u32[]{:S(2)}) collective-permute-start(bf16[1,256,128]{2,1,0:T(8,128)(2,1)S(1)} %get-tuple-element.49), channel_id=1, source_target_pairs={{0,4},{4,0},{8,12},{12,8},{16,20},{20,16},{24,28},{28,24},{32,36},... | collective-permute-start | bytes 196616 | tf_op jit(solution)/shard_map/ppermute | solution.py:274
  50.5 9.9 %collective-permute-start.8 = (bf16[5,256,128]{2,1,0:T(8,128)(2,1)S(1)}, bf16[5,256,128]{2,1,0:T(8,128)(2,1)S(1)}, u32[]{:S(2)}, u32[]{:S(2)}) collective-permute-start(bf16[5,256,128]{2,1,0:T(8,128)(2,1)S(1)} %get-tuple-element.52), channel_id=1, source_target_pairs={{0,252},{4,8},{8,4},{12,16},{16,12},{20,24},{24,20},{28,32},{32,28... | collective-permute-start | bytes 983048 | tf_op jit(solution)/shard_map/ppermute | solution.py:278
  60.5 1.8 %collective-permute-start.9 = (bf16[4,256,128]{2,1,0:T(8,128)(2,1)S(1)}, bf16[4,256,128]{2,1,0:T(8,128)(2,1)S(1)}, u32[]{:S(2)}, u32[]{:S(2)}) collective-permute-start(bf16[4,256,128]{2,1,0:T(8,128)(2,1)S(1)} %get-tuple-element.54.own), channel_id=1, source_target_pairs={{0,4},{4,0},{8,12},{12,8},{16,20},{20,16},{24,28},{28,24},{32,36},... | collective-permute-start | bytes 786440 | tf_op jit(solution)/shard_map/ppermute | solution.py:274
  64.3 1.3 %collective-permute-start.10 = (f32[6,128]{1,0:T(8,128)S(1)}, f32[6,128]{1,0:T(8,128)S(1)}, u32[]{:S(2)}, u32[]{:S(2)}) collective-permute-start(f32[6,128]{1,0:T(8,128)S(1)} %pad_maximum_fusion), channel_id=1, source_target_pairs={{0,4},{4,0},{8,12},{12,8},{16,20},{20,16},{24,28},{28,24},{32,36},... | collective-permute-start | bytes 9224 | tf_op jit(solution)/shard_map/ppermute | solution.py:274

commit v3 on v2

--- a/solution.py
+++ b/solution.py
@@ -18,8 +18,10 @@
 GROUP = 32
 F32 = jnp.float32
 BF16 = jnp.bfloat16
-GROUPS = 32
-CHUNKS = 4
+CHUNK = 8
+SPLIT = 2
+OWN = 1024
+FROM = 896
 ANY = pl.BlockSpec(memory_space=pl.ANY)
 VM = pl.BlockSpec(memory_space=pltpu.VMEM)
 SM = pl.BlockSpec(memory_space=pltpu.SMEM)
@@ -45,22 +47,25 @@
         v0b_ref[s] = v0_ref[s].astype(BF16)
 
 
-def coupling_kernel(half, flat, *rest):
-    if half == 0:
+def coupling_kernel(blocks, groups, first, flat, *rest):
+    if first:
         inverse, c_ref, inverse_ref, raw, x, lo, hi, sems = rest
     else:
         _, c_ref, raw, x, lo, hi, sems = rest
     lanes = GROUP * W
-    offset = half * (ROWS // GROUP // 2) * lanes
-    step = GROUPS // CHUNKS * lanes
+    count = groups[1] - groups[0]
+    step = CHUNK * lanes
+    chunks = count // CHUNK
     copies = [
         pltpu.make_async_copy(
-            flat.at[:, pl.ds(offset + c * step, step)], raw.at[:, pl.ds(c * step, step)], sems.at[c]
+            flat.at[:, pl.ds(groups[0] * lanes + c * step, step)],
+            raw.at[:, pl.ds(c * step, step)],
+            sems.at[c],
         )
-        for c in range(CHUNKS)
+        for c in range(chunks)
     ]
-    if half == 0:
-        copies.append(pltpu.make_async_copy(inverse.at[0], inverse_ref, sems.at[CHUNKS]))
+    if first:
+        copies.append(pltpu.make_async_copy(inverse.at[0], inverse_ref, sems.at[chunks]))
     for copy in copies:
         copy.start()
     lane = lax.broadcasted_iota(jnp.int32, (8, 128), 1)
@@ -88,82 +93,102 @@
                 hi[pl.ds(at, NS), :] = right[4 * h : 4 * h + 4]
         return carry
 
-    for c in range(CHUNKS):
+    for c in range(chunks):
         copies[c].wait()
-        pairs = GROUPS // CHUNKS // 2
-        lax.fori_loop(c * pairs, (c + 1) * pairs, pair, 0)
+        lax.fori_loop(c * CHUNK // 2, (c + 1) * CHUNK // 2, pair, 0)
     keep = lax.broadcasted_iota(jnp.int32, (WP, 128), 1) < W - 128
     pad = jnp.zeros((WP - W, 128), F32)
-    skip = half * (NB // 2 * W - (ROWS // GROUP // 2) * GROUP) * NS
+    skip = (blocks[0] * W - groups[0] * GROUP) * NS
+    number = blocks[1] - blocks[0]
 
     def place(k, carry):
         for p in range(NS):
-            first = skip + k * (W * NS) + p
-            left = lo[pl.ds(first, W, stride=NS), :]
-            right = hi[pl.ds(first, W, stride=NS), :]
+            row = skip + k * (W * NS) + p
+            left = lo[pl.ds(row, W, stride=NS), :]
+            right = hi[pl.ds(row, W, stride=NS), :]
             right = jnp.where(keep, jnp.concatenate([right, pad], axis=0), 0.0)
-            c_ref[p * (NB // 2) + k, :, :128] = jnp.concatenate([left, pad], axis=0).astype(BF16)
-            c_ref[p * (NB // 2) + k, :, 128:] = right.astype(BF16)
+            c_ref[p * number + k, :, :128] = jnp.concatenate([left, pad], axis=0).astype(BF16)
+            c_ref[p * number + k, :, 128:] = right.astype(BF16)
         return carry
 
-    lax.fori_loop(0, NB // 2, place, 0)
-    if half == 0:
-        copies[CHUNKS].wait()
-
-
-def solve_kernel(
-    place, margin, inverse, own, inner, outer,
-    out_ref, in_ref, out2_ref, ext, res,
-):
+    lax.fori_loop(0, number, place, 0)
+    if first:
+        copies[chunks].wait()
+
+
+def own_kernel(inverse, own, part_ref, ext):
+    for s in range(NS):
+        ext[s * W : (s + 1) * W, :] = own[s, :W, :]
+    ext[NS * W :, :] = jnp.zeros((OWN - NS * W, R), F32)
+    part_ref[...] = jnp.dot(inverse[:, :OWN], ext[...].astype(BF16), preferred_element_type=F32)
+
+
+def places(place, margin):
     here = place[0]
-    even = here % 2 == 0
     low = jnp.clip(margin[0, 0] - NS * jnp.maximum(here - 1, 0), 0, NS - 1)
     high = jnp.clip(margin[0, 1] - NS * jnp.minimum(here + 1, NSUB - 1), 0, NS - 1)
-    first, last = here == 0, here == NSUB - 1
-    for s in range(NS):
-        ext[s * W : (s + 1) * W, :] = own[s, :W, :]
+    return here % 2 == 0, here == 0, here == NSUB - 1, low, high
+
+
+def spilled(inverse, part, ext, block, index):
+    begin = block * W // 16 * 16
+    end = -(-(block + 1) * W // 16) * 16
+    end = min(end, 6 * W)
+    rows = jnp.dot(inverse[begin:end, FROM:], ext, preferred_element_type=F32)
+    rows = rows[block * W - begin : (block + 1) * W - begin] + part[block * W : (block + 1) * W, :]
+    mark = jnp.ones((WP - W, R), F32) * index.astype(F32)
+    return jnp.concatenate([rows, mark], axis=0)
+
+
+def margin_kernel(place, margin, inverse, part, own, inner, outer, in_ref, ext_ref, ext):
+    even, first, last, low, high = places(place, margin)
+    odd = jnp.logical_not(even)
+    ext[: NS * W - FROM, :] = jnp.zeros((NS * W - FROM, R), F32)
     some = inner.shape[0] > 1
 
     def put(when, block, source, index):
         @pl.when(when)
         def _():
-            ext[block * W : (block + 1) * W, :] = source[index].astype(F32)[:W]
+            ext[block * W - FROM : (block + 1) * W - FROM, :] = source[index].astype(F32)[:W]
 
     put(first, NS, own, low)
     put(jnp.logical_and(even, jnp.logical_not(first)), NS, outer, low if some else 0)
-    put(jnp.logical_not(even), NS, inner, low if some else 0)
+    put(odd, NS, inner, low if some else 0)
     put(last, NS + 1, own, high)
-    put(jnp.logical_not(jnp.logical_or(even, last)), NS + 1, outer, high if some else 0)
+    put(jnp.logical_and(odd, jnp.logical_not(last)), NS + 1, outer, high if some else 0)
     put(even, NS + 1, inner, high if some else 0)
-    res[...] = jnp.dot(inverse[...], ext[...].astype(BF16), preferred_element_type=F32)
-    pad = jnp.zeros((WP - W, R), F32)
-    mark = jnp.ones((WP - W, R), F32)
-    for s in range(NS):
-        out_ref[s] = jnp.concatenate([res[s * W : (s + 1) * W, :], pad], axis=0)
-
-    def spill(block):
-        return res[block * W : (block + 1) * W, :]
-
-    def marked(block, index):
-        return jnp.concatenate([spill(block), mark * index.astype(F32)], axis=0).astype(BF16)
-
-    @pl.when(first)
-    def _():
-        out_ref[low] += jnp.concatenate([spill(NS), pad], axis=0)
-
-    @pl.when(last)
-    def _():
-        out_ref[high] += jnp.concatenate([spill(NS + 1), pad], axis=0)
+    ext_ref[...] = ext[...].astype(BF16)
 
     @pl.when(even)
     def _():
-        in_ref[0] = marked(NS + 1, high)
-        out2_ref[0] = marked(NS, low)
-
-    @pl.when(jnp.logical_not(even))
+        in_ref[0] = spilled(inverse, part, ext_ref[...], NS + 1, high).astype(BF16)
+
+    @pl.when(odd)
     def _():
-        in_ref[0] = marked(NS, low)
-        out2_ref[0] = marked(NS + 1, high)
+        in_ref[0] = spilled(inverse, part, ext_ref[...], NS, low).astype(BF16)
+
+
+def solve_kernel(place, margin, inverse, part, ext, out_ref, out2_ref, res):
+    even, first, last, low, high = places(place, margin)
+    mine = NS * W
+    res[...] = part[:mine, :] + jnp.dot(inverse[:mine, FROM:], ext[...], preferred_element_type=F32)
+    pad = jnp.zeros((WP - W, R), F32)
+    for s in range(NS):
+        out_ref[s] = jnp.concatenate([res[s * W : (s + 1) * W, :], pad], axis=0)
+    keep = lax.broadcasted_iota(jnp.int32, (WP, R), 0) < W
+
+    def spill(when, ends, block, index):
+        @pl.when(when)
+        def _():
+            rows = spilled(inverse, part, ext[...], block, index)
+            out2_ref[0] = rows.astype(BF16)
+
+            @pl.when(ends)
+            def _():
+                out_ref[index] += jnp.where(keep, rows, 0.0)
+
+    spill(even, first, NS, low)
+    spill(jnp.logical_not(even), last, NS + 1, high)
 
 
 def opened(block):
@@ -181,7 +206,8 @@
     sent_ref[NS] = spill_out[0]
 
 
-def outer_kernel(place, counts, part, got, spill_in, spill_out, p_ref, own_ref, outer_ref, marks_ref):
+def outer_kernel(place, counts, part, got, spill_in, spill_out, *rest):
+    p_ref, own_ref, outer_ref, marks_ref = rest[-4:]
     here = place[0]
     ends = jnp.logical_or(here == 0, here == NSUB - 1)
     got_values, got_index = opened(got[NS])
@@ -214,8 +240,8 @@
         for k in range(NB):
             slot = jnp.clip(neighbours[s, k] - NS * (here - 1), 0, 3 * NS - 1)
             slot = jnp.where(odd, slot + 2 * NS * (1 - slot // NS), slot)
-            c_ref = ca if k < NB // 2 else cb
-            acc += jnp.dot(c_ref[s * (NB // 2) + k % (NB // 2)], u[slot], preferred_element_type=F32)
+            matrix = ca[s * SPLIT + k] if k < SPLIT else cb[s * (NB - SPLIT) + k - SPLIT]
+            acc += jnp.dot(matrix, u[slot], preferred_element_type=F32)
         alive = jnp.where(counts[0] > s, 1.0, 0.0)
         image = (p[s] + acc) * alive
         start = v0[s]
@@ -285,50 +311,72 @@
     v0, v0b = call(start_kernel, [(block, F32), (block, BF16)], [SM, VM])(counts, flat_right)
     outer, inner = to_outer(v0b), to_inner(v0b)
 
-    def matrices(half, *more):
+    coupling = pltpu.with_memory_space_constraint(coupling, pltpu.HBM)
+    inverse = pltpu.with_memory_space_constraint(inverse, pltpu.HBM)
+
+    def matrices(first, more):
         lanes = GROUP * W
-        outs = [((NS * NB // 2, WP, WP), BF16, True)]
-        if half == 0:
+        blocks = (0, SPLIT) if first else (SPLIT, NB)
+        begin = blocks[0] * W // GROUP
+        end = -(-blocks[1] * W // GROUP)
+        count = -(-(end - begin) // CHUNK) * CHUNK
+        groups = (begin, begin + count) if first else (end - count, end)
+        outs = [((NS * (blocks[1] - blocks[0]), WP, WP), BF16, True)]
+        if first:
             outs.append(((6 * W, 6 * W), BF16, True))
         return call(
-            functools.partial(coupling_kernel, half),
+            functools.partial(coupling_kernel, blocks, groups, first),
             outs,
             [ANY, ANY],
             [
-                pltpu.VMEM((NS, GROUPS * lanes), BF16),
+                pltpu.VMEM((NS, count * lanes), BF16),
                 pltpu.VMEM((2 * NS, lanes), F32),
-                pltpu.VMEM((GROUPS * GROUP * NS, 128), F32),
-                pltpu.VMEM((GROUPS * GROUP * NS, 128), F32),
-                pltpu.SemaphoreType.DMA((CHUNKS + 1,)),
+                pltpu.VMEM((count * GROUP * NS, 128), F32),
+                pltpu.VMEM((count * GROUP * NS, 128), F32),
+                pltpu.SemaphoreType.DMA((count // CHUNK + 1,)),
             ],
             limit=24,
             cost=pl.CostEstimate(flops=1 << 20, bytes_accessed=12 << 20, transcendentals=0),
-        )(coupling, *more)
-
-    first_half, held = matrices(0, inverse)
+        )(coupling, more)
+
+    first_part, held = matrices(True, inverse)
     held = pltpu.with_memory_space_constraint(held, pltpu.VMEM)
-    first_half = pltpu.with_memory_space_constraint(first_half, pltpu.VMEM)
+    first_part = pltpu.with_memory_space_constraint(first_part, pltpu.VMEM)
 
     def solve(own, inner, outer):
-        return call(
+        (part,) = call(
+            own_kernel, [((6 * W, R), F32, True)], [VM, VM], [pltpu.VMEM((OWN, R), F32)],
+            cost=pl.CostEstimate(flops=1 << 30, bytes_accessed=4 << 20, transcendentals=0),
+        )(held, own)
+        depth = 6 * W - FROM
+        spill_in, ext = call(
+            margin_kernel,
+            [(one, BF16), ((depth, R), BF16)],
+            [SM, SM] + [VM] * 5,
+            [pltpu.VMEM((depth, R), F32)],
+        )(here, margin, held, part, own, inner, outer)
+        got_in = to_inner(spill_in)
+        out, spill_out = call(
             solve_kernel,
-            [(block, F32), (one, BF16), (one, BF16)],
-            [SM, SM, VM, VM, VM, VM],
-            [pltpu.VMEM((6 * W, R), F32)] * 2,
-        )(here, margin, held, own, inner, outer)
-
-    def joined(out, spill_in, spill_out):
-        got_in = to_inner(spill_in)
+            [(block, F32), (one, BF16)],
+            [SM, SM] + [VM] * 3,
+            [pltpu.VMEM((NS * W, R), F32)],
+            cost=pl.CostEstimate(flops=1 << 30, bytes_accessed=4 << 20, transcendentals=0),
+        )(here, margin, held, part, ext)
+        return out, got_in, spill_out
+
+    def joined(out, got_in, spill_out, meanwhile=None):
         part, sent = call(inner_kernel, [(block, F32), ((NS + 1, WP, R), BF16)], [VM] * 3)(
             out, got_in, spill_out
         )
         got = to_outer(sent)
+        done = meanwhile(sent) if meanwhile else []
         p, own, outer, marks = call(
             outer_kernel,
             [(block, F32), (block, BF16), (block, BF16), ((8, R), F32)],
-            [SM, SM] + [VM] * 4,
-        )(here, counts, part, got, got_in, spill_out)
-        return sent, p, own, outer, to_inner(own), marks
+            [SM, SM] + [VM] * 4 + [ANY] * len(done),
+        )(here, counts, part, got, got_in, spill_out, *done)
+        return done, p, own, outer, to_inner(own), marks
 
     def system(first, halves, p, own, outer, inner, marks, *more):
         outs = [(block, F32), (one, BF16), (one, BF16)] if first else []
@@ -339,10 +387,12 @@
             [pltpu.VMEM((3 * NS, WP, R), BF16)],
         )(here, counts, neighbours, *halves, p, own, outer, inner, marks, *more)
 
-    sent, p0, *rest = joined(*solve(v0, inner, outer))
-    (second_half,) = matrices(1, sent)
-    second_half = pltpu.with_memory_space_constraint(second_half, pltpu.VMEM)
-    halves = first_half, second_half
+    def second(sent):
+        (made,) = matrices(False, sent)
+        return [pltpu.with_memory_space_constraint(made, pltpu.VMEM)]
+
+    (second_part,), p0, *rest = joined(*solve(v0, inner, outer), second)
+    halves = first_part, second_part
     w, w_in, w_out, sums_one = system(True, halves, p0, *rest, v0)
     _, q, *rest = joined(*solve(w, to_inner(w_in), to_outer(w_out)))
     (sums_two,) = system(False, halves, q, *rest, v0, w)

time: 80.7 us -> 73.2 us (0.907)
  waiting for transfers between devices: 28.4 us -> 12 us
  starting transfers between devices: 12.8 us -> 22.3 us
  local copies, waits for them, and re-layouts: 5.53 us -> 1.06 us
  blocking collectives: 13.9 us -> 16.4 us
  Pallas kernels: 19 us -> 20.2 us
    ppermute x4, waiting for transfers between devices: 23.7 us -> 7.95 us  [to_outer(): lax.ppermute(x, 'sub', [(i, ((i + 1 ^ 1) - 1) % NSUB) for i in range(NSUB)])]
    ppermute x4, starting transfers between devices: 10.9 us -> 21.2 us  [to_outer(): lax.ppermute(x, 'sub', [(i, ((i + 1 ^ 1) - 1) % NSUB) for i in range(NSUB)])]
    unnamed x12 -> x6, local copies, waits for them, and re-layouts: 5.51 us -> 1.04 us
    all_to_all x1, blocking collectives: 13.9 us -> 16.4 us  [body(): lax.all_to_all(jnp.broadcast_to(sums[None], (NSUB // 2, 6, R)), 'sub', 0,...]
    pallas_call x4 -> x8, Pallas kernels: 13.6 us -> 14.9 us  [the longest x2 8.34 us: matrices(): call(functools.partial(coupling_kernel, blocks, groups, first), outs, [AN...]
  transfers between devices with their start and end apart: 11 -> 11, of which waited for: 7 -> 6; matrix products, arithmetic and copies ran while one was open for 0% -> 0% of each run, Pallas kernels for 12% -> 18%
where the time goes in v3:
time: 73.2 us; the launch traced here: 73 us
  starting transfers between devices  22.3 us (30%)
  Pallas kernels  20.2 us (28%)
  blocking collectives  16.4 us (22%)
  waiting for transfers between devices  12 us (16%)
  local copies, waits for them, and re-layouts  1.06 us (1%)
  between operations  0.87 us (1%)
    ppermute x4, starting transfers between devices, to_outer(): lax.ppermute(x, 'sub', [(i, ((i + 1 ^ 1) - 1) % NSUB) for i in range(NSUB)])  21.2 us
    all_to_all x1, blocking collectives, body(): lax.all_to_all(jnp.broadcast_to(sums[None], (NSUB // 2, 6, R)), 'sub', 0,...  16.4 us
    pallas_call x2, Pallas kernels, matrices(): call(functools.partial(coupling_kernel, blocks, groups, first), outs, [AN...  8.34 us
    ppermute x4, waiting for transfers between devices, to_outer(): lax.ppermute(x, 'sub', [(i, ((i + 1 ^ 1) - 1) % NSUB) for i in range(NSUB)])  7.95 us
    ppermute x7, waiting for transfers between devices, to_inner(): return lax.ppermute(x, 'sub', [(i, i ^ 1) for i in range(NSUB)])  4.07 us
    pallas_call x2, Pallas kernels, system(): call(functools.partial(system_kernel, first), outs + [((8, R), F32)], [SM...  3.9 us
    pallas_call x2, Pallas kernels, solve(): call(solve_kernel, [(block, F32), (one, BF16)], [SM, SM] + [VM] * 3, [plt...  2.79 us
    pallas_call x2, Pallas kernels, solve(): call(own_kernel, [((6 * W, R), F32, True)], [VM, VM], [pltpu.VMEM((OWN, R...  1.97 us
  transfers between devices with their start and end apart: 11, of which 6 were waited for; matrix products, arithmetic and copies ran while one was open for 0% of the time, Pallas kernels for 18%

profile of v3, /device:TPU:2, one launch (start us, length us, event | category | flops | bytes accessed | tf_op | source)
XLA Modules:
  0.0 73.0 jit_solution(11330850948979613824)
XLA Ops:
  0.7 1.0 %copy-done = f32[4,252,128]{2,0,1:T(4,128)S(1)} copy-done((f32[4,252,128]{2,0,1:T(4,128)S(1)}, f32[4,252,128]{2,0,1:T(4,128)}, u32[]{:S(2)}) %copy-start) | copy-done | bytes 516120
  1.8 7.8 %collective-permute-start.1 = (bf16[4,256,128]{2,1,0:T(8,128)(2,1)S(1)}, bf16[4,256,128]{2,1,0:T(8,128)(2,1)S(1)}, u32[]{:S(2)}, u32[]{:S(2)}) collective-permute-start(bf16[4,256,128]{2,1,0:T(8,128)(2,1)S(1)} %get-tuple-element.36), channel_id=1, source_target_pairs={{0,252},{4,8},{8,4},{12,16},{16,12},{20,24},{24,20},{28,32},{32,28... | collective-permute-start | bytes 786440 | tf_op jit(solution)/shard_map/ppermute | solution.py:304
  9.6 2.7 %shard_map.64 = (bf16[8,256,256]{2,1,0:T(8,128)(2,1)S(1)}, bf16[1512,1512]{1,0:T(8,128)(2,1)S(1)}) custom-call(bf16[4,508032]{1,0:T(4,128)(2,1)} %flat.3, bf16[1,1512,1512]{2,1,0:T(8,128)(2,1)} %rest_0_.1), custom_call_target="tpu_custom_call" | custom-call | flops 1048576 | bytes 12582912 | tf_op jit(solution)/shard_map/pallas_call | solution.py:327
  12.3 1.0 %shard_map.66.part = f32[1512,128]{1,0:T(8,128)S(1)} custom-call(bf16[1512,1512]{1,0:T(8,128)(2,1)S(1)} %get-tuple-element.34.inverse, f32[4,256,128]{2,1,0:T(8,128)S(1)} %get-tuple-element.35.own.v0), custom_call_target="tpu_custom_call" | custom-call | flops 1073741824 | bytes 4194304 | tf_op jit(solution)/shard_map/pallas_call | solution.py:347
  13.3 0.4 collective-permute-done.1.outer
  13.7 0.9 %shard_map.67 = (bf16[1,256,128]{2,1,0:T(8,128)(2,1)S(1)}, bf16[616,128]{1,0:T(8,128)(2,1)S(1)}) custom-call(s32[1]{0:T(128)} %bitcast.place, s32[1,2]{1,0:T(1,128)S(1)} %copy-done.2, bf16[1512,1512]{1,0:T(8,128)(2,1)S(1)} %get-tuple-element.34.inverse, f32[1512,128]{1,0:T(8,128)S(1)} %shard_map.66.part, f32[4,256,128]{2,1,0:T(8,128)S(1)} %get-tuple-element.35.own.v0, ...), custom_call_target="tpu_custom_call" | custom-call | tf_op jit(solution)/shard_map/pallas_call | solution.py:352
  14.5 0.2 collective-permute-start.2
  14.8 1.4 %shard_map.68 = (f32[4,256,128]{2,1,0:T(8,128)S(1)}, bf16[1,256,128]{2,1,0:T(8,128)(2,1)S(1)}) custom-call(s32[1]{0:T(128)} %bitcast.place, s32[1,2]{1,0:T(1,128)S(1)} %copy-done.2, bf16[1512,1512]{1,0:T(8,128)(2,1)S(1)} %get-tuple-element.34.inverse, f32[1512,128]{1,0:T(8,128)S(1)} %shard_map.66.part, bf16[616,128]{1,0:T(8,128)(2,1)S(1)} %get-tuple-element.37.ext), custom_call_target="tpu_custom_call" | custom-call | flops 1073741824 | bytes 4194304 | tf_op jit(solution)/shard_map/pallas_call | solution.py:359
  16.2 0.1 shard_map.69
  16.3 5.1 %collective-permute-start.3 = (bf16[5,256,128]{2,1,0:T(8,128)(2,1)S(1)}, bf16[5,256,128]{2,1,0:T(8,128)(2,1)S(1)}, u32[]{:S(2)}, u32[]{:S(2)}) collective-permute-start(bf16[5,256,128]{2,1,0:T(8,128)(2,1)S(1)} %get-tuple-element.41.rest_0_), channel_id=1, source_target_pairs={{0,252},{4,8},{8,4},{12,16},{16,12},{20,24},{24,20},{28,32},{32,28... | collective-permute-start | bytes 983048 | tf_op jit(solution)/shard_map/ppermute | solution.py:304
  21.3 5.7 %shard_map.70.rest_0_.cb = bf16[24,256,256]{2,1,0:T(8,128)(2,1)S(1)} custom-call(bf16[4,508032]{1,0:T(4,128)(2,1)} %flat.3, bf16[5,256,128]{2,1,0:T(8,128)(2,1)S(1)} %get-tuple-element.41.rest_0_), custom_call_target="tpu_custom_call" | custom-call | flops 1048576 | bytes 12582912 | tf_op jit(solution)/shard_map/pallas_call | solution.py:327
  27.0 0.1 shard_map.71
  27.2 0.1 collective-permute-start.4
  27.3 1.5 %collective-permute-done.4.inner = bf16[4,256,128]{2,1,0:T(8,128)(2,1)S(1)} collective-permute-done((bf16[4,256,128]{2,1,0:T(8,128)(2,1)S(1)}, bf16[4,256,128]{2,1,0:T(8,128)(2,1)S(1)}, u32[]{:S(2)}, u32[]{:S(2)}) %collective-permute-start.4) | collective-permute-done | bytes 262176 | tf_op jit(solution)/shard_map/ppermute | solution.py:300
  28.8 2.0 %shard_map.72 = (f32[4,256,128]{2,1,0:T(8,128)S(1)}, bf16[1,256,128]{2,1,0:T(8,128)(2,1)S(1)}, bf16[1,256,128]{2,1,0:T(8,128)(2,1)S(1)}, f32[8,128]{1,0:T(8,128)S(1)}) custom-call(s32[1]{0:T(128)} %bitcast.place, s32[1]{0:T(128)S(6)} %copy.7.counts, s32[4,8]{1,0:T(4,128)S(1)} %copy-done.1, bf16[8,256,256]{2,1,0:T(8,128)(2,1)S(1)} %get-tuple-element.33.ca, ...), custom_call_target="tpu_custom_call" | custom-call | tf_op jit(solution)/shard_map/pallas_call | solution.py:383
  30.7 0.2 collective-permute-start.5
  31.0 4.1 %collective-permute-start.6 = (bf16[1,256,128]{2,1,0:T(8,128)(2,1)S(1)}, bf16[1,256,128]{2,1,0:T(8,128)(2,1)S(1)}, u32[]{:S(2)}, u32[]{:S(2)}) collective-permute-start(bf16[1,256,128]{2,1,0:T(8,128)(2,1)S(1)} %get-tuple-element.50), channel_id=1, source_target_pairs={{0,252},{4,8},{8,4},{12,16},{16,12},{20,24},{24,20},{28,32},{32,28... | collective-permute-start | bytes 196616 | tf_op jit(solution)/shard_map/ppermute | solution.py:304
  35.1 1.0 %shard_map.73.part = f32[1512,128]{1,0:T(8,128)S(1)} custom-call(bf16[1512,1512]{1,0:T(8,128)(2,1)S(1)} %get-tuple-element.34.inverse, f32[4,256,128]{2,1,0:T(8,128)S(1)} %get-tuple-element.48.own.rest_0_), custom_call_target="tpu_custom_call" | custom-call | flops 1073741824 | bytes 4194304 | tf_op jit(solution)/shard_map/pallas_call | solution.py:347
  36.1 1.9 %collective-permute-done.6.outer = bf16[1,256,128]{2,1,0:T(8,128)(2,1)S(1)} collective-permute-done((bf16[1,256,128]{2,1,0:T(8,128)(2,1)S(1)}, bf16[1,256,128]{2,1,0:T(8,128)(2,1)S(1)}, u32[]{:S(2)}, u32[]{:S(2)}) %collective-permute-start.6) | collective-permute-done | bytes 65568 | tf_op jit(solution)/shard_map/ppermute | solution.py:304
  38.0 0.9 %shard_map.74 = (bf16[1,256,128]{2,1,0:T(8,128)(2,1)S(1)}, bf16[616,128]{1,0:T(8,128)(2,1)S(1)}) custom-call(s32[1]{0:T(128)} %bitcast.place, s32[1,2]{1,0:T(1,128)S(1)} %copy-done.2, bf16[1512,1512]{1,0:T(8,128)(2,1)S(1)} %get-tuple-element.34.inverse, f32[1512,128]{1,0:T(8,128)S(1)} %shard_map.73.part, f32[4,256,128]{2,1,0:T(8,128)S(1)} %get-tuple-element.48.own.rest_0_, ...), custom_call_target="tpu_custom_call" | custom-call | tf_op jit(solution)/shard_map/pallas_call | solution.py:352
  38.9 0.1 collective-permute-start.7
  39.0 1.4 %shard_map.75 = (f32[4,256,128]{2,1,0:T(8,128)S(1)}, bf16[1,256,128]{2,1,0:T(8,128)(2,1)S(1)}) custom-call(s32[1]{0:T(128)} %bitcast.place, s32[1,2]{1,0:T(1,128)S(1)} %copy-done.2, bf16[1512,1512]{1,0:T(8,128)(2,1)S(1)} %get-tuple-element.34.inverse, f32[1512,128]{1,0:T(8,128)S(1)} %shard_map.73.part, bf16[616,128]{1,0:T(8,128)(2,1)S(1)} %get-tuple-element.51.ext), custom_call_target="tpu_custom_call" | custom-call | flops 1073741824 | bytes 4194304 | tf_op jit(solution)/shard_map/pallas_call | solution.py:359
  40.5 4.2 %collective-permute-start.8 = (bf16[5,256,128]{2,1,0:T(8,128)(2,1)S(1)}, bf16[5,256,128]{2,1,0:T(8,128)(2,1)S(1)}, u32[]{:S(2)}, u32[]{:S(2)}) collective-permute-start(bf16[5,256,128]{2,1,0:T(8,128)(2,1)S(1)} %get-tuple-element.56), channel_id=1, source_target_pairs={{0,252},{4,8},{8,4},{12,16},{16,12},{20,24},{24,20},{28,32},{32,28... | collective-permute-start | bytes 983048 | tf_op jit(solution)/shard_map/ppermute | solution.py:304
  44.7 5.7 %collective-permute-done.8.got = bf16[5,256,128]{2,1,0:T(8,128)(2,1)S(1)} collective-permute-done((bf16[5,256,128]{2,1,0:T(8,128)(2,1)S(1)}, bf16[5,256,128]{2,1,0:T(8,128)(2,1)S(1)}, u32[]{:S(2)}, u32[]{:S(2)}) %collective-permute-start.8) | collective-permute-done | bytes 327712 | tf_op jit(solution)/shard_map/ppermute | solution.py:304
  50.4 0.2 shard_map.77
  50.5 0.3 collective-permute-start.9
  50.8 1.5 %collective-permute-done.9.inner = bf16[4,256,128]{2,1,0:T(8,128)(2,1)S(1)} collective-permute-done((bf16[4,256,128]{2,1,0:T(8,128)(2,1)S(1)}, bf16[4,256,128]{2,1,0:T(8,128)(2,1)S(1)}, u32[]{:S(2)}, u32[]{:S(2)}) %collective-permute-start.9) | collective-permute-done | bytes 262176 | tf_op jit(solution)/shard_map/ppermute | solution.py:300
  52.3 1.9 %shard_map.78 = f32[8,128]{1,0:T(8,128)S(1)} custom-call(s32[1]{0:T(128)} %bitcast.place, s32[1]{0:T(128)S(6)} %copy.7.counts, s32[4,8]{1,0:T(4,128)S(1)} %copy-done.1, bf16[8,256,256]{2,1,0:T(8,128)(2,1)S(1)} %get-tuple-element.33.ca, bf16[24,256,256]{2,1,0:T(8,128)(2,1)S(1)} %shard_map.70.rest_0_.cb, f32[4,256,128]{2,1,0:T(8,128)S(1)} %get-tuple-element.57.p.q, ...), custom_call_target="tpu_custom_call" | custom-call | tf_op jit(solution)/shard_map/pallas_call | solution.py:383
  54.3 0.2 collective-permute-start.10
  54.5 1.0 %collective-permute-done.10 = f32[6,128]{1,0:T(8,128)S(1)} collective-permute-done((f32[6,128]{1,0:T(8,128)S(1)}, f32[6,128]{1,0:T(8,128)S(1)}, u32[]{:S(2)}, u32[]{:S(2)}) %collective-permute-start.10) | collective-permute-done | bytes 3104 | tf_op jit(solution)/shard_map/ppermute | solution.py:300
  55.6 16.4 %all_to_all.5.gathered = f32[32,6,128]{2,1,0:T(8,128)S(1)} all-to-all(f32[32,6,128]{2,1,0:T(8,128)S(1)} %broadcast_in_dim.2), channel_id=1, replica_groups={{0,8,16,24,32,40,48,56,64,72,80,88,96,104,112,120,128,136,144,152,160,1..., dimensions={0} | all-to-all | bytes 196608 | tf_op jit(solution)/shard_map/all_to_all | solution.py:401
  72.0 1.0 %shard_map.79 = f32[1008,128]{1,0:T(8,128)} custom-call(f32[32,6,128]{2,1,0:T(8,128)S(1)} %all_to_all.5.gathered, f32[4,256,128]{2,1,0:T(8,128)S(1)} %get-tuple-element.43.p.p0, f32[4,256,128]{2,1,0:T(8,128)S(1)} %get-tuple-element.57.p.q), custom_call_target="tpu_custom_call" | custom-call | tf_op jit(solution)/shard_map/pallas_call | solution.py:405
  (18 shorter events, 0.2 us)
Async XLA Ops:
  0.7 1.0 %copy-start = (f32[4,252,128]{2,0,1:T(4,128)S(1)}, f32[4,252,128]{2,0,1:T(4,128)}, u32[]{:S(2)}) copy-start(f32[4,252,128]{2,0,1:T(4,128)} %param.6) | copy-start | bytes 1548292
  1.8 11.9 %collective-permute-start.1 = (bf16[4,256,128]{2,1,0:T(8,128)(2,1)S(1)}, bf16[4,256,128]{2,1,0:T(8,128)(2,1)S(1)}, u32[]{:S(2)}, u32[]{:S(2)}) collective-permute-start(bf16[4,256,128]{2,1,0:T(8,128)(2,1)S(1)} %get-tuple-element.36), channel_id=1, source_target_pairs={{0,252},{4,8},{8,4},{12,16},{16,12},{20,24},{24,20},{28,32},{32,28... | collective-permute-start | bytes 786440 | tf_op jit(solution)/shard_map/ppermute | solution.py:304
  9.6 4.1 %collective-permute-start = (bf16[4,256,128]{2,1,0:T(8,128)(2,1)S(1)}, bf16[4,256,128]{2,1,0:T(8,128)(2,1)S(1)}, u32[]{:S(2)}, u32[]{:S(2)}) collective-permute-start(bf16[4,256,128]{2,1,0:T(8,128)(2,1)S(1)} %get-tuple-element.36), channel_id=1, source_target_pairs={{0,4},{4,0},{8,12},{12,8},{16,20},{20,16},{24,28},{28,24},{32,36},... | collective-permute-start | bytes 786440 | tf_op jit(solution)/shard_map/ppermute | solution.py:300
  12.3 1.4 %copy-start.2 = (s32[1,2]{1,0:T(1,128)S(1)}, s32[1,2]{1,0:T(1,128)}, u32[]{:S(2)}) copy-start(s32[1,2]{1,0:T(1,128)} %margin.7) | copy-start | bytes 28
  14.5 1.6 %collective-permute-start.2 = (bf16[1,256,128]{2,1,0:T(8,128)(2,1)S(1)}, bf16[1,256,128]{2,1,0:T(8,128)(2,1)S(1)}, u32[]{:S(2)}, u32[]{:S(2)}) collective-permute-start(bf16[1,256,128]{2,1,0:T(8,128)(2,1)S(1)} %get-tuple-element.39), channel_id=1, source_target_pairs={{0,4},{4,0},{8,12},{12,8},{16,20},{20,16},{24,28},{28,24},{32,36},... | collective-permute-start | bytes 196616 | tf_op jit(solution)/shard_map/ppermute | solution.py:300
  16.2 12.5 %copy-start.1 = (s32[4,8]{1,0:T(4,128)S(1)}, s32[4,8]{1,0:T(4,128)}, u32[]{:S(2)}) copy-start(s32[4,8]{1,0:T(4,128)} %neighbours.3) | copy-start | bytes 388
  16.3 10.7 %collective-permute-start.3 = (bf16[5,256,128]{2,1,0:T(8,128)(2,1)S(1)}, bf16[5,256,128]{2,1,0:T(8,128)(2,1)S(1)}, u32[]{:S(2)}, u32[]{:S(2)}) collective-permute-start(bf16[5,256,128]{2,1,0:T(8,128)(2,1)S(1)} %get-tuple-element.41.rest_0_), channel_id=1, source_target_pairs={{0,252},{4,8},{8,4},{12,16},{16,12},{20,24},{24,20},{28,32},{32,28... | collective-permute-start | bytes 983048 | tf_op jit(solution)/shard_map/ppermute | solution.py:304
  27.2 1.6 %collective-permute-start.4 = (bf16[4,256,128]{2,1,0:T(8,128)(2,1)S(1)}, bf16[4,256,128]{2,1,0:T(8,128)(2,1)S(1)}, u32[]{:S(2)}, u32[]{:S(2)}) collective-permute-start(bf16[4,256,128]{2,1,0:T(8,128)(2,1)S(1)} %get-tuple-element.44.own), channel_id=1, source_target_pairs={{0,4},{4,0},{8,12},{12,8},{16,20},{20,16},{24,28},{28,24},{32,36},... | collective-permute-start | bytes 786440 | tf_op jit(solution)/shard_map/ppermute | solution.py:300
  30.7 5.3 %collective-permute-start.5 = (bf16[1,256,128]{2,1,0:T(8,128)(2,1)S(1)}, bf16[1,256,128]{2,1,0:T(8,128)(2,1)S(1)}, u32[]{:S(2)}, u32[]{:S(2)}) collective-permute-start(bf16[1,256,128]{2,1,0:T(8,128)(2,1)S(1)} %get-tuple-element.49), channel_id=1, source_target_pairs={{0,4},{4,0},{8,12},{12,8},{16,20},{20,16},{24,28},{28,24},{32,36},... | collective-permute-start | bytes 196616 | tf_op jit(solution)/shard_map/ppermute | solution.py:300
  31.0 7.0 %collective-permute-start.6 = (bf16[1,256,128]{2,1,0:T(8,128)(2,1)S(1)}, bf16[1,256,128]{2,1,0:T(8,128)(2,1)S(1)}, u32[]{:S(2)}, u32[]{:S(2)}) collective-permute-start(bf16[1,256,128]{2,1,0:T(8,128)(2,1)S(1)} %get-tuple-element.50), channel_id=1, source_target_pairs={{0,252},{4,8},{8,4},{12,16},{16,12},{20,24},{24,20},{28,32},{32,28... | collective-permute-start | bytes 196616 | tf_op jit(solution)/shard_map/ppermute | solution.py:304
  38.9 1.5 %collective-permute-start.7 = (bf16[1,256,128]{2,1,0:T(8,128)(2,1)S(1)}, bf16[1,256,128]{2,1,0:T(8,128)(2,1)S(1)}, u32[]{:S(2)}, u32[]{:S(2)}) collective-permute-start(bf16[1,256,128]{2,1,0:T(8,128)(2,1)S(1)} %get-tuple-element.53), channel_id=1, source_target_pairs={{0,4},{4,0},{8,12},{12,8},{16,20},{20,16},{24,28},{28,24},{32,36},... | collective-permute-start | bytes 196616 | tf_op jit(solution)/shard_map/ppermute | solution.py:300
  40.5 9.9 %collective-permute-start.8 = (bf16[5,256,128]{2,1,0:T(8,128)(2,1)S(1)}, bf16[5,256,128]{2,1,0:T(8,128)(2,1)S(1)}, u32[]{:S(2)}, u32[]{:S(2)}) collective-permute-start(bf16[5,256,128]{2,1,0:T(8,128)(2,1)S(1)} %get-tuple-element.56), channel_id=1, source_target_pairs={{0,252},{4,8},{8,4},{12,16},{16,12},{20,24},{24,20},{28,32},{32,28... | collective-permute-start | bytes 983048 | tf_op jit(solution)/shard_map/ppermute | solution.py:304
  50.5 1.8 %collective-permute-start.9 = (bf16[4,256,128]{2,1,0:T(8,128)(2,1)S(1)}, bf16[4,256,128]{2,1,0:T(8,128)(2,1)S(1)}, u32[]{:S(2)}, u32[]{:S(2)}) collective-permute-start(bf16[4,256,128]{2,1,0:T(8,128)(2,1)S(1)} %get-tuple-element.58.own), channel_id=1, source_target_pairs={{0,4},{4,0},{8,12},{12,8},{16,20},{20,16},{24,28},{28,24},{32,36},... | collective-permute-start | bytes 786440 | tf_op jit(solution)/shard_map/ppermute | solution.py:300
  54.3 1.3 %collective-permute-start.10 = (f32[6,128]{1,0:T(8,128)S(1)}, f32[6,128]{1,0:T(8,128)S(1)}, u32[]{:S(2)}, u32[]{:S(2)}) collective-permute-start(f32[6,128]{1,0:T(8,128)S(1)} %pad_maximum_fusion), channel_id=1, source_target_pairs={{0,4},{4,0},{8,12},{12,8},{16,20},{20,16},{24,28},{28,24},{32,36},... | collective-permute-start | bytes 9224 | tf_op jit(solution)/shard_map/ppermute | solution.py:300

commit v4 on v3

--- a/solution.py
+++ b/solution.py
@@ -197,53 +197,50 @@
     return jnp.where(rows < W, x, 0.0), x[W : W + 1, :]
 
 
-def inner_kernel(out, spill_in, spill_out, part_ref, sent_ref):
+def inner_kernel(out, spill_in, spill_out, part_ref, sent_ref, near_ref):
     values, index = opened(spill_in[0])
     for s in range(NS):
         part = out[s] + jnp.where(index == s, values, 0.0)
         part_ref[s] = part
         sent_ref[s] = part.astype(BF16)
+        near_ref[s] = part.astype(BF16)
     sent_ref[NS] = spill_out[0]
 
 
-def outer_kernel(place, counts, part, got, spill_in, spill_out, *rest):
-    p_ref, own_ref, outer_ref, marks_ref = rest[-4:]
+def system_kernel(
+    first, place, counts, neighbours, ca, cb, part, got, near, far, spill_in, spill_out, v0, *rest
+):
+    if first:
+        p_ref, w_ref, win_ref, wout_ref, sums_ref, u = rest
+    else:
+        w, p_ref, sums_ref, u = rest
     here = place[0]
+    odd = here % 2 == 1
     ends = jnp.logical_or(here == 0, here == NSUB - 1)
     got_values, got_index = opened(got[NS])
     got_index = jnp.where(ends, -1.0, got_index)
+    far_values, far_index = opened(far[0])
+    far_index = jnp.where(jnp.logical_or(here == 1, here == NSUB - 2), -1.0, far_index)
     values, index = opened(spill_out[0])
     for s in range(NS):
         alive = jnp.where(counts[0] > s, 1.0, 0.0)
         p = (part[s] + jnp.where(got_index == s, got_values, 0.0)) * alive
         p_ref[s] = p
-        own_ref[s] = p.astype(BF16)
-        outer_ref[s] = (got[s].astype(F32) + jnp.where(index == s, values, 0.0)).astype(BF16)
-    marks_ref[...] = jnp.concatenate([spill_in[0][WP - 8 :].astype(F32)[4:5]] * 4 + [got_index] * 4, axis=0)
-
-
-def system_kernel(first, place, counts, neighbours, ca, cb, p, own, outer, inner, marks, v0, *rest):
-    if first:
-        w_ref, win_ref, wout_ref, sums_ref, u = rest
-    else:
-        w, sums_ref, u = rest
-    here = place[0]
-    odd = here % 2 == 1
-    for s in range(NS):
-        u[s] = outer[s]
-        u[NS + s] = own[s]
-        u[2 * NS + s] = inner[s]
-    zero = jnp.zeros((1, R), F32)
-    sums = [zero] * 3
-    for s in range(NS):
-        acc = jnp.zeros((WP, R), F32)
+        u[s] = (got[s].astype(F32) + jnp.where(index == s, values, 0.0)).astype(BF16)
+        u[NS + s] = p.astype(BF16)
+        u[2 * NS + s] = (near[s].astype(F32) + jnp.where(far_index == s, far_values, 0.0)).astype(BF16)
+    sums_ref[...] = jnp.zeros((8, R), F32)
+    if first:
+        w_ref[...] = jnp.zeros((NS, WP, R), F32)
+
+    def one(s):
+        acc = p_ref[s]
         for k in range(NB):
             slot = jnp.clip(neighbours[s, k] - NS * (here - 1), 0, 3 * NS - 1)
             slot = jnp.where(odd, slot + 2 * NS * (1 - slot // NS), slot)
             matrix = ca[s * SPLIT + k] if k < SPLIT else cb[s * (NB - SPLIT) + k - SPLIT]
             acc += jnp.dot(matrix, u[slot], preferred_element_type=F32)
-        alive = jnp.where(counts[0] > s, 1.0, 0.0)
-        image = (p[s] + acc) * alive
+        image = acc
         start = v0[s]
         if first:
             image = image - SHIFT * start
@@ -251,14 +248,18 @@
             terms = (start * start, start * image, image * image)
         else:
             terms = (start * image, w[s] * image, image * image)
-        sums = [t + jnp.sum(x, axis=0, keepdims=True) for t, x in zip(sums, terms)]
-    if first:
-        for ref, index in ((win_ref, marks[0:1, :]), (wout_ref, marks[4:5, :])):
+        sums = [jnp.sum(x, axis=0, keepdims=True) for x in terms]
+        sums_ref[...] += jnp.concatenate(sums + [jnp.zeros((5, R), F32)], axis=0)
+
+    for s in range(NS):
+        pl.when(counts[0] > s)(functools.partial(one, s))
+    if first:
+        wanted = opened(spill_in[0])[1]
+        for ref, index in ((win_ref, wanted), (wout_ref, got_index)):
             chosen = jnp.zeros((WP, R), F32)
             for s in range(NS):
                 chosen = chosen + jnp.where(index == s, w_ref[s], 0.0)
             ref[0] = chosen.astype(BF16)
-    sums_ref[...] = jnp.concatenate(sums + [zero] * 5, axis=0)
 
 
 def finish_kernel(gathered, p0, q, out):
@@ -301,7 +302,12 @@
 
 
 def to_outer(x):
-    return lax.ppermute(x, "sub", [(i, (((i + 1) ^ 1) - 1) % NSUB) for i in range(NSUB)])
+    ends = (0, NSUB - 1)
+    return lax.ppermute(x, "sub", [(i, i if i in ends else ((i + 1) ^ 1) - 1) for i in range(NSUB)])
+
+
+def to_far(x):
+    return lax.ppermute(x, "sub", [(i, (i + (2 if i % 2 else -2)) % NSUB) for i in range(NSUB)])
 
 
 def body(right_side, coupling, neighbours, inverse, margin, counts):
@@ -365,37 +371,25 @@
         )(here, margin, held, part, ext)
         return out, got_in, spill_out
 
-    def joined(out, got_in, spill_out, meanwhile=None):
-        part, sent = call(inner_kernel, [(block, F32), ((NS + 1, WP, R), BF16)], [VM] * 3)(
-            out, got_in, spill_out
-        )
-        got = to_outer(sent)
-        done = meanwhile(sent) if meanwhile else []
-        p, own, outer, marks = call(
-            outer_kernel,
-            [(block, F32), (block, BF16), (block, BF16), ((8, R), F32)],
-            [SM, SM] + [VM] * 4 + [ANY] * len(done),
-        )(here, counts, part, got, got_in, spill_out, *done)
-        return done, p, own, outer, to_inner(own), marks
-
-    def system(first, halves, p, own, outer, inner, marks, *more):
-        outs = [(block, F32), (one, BF16), (one, BF16)] if first else []
+    def system(first, out, got_in, spill_out, *more):
+        part, sent, near = call(
+            inner_kernel, [(block, F32), ((NS + 1, WP, R), BF16), (block, BF16)], [VM] * 3
+        )(out, got_in, spill_out)
+        got, near, far = to_outer(sent), to_inner(near), to_far(spill_out)
+        if first:
+            (made,) = matrices(False, sent)
+            matrix_parts.append(pltpu.with_memory_space_constraint(made, pltpu.VMEM))
+        outs = [(block, F32)] + ([(block, F32), (one, BF16), (one, BF16)] if first else [])
         return call(
             functools.partial(system_kernel, first),
             outs + [((8, R), F32)],
-            [SM, SM, SM] + [VM] * (7 + len(more)),
+            [SM, SM, SM] + [VM] * (8 + len(more)),
             [pltpu.VMEM((3 * NS, WP, R), BF16)],
-        )(here, counts, neighbours, *halves, p, own, outer, inner, marks, *more)
-
-    def second(sent):
-        (made,) = matrices(False, sent)
-        return [pltpu.with_memory_space_constraint(made, pltpu.VMEM)]
-
-    (second_part,), p0, *rest = joined(*solve(v0, inner, outer), second)
-    halves = first_part, second_part
-    w, w_in, w_out, sums_one = system(True, halves, p0, *rest, v0)
-    _, q, *rest = joined(*solve(w, to_inner(w_in), to_outer(w_out)))
-    (sums_two,) = system(False, halves, q, *rest, v0, w)
+        )(here, counts, neighbours, *matrix_parts, part, got, near, far, got_in, spill_out, *more)
+
+    matrix_parts = [first_part]
+    p0, w, w_in, w_out, sums_one = system(True, *solve(v0, inner, outer), v0)
+    q, sums_two = system(False, *solve(w, to_inner(w_in), to_outer(w_out)), v0, w)
     sums = jnp.concatenate([sums_one[:3], sums_two[:3]], axis=0)
     sums = sums + to_inner(sums)
     gathered = lax.all_to_all(

time: 73.2 us -> 73.7 us (level)
  waiting for transfers between devices: 12 us -> 5.29 us
  blocking collectives: 16.4 us -> 20.9 us
  starting transfers between devices: 22.3 us -> 26.1 us
  Pallas kernels: 20.2 us -> 18.7 us
    ppermute x7, starting transfers between devices: 1.11 us -> 13 us  [to_inner(): return lax.ppermute(x, 'sub', [(i, i ^ 1) for i in range(NSUB)])]
    ppermute x4 -> x6, starting transfers between devices: 21.2 us -> 13.1 us  [the longest x2 10.4 us: to_far(): lax.ppermute(x, 'sub', [(i, (i + (2 if i % 2 else -2)) % NSUB) for i in r...]
    all_to_all x1, blocking collectives: 16.4 us -> 20.9 us  [body(): lax.all_to_all(jnp.broadcast_to(sums[None], (NSUB // 2, 6, R)), 'sub', 0,...]
    ppermute x4 -> x6, waiting for transfers between devices: 7.95 us -> 4.12 us  [the longest x2 4.11 us: to_far(): lax.ppermute(x, 'sub', [(i, (i + (2 if i % 2 else -2)) % NSUB) for i in r...]
    ppermute x7, waiting for transfers between devices: 4.07 us -> 1.17 us  [to_inner(): return lax.ppermute(x, 'sub', [(i, i ^ 1) for i in range(NSUB)])]
    pallas_call x2, Pallas kernels: 3.9 us -> 2.62 us  [system(): call(functools.partial(system_kernel, first), outs + [((8, R), F32)], [SM...]
  transfers between devices with their start and end apart: 11 -> 13, of which waited for: 6 -> 2; matrix products, arithmetic and copies ran while one was open for 0% -> 0% of each run, Pallas kernels for 18% -> 18%
where the time goes in v4:
time: 73.7 us; the launch traced here: 73 us
  starting transfers between devices  26.1 us (35%)
  blocking collectives  20.9 us (28%)
  Pallas kernels  18.7 us (25%)
  waiting for transfers between devices  5.29 us (7%)
  local copies, waits for them, and re-layouts  1.06 us (1%)
  between operations  0.93 us (1%)
    all_to_all x1, blocking collectives, body(): lax.all_to_all(jnp.broadcast_to(sums[None], (NSUB // 2, 6, R)), 'sub', 0,...  20.9 us
    ppermute x7, starting transfers between devices, to_inner(): return lax.ppermute(x, 'sub', [(i, i ^ 1) for i in range(NSUB)])  13 us
    ppermute x2, starting transfers between devices, to_far(): lax.ppermute(x, 'sub', [(i, (i + (2 if i % 2 else -2)) % NSUB) for i in r...  10.4 us
    pallas_call x2, Pallas kernels, matrices(): call(functools.partial(coupling_kernel, blocks, groups, first), outs, [AN...  8.34 us
    ppermute x2, waiting for transfers between devices, to_far(): lax.ppermute(x, 'sub', [(i, (i + (2 if i % 2 else -2)) % NSUB) for i in r...  4.11 us
    pallas_call x2, Pallas kernels, solve(): call(solve_kernel, [(block, F32), (one, BF16)], [SM, SM] + [VM] * 3, [plt...  2.8 us
    ppermute x4, starting transfers between devices, to_outer(): lax.ppermute(x, 'sub', [(i, i if i in ends else (i + 1 ^ 1) - 1) for i in...  2.71 us
    pallas_call x2, Pallas kernels, system(): call(functools.partial(system_kernel, first), outs + [((8, R), F32)], [SM...  2.62 us
  transfers between devices with their start and end apart: 13, of which 2 were waited for; matrix products, arithmetic and copies ran while one was open for 0% of the time, Pallas kernels for 18%

profile of v4, /device:TPU:2, one launch (start us, length us, event | category | flops | bytes accessed | tf_op | source)
XLA Modules:
  0.0 73.0 jit_solution(12127597533244616343)
XLA Ops:
  0.7 1.0 %copy-done = f32[4,252,128]{2,0,1:T(4,128)S(1)} copy-done((f32[4,252,128]{2,0,1:T(4,128)S(1)}, f32[4,252,128]{2,0,1:T(4,128)}, u32[]{:S(2)}) %copy-start) | copy-done | bytes 516120
  1.7 0.1 shard_map.65
  1.8 0.7 collective-permute-start.1
  2.4 3.4 %collective-permute-start = (bf16[4,256,128]{2,1,0:T(8,128)(2,1)S(1)}, bf16[4,256,128]{2,1,0:T(8,128)(2,1)S(1)}, u32[]{:S(2)}, u32[]{:S(2)}) collective-permute-start(bf16[4,256,128]{2,1,0:T(8,128)(2,1)S(1)} %get-tuple-element.33), channel_id=1, source_target_pairs={{0,4},{4,0},{8,12},{12,8},{16,20},{20,16},{24,28},{28,24},{32,36},... | collective-permute-start | bytes 786440 | tf_op jit(solution)/shard_map/ppermute | solution.py:301
  5.8 2.7 %shard_map.64 = (bf16[8,256,256]{2,1,0:T(8,128)(2,1)S(1)}, bf16[1512,1512]{1,0:T(8,128)(2,1)S(1)}) custom-call(bf16[4,508032]{1,0:T(4,128)(2,1)} %flat.3, bf16[1,1512,1512]{2,1,0:T(8,128)(2,1)} %rest_0_.1), custom_call_target="tpu_custom_call" | custom-call | flops 1048576 | bytes 12582912 | tf_op jit(solution)/shard_map/pallas_call | solution.py:333
  8.5 0.0 copy-start.2
  8.5 1.0 %shard_map.66.part = f32[1512,128]{1,0:T(8,128)S(1)} custom-call(bf16[1512,1512]{1,0:T(8,128)(2,1)S(1)} %get-tuple-element.31.inverse, f32[4,256,128]{2,1,0:T(8,128)S(1)} %get-tuple-element.32.own.v0), custom_call_target="tpu_custom_call" | custom-call | flops 1073741824 | bytes 4194304 | tf_op jit(solution)/shard_map/pallas_call | solution.py:353
  9.5 0.9 %shard_map.67 = (bf16[1,256,128]{2,1,0:T(8,128)(2,1)S(1)}, bf16[616,128]{1,0:T(8,128)(2,1)S(1)}) custom-call(s32[1]{0:T(128)} %bitcast.place, s32[1,2]{1,0:T(1,128)S(1)} %copy-done.2, bf16[1512,1512]{1,0:T(8,128)(2,1)S(1)} %get-tuple-element.31.inverse, f32[1512,128]{1,0:T(8,128)S(1)} %shard_map.66.part, f32[4,256,128]{2,1,0:T(8,128)S(1)} %get-tuple-element.32.own.v0, ...), custom_call_target="tpu_custom_call" | custom-call | tf_op jit(solution)/shard_map/pallas_call | solution.py:358
  10.4 0.3 collective-permute-start.2
  10.7 1.4 %shard_map.68 = (f32[4,256,128]{2,1,0:T(8,128)S(1)}, bf16[1,256,128]{2,1,0:T(8,128)(2,1)S(1)}) custom-call(s32[1]{0:T(128)} %bitcast.place, s32[1,2]{1,0:T(1,128)S(1)} %copy-done.2, bf16[1512,1512]{1,0:T(8,128)(2,1)S(1)} %get-tuple-element.31.inverse, f32[1512,128]{1,0:T(8,128)S(1)} %shard_map.66.part, bf16[616,128]{1,0:T(8,128)(2,1)S(1)} %get-tuple-element.34.ext), custom_call_target="tpu_custom_call" | custom-call | flops 1073741824 | bytes 4194304 | tf_op jit(solution)/shard_map/pallas_call | solution.py:365
  12.1 0.1 shard_map.69
  12.2 0.7 collective-permute-start.3
  12.9 3.3 %collective-permute-start.4 = (bf16[4,256,128]{2,1,0:T(8,128)(2,1)S(1)}, bf16[4,256,128]{2,1,0:T(8,128)(2,1)S(1)}, u32[]{:S(2)}, u32[]{:S(2)}) collective-permute-start(bf16[4,256,128]{2,1,0:T(8,128)(2,1)S(1)} %get-tuple-element.40), channel_id=1, source_target_pairs={{0,4},{4,0},{8,12},{12,8},{16,20},{20,16},{24,28},{28,24},{32,36},... | collective-permute-start | bytes 786440 | tf_op jit(solution)/shard_map/ppermute | solution.py:301
  16.2 7.3 %collective-permute-start.5 = (bf16[1,256,128]{2,1,0:T(8,128)(2,1)S(1)}, bf16[1,256,128]{2,1,0:T(8,128)(2,1)S(1)}, u32[]{:S(2)}, u32[]{:S(2)}) collective-permute-start(bf16[1,256,128]{2,1,0:T(8,128)(2,1)S(1)} %get-tuple-element.37.spill_out), channel_id=1, source_target_pairs={{0,248},{4,12},{8,0},{12,20},{16,8},{20,28},{24,16},{28,36},{32,24... | collective-permute-start | bytes 196616 | tf_op jit(solution)/shard_map/ppermute | solution.py:310
  23.5 5.7 %shard_map.70.cb = bf16[24,256,256]{2,1,0:T(8,128)(2,1)S(1)} custom-call(bf16[4,508032]{1,0:T(4,128)(2,1)} %flat.3, bf16[5,256,128]{2,1,0:T(8,128)(2,1)S(1)} %get-tuple-element.38.rest_0_), custom_call_target="tpu_custom_call" | custom-call | flops 1048576 | bytes 12582912 | tf_op jit(solution)/shard_map/pallas_call | solution.py:333
  29.2 1.4 %shard_map.71 = (f32[4,256,128]{2,1,0:T(8,128)S(1)}, f32[4,256,128]{2,1,0:T(8,128)S(1)}, bf16[1,256,128]{2,1,0:T(8,128)(2,1)S(1)}, bf16[1,256,128]{2,1,0:T(8,128)(2,1)S(1)}, f32[8,128]{1,0:T(8,128)S(1)}) custom-call(s32[1]{0:T(128)} %bitcast.place, s32[1]{0:T(128)S(6)} %copy.7.counts, s32[4,8]{1,0:T(4,128)S(1)} %copy-done.1, ...), custom_call_target="tpu_custom_call" | custom-call | tf_op jit(solution)/shard_map/pallas_call | solution.py:383
  30.6 0.1 collective-permute-start.6
  30.7 0.7 collective-permute-start.7
  31.4 1.0 %shard_map.72.part = f32[1512,128]{1,0:T(8,128)S(1)} custom-call(bf16[1512,1512]{1,0:T(8,128)(2,1)S(1)} %get-tuple-element.31.inverse, f32[4,256,128]{2,1,0:T(8,128)S(1)} %get-tuple-element.42.own.rest_0_), custom_call_target="tpu_custom_call" | custom-call | flops 1073741824 | bytes 4194304 | tf_op jit(solution)/shard_map/pallas_call | solution.py:353
  32.4 0.9 %shard_map.73 = (bf16[1,256,128]{2,1,0:T(8,128)(2,1)S(1)}, bf16[616,128]{1,0:T(8,128)(2,1)S(1)}) custom-call(s32[1]{0:T(128)} %bitcast.place, s32[1,2]{1,0:T(1,128)S(1)} %copy-done.2, bf16[1512,1512]{1,0:T(8,128)(2,1)S(1)} %get-tuple-element.31.inverse, f32[1512,128]{1,0:T(8,128)S(1)} %shard_map.72.part, f32[4,256,128]{2,1,0:T(8,128)S(1)} %get-tuple-element.42.own.rest_0_, ...), custom_call_target="tpu_custom_call" | custom-call | tf_op jit(solution)/shard_map/pallas_call | solution.py:358
  33.3 4.4 %collective-permute-start.8 = (bf16[1,256,128]{2,1,0:T(8,128)(2,1)S(1)}, bf16[1,256,128]{2,1,0:T(8,128)(2,1)S(1)}, u32[]{:S(2)}, u32[]{:S(2)}) collective-permute-start(bf16[1,256,128]{2,1,0:T(8,128)(2,1)S(1)} %get-tuple-element.47), channel_id=1, source_target_pairs={{0,4},{4,0},{8,12},{12,8},{16,20},{20,16},{24,28},{28,24},{32,36},... | collective-permute-start | bytes 196616 | tf_op jit(solution)/shard_map/ppermute | solution.py:301
  37.7 1.4 %shard_map.74 = (f32[4,256,128]{2,1,0:T(8,128)S(1)}, bf16[1,256,128]{2,1,0:T(8,128)(2,1)S(1)}) custom-call(s32[1]{0:T(128)} %bitcast.place, s32[1,2]{1,0:T(1,128)S(1)} %copy-done.2, bf16[1512,1512]{1,0:T(8,128)(2,1)S(1)} %get-tuple-element.31.inverse, f32[1512,128]{1,0:T(8,128)S(1)} %shard_map.72.part, bf16[616,128]{1,0:T(8,128)(2,1)S(1)} %get-tuple-element.45.ext), custom_call_target="tpu_custom_call" | custom-call | flops 1073741824 | bytes 4194304 | tf_op jit(solution)/shard_map/pallas_call | solution.py:365
  39.1 0.1 shard_map.75
  39.2 0.7 collective-permute-start.9
  39.9 1.4 %collective-permute-start.10 = (bf16[4,256,128]{2,1,0:T(8,128)(2,1)S(1)}, bf16[4,256,128]{2,1,0:T(8,128)(2,1)S(1)}, u32[]{:S(2)}, u32[]{:S(2)}) collective-permute-start(bf16[4,256,128]{2,1,0:T(8,128)(2,1)S(1)} %get-tuple-element.51), channel_id=1, source_target_pairs={{0,4},{4,0},{8,12},{12,8},{16,20},{20,16},{24,28},{28,24},{32,36},... | collective-permute-start | bytes 786440 | tf_op jit(solution)/shard_map/ppermute | solution.py:301
  41.3 3.1 %collective-permute-start.11 = (bf16[1,256,128]{2,1,0:T(8,128)(2,1)S(1)}, bf16[1,256,128]{2,1,0:T(8,128)(2,1)S(1)}, u32[]{:S(2)}, u32[]{:S(2)}) collective-permute-start(bf16[1,256,128]{2,1,0:T(8,128)(2,1)S(1)} %get-tuple-element.48.spill_out), channel_id=1, source_target_pairs={{0,248},{4,12},{8,0},{12,20},{16,8},{20,28},{24,16},{28,36},{32,24... | collective-permute-start | bytes 196616 | tf_op jit(solution)/shard_map/ppermute | solution.py:310
  44.5 4.1 %collective-permute-done.11.far = bf16[1,256,128]{2,1,0:T(8,128)(2,1)S(1)} collective-permute-done((bf16[1,256,128]{2,1,0:T(8,128)(2,1)S(1)}, bf16[1,256,128]{2,1,0:T(8,128)(2,1)S(1)}, u32[]{:S(2)}, u32[]{:S(2)}) %collective-permute-start.11) | collective-permute-done | bytes 65568 | tf_op jit(solution)/shard_map/ppermute | solution.py:310
  48.6 1.3 %shard_map.76 = (f32[4,256,128]{2,1,0:T(8,128)S(1)}, f32[8,128]{1,0:T(8,128)S(1)}) custom-call(s32[1]{0:T(128)} %bitcast.place, s32[1]{0:T(128)S(6)} %copy.7.counts, s32[4,8]{1,0:T(4,128)S(1)} %copy-done.1, bf16[8,256,256]{2,1,0:T(8,128)(2,1)S(1)} %get-tuple-element.30.ca, bf16[24,256,256]{2,1,0:T(8,128)(2,1)S(1)} %shard_map.70.cb, ...), custom_call_target="tpu_custom_call" | custom-call | tf_op jit(solution)/shard_map/pallas_call | solution.py:383
  49.9 0.1 collective-permute-start.12
  50.0 1.2 %collective-permute-done.12 = f32[6,128]{1,0:T(8,128)S(1)} collective-permute-done((f32[6,128]{1,0:T(8,128)S(1)}, f32[6,128]{1,0:T(8,128)S(1)}, u32[]{:S(2)}, u32[]{:S(2)}) %collective-permute-start.12) | collective-permute-done | bytes 3104 | tf_op jit(solution)/shard_map/ppermute | solution.py:301
  51.1 20.9 %all_to_all.5.gathered = f32[32,6,128]{2,1,0:T(8,128)S(1)} all-to-all(f32[32,6,128]{2,1,0:T(8,128)S(1)} %broadcast_in_dim.2), channel_id=1, replica_groups={{0,8,16,24,32,40,48,56,64,72,80,88,96,104,112,120,128,136,144,152,160,1..., dimensions={0} | all-to-all | bytes 196608 | tf_op jit(solution)/shard_map/all_to_all | solution.py:395
  72.0 1.0 %shard_map.77 = f32[1008,128]{1,0:T(8,128)} custom-call(f32[32,6,128]{2,1,0:T(8,128)S(1)} %all_to_all.5.gathered, f32[4,256,128]{2,1,0:T(8,128)S(1)} %get-tuple-element.53.p0, f32[4,256,128]{2,1,0:T(8,128)S(1)} %get-tuple-element.54.q), custom_call_target="tpu_custom_call" | custom-call | tf_op jit(solution)/shard_map/pallas_call | solution.py:399
  (20 shorter events, 0.1 us)
Async XLA Ops:
  0.7 1.0 %copy-start = (f32[4,252,128]{2,0,1:T(4,128)S(1)}, f32[4,252,128]{2,0,1:T(4,128)}, u32[]{:S(2)}) copy-start(f32[4,252,128]{2,0,1:T(4,128)} %param.6) | copy-start | bytes 1548292
  1.8 7.7 %collective-permute-start.1 = (bf16[4,256,128]{2,1,0:T(8,128)(2,1)S(1)}, bf16[4,256,128]{2,1,0:T(8,128)(2,1)S(1)}, u32[]{:S(2)}, u32[]{:S(2)}) collective-permute-start(bf16[4,256,128]{2,1,0:T(8,128)(2,1)S(1)} %get-tuple-element.33), channel_id=1, source_target_pairs={{0,0},{4,8},{8,4},{12,16},{16,12},{20,24},{24,20},{28,32},{32,28},... | collective-permute-start | bytes 786440 | tf_op jit(solution)/shard_map/ppermute | solution.py:306
  2.4 7.0 %collective-permute-start = (bf16[4,256,128]{2,1,0:T(8,128)(2,1)S(1)}, bf16[4,256,128]{2,1,0:T(8,128)(2,1)S(1)}, u32[]{:S(2)}, u32[]{:S(2)}) collective-permute-start(bf16[4,256,128]{2,1,0:T(8,128)(2,1)S(1)} %get-tuple-element.33), channel_id=1, source_target_pairs={{0,4},{4,0},{8,12},{12,8},{16,20},{20,16},{24,28},{28,24},{32,36},... | collective-permute-start | bytes 786440 | tf_op jit(solution)/shard_map/ppermute | solution.py:301
  8.5 1.0 %copy-start.2 = (s32[1,2]{1,0:T(1,128)S(1)}, s32[1,2]{1,0:T(1,128)}, u32[]{:S(2)}) copy-start(s32[1,2]{1,0:T(1,128)} %margin.7) | copy-start | bytes 28
  10.4 1.7 %collective-permute-start.2 = (bf16[1,256,128]{2,1,0:T(8,128)(2,1)S(1)}, bf16[1,256,128]{2,1,0:T(8,128)(2,1)S(1)}, u32[]{:S(2)}, u32[]{:S(2)}) collective-permute-start(bf16[1,256,128]{2,1,0:T(8,128)(2,1)S(1)} %get-tuple-element.36), channel_id=1, source_target_pairs={{0,4},{4,0},{8,12},{12,8},{16,20},{20,16},{24,28},{28,24},{32,36},... | collective-permute-start | bytes 196616 | tf_op jit(solution)/shard_map/ppermute | solution.py:301
  12.1 17.1 %copy-start.1 = (s32[4,8]{1,0:T(4,128)S(1)}, s32[4,8]{1,0:T(4,128)}, u32[]{:S(2)}) copy-start(s32[4,8]{1,0:T(4,128)} %neighbours.3) | copy-start | bytes 388
  12.2 17.0 %collective-permute-start.3 = (bf16[5,256,128]{2,1,0:T(8,128)(2,1)S(1)}, bf16[5,256,128]{2,1,0:T(8,128)(2,1)S(1)}, u32[]{:S(2)}, u32[]{:S(2)}) collective-permute-start(bf16[5,256,128]{2,1,0:T(8,128)(2,1)S(1)} %get-tuple-element.38.rest_0_), channel_id=1, source_target_pairs={{0,0},{4,8},{8,4},{12,16},{16,12},{20,24},{24,20},{28,32},{32,28},... | collective-permute-start | bytes 983048 | tf_op jit(solution)/shard_map/ppermute | solution.py:306
  12.9 16.3 %collective-permute-start.4 = (bf16[4,256,128]{2,1,0:T(8,128)(2,1)S(1)}, bf16[4,256,128]{2,1,0:T(8,128)(2,1)S(1)}, u32[]{:S(2)}, u32[]{:S(2)}) collective-permute-start(bf16[4,256,128]{2,1,0:T(8,128)(2,1)S(1)} %get-tuple-element.40), channel_id=1, source_target_pairs={{0,4},{4,0},{8,12},{12,8},{16,20},{20,16},{24,28},{28,24},{32,36},... | collective-permute-start | bytes 786440 | tf_op jit(solution)/shard_map/ppermute | solution.py:301
  16.2 13.0 %collective-permute-start.5 = (bf16[1,256,128]{2,1,0:T(8,128)(2,1)S(1)}, bf16[1,256,128]{2,1,0:T(8,128)(2,1)S(1)}, u32[]{:S(2)}, u32[]{:S(2)}) collective-permute-start(bf16[1,256,128]{2,1,0:T(8,128)(2,1)S(1)} %get-tuple-element.37.spill_out), channel_id=1, source_target_pairs={{0,248},{4,12},{8,0},{12,20},{16,8},{20,28},{24,16},{28,36},{32,24... | collective-permute-start | bytes 196616 | tf_op jit(solution)/shard_map/ppermute | solution.py:310
  30.6 1.8 %collective-permute-start.6 = (bf16[1,256,128]{2,1,0:T(8,128)(2,1)S(1)}, bf16[1,256,128]{2,1,0:T(8,128)(2,1)S(1)}, u32[]{:S(2)}, u32[]{:S(2)}) collective-permute-start(bf16[1,256,128]{2,1,0:T(8,128)(2,1)S(1)} %get-tuple-element.43), channel_id=1, source_target_pairs={{0,4},{4,0},{8,12},{12,8},{16,20},{20,16},{24,28},{28,24},{32,36},... | collective-permute-start | bytes 196616 | tf_op jit(solution)/shard_map/ppermute | solution.py:301
  30.7 1.7 %collective-permute-start.7 = (bf16[1,256,128]{2,1,0:T(8,128)(2,1)S(1)}, bf16[1,256,128]{2,1,0:T(8,128)(2,1)S(1)}, u32[]{:S(2)}, u32[]{:S(2)}) collective-permute-start(bf16[1,256,128]{2,1,0:T(8,128)(2,1)S(1)} %get-tuple-element.44), channel_id=1, source_target_pairs={{0,0},{4,8},{8,4},{12,16},{16,12},{20,24},{24,20},{28,32},{32,28},... | collective-permute-start | bytes 196616 | tf_op jit(solution)/shard_map/ppermute | solution.py:306
  33.3 5.8 %collective-permute-start.8 = (bf16[1,256,128]{2,1,0:T(8,128)(2,1)S(1)}, bf16[1,256,128]{2,1,0:T(8,128)(2,1)S(1)}, u32[]{:S(2)}, u32[]{:S(2)}) collective-permute-start(bf16[1,256,128]{2,1,0:T(8,128)(2,1)S(1)} %get-tuple-element.47), channel_id=1, source_target_pairs={{0,4},{4,0},{8,12},{12,8},{16,20},{20,16},{24,28},{28,24},{32,36},... | collective-permute-start | bytes 196616 | tf_op jit(solution)/shard_map/ppermute | solution.py:301
  39.2 9.3 %collective-permute-start.9 = (bf16[5,256,128]{2,1,0:T(8,128)(2,1)S(1)}, bf16[5,256,128]{2,1,0:T(8,128)(2,1)S(1)}, u32[]{:S(2)}, u32[]{:S(2)}) collective-permute-start(bf16[5,256,128]{2,1,0:T(8,128)(2,1)S(1)} %get-tuple-element.50), channel_id=1, source_target_pairs={{0,0},{4,8},{8,4},{12,16},{16,12},{20,24},{24,20},{28,32},{32,28},... | collective-permute-start | bytes 983048 | tf_op jit(solution)/shard_map/ppermute | solution.py:306
  39.9 8.7 %collective-permute-start.10 = (bf16[4,256,128]{2,1,0:T(8,128)(2,1)S(1)}, bf16[4,256,128]{2,1,0:T(8,128)(2,1)S(1)}, u32[]{:S(2)}, u32[]{:S(2)}) collective-permute-start(bf16[4,256,128]{2,1,0:T(8,128)(2,1)S(1)} %get-tuple-element.51), channel_id=1, source_target_pairs={{0,4},{4,0},{8,12},{12,8},{16,20},{20,16},{24,28},{28,24},{32,36},... | collective-permute-start | bytes 786440 | tf_op jit(solution)/shard_map/ppermute | solution.py:301
  41.3 7.3 %collective-permute-start.11 = (bf16[1,256,128]{2,1,0:T(8,128)(2,1)S(1)}, bf16[1,256,128]{2,1,0:T(8,128)(2,1)S(1)}, u32[]{:S(2)}, u32[]{:S(2)}) collective-permute-start(bf16[1,256,128]{2,1,0:T(8,128)(2,1)S(1)} %get-tuple-element.48.spill_out), channel_id=1, source_target_pairs={{0,248},{4,12},{8,0},{12,20},{16,8},{20,28},{24,16},{28,36},{32,24... | collective-permute-start | bytes 196616 | tf_op jit(solution)/shard_map/ppermute | solution.py:310
  49.9 1.3 %collective-permute-start.12 = (f32[6,128]{1,0:T(8,128)S(1)}, f32[6,128]{1,0:T(8,128)S(1)}, u32[]{:S(2)}, u32[]{:S(2)}) collective-permute-start(f32[6,128]{1,0:T(8,128)S(1)} %pad_maximum_fusion), channel_id=1, source_target_pairs={{0,4},{4,0},{8,12},{12,8},{16,20},{20,16},{24,28},{28,24},{32,36},... | collective-permute-start | bytes 9224 | tf_op jit(solution)/shard_map/ppermute | solution.py:301

commit v5 on v4

--- a/solution.py
+++ b/solution.py
@@ -297,17 +297,29 @@
         out[pl.ds(s, W, stride=NS), :] = one * p0[s, :W, :] + two * q[s, :W, :]
 
 
+def permuted(x, target):
+    parts = lax.axis_size("rhs")
+    pairs = [(i, j) for i in range(NSUB) for j in range(parts)]
+    return lax.ppermute(
+        x, ("sub", "rhs"), [(i * parts + j, t[0] * parts + t[1]) for i, j in pairs for t in [target(i, j)]]
+    )
+
+
 def to_inner(x):
-    return lax.ppermute(x, "sub", [(i, i ^ 1) for i in range(NSUB)])
+    return permuted(x, lambda i, j: (i ^ 1, j))
 
 
 def to_outer(x):
-    ends = (0, NSUB - 1)
-    return lax.ppermute(x, "sub", [(i, i if i in ends else ((i + 1) ^ 1) - 1) for i in range(NSUB)])
+    return permuted(x, lambda i, j: (i, j ^ 1) if i in (0, NSUB - 1) else (((i + 1) ^ 1) - 1, j))
 
 
 def to_far(x):
-    return lax.ppermute(x, "sub", [(i, (i + (2 if i % 2 else -2)) % NSUB) for i in range(NSUB)])
+    def target(i, j):
+        if i in (0, NSUB - 1):
+            return i ^ 1, j
+        return i + (2 if i % 2 else -2), j
+
+    return permuted(x, target)
 
 
 def body(right_side, coupling, neighbours, inverse, margin, counts):

time: 73.7 us -> 67.7 us (0.919)
  starting transfers between devices: 26.1 us -> 11 us
  waiting for transfers between devices: 5.29 us -> 9.38 us
  blocking collectives: 20.9 us -> 24.6 us
  Pallas kernels: 18.7 us -> 19.6 us
    ppermute x13, starting transfers between devices: 26.1 us -> 11 us  [permuted(): lax.ppermute(x, ('sub', 'rhs'), [(i * parts + j, t[0] * parts + t[1]) for...]
    ppermute x13, waiting for transfers between devices: 5.29 us -> 9.38 us  [permuted(): lax.ppermute(x, ('sub', 'rhs'), [(i * parts + j, t[0] * parts + t[1]) for...]
    all_to_all x1, blocking collectives: 20.9 us -> 24.6 us  [body(): lax.all_to_all(jnp.broadcast_to(sums[None], (NSUB // 2, 6, R)), 'sub', 0,...]
    pallas_call x2, Pallas kernels: 2.62 us -> 3.52 us  [system(): call(functools.partial(system_kernel, first), outs + [((8, R), F32)], [SM...]
  transfers between devices with their start and end apart: 13 -> 13, of which waited for: 2 -> 4; matrix products, arithmetic and copies ran while one was open for 0% -> 0% of each run, Pallas kernels for 18% -> 20%
where the time goes in v5:
time: 67.7 us; the launch traced here: 66.5 us
  blocking collectives  24.6 us (36%)
  Pallas kernels  19.6 us (29%)
  starting transfers between devices  11 us (16%)
  waiting for transfers between devices  9.38 us (14%)
  local copies, waits for them, and re-layouts  1.06 us (2%)
  between operations  0.87 us (1%)
    all_to_all x1, blocking collectives, body(): lax.all_to_all(jnp.broadcast_to(sums[None], (NSUB // 2, 6, R)), 'sub', 0,...  24.6 us
    ppermute x13, starting transfers between devices, permuted(): lax.ppermute(x, ('sub', 'rhs'), [(i * parts + j, t[0] * parts + t[1]) for...  11 us
    ppermute x13, waiting for transfers between devices, permuted(): lax.ppermute(x, ('sub', 'rhs'), [(i * parts + j, t[0] * parts + t[1]) for...  9.38 us
    pallas_call x2, Pallas kernels, matrices(): call(functools.partial(coupling_kernel, blocks, groups, first), outs, [AN...  8.34 us
    pallas_call x2, Pallas kernels, system(): call(functools.partial(system_kernel, first), outs + [((8, R), F32)], [SM...  3.52 us
    pallas_call x2, Pallas kernels, solve(): call(solve_kernel, [(block, F32), (one, BF16)], [SM, SM] + [VM] * 3, [plt...  2.8 us
    pallas_call x2, Pallas kernels, solve(): call(own_kernel, [((6 * W, R), F32, True)], [VM, VM], [pltpu.VMEM((OWN, R...  1.97 us
    pallas_call x2, Pallas kernels, solve(): call(margin_kernel, [(one, BF16), ((depth, R), BF16)], [SM, SM] + [VM] *...  1.76 us
  transfers between devices with their start and end apart: 13, of which 4 were waited for; matrix products, arithmetic and copies ran while one was open for 0% of the time, Pallas kernels for 20%

profile of v5, /device:TPU:2, one launch (start us, length us, event | category | flops | bytes accessed | tf_op | source)
XLA Modules:
  0.0 66.5 jit_solution(4377113485326748056)
XLA Ops:
  0.7 1.0 %copy-done = f32[4,252,128]{2,0,1:T(4,128)S(1)} copy-done((f32[4,252,128]{2,0,1:T(4,128)S(1)}, f32[4,252,128]{2,0,1:T(4,128)}, u32[]{:S(2)}) %copy-start) | copy-done | bytes 516120
  1.7 0.1 shard_map.65
  1.8 2.4 %collective-permute-start.1 = (bf16[4,256,128]{2,1,0:T(8,128)(2,1)S(1)}, bf16[4,256,128]{2,1,0:T(8,128)(2,1)S(1)}, u32[]{:S(2)}, u32[]{:S(2)}) collective-permute-start(bf16[4,256,128]{2,1,0:T(8,128)(2,1)S(1)} %get-tuple-element.33), channel_id=1, source_target_pairs={{0,1},{1,0},{2,3},{3,2},{4,8},{5,9},{6,10},{7,11},{8,4},{9,5},{10,... | collective-permute-start | bytes 786440 | tf_op jit(solution)/shard_map/ppermute | solution.py:303
  4.1 2.7 %shard_map.64 = (bf16[8,256,256]{2,1,0:T(8,128)(2,1)S(1)}, bf16[1512,1512]{1,0:T(8,128)(2,1)S(1)}) custom-call(bf16[4,508032]{1,0:T(4,128)(2,1)} %flat.3, bf16[1,1512,1512]{2,1,0:T(8,128)(2,1)} %rest_0_.1), custom_call_target="tpu_custom_call" | custom-call | flops 1048576 | bytes 12582912 | tf_op jit(solution)/shard_map/pallas_call | solution.py:345
  6.8 0.0 copy-start.2
  6.8 1.0 %shard_map.66.part = f32[1512,128]{1,0:T(8,128)S(1)} custom-call(bf16[1512,1512]{1,0:T(8,128)(2,1)S(1)} %get-tuple-element.31.inverse, f32[4,256,128]{2,1,0:T(8,128)S(1)} %get-tuple-element.32.own.v0), custom_call_target="tpu_custom_call" | custom-call | flops 1073741824 | bytes 4194304 | tf_op jit(solution)/shard_map/pallas_call | solution.py:365
  7.8 0.7 collective-permute-done.1.outer
  8.5 0.9 %shard_map.67 = (bf16[1,256,128]{2,1,0:T(8,128)(2,1)S(1)}, bf16[616,128]{1,0:T(8,128)(2,1)S(1)}) custom-call(s32[1]{0:T(128)} %bitcast.place, s32[1,2]{1,0:T(1,128)S(1)} %copy-done.2, bf16[1512,1512]{1,0:T(8,128)(2,1)S(1)} %get-tuple-element.31.inverse, f32[1512,128]{1,0:T(8,128)S(1)} %shard_map.66.part, f32[4,256,128]{2,1,0:T(8,128)S(1)} %get-tuple-element.32.own.v0, ...), custom_call_target="tpu_custom_call" | custom-call | tf_op jit(solution)/shard_map/pallas_call | solution.py:370
  9.4 0.1 collective-permute-start.2
  9.5 1.4 %shard_map.68 = (f32[4,256,128]{2,1,0:T(8,128)S(1)}, bf16[1,256,128]{2,1,0:T(8,128)(2,1)S(1)}) custom-call(s32[1]{0:T(128)} %bitcast.place, s32[1,2]{1,0:T(1,128)S(1)} %copy-done.2, bf16[1512,1512]{1,0:T(8,128)(2,1)S(1)} %get-tuple-element.31.inverse, f32[1512,128]{1,0:T(8,128)S(1)} %shard_map.66.part, bf16[616,128]{1,0:T(8,128)(2,1)S(1)} %get-tuple-element.34.ext), custom_call_target="tpu_custom_call" | custom-call | flops 1073741824 | bytes 4194304 | tf_op jit(solution)/shard_map/pallas_call | solution.py:377
  10.9 0.0 copy-start.1
  10.9 0.1 shard_map.69
  11.0 2.1 %collective-permute-start.3 = (bf16[5,256,128]{2,1,0:T(8,128)(2,1)S(1)}, bf16[5,256,128]{2,1,0:T(8,128)(2,1)S(1)}, u32[]{:S(2)}, u32[]{:S(2)}) collective-permute-start(bf16[5,256,128]{2,1,0:T(8,128)(2,1)S(1)} %get-tuple-element.38.rest_0_), channel_id=1, source_target_pairs={{0,1},{1,0},{2,3},{3,2},{4,8},{5,9},{6,10},{7,11},{8,4},{9,5},{10,... | collective-permute-start | bytes 983048 | tf_op jit(solution)/shard_map/ppermute | solution.py:303
  13.1 0.5 collective-permute-start.5
  13.6 5.7 %shard_map.70.cb = bf16[24,256,256]{2,1,0:T(8,128)(2,1)S(1)} custom-call(bf16[4,508032]{1,0:T(4,128)(2,1)} %flat.3, bf16[5,256,128]{2,1,0:T(8,128)(2,1)S(1)} %get-tuple-element.38.rest_0_), custom_call_target="tpu_custom_call" | custom-call | flops 1048576 | bytes 12582912 | tf_op jit(solution)/shard_map/pallas_call | solution.py:345
  19.3 1.8 %shard_map.71 = (f32[4,256,128]{2,1,0:T(8,128)S(1)}, f32[4,256,128]{2,1,0:T(8,128)S(1)}, bf16[1,256,128]{2,1,0:T(8,128)(2,1)S(1)}, bf16[1,256,128]{2,1,0:T(8,128)(2,1)S(1)}, f32[8,128]{1,0:T(8,128)S(1)}) custom-call(s32[1]{0:T(128)} %bitcast.place, s32[1]{0:T(128)S(6)} %copy.7.counts, s32[4,8]{1,0:T(4,128)S(1)} %copy-done.1, ...), custom_call_target="tpu_custom_call" | custom-call | tf_op jit(solution)/shard_map/pallas_call | solution.py:395
  21.1 0.6 collective-permute-start.6
  21.8 1.4 %collective-permute-start.7 = (bf16[1,256,128]{2,1,0:T(8,128)(2,1)S(1)}, bf16[1,256,128]{2,1,0:T(8,128)(2,1)S(1)}, u32[]{:S(2)}, u32[]{:S(2)}) collective-permute-start(bf16[1,256,128]{2,1,0:T(8,128)(2,1)S(1)} %get-tuple-element.44), channel_id=1, source_target_pairs={{0,1},{1,0},{2,3},{3,2},{4,8},{5,9},{6,10},{7,11},{8,4},{9,5},{10,... | collective-permute-start | bytes 196616 | tf_op jit(solution)/shard_map/ppermute | solution.py:303
  23.1 1.0 %shard_map.72.part = f32[1512,128]{1,0:T(8,128)S(1)} custom-call(bf16[1512,1512]{1,0:T(8,128)(2,1)S(1)} %get-tuple-element.31.inverse, f32[4,256,128]{2,1,0:T(8,128)S(1)} %get-tuple-element.42.own.rest_0_), custom_call_target="tpu_custom_call" | custom-call | flops 1073741824 | bytes 4194304 | tf_op jit(solution)/shard_map/pallas_call | solution.py:365
  24.1 1.9 %collective-permute-done.7.outer = bf16[1,256,128]{2,1,0:T(8,128)(2,1)S(1)} collective-permute-done((bf16[1,256,128]{2,1,0:T(8,128)(2,1)S(1)}, bf16[1,256,128]{2,1,0:T(8,128)(2,1)S(1)}, u32[]{:S(2)}, u32[]{:S(2)}) %collective-permute-start.7) | collective-permute-done | bytes 65568 | tf_op jit(solution)/shard_map/ppermute | solution.py:303
  26.0 0.9 %shard_map.73 = (bf16[1,256,128]{2,1,0:T(8,128)(2,1)S(1)}, bf16[616,128]{1,0:T(8,128)(2,1)S(1)}) custom-call(s32[1]{0:T(128)} %bitcast.place, s32[1,2]{1,0:T(1,128)S(1)} %copy-done.2, bf16[1512,1512]{1,0:T(8,128)(2,1)S(1)} %get-tuple-element.31.inverse, f32[1512,128]{1,0:T(8,128)S(1)} %shard_map.72.part, f32[4,256,128]{2,1,0:T(8,128)S(1)} %get-tuple-element.42.own.rest_0_, ...), custom_call_target="tpu_custom_call" | custom-call | tf_op jit(solution)/shard_map/pallas_call | solution.py:370
  26.9 0.7 %collective-permute-start.8 = (bf16[1,256,128]{2,1,0:T(8,128)(2,1)S(1)}, bf16[1,256,128]{2,1,0:T(8,128)(2,1)S(1)}, u32[]{:S(2)}, u32[]{:S(2)}) collective-permute-start(bf16[1,256,128]{2,1,0:T(8,128)(2,1)S(1)} %get-tuple-element.47), channel_id=1, source_target_pairs={{0,4},{1,5},{2,6},{3,7},{4,0},{5,1},{6,2},{7,3},{8,12},{9,13},{10,... | collective-permute-start | bytes 196616 | tf_op jit(solution)/shard_map/ppermute | solution.py:303
  27.6 1.4 %shard_map.74 = (f32[4,256,128]{2,1,0:T(8,128)S(1)}, bf16[1,256,128]{2,1,0:T(8,128)(2,1)S(1)}) custom-call(s32[1]{0:T(128)} %bitcast.place, s32[1,2]{1,0:T(1,128)S(1)} %copy-done.2, bf16[1512,1512]{1,0:T(8,128)(2,1)S(1)} %get-tuple-element.31.inverse, f32[1512,128]{1,0:T(8,128)S(1)} %shard_map.72.part, bf16[616,128]{1,0:T(8,128)(2,1)S(1)} %get-tuple-element.45.ext), custom_call_target="tpu_custom_call" | custom-call | flops 1073741824 | bytes 4194304 | tf_op jit(solution)/shard_map/pallas_call | solution.py:377
  29.0 0.1 shard_map.75
  29.1 1.0 %collective-permute-start.9 = (bf16[5,256,128]{2,1,0:T(8,128)(2,1)S(1)}, bf16[5,256,128]{2,1,0:T(8,128)(2,1)S(1)}, u32[]{:S(2)}, u32[]{:S(2)}) collective-permute-start(bf16[5,256,128]{2,1,0:T(8,128)(2,1)S(1)} %get-tuple-element.50), channel_id=1, source_target_pairs={{0,1},{1,0},{2,3},{3,2},{4,8},{5,9},{6,10},{7,11},{8,4},{9,5},{10,... | collective-permute-start | bytes 983048 | tf_op jit(solution)/shard_map/ppermute | solution.py:303
  30.2 2.1 %collective-permute-start.10 = (bf16[4,256,128]{2,1,0:T(8,128)(2,1)S(1)}, bf16[4,256,128]{2,1,0:T(8,128)(2,1)S(1)}, u32[]{:S(2)}, u32[]{:S(2)}) collective-permute-start(bf16[4,256,128]{2,1,0:T(8,128)(2,1)S(1)} %get-tuple-element.51), channel_id=1, source_target_pairs={{0,4},{1,5},{2,6},{3,7},{4,0},{5,1},{6,2},{7,3},{8,12},{9,13},{10,... | collective-permute-start | bytes 786440 | tf_op jit(solution)/shard_map/ppermute | solution.py:303
  32.2 5.6 %collective-permute-done.11.far = bf16[1,256,128]{2,1,0:T(8,128)(2,1)S(1)} collective-permute-done((bf16[1,256,128]{2,1,0:T(8,128)(2,1)S(1)}, bf16[1,256,128]{2,1,0:T(8,128)(2,1)S(1)}, u32[]{:S(2)}, u32[]{:S(2)}) %collective-permute-start.11) | collective-permute-done | bytes 65568 | tf_op jit(solution)/shard_map/ppermute | solution.py:303
  37.9 1.7 %shard_map.76 = (f32[4,256,128]{2,1,0:T(8,128)S(1)}, f32[8,128]{1,0:T(8,128)S(1)}) custom-call(s32[1]{0:T(128)} %bitcast.place, s32[1]{0:T(128)S(6)} %copy.7.counts, s32[4,8]{1,0:T(4,128)S(1)} %copy-done.1, bf16[8,256,256]{2,1,0:T(8,128)(2,1)S(1)} %get-tuple-element.30.ca, bf16[24,256,256]{2,1,0:T(8,128)(2,1)S(1)} %shard_map.70.cb, ...), custom_call_target="tpu_custom_call" | custom-call | tf_op jit(solution)/shard_map/pallas_call | solution.py:395
  39.6 0.1 collective-permute-start.12
  39.7 1.2 %collective-permute-done.12 = f32[6,128]{1,0:T(8,128)S(1)} collective-permute-done((f32[6,128]{1,0:T(8,128)S(1)}, f32[6,128]{1,0:T(8,128)S(1)}, u32[]{:S(2)}, u32[]{:S(2)}) %collective-permute-start.12) | collective-permute-done | bytes 3104 | tf_op jit(solution)/shard_map/ppermute | solution.py:303
  40.9 24.6 %all_to_all.5.gathered = f32[32,6,128]{2,1,0:T(8,128)S(1)} all-to-all(f32[32,6,128]{2,1,0:T(8,128)S(1)} %broadcast_in_dim.2), channel_id=1, replica_groups={{0,8,16,24,32,40,48,56,64,72,80,88,96,104,112,120,128,136,144,152,160,1..., dimensions={0} | all-to-all | bytes 196608 | tf_op jit(solution)/shard_map/all_to_all | solution.py:407
  65.6 1.0 %shard_map.77 = f32[1008,128]{1,0:T(8,128)} custom-call(f32[32,6,128]{2,1,0:T(8,128)S(1)} %all_to_all.5.gathered, f32[4,256,128]{2,1,0:T(8,128)S(1)} %get-tuple-element.53.p0, f32[4,256,128]{2,1,0:T(8,128)S(1)} %get-tuple-element.54.q), custom_call_target="tpu_custom_call" | custom-call | tf_op jit(solution)/shard_map/pallas_call | solution.py:411
  (20 shorter events, 0.1 us)
Async XLA Ops:
  0.7 1.0 %copy-start = (f32[4,252,128]{2,0,1:T(4,128)S(1)}, f32[4,252,128]{2,0,1:T(4,128)}, u32[]{:S(2)}) copy-start(f32[4,252,128]{2,0,1:T(4,128)} %param.6) | copy-start | bytes 1548292
  1.8 6.7 %collective-permute-start.1 = (bf16[4,256,128]{2,1,0:T(8,128)(2,1)S(1)}, bf16[4,256,128]{2,1,0:T(8,128)(2,1)S(1)}, u32[]{:S(2)}, u32[]{:S(2)}) collective-permute-start(bf16[4,256,128]{2,1,0:T(8,128)(2,1)S(1)} %get-tuple-element.33), channel_id=1, source_target_pairs={{0,1},{1,0},{2,3},{3,2},{4,8},{5,9},{6,10},{7,11},{8,4},{9,5},{10,... | collective-permute-start | bytes 786440 | tf_op jit(solution)/shard_map/ppermute | solution.py:303
  4.1 4.4 %collective-permute-start = (bf16[4,256,128]{2,1,0:T(8,128)(2,1)S(1)}, bf16[4,256,128]{2,1,0:T(8,128)(2,1)S(1)}, u32[]{:S(2)}, u32[]{:S(2)}) collective-permute-start(bf16[4,256,128]{2,1,0:T(8,128)(2,1)S(1)} %get-tuple-element.33), channel_id=1, source_target_pairs={{0,4},{1,5},{2,6},{3,7},{4,0},{5,1},{6,2},{7,3},{8,12},{9,13},{10,... | collective-permute-start | bytes 786440 | tf_op jit(solution)/shard_map/ppermute | solution.py:303
  6.8 1.7 %copy-start.2 = (s32[1,2]{1,0:T(1,128)S(1)}, s32[1,2]{1,0:T(1,128)}, u32[]{:S(2)}) copy-start(s32[1,2]{1,0:T(1,128)} %margin.7) | copy-start | bytes 28
  9.4 1.5 %collective-permute-start.2 = (bf16[1,256,128]{2,1,0:T(8,128)(2,1)S(1)}, bf16[1,256,128]{2,1,0:T(8,128)(2,1)S(1)}, u32[]{:S(2)}, u32[]{:S(2)}) collective-permute-start(bf16[1,256,128]{2,1,0:T(8,128)(2,1)S(1)} %get-tuple-element.36), channel_id=1, source_target_pairs={{0,4},{1,5},{2,6},{3,7},{4,0},{5,1},{6,2},{7,3},{8,12},{9,13},{10,... | collective-permute-start | bytes 196616 | tf_op jit(solution)/shard_map/ppermute | solution.py:303
  10.9 8.4 %copy-start.1 = (s32[4,8]{1,0:T(4,128)S(1)}, s32[4,8]{1,0:T(4,128)}, u32[]{:S(2)}) copy-start(s32[4,8]{1,0:T(4,128)} %neighbours.3) | copy-start | bytes 388
  11.0 8.3 %collective-permute-start.3 = (bf16[5,256,128]{2,1,0:T(8,128)(2,1)S(1)}, bf16[5,256,128]{2,1,0:T(8,128)(2,1)S(1)}, u32[]{:S(2)}, u32[]{:S(2)}) collective-permute-start(bf16[5,256,128]{2,1,0:T(8,128)(2,1)S(1)} %get-tuple-element.38.rest_0_), channel_id=1, source_target_pairs={{0,1},{1,0},{2,3},{3,2},{4,8},{5,9},{6,10},{7,11},{8,4},{9,5},{10,... | collective-permute-start | bytes 983048 | tf_op jit(solution)/shard_map/ppermute | solution.py:303
  13.1 6.2 %collective-permute-start.4 = (bf16[4,256,128]{2,1,0:T(8,128)(2,1)S(1)}, bf16[4,256,128]{2,1,0:T(8,128)(2,1)S(1)}, u32[]{:S(2)}, u32[]{:S(2)}) collective-permute-start(bf16[4,256,128]{2,1,0:T(8,128)(2,1)S(1)} %get-tuple-element.40), channel_id=1, source_target_pairs={{0,4},{1,5},{2,6},{3,7},{4,0},{5,1},{6,2},{7,3},{8,12},{9,13},{10,... | collective-permute-start | bytes 786440 | tf_op jit(solution)/shard_map/ppermute | solution.py:303
  13.1 6.2 %collective-permute-start.5 = (bf16[1,256,128]{2,1,0:T(8,128)(2,1)S(1)}, bf16[1,256,128]{2,1,0:T(8,128)(2,1)S(1)}, u32[]{:S(2)}, u32[]{:S(2)}) collective-permute-start(bf16[1,256,128]{2,1,0:T(8,128)(2,1)S(1)} %get-tuple-element.37.spill_out), channel_id=1, source_target_pairs={{0,4},{1,5},{2,6},{3,7},{4,12},{5,13},{6,14},{7,15},{8,0},{9,1},{1... | collective-permute-start | bytes 196616 | tf_op jit(solution)/shard_map/ppermute | solution.py:303
  21.1 3.0 %collective-permute-start.6 = (bf16[1,256,128]{2,1,0:T(8,128)(2,1)S(1)}, bf16[1,256,128]{2,1,0:T(8,128)(2,1)S(1)}, u32[]{:S(2)}, u32[]{:S(2)}) collective-permute-start(bf16[1,256,128]{2,1,0:T(8,128)(2,1)S(1)} %get-tuple-element.43), channel_id=1, source_target_pairs={{0,4},{1,5},{2,6},{3,7},{4,0},{5,1},{6,2},{7,3},{8,12},{9,13},{10,... | collective-permute-start | bytes 196616 | tf_op jit(solution)/shard_map/ppermute | solution.py:303
  21.8 4.3 %collective-permute-start.7 = (bf16[1,256,128]{2,1,0:T(8,128)(2,1)S(1)}, bf16[1,256,128]{2,1,0:T(8,128)(2,1)S(1)}, u32[]{:S(2)}, u32[]{:S(2)}) collective-permute-start(bf16[1,256,128]{2,1,0:T(8,128)(2,1)S(1)} %get-tuple-element.44), channel_id=1, source_target_pairs={{0,1},{1,0},{2,3},{3,2},{4,8},{5,9},{6,10},{7,11},{8,4},{9,5},{10,... | collective-permute-start | bytes 196616 | tf_op jit(solution)/shard_map/ppermute | solution.py:303
  26.9 2.1 %collective-permute-start.8 = (bf16[1,256,128]{2,1,0:T(8,128)(2,1)S(1)}, bf16[1,256,128]{2,1,0:T(8,128)(2,1)S(1)}, u32[]{:S(2)}, u32[]{:S(2)}) collective-permute-start(bf16[1,256,128]{2,1,0:T(8,128)(2,1)S(1)} %get-tuple-element.47), channel_id=1, source_target_pairs={{0,4},{1,5},{2,6},{3,7},{4,0},{5,1},{6,2},{7,3},{8,12},{9,13},{10,... | collective-permute-start | bytes 196616 | tf_op jit(solution)/shard_map/ppermute | solution.py:303
  29.1 8.7 %collective-permute-start.9 = (bf16[5,256,128]{2,1,0:T(8,128)(2,1)S(1)}, bf16[5,256,128]{2,1,0:T(8,128)(2,1)S(1)}, u32[]{:S(2)}, u32[]{:S(2)}) collective-permute-start(bf16[5,256,128]{2,1,0:T(8,128)(2,1)S(1)} %get-tuple-element.50), channel_id=1, source_target_pairs={{0,1},{1,0},{2,3},{3,2},{4,8},{5,9},{6,10},{7,11},{8,4},{9,5},{10,... | collective-permute-start | bytes 983048 | tf_op jit(solution)/shard_map/ppermute | solution.py:303
  30.2 7.7 %collective-permute-start.10 = (bf16[4,256,128]{2,1,0:T(8,128)(2,1)S(1)}, bf16[4,256,128]{2,1,0:T(8,128)(2,1)S(1)}, u32[]{:S(2)}, u32[]{:S(2)}) collective-permute-start(bf16[4,256,128]{2,1,0:T(8,128)(2,1)S(1)} %get-tuple-element.51), channel_id=1, source_target_pairs={{0,4},{1,5},{2,6},{3,7},{4,0},{5,1},{6,2},{7,3},{8,12},{9,13},{10,... | collective-permute-start | bytes 786440 | tf_op jit(solution)/shard_map/ppermute | solution.py:303
  32.2 5.6 %collective-permute-start.11 = (bf16[1,256,128]{2,1,0:T(8,128)(2,1)S(1)}, bf16[1,256,128]{2,1,0:T(8,128)(2,1)S(1)}, u32[]{:S(2)}, u32[]{:S(2)}) collective-permute-start(bf16[1,256,128]{2,1,0:T(8,128)(2,1)S(1)} %get-tuple-element.48.spill_out), channel_id=1, source_target_pairs={{0,4},{1,5},{2,6},{3,7},{4,12},{5,13},{6,14},{7,15},{8,0},{9,1},{1... | collective-permute-start | bytes 196616 | tf_op jit(solution)/shard_map/ppermute | solution.py:303
  39.6 1.3 %collective-permute-start.12 = (f32[6,128]{1,0:T(8,128)S(1)}, f32[6,128]{1,0:T(8,128)S(1)}, u32[]{:S(2)}, u32[]{:S(2)}) collective-permute-start(f32[6,128]{1,0:T(8,128)S(1)} %pad_maximum_fusion), channel_id=1, source_target_pairs={{0,4},{1,5},{2,6},{3,7},{4,0},{5,1},{6,2},{7,3},{8,12},{9,13},{10,... | collective-permute-start | bytes 9224 | tf_op jit(solution)/shard_map/ppermute | solution.py:303

commit v6 on v5

--- a/solution.py
+++ b/solution.py
@@ -19,7 +19,7 @@
 F32 = jnp.float32
 BF16 = jnp.bfloat16
 CHUNK = 8
-SPLIT = 2
+SPLIT = 4
 OWN = 1024
 FROM = 896
 ANY = pl.BlockSpec(memory_space=pl.ANY)
@@ -68,13 +68,13 @@
         copies.append(pltpu.make_async_copy(inverse.at[0], inverse_ref, sems.at[chunks]))
     for copy in copies:
         copy.start()
-    lane = lax.broadcasted_iota(jnp.int32, (8, 128), 1)
-
-    def pair(i, carry):
-        for h in range(2):
-            at = pl.multiple_of((2 * i + h) * lanes, 128)
-            x[4 * h : 4 * h + 4, :] = raw[:, pl.ds(at, lanes)].astype(F32)
-        base = pl.multiple_of(2 * i * (GROUP * NS), 8)
+    lane = lax.broadcasted_iota(jnp.int32, (4 * NS, 128), 1)
+
+    def four(i, carry):
+        for h in range(4):
+            at = pl.multiple_of((4 * i + h) * lanes, 128)
+            x[NS * h : NS * h + NS, :] = raw[:, pl.ds(at, lanes)]
+        base = pl.multiple_of(4 * i * (GROUP * NS), 8)
         for s in range(GROUP):
             def rolled(t):
                 piece = x[:, 128 * t : 128 * t + 128]
@@ -87,15 +87,16 @@
                 early = lane < 4 * s
                 left = jnp.where(early, rolled(2 * s - 1), middle)
                 right = jnp.where(early, middle, rolled(2 * s + 1)) if s < GROUP - 1 else middle
-            for h in range(2):
+            left, right = left.astype(F32), right.astype(F32)
+            for h in range(4):
                 at = base + (h * GROUP + s) * NS
-                lo[pl.ds(at, NS), :] = left[4 * h : 4 * h + 4]
-                hi[pl.ds(at, NS), :] = right[4 * h : 4 * h + 4]
+                lo[pl.ds(at, NS), :] = left[NS * h : NS * h + NS]
+                hi[pl.ds(at, NS), :] = right[NS * h : NS * h + NS]
         return carry
 
     for c in range(chunks):
         copies[c].wait()
-        lax.fori_loop(c * CHUNK // 2, (c + 1) * CHUNK // 2, pair, 0)
+        lax.fori_loop(c * CHUNK // 4, (c + 1) * CHUNK // 4, four, 0)
     keep = lax.broadcasted_iota(jnp.int32, (WP, 128), 1) < W - 128
     pad = jnp.zeros((WP - W, 128), F32)
     skip = (blocks[0] * W - groups[0] * GROUP) * NS
@@ -348,7 +349,7 @@
             [ANY, ANY],
             [
                 pltpu.VMEM((NS, count * lanes), BF16),
-                pltpu.VMEM((2 * NS, lanes), F32),
+                pltpu.VMEM((4 * NS, lanes), BF16),
                 pltpu.VMEM((count * GROUP * NS, 128), F32),
                 pltpu.VMEM((count * GROUP * NS, 128), F32),
                 pltpu.SemaphoreType.DMA((count // CHUNK + 1,)),

time: 67.7 us -> 66 us (0.975); the launches traced: 66.5 us -> 65.9 us
  Pallas kernels: 19.6 us -> 16.9 us
  blocking collectives: 24.6 us -> 26.2 us
  waiting for transfers between devices: 9.38 us -> 10.2 us
    pallas_call x2, Pallas kernels: 8.34 us -> 6.56 us  [matrices(): call(functools.partial(coupling_kernel, blocks, groups, first), outs, [AN...]
    all_to_all x1, blocking collectives: 24.6 us -> 26.2 us  [body(): lax.all_to_all(jnp.broadcast_to(sums[None], (NSUB // 2, 6, R)), 'sub', 0,...]
    pallas_call x2, Pallas kernels: 3.52 us -> 2.62 us  [system(): call(functools.partial(system_kernel, first), outs + [((8, R), F32)], [SM...]
    ppermute x13, waiting for transfers between devices: 9.38 us -> 10.2 us  [permuted(): lax.ppermute(x, ('sub', 'rhs'), [(i * parts + j, t[0] * parts + t[1]) for...]
  transfers between devices with their start and end apart: 13 -> 13, of which waited for: 4 -> 5; matrix products, arithmetic and copies ran while one was open for 0% -> 0% of each run, Pallas kernels for 20% -> 17%
where the time goes in v6:
time: 66 us; the launch traced here: 65.9 us
  blocking collectives  26.2 us (40%)
  Pallas kernels  16.9 us (26%)
  starting transfers between devices  10.6 us (16%)
  waiting for transfers between devices  10.2 us (15%)
  local copies, waits for them, and re-layouts  1.06 us (2%)
  between operations  0.84 us (1%)
    all_to_all x1, blocking collectives, body(): lax.all_to_all(jnp.broadcast_to(sums[None], (NSUB // 2, 6, R)), 'sub', 0,...  26.2 us
    ppermute x13, starting transfers between devices, permuted(): lax.ppermute(x, ('sub', 'rhs'), [(i * parts + j, t[0] * parts + t[1]) for...  10.6 us
    ppermute x13, waiting for transfers between devices, permuted(): lax.ppermute(x, ('sub', 'rhs'), [(i * parts + j, t[0] * parts + t[1]) for...  10.2 us
    pallas_call x2, Pallas kernels, matrices(): call(functools.partial(coupling_kernel, blocks, groups, first), outs, [AN...  6.56 us
    pallas_call x2, Pallas kernels, solve(): call(solve_kernel, [(block, F32), (one, BF16)], [SM, SM] + [VM] * 3, [plt...  2.81 us
    pallas_call x2, Pallas kernels, system(): call(functools.partial(system_kernel, first), outs + [((8, R), F32)], [SM...  2.62 us
    pallas_call x2, Pallas kernels, solve(): call(own_kernel, [((6 * W, R), F32, True)], [VM, VM], [pltpu.VMEM((OWN, R...  1.97 us
    pallas_call x2, Pallas kernels, solve(): call(margin_kernel, [(one, BF16), ((depth, R), BF16)], [SM, SM] + [VM] *...  1.76 us
  transfers between devices with their start and end apart: 13, of which 5 were waited for; matrix products, arithmetic and copies ran while one was open for 0% of the time, Pallas kernels for 17%

profile of v6, /device:TPU:2, one launch (start us, length us, event | category | flops | bytes accessed | tf_op | source)
XLA Modules:
  0.0 65.9 jit_solution(3331720252748268213)
XLA Ops:
  0.7 1.0 %copy-done = f32[4,252,128]{2,0,1:T(4,128)S(1)} copy-done((f32[4,252,128]{2,0,1:T(4,128)S(1)}, f32[4,252,128]{2,0,1:T(4,128)}, u32[]{:S(2)}) %copy-start) | copy-done | bytes 516120
  1.7 0.1 shard_map.65
  1.8 2.4 %collective-permute-start.1 = (bf16[4,256,128]{2,1,0:T(8,128)(2,1)S(1)}, bf16[4,256,128]{2,1,0:T(8,128)(2,1)S(1)}, u32[]{:S(2)}, u32[]{:S(2)}) collective-permute-start(bf16[4,256,128]{2,1,0:T(8,128)(2,1)S(1)} %get-tuple-element.33), channel_id=1, source_target_pairs={{0,1},{1,0},{2,3},{3,2},{4,8},{5,9},{6,10},{7,11},{8,4},{9,5},{10,... | collective-permute-start | bytes 786440 | tf_op jit(solution)/shard_map/ppermute | solution.py:304
  4.1 3.3 %shard_map.64 = (bf16[16,256,256]{2,1,0:T(8,128)(2,1)S(1)}, bf16[1512,1512]{1,0:T(8,128)(2,1)S(1)}) custom-call(bf16[4,508032]{1,0:T(4,128)(2,1)} %flat.3, bf16[1,1512,1512]{2,1,0:T(8,128)(2,1)} %rest_0_.1), custom_call_target="tpu_custom_call" | custom-call | flops 1048576 | bytes 12582912 | tf_op jit(solution)/shard_map/pallas_call | solution.py:346
  7.4 0.0 copy-start.2
  7.4 1.0 %shard_map.66.part = f32[1512,128]{1,0:T(8,128)S(1)} custom-call(bf16[1512,1512]{1,0:T(8,128)(2,1)S(1)} %get-tuple-element.31.inverse, f32[4,256,128]{2,1,0:T(8,128)S(1)} %get-tuple-element.32.own.v0), custom_call_target="tpu_custom_call" | custom-call | flops 1073741824 | bytes 4194304 | tf_op jit(solution)/shard_map/pallas_call | solution.py:366
  8.4 0.1 collective-permute-done.1.outer
  8.5 0.9 %shard_map.67 = (bf16[1,256,128]{2,1,0:T(8,128)(2,1)S(1)}, bf16[616,128]{1,0:T(8,128)(2,1)S(1)}) custom-call(s32[1]{0:T(128)} %bitcast.place, s32[1,2]{1,0:T(1,128)S(1)} %copy-done.2, bf16[1512,1512]{1,0:T(8,128)(2,1)S(1)} %get-tuple-element.31.inverse, f32[1512,128]{1,0:T(8,128)S(1)} %shard_map.66.part, f32[4,256,128]{2,1,0:T(8,128)S(1)} %get-tuple-element.32.own.v0, ...), custom_call_target="tpu_custom_call" | custom-call | tf_op jit(solution)/shard_map/pallas_call | solution.py:371
  9.4 0.5 collective-permute-start.2
  9.9 1.4 %shard_map.68 = (f32[4,256,128]{2,1,0:T(8,128)S(1)}, bf16[1,256,128]{2,1,0:T(8,128)(2,1)S(1)}) custom-call(s32[1]{0:T(128)} %bitcast.place, s32[1,2]{1,0:T(1,128)S(1)} %copy-done.2, bf16[1512,1512]{1,0:T(8,128)(2,1)S(1)} %get-tuple-element.31.inverse, f32[1512,128]{1,0:T(8,128)S(1)} %shard_map.66.part, bf16[616,128]{1,0:T(8,128)(2,1)S(1)} %get-tuple-element.34.ext), custom_call_target="tpu_custom_call" | custom-call | flops 1073741824 | bytes 4194304 | tf_op jit(solution)/shard_map/pallas_call | solution.py:378
  11.3 0.1 shard_map.69
  11.4 1.7 %collective-permute-start.3 = (bf16[5,256,128]{2,1,0:T(8,128)(2,1)S(1)}, bf16[5,256,128]{2,1,0:T(8,128)(2,1)S(1)}, u32[]{:S(2)}, u32[]{:S(2)}) collective-permute-start(bf16[5,256,128]{2,1,0:T(8,128)(2,1)S(1)} %get-tuple-element.38.rest_0_), channel_id=1, source_target_pairs={{0,1},{1,0},{2,3},{3,2},{4,8},{5,9},{6,10},{7,11},{8,4},{9,5},{10,... | collective-permute-start | bytes 983048 | tf_op jit(solution)/shard_map/ppermute | solution.py:304
  13.1 0.5 collective-permute-start.5
  13.6 3.3 %shard_map.70.cb = bf16[16,256,256]{2,1,0:T(8,128)(2,1)S(1)} custom-call(bf16[4,508032]{1,0:T(4,128)(2,1)} %flat.3, bf16[5,256,128]{2,1,0:T(8,128)(2,1)S(1)} %get-tuple-element.38.rest_0_), custom_call_target="tpu_custom_call" | custom-call | flops 1048576 | bytes 12582912 | tf_op jit(solution)/shard_map/pallas_call | solution.py:346
  16.9 2.1 %collective-permute-done.5.far = bf16[1,256,128]{2,1,0:T(8,128)(2,1)S(1)} collective-permute-done((bf16[1,256,128]{2,1,0:T(8,128)(2,1)S(1)}, bf16[1,256,128]{2,1,0:T(8,128)(2,1)S(1)}, u32[]{:S(2)}, u32[]{:S(2)}) %collective-permute-start.5) | collective-permute-done | bytes 65568 | tf_op jit(solution)/shard_map/ppermute | solution.py:304
  19.0 1.4 %shard_map.71 = (f32[4,256,128]{2,1,0:T(8,128)S(1)}, f32[4,256,128]{2,1,0:T(8,128)S(1)}, bf16[1,256,128]{2,1,0:T(8,128)(2,1)S(1)}, bf16[1,256,128]{2,1,0:T(8,128)(2,1)S(1)}, f32[8,128]{1,0:T(8,128)S(1)}) custom-call(s32[1]{0:T(128)} %bitcast.place, s32[1]{0:T(128)S(6)} %copy.7.counts, s32[4,8]{1,0:T(4,128)S(1)} %copy-done.1, ...), custom_call_target="tpu_custom_call" | custom-call | tf_op jit(solution)/shard_map/pallas_call | solution.py:396
  20.4 0.1 collective-permute-start.6
  20.5 2.1 %collective-permute-start.7 = (bf16[1,256,128]{2,1,0:T(8,128)(2,1)S(1)}, bf16[1,256,128]{2,1,0:T(8,128)(2,1)S(1)}, u32[]{:S(2)}, u32[]{:S(2)}) collective-permute-start(bf16[1,256,128]{2,1,0:T(8,128)(2,1)S(1)} %get-tuple-element.44), channel_id=1, source_target_pairs={{0,1},{1,0},{2,3},{3,2},{4,8},{5,9},{6,10},{7,11},{8,4},{9,5},{10,... | collective-permute-start | bytes 196616 | tf_op jit(solution)/shard_map/ppermute | solution.py:304
  22.6 1.0 %shard_map.72.part = f32[1512,128]{1,0:T(8,128)S(1)} custom-call(bf16[1512,1512]{1,0:T(8,128)(2,1)S(1)} %get-tuple-element.31.inverse, f32[4,256,128]{2,1,0:T(8,128)S(1)} %get-tuple-element.42.own.rest_0_), custom_call_target="tpu_custom_call" | custom-call | flops 1073741824 | bytes 4194304 | tf_op jit(solution)/shard_map/pallas_call | solution.py:366
  23.6 1.2 %collective-permute-done.7.outer = bf16[1,256,128]{2,1,0:T(8,128)(2,1)S(1)} collective-permute-done((bf16[1,256,128]{2,1,0:T(8,128)(2,1)S(1)}, bf16[1,256,128]{2,1,0:T(8,128)(2,1)S(1)}, u32[]{:S(2)}, u32[]{:S(2)}) %collective-permute-start.7) | collective-permute-done | bytes 65568 | tf_op jit(solution)/shard_map/ppermute | solution.py:304
  24.8 0.9 %shard_map.73 = (bf16[1,256,128]{2,1,0:T(8,128)(2,1)S(1)}, bf16[616,128]{1,0:T(8,128)(2,1)S(1)}) custom-call(s32[1]{0:T(128)} %bitcast.place, s32[1,2]{1,0:T(1,128)S(1)} %copy-done.2, bf16[1512,1512]{1,0:T(8,128)(2,1)S(1)} %get-tuple-element.31.inverse, f32[1512,128]{1,0:T(8,128)S(1)} %shard_map.72.part, f32[4,256,128]{2,1,0:T(8,128)S(1)} %get-tuple-element.42.own.rest_0_, ...), custom_call_target="tpu_custom_call" | custom-call | tf_op jit(solution)/shard_map/pallas_call | solution.py:371
  25.7 0.3 collective-permute-start.8
  26.1 1.4 %shard_map.74 = (f32[4,256,128]{2,1,0:T(8,128)S(1)}, bf16[1,256,128]{2,1,0:T(8,128)(2,1)S(1)}) custom-call(s32[1]{0:T(128)} %bitcast.place, s32[1,2]{1,0:T(1,128)S(1)} %copy-done.2, bf16[1512,1512]{1,0:T(8,128)(2,1)S(1)} %get-tuple-element.31.inverse, f32[1512,128]{1,0:T(8,128)S(1)} %shard_map.72.part, bf16[616,128]{1,0:T(8,128)(2,1)S(1)} %get-tuple-element.45.ext), custom_call_target="tpu_custom_call" | custom-call | flops 1073741824 | bytes 4194304 | tf_op jit(solution)/shard_map/pallas_call | solution.py:378
  27.5 0.1 shard_map.75
  27.6 2.1 %collective-permute-start.9 = (bf16[5,256,128]{2,1,0:T(8,128)(2,1)S(1)}, bf16[5,256,128]{2,1,0:T(8,128)(2,1)S(1)}, u32[]{:S(2)}, u32[]{:S(2)}) collective-permute-start(bf16[5,256,128]{2,1,0:T(8,128)(2,1)S(1)} %get-tuple-element.50), channel_id=1, source_target_pairs={{0,1},{1,0},{2,3},{3,2},{4,8},{5,9},{6,10},{7,11},{8,4},{9,5},{10,... | collective-permute-start | bytes 983048 | tf_op jit(solution)/shard_map/ppermute | solution.py:304
  29.7 0.7 %collective-permute-start.10 = (bf16[4,256,128]{2,1,0:T(8,128)(2,1)S(1)}, bf16[4,256,128]{2,1,0:T(8,128)(2,1)S(1)}, u32[]{:S(2)}, u32[]{:S(2)}) collective-permute-start(bf16[4,256,128]{2,1,0:T(8,128)(2,1)S(1)} %get-tuple-element.51), channel_id=1, source_target_pairs={{0,4},{1,5},{2,6},{3,7},{4,0},{5,1},{6,2},{7,3},{8,12},{9,13},{10,... | collective-permute-start | bytes 786440 | tf_op jit(solution)/shard_map/ppermute | solution.py:304
  30.4 5.6 %collective-permute-done.11.far = bf16[1,256,128]{2,1,0:T(8,128)(2,1)S(1)} collective-permute-done((bf16[1,256,128]{2,1,0:T(8,128)(2,1)S(1)}, bf16[1,256,128]{2,1,0:T(8,128)(2,1)S(1)}, u32[]{:S(2)}, u32[]{:S(2)}) %collective-permute-start.11) | collective-permute-done | bytes 65568 | tf_op jit(solution)/shard_map/ppermute | solution.py:304
  36.1 1.3 %shard_map.76 = (f32[4,256,128]{2,1,0:T(8,128)S(1)}, f32[8,128]{1,0:T(8,128)S(1)}) custom-call(s32[1]{0:T(128)} %bitcast.place, s32[1]{0:T(128)S(6)} %copy.7.counts, s32[4,8]{1,0:T(4,128)S(1)} %copy-done.1, bf16[16,256,256]{2,1,0:T(8,128)(2,1)S(1)} %get-tuple-element.30.ca, bf16[16,256,256]{2,1,0:T(8,128)(2,1)S(1)} %shard_map.70.cb, ...), custom_call_target="tpu_custom_call" | custom-call | tf_op jit(solution)/shard_map/pallas_call | solution.py:396
  37.4 0.1 collective-permute-start.12
  37.5 1.2 %collective-permute-done.12 = f32[6,128]{1,0:T(8,128)S(1)} collective-permute-done((f32[6,128]{1,0:T(8,128)S(1)}, f32[6,128]{1,0:T(8,128)S(1)}, u32[]{:S(2)}, u32[]{:S(2)}) %collective-permute-start.12) | collective-permute-done | bytes 3104 | tf_op jit(solution)/shard_map/ppermute | solution.py:304
  38.6 26.2 %all_to_all.5.gathered = f32[32,6,128]{2,1,0:T(8,128)S(1)} all-to-all(f32[32,6,128]{2,1,0:T(8,128)S(1)} %broadcast_in_dim.2), channel_id=1, replica_groups={{0,8,16,24,32,40,48,56,64,72,80,88,96,104,112,120,128,136,144,152,160,1..., dimensions={0} | all-to-all | bytes 196608 | tf_op jit(solution)/shard_map/all_to_all | solution.py:408
  64.9 1.0 %shard_map.77 = f32[1008,128]{1,0:T(8,128)} custom-call(f32[32,6,128]{2,1,0:T(8,128)S(1)} %all_to_all.5.gathered, f32[4,256,128]{2,1,0:T(8,128)S(1)} %get-tuple-element.53.p0, f32[4,256,128]{2,1,0:T(8,128)S(1)} %get-tuple-element.54.q), custom_call_target="tpu_custom_call" | custom-call | tf_op jit(solution)/shard_map/pallas_call | solution.py:412
  (20 shorter events, 0.1 us)
Async XLA Ops:
  0.7 1.0 %copy-start = (f32[4,252,128]{2,0,1:T(4,128)S(1)}, f32[4,252,128]{2,0,1:T(4,128)}, u32[]{:S(2)}) copy-start(f32[4,252,128]{2,0,1:T(4,128)} %param.6) | copy-start | bytes 1548292
  1.8 6.7 %collective-permute-start.1 = (bf16[4,256,128]{2,1,0:T(8,128)(2,1)S(1)}, bf16[4,256,128]{2,1,0:T(8,128)(2,1)S(1)}, u32[]{:S(2)}, u32[]{:S(2)}) collective-permute-start(bf16[4,256,128]{2,1,0:T(8,128)(2,1)S(1)} %get-tuple-element.33), channel_id=1, source_target_pairs={{0,1},{1,0},{2,3},{3,2},{4,8},{5,9},{6,10},{7,11},{8,4},{9,5},{10,... | collective-permute-start | bytes 786440 | tf_op jit(solution)/shard_map/ppermute | solution.py:304
  4.1 4.4 %collective-permute-start = (bf16[4,256,128]{2,1,0:T(8,128)(2,1)S(1)}, bf16[4,256,128]{2,1,0:T(8,128)(2,1)S(1)}, u32[]{:S(2)}, u32[]{:S(2)}) collective-permute-start(bf16[4,256,128]{2,1,0:T(8,128)(2,1)S(1)} %get-tuple-element.33), channel_id=1, source_target_pairs={{0,4},{1,5},{2,6},{3,7},{4,0},{5,1},{6,2},{7,3},{8,12},{9,13},{10,... | collective-permute-start | bytes 786440 | tf_op jit(solution)/shard_map/ppermute | solution.py:304
  7.4 1.1 %copy-start.2 = (s32[1,2]{1,0:T(1,128)S(1)}, s32[1,2]{1,0:T(1,128)}, u32[]{:S(2)}) copy-start(s32[1,2]{1,0:T(1,128)} %margin.7) | copy-start | bytes 28
  9.4 1.9 %collective-permute-start.2 = (bf16[1,256,128]{2,1,0:T(8,128)(2,1)S(1)}, bf16[1,256,128]{2,1,0:T(8,128)(2,1)S(1)}, u32[]{:S(2)}, u32[]{:S(2)}) collective-permute-start(bf16[1,256,128]{2,1,0:T(8,128)(2,1)S(1)} %get-tuple-element.36), channel_id=1, source_target_pairs={{0,4},{1,5},{2,6},{3,7},{4,0},{5,1},{6,2},{7,3},{8,12},{9,13},{10,... | collective-permute-start | bytes 196616 | tf_op jit(solution)/shard_map/ppermute | solution.py:304
  11.3 7.7 %copy-start.1 = (s32[4,8]{1,0:T(4,128)S(1)}, s32[4,8]{1,0:T(4,128)}, u32[]{:S(2)}) copy-start(s32[4,8]{1,0:T(4,128)} %neighbours.3) | copy-start | bytes 388
  11.4 7.6 %collective-permute-start.3 = (bf16[5,256,128]{2,1,0:T(8,128)(2,1)S(1)}, bf16[5,256,128]{2,1,0:T(8,128)(2,1)S(1)}, u32[]{:S(2)}, u32[]{:S(2)}) collective-permute-start(bf16[5,256,128]{2,1,0:T(8,128)(2,1)S(1)} %get-tuple-element.38.rest_0_), channel_id=1, source_target_pairs={{0,1},{1,0},{2,3},{3,2},{4,8},{5,9},{6,10},{7,11},{8,4},{9,5},{10,... | collective-permute-start | bytes 983048 | tf_op jit(solution)/shard_map/ppermute | solution.py:304
  13.1 5.9 %collective-permute-start.4 = (bf16[4,256,128]{2,1,0:T(8,128)(2,1)S(1)}, bf16[4,256,128]{2,1,0:T(8,128)(2,1)S(1)}, u32[]{:S(2)}, u32[]{:S(2)}) collective-permute-start(bf16[4,256,128]{2,1,0:T(8,128)(2,1)S(1)} %get-tuple-element.40), channel_id=1, source_target_pairs={{0,4},{1,5},{2,6},{3,7},{4,0},{5,1},{6,2},{7,3},{8,12},{9,13},{10,... | collective-permute-start | bytes 786440 | tf_op jit(solution)/shard_map/ppermute | solution.py:304
  13.1 5.9 %collective-permute-start.5 = (bf16[1,256,128]{2,1,0:T(8,128)(2,1)S(1)}, bf16[1,256,128]{2,1,0:T(8,128)(2,1)S(1)}, u32[]{:S(2)}, u32[]{:S(2)}) collective-permute-start(bf16[1,256,128]{2,1,0:T(8,128)(2,1)S(1)} %get-tuple-element.37.spill_out), channel_id=1, source_target_pairs={{0,4},{1,5},{2,6},{3,7},{4,12},{5,13},{6,14},{7,15},{8,0},{9,1},{1... | collective-permute-start | bytes 196616 | tf_op jit(solution)/shard_map/ppermute | solution.py:304
  20.4 3.2 %collective-permute-start.6 = (bf16[1,256,128]{2,1,0:T(8,128)(2,1)S(1)}, bf16[1,256,128]{2,1,0:T(8,128)(2,1)S(1)}, u32[]{:S(2)}, u32[]{:S(2)}) collective-permute-start(bf16[1,256,128]{2,1,0:T(8,128)(2,1)S(1)} %get-tuple-element.43), channel_id=1, source_target_pairs={{0,4},{1,5},{2,6},{3,7},{4,0},{5,1},{6,2},{7,3},{8,12},{9,13},{10,... | collective-permute-start | bytes 196616 | tf_op jit(solution)/shard_map/ppermute | solution.py:304
  20.5 4.4 %collective-permute-start.7 = (bf16[1,256,128]{2,1,0:T(8,128)(2,1)S(1)}, bf16[1,256,128]{2,1,0:T(8,128)(2,1)S(1)}, u32[]{:S(2)}, u32[]{:S(2)}) collective-permute-start(bf16[1,256,128]{2,1,0:T(8,128)(2,1)S(1)} %get-tuple-element.44), channel_id=1, source_target_pairs={{0,1},{1,0},{2,3},{3,2},{4,8},{5,9},{6,10},{7,11},{8,4},{9,5},{10,... | collective-permute-start | bytes 196616 | tf_op jit(solution)/shard_map/ppermute | solution.py:304
  25.7 1.8 %collective-permute-start.8 = (bf16[1,256,128]{2,1,0:T(8,128)(2,1)S(1)}, bf16[1,256,128]{2,1,0:T(8,128)(2,1)S(1)}, u32[]{:S(2)}, u32[]{:S(2)}) collective-permute-start(bf16[1,256,128]{2,1,0:T(8,128)(2,1)S(1)} %get-tuple-element.47), channel_id=1, source_target_pairs={{0,4},{1,5},{2,6},{3,7},{4,0},{5,1},{6,2},{7,3},{8,12},{9,13},{10,... | collective-permute-start | bytes 196616 | tf_op jit(solution)/shard_map/ppermute | solution.py:304
  27.6 8.5 %collective-permute-start.9 = (bf16[5,256,128]{2,1,0:T(8,128)(2,1)S(1)}, bf16[5,256,128]{2,1,0:T(8,128)(2,1)S(1)}, u32[]{:S(2)}, u32[]{:S(2)}) collective-permute-start(bf16[5,256,128]{2,1,0:T(8,128)(2,1)S(1)} %get-tuple-element.50), channel_id=1, source_target_pairs={{0,1},{1,0},{2,3},{3,2},{4,8},{5,9},{6,10},{7,11},{8,4},{9,5},{10,... | collective-permute-start | bytes 983048 | tf_op jit(solution)/shard_map/ppermute | solution.py:304
  29.7 6.4 %collective-permute-start.10 = (bf16[4,256,128]{2,1,0:T(8,128)(2,1)S(1)}, bf16[4,256,128]{2,1,0:T(8,128)(2,1)S(1)}, u32[]{:S(2)}, u32[]{:S(2)}) collective-permute-start(bf16[4,256,128]{2,1,0:T(8,128)(2,1)S(1)} %get-tuple-element.51), channel_id=1, source_target_pairs={{0,4},{1,5},{2,6},{3,7},{4,0},{5,1},{6,2},{7,3},{8,12},{9,13},{10,... | collective-permute-start | bytes 786440 | tf_op jit(solution)/shard_map/ppermute | solution.py:304
  30.4 5.6 %collective-permute-start.11 = (bf16[1,256,128]{2,1,0:T(8,128)(2,1)S(1)}, bf16[1,256,128]{2,1,0:T(8,128)(2,1)S(1)}, u32[]{:S(2)}, u32[]{:S(2)}) collective-permute-start(bf16[1,256,128]{2,1,0:T(8,128)(2,1)S(1)} %get-tuple-element.48.spill_out), channel_id=1, source_target_pairs={{0,4},{1,5},{2,6},{3,7},{4,12},{5,13},{6,14},{7,15},{8,0},{9,1},{1... | collective-permute-start | bytes 196616 | tf_op jit(solution)/shard_map/ppermute | solution.py:304
  37.4 1.3 %collective-permute-start.12 = (f32[6,128]{1,0:T(8,128)S(1)}, f32[6,128]{1,0:T(8,128)S(1)}, u32[]{:S(2)}, u32[]{:S(2)}) collective-permute-start(f32[6,128]{1,0:T(8,128)S(1)} %pad_maximum_fusion), channel_id=1, source_target_pairs={{0,4},{1,5},{2,6},{3,7},{4,0},{5,1},{6,2},{7,3},{8,12},{9,13},{10,... | collective-permute-start | bytes 9224 | tf_op jit(solution)/shard_map/ppermute | solution.py:304

commit v7 on v6

--- a/solution.py
+++ b/solution.py
@@ -20,6 +20,8 @@
 BF16 = jnp.bfloat16
 CHUNK = 8
 SPLIT = 4
+EVEN, FIRST, LAST, LOW, HIGH, COUNT, ENDS, NEXT, OUT, SLOTS = range(10)
+TABLE = SLOTS + NS * NB
 OWN = 1024
 FROM = 896
 ANY = pl.BlockSpec(memory_space=pl.ANY)
@@ -30,9 +32,9 @@
 def call(kernel, outs, ins, scratch=(), limit=24, cost=None):
     return pl.pallas_call(
         kernel,
-        out_shape=[pltpu.VMEM(s, d) if keep else jax.ShapeDtypeStruct(s, d) for s, d, *keep in outs],
+        out_shape=[keep[0](s, d) if keep else jax.ShapeDtypeStruct(s, d) for s, d, *keep in outs],
         in_specs=ins,
-        out_specs=[VM] * len(outs),
+        out_specs=[SM if keep == [pltpu.SMEM] else VM for _, _, *keep in outs],
         scratch_shapes=list(scratch),
         compiler_params=pltpu.CompilerParams(vmem_limit_bytes=limit << 20),
         cost_estimate=cost,
@@ -47,9 +49,30 @@
         v0b_ref[s] = v0_ref[s].astype(BF16)
 
 
+def fill_table(table, place, counts, margin, neighbours):
+    here = place[0]
+    even = here % 2 == 0
+    first, last = here == 0, here == NSUB - 1
+    low = jnp.clip(margin[0, 0] - NS * jnp.maximum(here - 1, 0), 0, NS - 1)
+    high = jnp.clip(margin[0, 1] - NS * jnp.minimum(here + 1, NSUB - 1), 0, NS - 1)
+    table[EVEN] = jnp.where(even, 1, 0)
+    table[FIRST] = jnp.where(first, 1, 0)
+    table[LAST] = jnp.where(last, 1, 0)
+    table[LOW] = low
+    table[HIGH] = high
+    table[COUNT] = counts[0]
+    table[ENDS] = jnp.where(jnp.logical_or(first, last), 1, 0)
+    table[NEXT] = jnp.where(jnp.logical_or(here == 1, here == NSUB - 2), 1, 0)
+    table[OUT] = jnp.where(even, low, high)
+    for s in range(NS):
+        for k in range(NB):
+            slot = jnp.clip(neighbours[s, k] - NS * (here - 1), 0, 3 * NS - 1)
+            table[SLOTS + s * NB + k] = jnp.where(even, slot, slot + 2 * NS * (1 - slot // NS))
+
+
 def coupling_kernel(blocks, groups, first, flat, *rest):
     if first:
-        inverse, c_ref, inverse_ref, raw, x, lo, hi, sems = rest
+        inverse, place, counts, margin, neighbours, c_ref, inverse_ref, table, raw, x, lo, hi, sems = rest
     else:
         _, c_ref, raw, x, lo, hi, sems = rest
     lanes = GROUP * W
@@ -68,6 +91,8 @@
         copies.append(pltpu.make_async_copy(inverse.at[0], inverse_ref, sems.at[chunks]))
     for copy in copies:
         copy.start()
+    if first:
+        fill_table(table, place, counts, margin, neighbours)
     lane = lax.broadcasted_iota(jnp.int32, (4 * NS, 128), 1)
 
     def four(i, carry):
@@ -124,11 +149,8 @@
     part_ref[...] = jnp.dot(inverse[:, :OWN], ext[...].astype(BF16), preferred_element_type=F32)
 
 
-def places(place, margin):
-    here = place[0]
-    low = jnp.clip(margin[0, 0] - NS * jnp.maximum(here - 1, 0), 0, NS - 1)
-    high = jnp.clip(margin[0, 1] - NS * jnp.minimum(here + 1, NSUB - 1), 0, NS - 1)
-    return here % 2 == 0, here == 0, here == NSUB - 1, low, high
+def places(table):
+    return table[EVEN] == 1, table[FIRST] == 1, table[LAST] == 1, table[LOW], table[HIGH]
 
 
 def spilled(inverse, part, ext, block, index):
@@ -141,8 +163,8 @@
     return jnp.concatenate([rows, mark], axis=0)
 
 
-def margin_kernel(place, margin, inverse, part, own, inner, outer, in_ref, ext_ref, ext):
-    even, first, last, low, high = places(place, margin)
+def margin_kernel(table, inverse, part, own, inner, outer, in_ref, ext_ref, ext):
+    even, first, last, low, high = places(table)
     odd = jnp.logical_not(even)
     ext[: NS * W - FROM, :] = jnp.zeros((NS * W - FROM, R), F32)
     some = inner.shape[0] > 1
@@ -169,8 +191,8 @@
         in_ref[0] = spilled(inverse, part, ext_ref[...], NS, low).astype(BF16)
 
 
-def solve_kernel(place, margin, inverse, part, ext, out_ref, out2_ref, res):
-    even, first, last, low, high = places(place, margin)
+def solve_kernel(table, inverse, part, ext, out_ref, out2_ref, res):
+    even, first, last, low, high = places(table)
     mine = NS * W
     res[...] = part[:mine, :] + jnp.dot(inverse[:mine, FROM:], ext[...], preferred_element_type=F32)
     pad = jnp.zeros((WP - W, R), F32)
@@ -209,27 +231,26 @@
 
 
 def system_kernel(
-    first, place, counts, neighbours, ca, cb, part, got, near, far, spill_in, spill_out, v0, *rest
+    first, table, ca, cb, part, got, near, far, spill_out, v0, *rest
 ):
     if first:
-        p_ref, w_ref, win_ref, wout_ref, sums_ref, u = rest
+        p_ref, w_ref, wout_ref, sums_ref, u = rest
     else:
         w, p_ref, sums_ref, u = rest
-    here = place[0]
-    odd = here % 2 == 1
-    ends = jnp.logical_or(here == 0, here == NSUB - 1)
     got_values, got_index = opened(got[NS])
-    got_index = jnp.where(ends, -1.0, got_index)
+    got_index = jnp.where(table[ENDS] == 1, -1.0, got_index)
     far_values, far_index = opened(far[0])
-    far_index = jnp.where(jnp.logical_or(here == 1, here == NSUB - 2), -1.0, far_index)
-    values, index = opened(spill_out[0])
-    for s in range(NS):
-        alive = jnp.where(counts[0] > s, 1.0, 0.0)
+    far_index = jnp.where(table[NEXT] == 1, -1.0, far_index)
+    count = table[COUNT]
+    for s in range(NS):
+        alive = jnp.where(count > s, 1.0, 0.0)
         p = (part[s] + jnp.where(got_index == s, got_values, 0.0)) * alive
         p_ref[s] = p
-        u[s] = (got[s].astype(F32) + jnp.where(index == s, values, 0.0)).astype(BF16)
+        u[s] = got[s]
         u[NS + s] = p.astype(BF16)
         u[2 * NS + s] = (near[s].astype(F32) + jnp.where(far_index == s, far_values, 0.0)).astype(BF16)
+    index = table[OUT]
+    u[index] = (got[index].astype(F32) + opened(spill_out[0])[0]).astype(BF16)
     sums_ref[...] = jnp.zeros((8, R), F32)
     if first:
         w_ref[...] = jnp.zeros((NS, WP, R), F32)
@@ -237,8 +258,7 @@
     def one(s):
         acc = p_ref[s]
         for k in range(NB):
-            slot = jnp.clip(neighbours[s, k] - NS * (here - 1), 0, 3 * NS - 1)
-            slot = jnp.where(odd, slot + 2 * NS * (1 - slot // NS), slot)
+            slot = table[SLOTS + s * NB + k]
             matrix = ca[s * SPLIT + k] if k < SPLIT else cb[s * (NB - SPLIT) + k - SPLIT]
             acc += jnp.dot(matrix, u[slot], preferred_element_type=F32)
         image = acc
@@ -253,14 +273,20 @@
         sums_ref[...] += jnp.concatenate(sums + [jnp.zeros((5, R), F32)], axis=0)
 
     for s in range(NS):
-        pl.when(counts[0] > s)(functools.partial(one, s))
-    if first:
-        wanted = opened(spill_in[0])[1]
-        for ref, index in ((win_ref, wanted), (wout_ref, got_index)):
-            chosen = jnp.zeros((WP, R), F32)
-            for s in range(NS):
-                chosen = chosen + jnp.where(index == s, w_ref[s], 0.0)
-            ref[0] = chosen.astype(BF16)
+        pl.when(count > s)(functools.partial(one, s))
+    if first:
+        picked(wout_ref, w_ref, got_index)
+
+
+def picked(ref, w, index):
+    chosen = jnp.zeros((WP, R), F32)
+    for s in range(NS):
+        chosen = chosen + jnp.where(index == s, w[s], 0.0)
+    ref[0] = chosen.astype(BF16)
+
+
+def pick_kernel(w, spill_in, win_ref):
+    picked(win_ref, w, opened(spill_in[0])[1])
 
 
 def finish_kernel(gathered, p0, q, out):
@@ -331,22 +357,24 @@
     outer, inner = to_outer(v0b), to_inner(v0b)
 
     coupling = pltpu.with_memory_space_constraint(coupling, pltpu.HBM)
-    inverse = pltpu.with_memory_space_constraint(inverse, pltpu.HBM)
-
-    def matrices(first, more):
+    inverse, margin, neighbours = (
+        pltpu.with_memory_space_constraint(a, pltpu.HBM) for a in (inverse, margin, neighbours)
+    )
+
+    def matrices(first, *more):
         lanes = GROUP * W
         blocks = (0, SPLIT) if first else (SPLIT, NB)
         begin = blocks[0] * W // GROUP
         end = -(-blocks[1] * W // GROUP)
         count = -(-(end - begin) // CHUNK) * CHUNK
         groups = (begin, begin + count) if first else (end - count, end)
-        outs = [((NS * (blocks[1] - blocks[0]), WP, WP), BF16, True)]
+        outs = [((NS * (blocks[1] - blocks[0]), WP, WP), BF16, pltpu.VMEM)]
         if first:
-            outs.append(((6 * W, 6 * W), BF16, True))
+            outs += [((6 * W, 6 * W), BF16, pltpu.VMEM), ((TABLE,), jnp.int32, pltpu.SMEM)]
         return call(
             functools.partial(coupling_kernel, blocks, groups, first),
             outs,
-            [ANY, ANY],
+            [ANY, ANY] + [SM] * (len(more) - 1),
             [
                 pltpu.VMEM((NS, count * lanes), BF16),
                 pltpu.VMEM((4 * NS, lanes), BF16),
@@ -356,32 +384,33 @@
             ],
             limit=24,
             cost=pl.CostEstimate(flops=1 << 20, bytes_accessed=12 << 20, transcendentals=0),
-        )(coupling, more)
-
-    first_part, held = matrices(True, inverse)
+        )(coupling, *more)
+
+    first_part, held, table = matrices(True, inverse, here, counts, margin, neighbours)
+    table = pltpu.with_memory_space_constraint(table, pltpu.SMEM)
     held = pltpu.with_memory_space_constraint(held, pltpu.VMEM)
     first_part = pltpu.with_memory_space_constraint(first_part, pltpu.VMEM)
 
     def solve(own, inner, outer):
         (part,) = call(
-            own_kernel, [((6 * W, R), F32, True)], [VM, VM], [pltpu.VMEM((OWN, R), F32)],
+            own_kernel, [((6 * W, R), F32, pltpu.VMEM)], [VM, VM], [pltpu.VMEM((OWN, R), F32)],
             cost=pl.CostEstimate(flops=1 << 30, bytes_accessed=4 << 20, transcendentals=0),
         )(held, own)
         depth = 6 * W - FROM
         spill_in, ext = call(
             margin_kernel,
             [(one, BF16), ((depth, R), BF16)],
-            [SM, SM] + [VM] * 5,
+            [SM] + [VM] * 5,
             [pltpu.VMEM((depth, R), F32)],
-        )(here, margin, held, part, own, inner, outer)
+        )(table, held, part, own, inner, outer)
         got_in = to_inner(spill_in)
         out, spill_out = call(
             solve_kernel,
             [(block, F32), (one, BF16)],
-            [SM, SM] + [VM] * 3,
+            [SM] + [VM] * 3,
             [pltpu.VMEM((NS * W, R), F32)],
             cost=pl.CostEstimate(flops=1 << 30, bytes_accessed=4 << 20, transcendentals=0),
-        )(here, margin, held, part, ext)
+        )(table, held, part, ext)
         return out, got_in, spill_out
 
     def system(first, out, got_in, spill_out, *more):
@@ -392,17 +421,20 @@
         if first:
             (made,) = matrices(False, sent)
             matrix_parts.append(pltpu.with_memory_space_constraint(made, pltpu.VMEM))
-        outs = [(block, F32)] + ([(block, F32), (one, BF16), (one, BF16)] if first else [])
+        outs = [(block, F32)] + ([(block, F32), (one, BF16)] if first else [])
         return call(
             functools.partial(system_kernel, first),
             outs + [((8, R), F32)],
-            [SM, SM, SM] + [VM] * (8 + len(more)),
+            [SM] + [VM] * (7 + len(more)),
             [pltpu.VMEM((3 * NS, WP, R), BF16)],
-        )(here, counts, neighbours, *matrix_parts, part, got, near, far, got_in, spill_out, *more)
+        )(table, *matrix_parts, part, got, near, far, spill_out, *more)
 
     matrix_parts = [first_part]
-    p0, w, w_in, w_out, sums_one = system(True, *solve(v0, inner, outer), v0)
-    q, sums_two = system(False, *solve(w, to_inner(w_in), to_outer(w_out)), v0, w)
+    out, got_in, spill_out = solve(v0, inner, outer)
+    p0, w, w_out, sums_one = system(True, out, got_in, spill_out, v0)
+    outer = to_outer(w_out)
+    (w_in,) = call(pick_kernel, [(one, BF16)], [VM] * 2)(w, got_in)
+    q, sums_two = system(False, *solve(w, to_inner(w_in), outer), v0, w)
     sums = jnp.concatenate([sums_one[:3], sums_two[:3]], axis=0)
     sums = sums + to_inner(sums)
     gathered = lax.all_to_all(

time: 66 us -> 62.7 us (0.950)
  Pallas kernels: 16.9 us -> 14.2 us
  starting transfers between devices: 10.6 us -> 9.18 us
  waiting for transfers between devices: 10.2 us -> 11.4 us
  blocking collectives: 26.2 us -> 25.4 us
    pallas_call x6 -> x7, Pallas kernels: 6.54 us -> 4.41 us  [the longest x2 1.97 us: solve(): call(own_kernel, [((6 * W, R), F32, pltpu.VMEM)], [VM, VM], [pltpu.VMEM((...]
    ppermute x13, starting transfers between devices: 10.6 us -> 9.18 us  [permuted(): lax.ppermute(x, ('sub', 'rhs'), [(i * parts + j, t[0] * parts + t[1]) for...]
    pallas_call x2, Pallas kernels: 2.62 us -> 1.31 us  [system(): call(functools.partial(system_kernel, first), outs + [((8, R), F32)], [SM...]
    ppermute x13, waiting for transfers between devices: 10.2 us -> 11.4 us  [permuted(): lax.ppermute(x, ('sub', 'rhs'), [(i * parts + j, t[0] * parts + t[1]) for...]
    all_to_all x1, blocking collectives: 26.2 us -> 25.4 us  [body(): lax.all_to_all(jnp.broadcast_to(sums[None], (NSUB // 2, 6, R)), 'sub', 0,...]
    pallas_call x2, Pallas kernels: 6.56 us -> 7.25 us  [matrices(): call(functools.partial(coupling_kernel, blocks, groups, first), outs, [AN...]
  transfers between devices with their start and end apart: 13 -> 13, of which waited for: 5 -> 5; matrix products, arithmetic and copies ran while one was open for 0% -> 0% of each run, Pallas kernels for 17% -> 18%
where the time goes in v7:
time: 62.7 us; the launch traced here: 62 us
  blocking collectives  25.4 us (41%)
  Pallas kernels  14.2 us (23%)
  waiting for transfers between devices  11.4 us (18%)
  starting transfers between devices  9.18 us (15%)
  local copies, waits for them, and re-layouts  1.05 us (2%)
  between operations  0.81 us (1%)
    all_to_all x1, blocking collectives, body(): lax.all_to_all(jnp.broadcast_to(sums[None], (NSUB // 2, 6, R)), 'sub', 0,...  25.4 us
    ppermute x13, waiting for transfers between devices, permuted(): lax.ppermute(x, ('sub', 'rhs'), [(i * parts + j, t[0] * parts + t[1]) for...  11.4 us
    ppermute x13, starting transfers between devices, permuted(): lax.ppermute(x, ('sub', 'rhs'), [(i * parts + j, t[0] * parts + t[1]) for...  9.18 us
    pallas_call x2, Pallas kernels, matrices(): call(functools.partial(coupling_kernel, blocks, groups, first), outs, [AN...  7.25 us
    pallas_call x2, Pallas kernels, solve(): call(own_kernel, [((6 * W, R), F32, pltpu.VMEM)], [VM, VM], [pltpu.VMEM((...  1.97 us
    pallas_call x2, Pallas kernels, solve(): call(solve_kernel, [(block, F32), (one, BF16)], [SM] + [VM] * 3, [pltpu.V...  1.73 us
    pallas_call x2, Pallas kernels, system(): call(functools.partial(system_kernel, first), outs + [((8, R), F32)], [SM...  1.31 us
  transfers between devices with their start and end apart: 13, of which 5 were waited for; matrix products, arithmetic and copies ran while one was open for 0% of the time, Pallas kernels for 18%

profile of v7, /device:TPU:2, one launch (start us, length us, event | category | flops | bytes accessed | tf_op | source)
XLA Modules:
  0.0 62.0 jit_solution(17566627723467123173)
XLA Ops:
  0.7 1.0 %copy-done = f32[4,252,128]{2,0,1:T(4,128)S(1)} copy-done((f32[4,252,128]{2,0,1:T(4,128)S(1)}, f32[4,252,128]{2,0,1:T(4,128)}, u32[]{:S(2)}) %copy-start) | copy-done | bytes 516120
  1.7 0.1 shard_map.65
  1.8 2.4 %collective-permute-start.1 = (bf16[4,256,128]{2,1,0:T(8,128)(2,1)S(1)}, bf16[4,256,128]{2,1,0:T(8,128)(2,1)S(1)}, u32[]{:S(2)}, u32[]{:S(2)}) collective-permute-start(bf16[4,256,128]{2,1,0:T(8,128)(2,1)S(1)} %get-tuple-element.34), channel_id=1, source_target_pairs={{0,1},{1,0},{2,3},{3,2},{4,8},{5,9},{6,10},{7,11},{8,4},{9,5},{10,... | collective-permute-start | bytes 786440 | tf_op jit(solution)/shard_map/ppermute | solution.py:330
  4.1 4.0 %shard_map.64 = (bf16[16,256,256]{2,1,0:T(8,128)(2,1)S(1)}, bf16[1512,1512]{1,0:T(8,128)(2,1)S(1)}, s32[41]{0:T(128)S(4)}) custom-call(bf16[4,508032]{1,0:T(4,128)(2,1)} %flat.3, bf16[1,1512,1512]{2,1,0:T(8,128)(2,1)} %rest_0_.1, s32[1]{0:T(128)} %bitcast.rest_1_, s32[1]{0:T(128)S(6)} %copy.7.rest_2_.counts, s32[1,2]{1,0:T(1,128)} %rest_3_.1, s32[4,8]{1,0:T(4,128)} %rest_4_.1), custom_call_target="tpu_custom_call" | custom-call | flops 1048576 | bytes 12582912 | tf_op jit(solution)/shard_map/pallas_call | solution.py:374
  8.1 1.0 %shard_map.66.part = f32[1512,128]{1,0:T(8,128)S(1)} custom-call(bf16[1512,1512]{1,0:T(8,128)(2,1)S(1)} %get-tuple-element.32.inverse, f32[4,256,128]{2,1,0:T(8,128)S(1)} %get-tuple-element.33.own.v0), custom_call_target="tpu_custom_call" | custom-call | flops 1073741824 | bytes 4194304 | tf_op jit(solution)/shard_map/pallas_call | solution.py:395
  9.1 0.3 shard_map.67
  9.5 0.5 collective-permute-start.2
  10.0 0.9 %shard_map.68 = (f32[4,256,128]{2,1,0:T(8,128)S(1)}, bf16[1,256,128]{2,1,0:T(8,128)(2,1)S(1)}) custom-call(s32[41]{0:T(128)S(4)} %get-tuple-element.30.table, bf16[1512,1512]{1,0:T(8,128)(2,1)S(1)} %get-tuple-element.32.inverse, f32[1512,128]{1,0:T(8,128)S(1)} %shard_map.66.part, bf16[616,128]{1,0:T(8,128)(2,1)S(1)} %get-tuple-element.35.ext), custom_call_target="tpu_custom_call" | custom-call | flops 1073741824 | bytes 4194304 | tf_op jit(solution)/shard_map/pallas_call | solution.py:407
  10.9 0.1 shard_map.69
  11.0 1.3 %collective-permute-start.3 = (bf16[5,256,128]{2,1,0:T(8,128)(2,1)S(1)}, bf16[5,256,128]{2,1,0:T(8,128)(2,1)S(1)}, u32[]{:S(2)}, u32[]{:S(2)}) collective-permute-start(bf16[5,256,128]{2,1,0:T(8,128)(2,1)S(1)} %get-tuple-element.39.rest_0_), channel_id=1, source_target_pairs={{0,1},{1,0},{2,3},{3,2},{4,8},{5,9},{6,10},{7,11},{8,4},{9,5},{10,... | collective-permute-start | bytes 983048 | tf_op jit(solution)/shard_map/ppermute | solution.py:330
  12.4 0.4 collective-permute-start.4
  12.8 0.1 collective-permute-start.5
  12.9 3.3 %shard_map.70.cb = bf16[16,256,256]{2,1,0:T(8,128)(2,1)S(1)} custom-call(bf16[4,508032]{1,0:T(4,128)(2,1)} %flat.3, bf16[5,256,128]{2,1,0:T(8,128)(2,1)S(1)} %get-tuple-element.39.rest_0_), custom_call_target="tpu_custom_call" | custom-call | flops 1048576 | bytes 12582912 | tf_op jit(solution)/shard_map/pallas_call | solution.py:374
  16.1 2.7 %collective-permute-done.5.far = bf16[1,256,128]{2,1,0:T(8,128)(2,1)S(1)} collective-permute-done((bf16[1,256,128]{2,1,0:T(8,128)(2,1)S(1)}, bf16[1,256,128]{2,1,0:T(8,128)(2,1)S(1)}, u32[]{:S(2)}, u32[]{:S(2)}) %collective-permute-start.5) | collective-permute-done | bytes 65568 | tf_op jit(solution)/shard_map/ppermute | solution.py:330
  18.8 0.7 %shard_map.71 = (f32[4,256,128]{2,1,0:T(8,128)S(1)}, f32[4,256,128]{2,1,0:T(8,128)S(1)}, bf16[1,256,128]{2,1,0:T(8,128)(2,1)S(1)}, f32[8,128]{1,0:T(8,128)S(1)}) custom-call(s32[41]{0:T(128)S(4)} %get-tuple-element.30.table, bf16[16,256,256]{2,1,0:T(8,128)(2,1)S(1)} %get-tuple-element.31.ca, bf16[16,256,256]{2,1,0:T(8,128)(2,1)S(1)} %shard_map.70.cb, ...), custom_call_target="tpu_custom_call" | custom-call | tf_op jit(solution)/shard_map/pallas_call | solution.py:425
  19.5 1.2 %collective-permute-start.7 = (bf16[1,256,128]{2,1,0:T(8,128)(2,1)S(1)}, bf16[1,256,128]{2,1,0:T(8,128)(2,1)S(1)}, u32[]{:S(2)}, u32[]{:S(2)}) collective-permute-start(bf16[1,256,128]{2,1,0:T(8,128)(2,1)S(1)} %get-tuple-element.44), channel_id=1, source_target_pairs={{0,1},{1,0},{2,3},{3,2},{4,8},{5,9},{6,10},{7,11},{8,4},{9,5},{10,... | collective-permute-start | bytes 196616 | tf_op jit(solution)/shard_map/ppermute | solution.py:330
  20.7 0.6 %collective-permute-start.6 = (bf16[1,256,128]{2,1,0:T(8,128)(2,1)S(1)}, bf16[1,256,128]{2,1,0:T(8,128)(2,1)S(1)}, u32[]{:S(2)}, u32[]{:S(2)}) collective-permute-start(bf16[1,256,128]{2,1,0:T(8,128)(2,1)S(1)} %shard_map.73), channel_id=1, source_target_pairs={{0,4},{1,5},{2,6},{3,7},{4,0},{5,1},{6,2},{7,3},{8,12},{9,13},{10,... | collective-permute-start | bytes 196616 | tf_op jit(solution)/shard_map/ppermute | solution.py:330
  21.4 1.0 %shard_map.72.part = f32[1512,128]{1,0:T(8,128)S(1)} custom-call(bf16[1512,1512]{1,0:T(8,128)(2,1)S(1)} %get-tuple-element.32.inverse, f32[4,256,128]{2,1,0:T(8,128)S(1)} %get-tuple-element.43.own.w.rest_0_), custom_call_target="tpu_custom_call" | custom-call | flops 1073741824 | bytes 4194304 | tf_op jit(solution)/shard_map/pallas_call | solution.py:395
  22.4 1.5 %collective-permute-done.7.outer = bf16[1,256,128]{2,1,0:T(8,128)(2,1)S(1)} collective-permute-done((bf16[1,256,128]{2,1,0:T(8,128)(2,1)S(1)}, bf16[1,256,128]{2,1,0:T(8,128)(2,1)S(1)}, u32[]{:S(2)}, u32[]{:S(2)}) %collective-permute-start.7) | collective-permute-done | bytes 65568 | tf_op jit(solution)/shard_map/ppermute | solution.py:330
  23.9 0.3 shard_map.74
  24.2 0.3 collective-permute-start.8
  24.5 0.9 %shard_map.75 = (f32[4,256,128]{2,1,0:T(8,128)S(1)}, bf16[1,256,128]{2,1,0:T(8,128)(2,1)S(1)}) custom-call(s32[41]{0:T(128)S(4)} %get-tuple-element.30.table, bf16[1512,1512]{1,0:T(8,128)(2,1)S(1)} %get-tuple-element.32.inverse, f32[1512,128]{1,0:T(8,128)S(1)} %shard_map.72.part, bf16[616,128]{1,0:T(8,128)(2,1)S(1)} %get-tuple-element.45.ext), custom_call_target="tpu_custom_call" | custom-call | flops 1073741824 | bytes 4194304 | tf_op jit(solution)/shard_map/pallas_call | solution.py:407
  25.4 0.4 collective-permute-done.8.spill_in
  25.7 0.1 shard_map.76
  25.8 1.2 %collective-permute-start.9 = (bf16[5,256,128]{2,1,0:T(8,128)(2,1)S(1)}, bf16[5,256,128]{2,1,0:T(8,128)(2,1)S(1)}, u32[]{:S(2)}, u32[]{:S(2)}) collective-permute-start(bf16[5,256,128]{2,1,0:T(8,128)(2,1)S(1)} %get-tuple-element.50), channel_id=1, source_target_pairs={{0,1},{1,0},{2,3},{3,2},{4,8},{5,9},{6,10},{7,11},{8,4},{9,5},{10,... | collective-permute-start | bytes 983048 | tf_op jit(solution)/shard_map/ppermute | solution.py:330
  27.0 1.1 %collective-permute-start.10 = (bf16[4,256,128]{2,1,0:T(8,128)(2,1)S(1)}, bf16[4,256,128]{2,1,0:T(8,128)(2,1)S(1)}, u32[]{:S(2)}, u32[]{:S(2)}) collective-permute-start(bf16[4,256,128]{2,1,0:T(8,128)(2,1)S(1)} %get-tuple-element.51), channel_id=1, source_target_pairs={{0,4},{1,5},{2,6},{3,7},{4,0},{5,1},{6,2},{7,3},{8,12},{9,13},{10,... | collective-permute-start | bytes 786440 | tf_op jit(solution)/shard_map/ppermute | solution.py:330
  28.1 5.6 %collective-permute-done.11.far = bf16[1,256,128]{2,1,0:T(8,128)(2,1)S(1)} collective-permute-done((bf16[1,256,128]{2,1,0:T(8,128)(2,1)S(1)}, bf16[1,256,128]{2,1,0:T(8,128)(2,1)S(1)}, u32[]{:S(2)}, u32[]{:S(2)}) %collective-permute-start.11) | collective-permute-done | bytes 65568 | tf_op jit(solution)/shard_map/ppermute | solution.py:330
  33.7 0.6 shard_map.77
  34.4 0.1 collective-permute-start.12
  34.5 1.2 %collective-permute-done.12 = f32[6,128]{1,0:T(8,128)S(1)} collective-permute-done((f32[6,128]{1,0:T(8,128)S(1)}, f32[6,128]{1,0:T(8,128)S(1)}, u32[]{:S(2)}, u32[]{:S(2)}) %collective-permute-start.12) | collective-permute-done | bytes 3104 | tf_op jit(solution)/shard_map/ppermute | solution.py:330
  35.7 25.4 %all_to_all.5.gathered = f32[32,6,128]{2,1,0:T(8,128)S(1)} all-to-all(f32[32,6,128]{2,1,0:T(8,128)S(1)} %broadcast_in_dim.2), channel_id=1, replica_groups={{0,8,16,24,32,40,48,56,64,72,80,88,96,104,112,120,128,136,144,152,160,1..., dimensions={0} | all-to-all | bytes 196608 | tf_op jit(solution)/shard_map/all_to_all | solution.py:440
  61.0 1.0 %shard_map.78 = f32[1008,128]{1,0:T(8,128)} custom-call(f32[32,6,128]{2,1,0:T(8,128)S(1)} %all_to_all.5.gathered, f32[4,256,128]{2,1,0:T(8,128)S(1)} %get-tuple-element.53.p0, f32[4,256,128]{2,1,0:T(8,128)S(1)} %get-tuple-element.54.q), custom_call_target="tpu_custom_call" | custom-call | tf_op jit(solution)/shard_map/pallas_call | solution.py:444
  (17 shorter events, 0.1 us)
Async XLA Ops:
  0.7 1.0 %copy-start = (f32[4,252,128]{2,0,1:T(4,128)S(1)}, f32[4,252,128]{2,0,1:T(4,128)}, u32[]{:S(2)}) copy-start(f32[4,252,128]{2,0,1:T(4,128)} %param.6) | copy-start | bytes 1548292
  1.8 7.3 %collective-permute-start.1 = (bf16[4,256,128]{2,1,0:T(8,128)(2,1)S(1)}, bf16[4,256,128]{2,1,0:T(8,128)(2,1)S(1)}, u32[]{:S(2)}, u32[]{:S(2)}) collective-permute-start(bf16[4,256,128]{2,1,0:T(8,128)(2,1)S(1)} %get-tuple-element.34), channel_id=1, source_target_pairs={{0,1},{1,0},{2,3},{3,2},{4,8},{5,9},{6,10},{7,11},{8,4},{9,5},{10,... | collective-permute-start | bytes 786440 | tf_op jit(solution)/shard_map/ppermute | solution.py:330
  4.1 5.0 %collective-permute-start = (bf16[4,256,128]{2,1,0:T(8,128)(2,1)S(1)}, bf16[4,256,128]{2,1,0:T(8,128)(2,1)S(1)}, u32[]{:S(2)}, u32[]{:S(2)}) collective-permute-start(bf16[4,256,128]{2,1,0:T(8,128)(2,1)S(1)} %get-tuple-element.34), channel_id=1, source_target_pairs={{0,4},{1,5},{2,6},{3,7},{4,0},{5,1},{6,2},{7,3},{8,12},{9,13},{10,... | collective-permute-start | bytes 786440 | tf_op jit(solution)/shard_map/ppermute | solution.py:330
  9.5 1.4 %collective-permute-start.2 = (bf16[1,256,128]{2,1,0:T(8,128)(2,1)S(1)}, bf16[1,256,128]{2,1,0:T(8,128)(2,1)S(1)}, u32[]{:S(2)}, u32[]{:S(2)}) collective-permute-start(bf16[1,256,128]{2,1,0:T(8,128)(2,1)S(1)} %get-tuple-element.37), channel_id=1, source_target_pairs={{0,4},{1,5},{2,6},{3,7},{4,0},{5,1},{6,2},{7,3},{8,12},{9,13},{10,... | collective-permute-start | bytes 196616 | tf_op jit(solution)/shard_map/ppermute | solution.py:330
  11.0 7.8 %collective-permute-start.3 = (bf16[5,256,128]{2,1,0:T(8,128)(2,1)S(1)}, bf16[5,256,128]{2,1,0:T(8,128)(2,1)S(1)}, u32[]{:S(2)}, u32[]{:S(2)}) collective-permute-start(bf16[5,256,128]{2,1,0:T(8,128)(2,1)S(1)} %get-tuple-element.39.rest_0_), channel_id=1, source_target_pairs={{0,1},{1,0},{2,3},{3,2},{4,8},{5,9},{6,10},{7,11},{8,4},{9,5},{10,... | collective-permute-start | bytes 983048 | tf_op jit(solution)/shard_map/ppermute | solution.py:330
  12.4 6.5 %collective-permute-start.4 = (bf16[4,256,128]{2,1,0:T(8,128)(2,1)S(1)}, bf16[4,256,128]{2,1,0:T(8,128)(2,1)S(1)}, u32[]{:S(2)}, u32[]{:S(2)}) collective-permute-start(bf16[4,256,128]{2,1,0:T(8,128)(2,1)S(1)} %get-tuple-element.41), channel_id=1, source_target_pairs={{0,4},{1,5},{2,6},{3,7},{4,0},{5,1},{6,2},{7,3},{8,12},{9,13},{10,... | collective-permute-start | bytes 786440 | tf_op jit(solution)/shard_map/ppermute | solution.py:330
  12.8 6.0 %collective-permute-start.5 = (bf16[1,256,128]{2,1,0:T(8,128)(2,1)S(1)}, bf16[1,256,128]{2,1,0:T(8,128)(2,1)S(1)}, u32[]{:S(2)}, u32[]{:S(2)}) collective-permute-start(bf16[1,256,128]{2,1,0:T(8,128)(2,1)S(1)} %get-tuple-element.38.spill_out), channel_id=1, source_target_pairs={{0,4},{1,5},{2,6},{3,7},{4,12},{5,13},{6,14},{7,15},{8,0},{9,1},{1... | collective-permute-start | bytes 196616 | tf_op jit(solution)/shard_map/ppermute | solution.py:330
  19.5 4.4 %collective-permute-start.7 = (bf16[1,256,128]{2,1,0:T(8,128)(2,1)S(1)}, bf16[1,256,128]{2,1,0:T(8,128)(2,1)S(1)}, u32[]{:S(2)}, u32[]{:S(2)}) collective-permute-start(bf16[1,256,128]{2,1,0:T(8,128)(2,1)S(1)} %get-tuple-element.44), channel_id=1, source_target_pairs={{0,1},{1,0},{2,3},{3,2},{4,8},{5,9},{6,10},{7,11},{8,4},{9,5},{10,... | collective-permute-start | bytes 196616 | tf_op jit(solution)/shard_map/ppermute | solution.py:330
  20.7 3.1 %collective-permute-start.6 = (bf16[1,256,128]{2,1,0:T(8,128)(2,1)S(1)}, bf16[1,256,128]{2,1,0:T(8,128)(2,1)S(1)}, u32[]{:S(2)}, u32[]{:S(2)}) collective-permute-start(bf16[1,256,128]{2,1,0:T(8,128)(2,1)S(1)} %shard_map.73), channel_id=1, source_target_pairs={{0,4},{1,5},{2,6},{3,7},{4,0},{5,1},{6,2},{7,3},{8,12},{9,13},{10,... | collective-permute-start | bytes 196616 | tf_op jit(solution)/shard_map/ppermute | solution.py:330
  24.2 1.5 %collective-permute-start.8 = (bf16[1,256,128]{2,1,0:T(8,128)(2,1)S(1)}, bf16[1,256,128]{2,1,0:T(8,128)(2,1)S(1)}, u32[]{:S(2)}, u32[]{:S(2)}) collective-permute-start(bf16[1,256,128]{2,1,0:T(8,128)(2,1)S(1)} %get-tuple-element.47), channel_id=1, source_target_pairs={{0,4},{1,5},{2,6},{3,7},{4,0},{5,1},{6,2},{7,3},{8,12},{9,13},{10,... | collective-permute-start | bytes 196616 | tf_op jit(solution)/shard_map/ppermute | solution.py:330
  25.8 7.9 %collective-permute-start.9 = (bf16[5,256,128]{2,1,0:T(8,128)(2,1)S(1)}, bf16[5,256,128]{2,1,0:T(8,128)(2,1)S(1)}, u32[]{:S(2)}, u32[]{:S(2)}) collective-permute-start(bf16[5,256,128]{2,1,0:T(8,128)(2,1)S(1)} %get-tuple-element.50), channel_id=1, source_target_pairs={{0,1},{1,0},{2,3},{3,2},{4,8},{5,9},{6,10},{7,11},{8,4},{9,5},{10,... | collective-permute-start | bytes 983048 | tf_op jit(solution)/shard_map/ppermute | solution.py:330
  27.0 6.7 %collective-permute-start.10 = (bf16[4,256,128]{2,1,0:T(8,128)(2,1)S(1)}, bf16[4,256,128]{2,1,0:T(8,128)(2,1)S(1)}, u32[]{:S(2)}, u32[]{:S(2)}) collective-permute-start(bf16[4,256,128]{2,1,0:T(8,128)(2,1)S(1)} %get-tuple-element.51), channel_id=1, source_target_pairs={{0,4},{1,5},{2,6},{3,7},{4,0},{5,1},{6,2},{7,3},{8,12},{9,13},{10,... | collective-permute-start | bytes 786440 | tf_op jit(solution)/shard_map/ppermute | solution.py:330
  28.1 5.6 %collective-permute-start.11 = (bf16[1,256,128]{2,1,0:T(8,128)(2,1)S(1)}, bf16[1,256,128]{2,1,0:T(8,128)(2,1)S(1)}, u32[]{:S(2)}, u32[]{:S(2)}) collective-permute-start(bf16[1,256,128]{2,1,0:T(8,128)(2,1)S(1)} %get-tuple-element.48.spill_out), channel_id=1, source_target_pairs={{0,4},{1,5},{2,6},{3,7},{4,12},{5,13},{6,14},{7,15},{8,0},{9,1},{1... | collective-permute-start | bytes 196616 | tf_op jit(solution)/shard_map/ppermute | solution.py:330
  34.4 1.3 %collective-permute-start.12 = (f32[6,128]{1,0:T(8,128)S(1)}, f32[6,128]{1,0:T(8,128)S(1)}, u32[]{:S(2)}, u32[]{:S(2)}) collective-permute-start(f32[6,128]{1,0:T(8,128)S(1)} %pad_maximum_fusion), channel_id=1, source_target_pairs={{0,4},{1,5},{2,6},{3,7},{4,0},{5,1},{6,2},{7,3},{8,12},{9,13},{10,... | collective-permute-start | bytes 9224 | tf_op jit(solution)/shard_map/ppermute | solution.py:330

commit v8 on v7

--- a/solution.py
+++ b/solution.py
@@ -25,6 +25,7 @@
 OWN = 1024
 FROM = 896
 ANY = pl.BlockSpec(memory_space=pl.ANY)
+PARTS = ((0, 64), (64, 64), (128, 64), (192, 60))
 VM = pl.BlockSpec(memory_space=pltpu.VMEM)
 SM = pl.BlockSpec(memory_space=pltpu.SMEM)
 
@@ -34,19 +35,28 @@
         kernel,
         out_shape=[keep[0](s, d) if keep else jax.ShapeDtypeStruct(s, d) for s, d, *keep in outs],
         in_specs=ins,
-        out_specs=[SM if keep == [pltpu.SMEM] else VM for _, _, *keep in outs],
+        out_specs=[{pltpu.SMEM: SM, pltpu.HBM: ANY}.get(keep[0], VM) if keep else VM for _, _, *keep in outs],
         scratch_shapes=list(scratch),
         compiler_params=pltpu.CompilerParams(vmem_limit_bytes=limit << 20),
         cost_estimate=cost,
     )
 
 
-def start_kernel(counts, right, v0_ref, v0b_ref):
-    for s in range(NS):
-        alive = jnp.where(counts[0] > s, 1.0, 0.0)
-        v0_ref[s, :W, :] = right[pl.ds(s, W, stride=NS), :] * alive
-        v0_ref[s, W:, :] = jnp.zeros((WP - W, R), F32)
-        v0b_ref[s] = v0_ref[s].astype(BF16)
+def start_kernel(counts, right, v0_ref, v0b_ref, rows, sems):
+    copies = []
+    for begin, size in PARTS:
+        part = pl.ds(begin * NS, size * NS)
+        copies.append(pltpu.make_async_copy(right.at[part, :], rows.at[part, :], sems.at[len(copies)]))
+        copies[-1].start()
+    for (begin, size), copy in zip(PARTS, copies):
+        copy.wait()
+        for s in range(NS):
+            alive = jnp.where(counts[0] > s, 1.0, 0.0)
+            block = rows[pl.ds(begin * NS + s, size, stride=NS), :] * alive
+            if begin + size == W:
+                block = jnp.concatenate([block, jnp.zeros((WP - W, R), F32)], axis=0)
+            v0_ref[s, begin : begin + block.shape[0], :] = block
+            v0b_ref[s, begin : begin + block.shape[0], :] = block.astype(BF16)
 
 
 def fill_table(table, place, counts, margin, neighbours):
@@ -289,7 +299,7 @@
     picked(win_ref, w, opened(spill_in[0])[1])
 
 
-def finish_kernel(gathered, p0, q, out):
+def finish_kernel(gathered, p0, q, out_ref, out, sems):
     total = jnp.sum(gathered[...], axis=0)
     s00, s01, s11, s02, s12, s22 = (total[i : i + 1, :] for i in range(6))
     c = SHIFT
@@ -320,8 +330,16 @@
     y2 = beta * (g00 * h12 - g01 * h11) / det
     two = y2 / (beta * h21)
     one = y1 / beta + a * two
-    for s in range(NS):
-        out[pl.ds(s, W, stride=NS), :] = one * p0[s, :W, :] + two * q[s, :W, :]
+    copies = []
+    for begin, size in PARTS:
+        for s in range(NS):
+            p, r = p0[s, begin : begin + size, :], q[s, begin : begin + size, :]
+            out[pl.ds(begin * NS + s, size, stride=NS), :] = one * p + two * r
+        rows = pl.ds(begin * NS, size * NS)
+        copies.append(pltpu.make_async_copy(out.at[rows, :], out_ref.at[rows, :], sems.at[len(copies)]))
+        copies[-1].start()
+    for copy in copies:
+        copy.wait()
 
 
 def permuted(x, target):
@@ -353,7 +371,13 @@
     here = lax.axis_index("sub").astype(jnp.int32).reshape(1)
     flat_right = right_side.transpose(1, 0, 2).reshape(W * NS, R)
     block, one = (NS, WP, R), (1, WP, R)
-    v0, v0b = call(start_kernel, [(block, F32), (block, BF16)], [SM, VM])(counts, flat_right)
+    flat_right = pltpu.with_memory_space_constraint(flat_right, pltpu.HBM)
+    v0, v0b = call(
+        start_kernel,
+        [(block, F32), (block, BF16)],
+        [SM, ANY],
+        [pltpu.VMEM((W * NS, R), F32), pltpu.SemaphoreType.DMA((len(PARTS),))],
+    )(counts, flat_right)
     outer, inner = to_outer(v0b), to_inner(v0b)
 
     coupling = pltpu.with_memory_space_constraint(coupling, pltpu.HBM)
@@ -441,7 +465,12 @@
         jnp.broadcast_to(sums[None], (NSUB // 2, 6, R)), "sub", 0, 0,
         axis_index_groups=[list(range(c, NSUB, 2)) for c in range(2)],
     )
-    (flat,) = call(finish_kernel, [((W * NS, R), F32)], [VM] * 3)(gathered, p0, q)
+    (flat,) = call(
+        finish_kernel,
+        [((W * NS, R), F32, pltpu.HBM)],
+        [VM] * 3,
+        [pltpu.VMEM((W * NS, R), F32), pltpu.SemaphoreType.DMA((len(PARTS),))],
+    )(gathered, p0, q)
     return flat.reshape(W, NS, R).transpose(1, 0, 2)
 
 

time: 62.7 us -> 62 us (0.989)
  Pallas kernels: 14.2 us -> 16.1 us
  local copies, waits for them, and re-layouts: 1.05 us -> 0.02 us
  blocking collectives: 25.4 us -> 24.4 us
    pallas_call x2, Pallas kernels: 1.03 us -> 2.07 us  [the longest x1 1.14 us: body(): call(start_kernel, [(block, F32), (block, BF16)], [SM, ANY], [pltpu.VMEM(...]
    unnamed x2 -> x0, local copies, waits for them, and re-layouts: 1.03 us -> none
    all_to_all x1, blocking collectives: 25.4 us -> 24.4 us  [body(): lax.all_to_all(jnp.broadcast_to(sums[None], (NSUB // 2, 6, R)), 'sub', 0,...]
    pallas_call x2, Pallas kernels: 1.31 us -> 2.18 us  [system(): call(functools.partial(system_kernel, first), outs + [((8, R), F32)], [SM...]
where the time goes in v8:
time: 62 us; the launch traced here: 61.9 us
  blocking collectives  24.4 us (39%)
  Pallas kernels  16.1 us (26%)
  waiting for transfers between devices  11.6 us (19%)
  starting transfers between devices  8.72 us (14%)
  between operations  0.97 us (2%)
    all_to_all x1, blocking collectives, body(): lax.all_to_all(jnp.broadcast_to(sums[None], (NSUB // 2, 6, R)), 'sub', 0,...  24.4 us
    ppermute x13, waiting for transfers between devices, permuted(): lax.ppermute(x, ('sub', 'rhs'), [(i * parts + j, t[0] * parts + t[1]) for...  11.6 us
    ppermute x13, starting transfers between devices, permuted(): lax.ppermute(x, ('sub', 'rhs'), [(i * parts + j, t[0] * parts + t[1]) for...  8.72 us
    pallas_call x2, Pallas kernels, matrices(): call(functools.partial(coupling_kernel, blocks, groups, first), outs, [AN...  7.25 us
    pallas_call x2, Pallas kernels, system(): call(functools.partial(system_kernel, first), outs + [((8, R), F32)], [SM...  2.18 us
    pallas_call x2, Pallas kernels, solve(): call(own_kernel, [((6 * W, R), F32, pltpu.VMEM)], [VM, VM], [pltpu.VMEM((...  1.97 us
    pallas_call x2, Pallas kernels, solve(): call(solve_kernel, [(block, F32), (one, BF16)], [SM] + [VM] * 3, [pltpu.V...  1.72 us
  transfers between devices with their start and end apart: 13, of which 5 were waited for; matrix products, arithmetic and copies ran while one was open for 0% of the time, Pallas kernels for 18%

profile of v8, /device:TPU:2, one launch (start us, length us, event | category | flops | bytes accessed | tf_op | source)
XLA Modules:
  0.0 61.9 jit_solution(9128033599525979416)
XLA Ops:
  0.7 1.1 %shard_map.65 = (f32[4,256,128]{2,1,0:T(8,128)S(1)}, bf16[4,256,128]{2,1,0:T(8,128)(2,1)S(1)}) custom-call(s32[1]{0:T(128)S(6)} %copy.7.rest_2_.counts, f32[1008,128]{1,0:T(8,128)} %bitcast.7), custom_call_target="tpu_custom_call" | custom-call | tf_op jit(solution)/shard_map/pallas_call | solution.py:375
  1.8 2.4 %collective-permute-start.1 = (bf16[4,256,128]{2,1,0:T(8,128)(2,1)S(1)}, bf16[4,256,128]{2,1,0:T(8,128)(2,1)S(1)}, u32[]{:S(2)}, u32[]{:S(2)}) collective-permute-start(bf16[4,256,128]{2,1,0:T(8,128)(2,1)S(1)} %get-tuple-element.34), channel_id=1, source_target_pairs={{0,1},{1,0},{2,3},{3,2},{4,8},{5,9},{6,10},{7,11},{8,4},{9,5},{10,... | collective-permute-start | bytes 786440 | tf_op jit(solution)/shard_map/ppermute | solution.py:348
  4.2 4.0 %shard_map.64 = (bf16[16,256,256]{2,1,0:T(8,128)(2,1)S(1)}, bf16[1512,1512]{1,0:T(8,128)(2,1)S(1)}, s32[41]{0:T(128)S(4)}) custom-call(bf16[4,508032]{1,0:T(4,128)(2,1)} %flat.3, bf16[1,1512,1512]{2,1,0:T(8,128)(2,1)} %rest_0_.1, s32[1]{0:T(128)} %bitcast.rest_1_, s32[1]{0:T(128)S(6)} %copy.7.rest_2_.counts, s32[1,2]{1,0:T(1,128)} %rest_3_.1, s32[4,8]{1,0:T(4,128)} %rest_4_.1), custom_call_target="tpu_custom_call" | custom-call | flops 1048576 | bytes 12582912 | tf_op jit(solution)/shard_map/pallas_call | solution.py:398
  8.1 1.0 %shard_map.66.part = f32[1512,128]{1,0:T(8,128)S(1)} custom-call(bf16[1512,1512]{1,0:T(8,128)(2,1)S(1)} %get-tuple-element.32.inverse, f32[4,256,128]{2,1,0:T(8,128)S(1)} %get-tuple-element.33.own.v0), custom_call_target="tpu_custom_call" | custom-call | flops 1073741824 | bytes 4194304 | tf_op jit(solution)/shard_map/pallas_call | solution.py:419
  9.2 0.3 shard_map.67
  9.5 0.6 collective-permute-start.2
  10.1 0.9 %shard_map.68 = (f32[4,256,128]{2,1,0:T(8,128)S(1)}, bf16[1,256,128]{2,1,0:T(8,128)(2,1)S(1)}) custom-call(s32[41]{0:T(128)S(4)} %get-tuple-element.30.table, bf16[1512,1512]{1,0:T(8,128)(2,1)S(1)} %get-tuple-element.32.inverse, f32[1512,128]{1,0:T(8,128)S(1)} %shard_map.66.part, bf16[616,128]{1,0:T(8,128)(2,1)S(1)} %get-tuple-element.35.ext), custom_call_target="tpu_custom_call" | custom-call | flops 1073741824 | bytes 4194304 | tf_op jit(solution)/shard_map/pallas_call | solution.py:431
  10.9 0.0 collective-permute-done.2.spill_in
  11.0 0.1 shard_map.69
  11.1 1.3 %collective-permute-start.3 = (bf16[5,256,128]{2,1,0:T(8,128)(2,1)S(1)}, bf16[5,256,128]{2,1,0:T(8,128)(2,1)S(1)}, u32[]{:S(2)}, u32[]{:S(2)}) collective-permute-start(bf16[5,256,128]{2,1,0:T(8,128)(2,1)S(1)} %get-tuple-element.39.rest_0_), channel_id=1, source_target_pairs={{0,1},{1,0},{2,3},{3,2},{4,8},{5,9},{6,10},{7,11},{8,4},{9,5},{10,... | collective-permute-start | bytes 983048 | tf_op jit(solution)/shard_map/ppermute | solution.py:348
  12.4 0.4 collective-permute-start.4
  12.8 0.1 collective-permute-start.5
  12.9 3.3 %shard_map.70.cb = bf16[16,256,256]{2,1,0:T(8,128)(2,1)S(1)} custom-call(bf16[4,508032]{1,0:T(4,128)(2,1)} %flat.3, bf16[5,256,128]{2,1,0:T(8,128)(2,1)S(1)} %get-tuple-element.39.rest_0_), custom_call_target="tpu_custom_call" | custom-call | flops 1048576 | bytes 12582912 | tf_op jit(solution)/shard_map/pallas_call | solution.py:398
  16.2 2.7 %collective-permute-done.5.far = bf16[1,256,128]{2,1,0:T(8,128)(2,1)S(1)} collective-permute-done((bf16[1,256,128]{2,1,0:T(8,128)(2,1)S(1)}, bf16[1,256,128]{2,1,0:T(8,128)(2,1)S(1)}, u32[]{:S(2)}, u32[]{:S(2)}) %collective-permute-start.5) | collective-permute-done | bytes 65568 | tf_op jit(solution)/shard_map/ppermute | solution.py:348
  18.9 1.1 %shard_map.71 = (f32[4,256,128]{2,1,0:T(8,128)S(1)}, f32[4,256,128]{2,1,0:T(8,128)S(1)}, bf16[1,256,128]{2,1,0:T(8,128)(2,1)S(1)}, f32[8,128]{1,0:T(8,128)S(1)}) custom-call(s32[41]{0:T(128)S(4)} %get-tuple-element.30.table, bf16[16,256,256]{2,1,0:T(8,128)(2,1)S(1)} %get-tuple-element.31.ca, bf16[16,256,256]{2,1,0:T(8,128)(2,1)S(1)} %shard_map.70.cb, ...), custom_call_target="tpu_custom_call" | custom-call | tf_op jit(solution)/shard_map/pallas_call | solution.py:449
  20.0 1.2 %collective-permute-start.7 = (bf16[1,256,128]{2,1,0:T(8,128)(2,1)S(1)}, bf16[1,256,128]{2,1,0:T(8,128)(2,1)S(1)}, u32[]{:S(2)}, u32[]{:S(2)}) collective-permute-start(bf16[1,256,128]{2,1,0:T(8,128)(2,1)S(1)} %get-tuple-element.44), channel_id=1, source_target_pairs={{0,1},{1,0},{2,3},{3,2},{4,8},{5,9},{6,10},{7,11},{8,4},{9,5},{10,... | collective-permute-start | bytes 196616 | tf_op jit(solution)/shard_map/ppermute | solution.py:348
  21.2 0.6 %collective-permute-start.6 = (bf16[1,256,128]{2,1,0:T(8,128)(2,1)S(1)}, bf16[1,256,128]{2,1,0:T(8,128)(2,1)S(1)}, u32[]{:S(2)}, u32[]{:S(2)}) collective-permute-start(bf16[1,256,128]{2,1,0:T(8,128)(2,1)S(1)} %shard_map.73), channel_id=1, source_target_pairs={{0,4},{1,5},{2,6},{3,7},{4,0},{5,1},{6,2},{7,3},{8,12},{9,13},{10,... | collective-permute-start | bytes 196616 | tf_op jit(solution)/shard_map/ppermute | solution.py:348
  21.9 1.0 %shard_map.72.part = f32[1512,128]{1,0:T(8,128)S(1)} custom-call(bf16[1512,1512]{1,0:T(8,128)(2,1)S(1)} %get-tuple-element.32.inverse, f32[4,256,128]{2,1,0:T(8,128)S(1)} %get-tuple-element.43.own.w.rest_0_), custom_call_target="tpu_custom_call" | custom-call | flops 1073741824 | bytes 4194304 | tf_op jit(solution)/shard_map/pallas_call | solution.py:419
  22.8 1.5 %collective-permute-done.7.outer = bf16[1,256,128]{2,1,0:T(8,128)(2,1)S(1)} collective-permute-done((bf16[1,256,128]{2,1,0:T(8,128)(2,1)S(1)}, bf16[1,256,128]{2,1,0:T(8,128)(2,1)S(1)}, u32[]{:S(2)}, u32[]{:S(2)}) %collective-permute-start.7) | collective-permute-done | bytes 65568 | tf_op jit(solution)/shard_map/ppermute | solution.py:348
  24.4 0.3 shard_map.74
  24.7 0.3 collective-permute-start.8
  25.0 0.9 %shard_map.75 = (f32[4,256,128]{2,1,0:T(8,128)S(1)}, bf16[1,256,128]{2,1,0:T(8,128)(2,1)S(1)}) custom-call(s32[41]{0:T(128)S(4)} %get-tuple-element.30.table, bf16[1512,1512]{1,0:T(8,128)(2,1)S(1)} %get-tuple-element.32.inverse, f32[1512,128]{1,0:T(8,128)S(1)} %shard_map.72.part, bf16[616,128]{1,0:T(8,128)(2,1)S(1)} %get-tuple-element.45.ext), custom_call_target="tpu_custom_call" | custom-call | flops 1073741824 | bytes 4194304 | tf_op jit(solution)/shard_map/pallas_call | solution.py:431
  25.9 0.4 collective-permute-done.8.spill_in
  26.2 0.1 shard_map.76
  26.3 1.2 %collective-permute-start.9 = (bf16[5,256,128]{2,1,0:T(8,128)(2,1)S(1)}, bf16[5,256,128]{2,1,0:T(8,128)(2,1)S(1)}, u32[]{:S(2)}, u32[]{:S(2)}) collective-permute-start(bf16[5,256,128]{2,1,0:T(8,128)(2,1)S(1)} %get-tuple-element.50), channel_id=1, source_target_pairs={{0,1},{1,0},{2,3},{3,2},{4,8},{5,9},{6,10},{7,11},{8,4},{9,5},{10,... | collective-permute-start | bytes 983048 | tf_op jit(solution)/shard_map/ppermute | solution.py:348
  27.5 0.6 %collective-permute-start.10 = (bf16[4,256,128]{2,1,0:T(8,128)(2,1)S(1)}, bf16[4,256,128]{2,1,0:T(8,128)(2,1)S(1)}, u32[]{:S(2)}, u32[]{:S(2)}) collective-permute-start(bf16[4,256,128]{2,1,0:T(8,128)(2,1)S(1)} %get-tuple-element.51), channel_id=1, source_target_pairs={{0,4},{1,5},{2,6},{3,7},{4,0},{5,1},{6,2},{7,3},{8,12},{9,13},{10,... | collective-permute-start | bytes 786440 | tf_op jit(solution)/shard_map/ppermute | solution.py:348
  28.1 5.9 %collective-permute-done.11.far = bf16[1,256,128]{2,1,0:T(8,128)(2,1)S(1)} collective-permute-done((bf16[1,256,128]{2,1,0:T(8,128)(2,1)S(1)}, bf16[1,256,128]{2,1,0:T(8,128)(2,1)S(1)}, u32[]{:S(2)}, u32[]{:S(2)}) %collective-permute-start.11) | collective-permute-done | bytes 65568 | tf_op jit(solution)/shard_map/ppermute | solution.py:348
  34.0 1.1 %shard_map.77 = (f32[4,256,128]{2,1,0:T(8,128)S(1)}, f32[8,128]{1,0:T(8,128)S(1)}) custom-call(s32[41]{0:T(128)S(4)} %get-tuple-element.30.table, bf16[16,256,256]{2,1,0:T(8,128)(2,1)S(1)} %get-tuple-element.31.ca, bf16[16,256,256]{2,1,0:T(8,128)(2,1)S(1)} %shard_map.70.cb, f32[4,256,128]{2,1,0:T(8,128)S(1)} %get-tuple-element.49.part, ...), custom_call_target="tpu_custom_call" | custom-call | tf_op jit(solution)/shard_map/pallas_call | solution.py:449
  35.1 0.1 collective-permute-start.12
  35.2 1.2 %collective-permute-done.12 = f32[6,128]{1,0:T(8,128)S(1)} collective-permute-done((f32[6,128]{1,0:T(8,128)S(1)}, f32[6,128]{1,0:T(8,128)S(1)}, u32[]{:S(2)}, u32[]{:S(2)}) %collective-permute-start.12) | collective-permute-done | bytes 3104 | tf_op jit(solution)/shard_map/ppermute | solution.py:348
  36.4 24.4 %all_to_all.5.gathered = f32[32,6,128]{2,1,0:T(8,128)S(1)} all-to-all(f32[32,6,128]{2,1,0:T(8,128)S(1)} %broadcast_in_dim.2), channel_id=1, replica_groups={{0,8,16,24,32,40,48,56,64,72,80,88,96,104,112,120,128,136,144,152,160,1..., dimensions={0} | all-to-all | bytes 196608 | tf_op jit(solution)/shard_map/all_to_all | solution.py:464
  60.8 0.9 %shard_map.78 = f32[1008,128]{1,0:T(8,128)} custom-call(f32[32,6,128]{2,1,0:T(8,128)S(1)} %all_to_all.5.gathered, f32[4,256,128]{2,1,0:T(8,128)S(1)} %get-tuple-element.53.p0, f32[4,256,128]{2,1,0:T(8,128)S(1)} %get-tuple-element.54.q), custom_call_target="tpu_custom_call" | custom-call | tf_op jit(solution)/shard_map/pallas_call | solution.py:468
  (15 shorter events, 0.1 us)
Async XLA Ops:
  1.8 7.3 %collective-permute-start.1 = (bf16[4,256,128]{2,1,0:T(8,128)(2,1)S(1)}, bf16[4,256,128]{2,1,0:T(8,128)(2,1)S(1)}, u32[]{:S(2)}, u32[]{:S(2)}) collective-permute-start(bf16[4,256,128]{2,1,0:T(8,128)(2,1)S(1)} %get-tuple-element.34), channel_id=1, source_target_pairs={{0,1},{1,0},{2,3},{3,2},{4,8},{5,9},{6,10},{7,11},{8,4},{9,5},{10,... | collective-permute-start | bytes 786440 | tf_op jit(solution)/shard_map/ppermute | solution.py:348
  4.2 5.0 %collective-permute-start = (bf16[4,256,128]{2,1,0:T(8,128)(2,1)S(1)}, bf16[4,256,128]{2,1,0:T(8,128)(2,1)S(1)}, u32[]{:S(2)}, u32[]{:S(2)}) collective-permute-start(bf16[4,256,128]{2,1,0:T(8,128)(2,1)S(1)} %get-tuple-element.34), channel_id=1, source_target_pairs={{0,4},{1,5},{2,6},{3,7},{4,0},{5,1},{6,2},{7,3},{8,12},{9,13},{10,... | collective-permute-start | bytes 786440 | tf_op jit(solution)/shard_map/ppermute | solution.py:348
  9.5 1.5 %collective-permute-start.2 = (bf16[1,256,128]{2,1,0:T(8,128)(2,1)S(1)}, bf16[1,256,128]{2,1,0:T(8,128)(2,1)S(1)}, u32[]{:S(2)}, u32[]{:S(2)}) collective-permute-start(bf16[1,256,128]{2,1,0:T(8,128)(2,1)S(1)} %get-tuple-element.37), channel_id=1, source_target_pairs={{0,4},{1,5},{2,6},{3,7},{4,0},{5,1},{6,2},{7,3},{8,12},{9,13},{10,... | collective-permute-start | bytes 196616 | tf_op jit(solution)/shard_map/ppermute | solution.py:348
  11.1 7.8 %collective-permute-start.3 = (bf16[5,256,128]{2,1,0:T(8,128)(2,1)S(1)}, bf16[5,256,128]{2,1,0:T(8,128)(2,1)S(1)}, u32[]{:S(2)}, u32[]{:S(2)}) collective-permute-start(bf16[5,256,128]{2,1,0:T(8,128)(2,1)S(1)} %get-tuple-element.39.rest_0_), channel_id=1, source_target_pairs={{0,1},{1,0},{2,3},{3,2},{4,8},{5,9},{6,10},{7,11},{8,4},{9,5},{10,... | collective-permute-start | bytes 983048 | tf_op jit(solution)/shard_map/ppermute | solution.py:348
  12.4 6.5 %collective-permute-start.4 = (bf16[4,256,128]{2,1,0:T(8,128)(2,1)S(1)}, bf16[4,256,128]{2,1,0:T(8,128)(2,1)S(1)}, u32[]{:S(2)}, u32[]{:S(2)}) collective-permute-start(bf16[4,256,128]{2,1,0:T(8,128)(2,1)S(1)} %get-tuple-element.41), channel_id=1, source_target_pairs={{0,4},{1,5},{2,6},{3,7},{4,0},{5,1},{6,2},{7,3},{8,12},{9,13},{10,... | collective-permute-start | bytes 786440 | tf_op jit(solution)/shard_map/ppermute | solution.py:348
  12.8 6.1 %collective-permute-start.5 = (bf16[1,256,128]{2,1,0:T(8,128)(2,1)S(1)}, bf16[1,256,128]{2,1,0:T(8,128)(2,1)S(1)}, u32[]{:S(2)}, u32[]{:S(2)}) collective-permute-start(bf16[1,256,128]{2,1,0:T(8,128)(2,1)S(1)} %get-tuple-element.38.spill_out), channel_id=1, source_target_pairs={{0,4},{1,5},{2,6},{3,7},{4,12},{5,13},{6,14},{7,15},{8,0},{9,1},{1... | collective-permute-start | bytes 196616 | tf_op jit(solution)/shard_map/ppermute | solution.py:348
  20.0 4.4 %collective-permute-start.7 = (bf16[1,256,128]{2,1,0:T(8,128)(2,1)S(1)}, bf16[1,256,128]{2,1,0:T(8,128)(2,1)S(1)}, u32[]{:S(2)}, u32[]{:S(2)}) collective-permute-start(bf16[1,256,128]{2,1,0:T(8,128)(2,1)S(1)} %get-tuple-element.44), channel_id=1, source_target_pairs={{0,1},{1,0},{2,3},{3,2},{4,8},{5,9},{6,10},{7,11},{8,4},{9,5},{10,... | collective-permute-start | bytes 196616 | tf_op jit(solution)/shard_map/ppermute | solution.py:348
  21.2 3.1 %collective-permute-start.6 = (bf16[1,256,128]{2,1,0:T(8,128)(2,1)S(1)}, bf16[1,256,128]{2,1,0:T(8,128)(2,1)S(1)}, u32[]{:S(2)}, u32[]{:S(2)}) collective-permute-start(bf16[1,256,128]{2,1,0:T(8,128)(2,1)S(1)} %shard_map.73), channel_id=1, source_target_pairs={{0,4},{1,5},{2,6},{3,7},{4,0},{5,1},{6,2},{7,3},{8,12},{9,13},{10,... | collective-permute-start | bytes 196616 | tf_op jit(solution)/shard_map/ppermute | solution.py:348
  24.7 1.5 %collective-permute-start.8 = (bf16[1,256,128]{2,1,0:T(8,128)(2,1)S(1)}, bf16[1,256,128]{2,1,0:T(8,128)(2,1)S(1)}, u32[]{:S(2)}, u32[]{:S(2)}) collective-permute-start(bf16[1,256,128]{2,1,0:T(8,128)(2,1)S(1)} %get-tuple-element.47), channel_id=1, source_target_pairs={{0,4},{1,5},{2,6},{3,7},{4,0},{5,1},{6,2},{7,3},{8,12},{9,13},{10,... | collective-permute-start | bytes 196616 | tf_op jit(solution)/shard_map/ppermute | solution.py:348
  26.3 7.7 %collective-permute-start.9 = (bf16[5,256,128]{2,1,0:T(8,128)(2,1)S(1)}, bf16[5,256,128]{2,1,0:T(8,128)(2,1)S(1)}, u32[]{:S(2)}, u32[]{:S(2)}) collective-permute-start(bf16[5,256,128]{2,1,0:T(8,128)(2,1)S(1)} %get-tuple-element.50), channel_id=1, source_target_pairs={{0,1},{1,0},{2,3},{3,2},{4,8},{5,9},{6,10},{7,11},{8,4},{9,5},{10,... | collective-permute-start | bytes 983048 | tf_op jit(solution)/shard_map/ppermute | solution.py:348
  27.5 6.5 %collective-permute-start.10 = (bf16[4,256,128]{2,1,0:T(8,128)(2,1)S(1)}, bf16[4,256,128]{2,1,0:T(8,128)(2,1)S(1)}, u32[]{:S(2)}, u32[]{:S(2)}) collective-permute-start(bf16[4,256,128]{2,1,0:T(8,128)(2,1)S(1)} %get-tuple-element.51), channel_id=1, source_target_pairs={{0,4},{1,5},{2,6},{3,7},{4,0},{5,1},{6,2},{7,3},{8,12},{9,13},{10,... | collective-permute-start | bytes 786440 | tf_op jit(solution)/shard_map/ppermute | solution.py:348
  28.1 5.9 %collective-permute-start.11 = (bf16[1,256,128]{2,1,0:T(8,128)(2,1)S(1)}, bf16[1,256,128]{2,1,0:T(8,128)(2,1)S(1)}, u32[]{:S(2)}, u32[]{:S(2)}) collective-permute-start(bf16[1,256,128]{2,1,0:T(8,128)(2,1)S(1)} %get-tuple-element.48.spill_out), channel_id=1, source_target_pairs={{0,4},{1,5},{2,6},{3,7},{4,12},{5,13},{6,14},{7,15},{8,0},{9,1},{1... | collective-permute-start | bytes 196616 | tf_op jit(solution)/shard_map/ppermute | solution.py:348
  35.1 1.3 %collective-permute-start.12 = (f32[6,128]{1,0:T(8,128)S(1)}, f32[6,128]{1,0:T(8,128)S(1)}, u32[]{:S(2)}, u32[]{:S(2)}) collective-permute-start(f32[6,128]{1,0:T(8,128)S(1)} %pad_maximum_fusion), channel_id=1, source_target_pairs={{0,4},{1,5},{2,6},{3,7},{4,0},{5,1},{6,2},{7,3},{8,12},{9,13},{10,... | collective-permute-start | bytes 9224 | tf_op jit(solution)/shard_map/ppermute | solution.py:348

commit v9 on v7

--- a/solution.py
+++ b/solution.py
@@ -22,9 +22,11 @@
 SPLIT = 4
 EVEN, FIRST, LAST, LOW, HIGH, COUNT, ENDS, NEXT, OUT, SLOTS = range(10)
 TABLE = SLOTS + NS * NB
+FAR_WEIGHT = 2450000000
 OWN = 1024
 FROM = 896
 ANY = pl.BlockSpec(memory_space=pl.ANY)
+PARTS = ((0, 64), (64, 64), (128, 64), (192, 60))
 VM = pl.BlockSpec(memory_space=pltpu.VMEM)
 SM = pl.BlockSpec(memory_space=pltpu.SMEM)
 
@@ -34,7 +36,7 @@
         kernel,
         out_shape=[keep[0](s, d) if keep else jax.ShapeDtypeStruct(s, d) for s, d, *keep in outs],
         in_specs=ins,
-        out_specs=[SM if keep == [pltpu.SMEM] else VM for _, _, *keep in outs],
+        out_specs=[{pltpu.SMEM: SM, pltpu.HBM: ANY}.get(keep[0], VM) if keep else VM for _, _, *keep in outs],
         scratch_shapes=list(scratch),
         compiler_params=pltpu.CompilerParams(vmem_limit_bytes=limit << 20),
         cost_estimate=cost,
@@ -230,8 +232,14 @@
     sent_ref[NS] = spill_out[0]
 
 
+def far_kernel(table, far, values_ref, mark_ref):
+    values, index = opened(far[0])
+    values_ref[...] = values
+    mark_ref[...] = jnp.zeros((8, R), F32) + jnp.where(table[NEXT] == 1, -1.0, index)
+
+
 def system_kernel(
-    first, table, ca, cb, part, got, near, far, spill_out, v0, *rest
+    first, table, ca, cb, part, got, near, far, mark, spill_out, v0, *rest
 ):
     if first:
         p_ref, w_ref, wout_ref, sums_ref, u = rest
@@ -239,8 +247,7 @@
         w, p_ref, sums_ref, u = rest
     got_values, got_index = opened(got[NS])
     got_index = jnp.where(table[ENDS] == 1, -1.0, got_index)
-    far_values, far_index = opened(far[0])
-    far_index = jnp.where(table[NEXT] == 1, -1.0, far_index)
+    far_values, far_index = far[...], mark[0:1, :]
     count = table[COUNT]
     for s in range(NS):
         alive = jnp.where(count > s, 1.0, 0.0)
@@ -289,7 +296,7 @@
     picked(win_ref, w, opened(spill_in[0])[1])
 
 
-def finish_kernel(gathered, p0, q, out):
+def finish_kernel(gathered, p0, q, out_ref, out, sems):
     total = jnp.sum(gathered[...], axis=0)
     s00, s01, s11, s02, s12, s22 = (total[i : i + 1, :] for i in range(6))
     c = SHIFT
@@ -320,8 +327,16 @@
     y2 = beta * (g00 * h12 - g01 * h11) / det
     two = y2 / (beta * h21)
     one = y1 / beta + a * two
-    for s in range(NS):
-        out[pl.ds(s, W, stride=NS), :] = one * p0[s, :W, :] + two * q[s, :W, :]
+    copies = []
+    for begin, size in PARTS:
+        for s in range(NS):
+            p, r = p0[s, begin : begin + size, :], q[s, begin : begin + size, :]
+            out[pl.ds(begin * NS + s, size, stride=NS), :] = one * p + two * r
+        rows = pl.ds(begin * NS, size * NS)
+        copies.append(pltpu.make_async_copy(out.at[rows, :], out_ref.at[rows, :], sems.at[len(copies)]))
+        copies[-1].start()
+    for copy in copies:
+        copy.wait()
 
 
 def permuted(x, target):
@@ -418,6 +433,12 @@
             inner_kernel, [(block, F32), ((NS + 1, WP, R), BF16), (block, BF16)], [VM] * 3
         )(out, got_in, spill_out)
         got, near, far = to_outer(sent), to_inner(near), to_far(spill_out)
+        far, mark = call(
+            far_kernel,
+            [((WP, R), F32), ((8, R), F32)],
+            [SM, VM],
+            cost=pl.CostEstimate(flops=FAR_WEIGHT, bytes_accessed=1 << 18, transcendentals=0),
+        )(table, far)
         if first:
             (made,) = matrices(False, sent)
             matrix_parts.append(pltpu.with_memory_space_constraint(made, pltpu.VMEM))
@@ -425,9 +446,9 @@
         return call(
             functools.partial(system_kernel, first),
             outs + [((8, R), F32)],
-            [SM] + [VM] * (7 + len(more)),
+            [SM] + [VM] * (8 + len(more)),
             [pltpu.VMEM((3 * NS, WP, R), BF16)],
-        )(table, *matrix_parts, part, got, near, far, spill_out, *more)
+        )(table, *matrix_parts, part, got, near, far, mark, spill_out, *more)
 
     matrix_parts = [first_part]
     out, got_in, spill_out = solve(v0, inner, outer)
@@ -441,7 +462,12 @@
         jnp.broadcast_to(sums[None], (NSUB // 2, 6, R)), "sub", 0, 0,
         axis_index_groups=[list(range(c, NSUB, 2)) for c in range(2)],
     )
-    (flat,) = call(finish_kernel, [((W * NS, R), F32)], [VM] * 3)(gathered, p0, q)
+    (flat,) = call(
+        finish_kernel,
+        [((W * NS, R), F32, pltpu.HBM)],
+        [VM] * 3,
+        [pltpu.VMEM((W * NS, R), F32), pltpu.SemaphoreType.DMA((len(PARTS),))],
+    )(gathered, p0, q)
     return flat.reshape(W, NS, R).transpose(1, 0, 2)
 
 

time: 62.7 us -> 62.2 us (level)
  waiting for transfers between devices: 11.4 us -> 6.57 us
  starting transfers between devices: 9.18 us -> 14 us
    ppermute x13, starting transfers between devices: 9.18 us -> 14 us  [permuted(): lax.ppermute(x, ('sub', 'rhs'), [(i * parts + j, t[0] * parts + t[1]) for...]
    ppermute x13, waiting for transfers between devices: 11.4 us -> 6.57 us  [permuted(): lax.ppermute(x, ('sub', 'rhs'), [(i * parts + j, t[0] * parts + t[1]) for...]
where the time goes in v9:
time: 62.2 us; the launch traced here: 61.7 us
  blocking collectives  24.9 us (40%)
  Pallas kernels  14.2 us (23%)
  starting transfers between devices  14 us (23%)
  waiting for transfers between devices  6.57 us (11%)
  local copies, waits for them, and re-layouts  1.05 us (2%)
  between operations  1 us (2%)
    all_to_all x1, blocking collectives, body(): lax.all_to_all(jnp.broadcast_to(sums[None], (NSUB // 2, 6, R)), 'sub', 0,...  24.9 us
    ppermute x13, starting transfers between devices, permuted(): lax.ppermute(x, ('sub', 'rhs'), [(i * parts + j, t[0] * parts + t[1]) for...  14 us
    pallas_call x2, Pallas kernels, matrices(): call(functools.partial(coupling_kernel, blocks, groups, first), outs, [AN...  7.25 us
    ppermute x13, waiting for transfers between devices, permuted(): lax.ppermute(x, ('sub', 'rhs'), [(i * parts + j, t[0] * parts + t[1]) for...  6.57 us
    pallas_call x2, Pallas kernels, solve(): call(own_kernel, [((6 * W, R), F32, pltpu.VMEM)], [VM, VM], [pltpu.VMEM((...  1.97 us
    pallas_call x2, Pallas kernels, solve(): call(solve_kernel, [(block, F32), (one, BF16)], [SM] + [VM] * 3, [pltpu.V...  1.72 us
    pallas_call x2, Pallas kernels, system(): call(functools.partial(system_kernel, first), outs + [((8, R), F32)], [SM...  1.31 us
  transfers between devices with their start and end apart: 13, of which 5 were waited for; matrix products, arithmetic and copies ran while one was open for 0% of the time, Pallas kernels for 18%

profile of v9, /device:TPU:2, one launch (start us, length us, event | category | flops | bytes accessed | tf_op | source)
XLA Modules:
  0.0 61.7 jit_solution(16861503459663459422)
XLA Ops:
  0.7 1.0 %copy-done = f32[4,252,128]{2,0,1:T(4,128)S(1)} copy-done((f32[4,252,128]{2,0,1:T(4,128)S(1)}, f32[4,252,128]{2,0,1:T(4,128)}, u32[]{:S(2)}) %copy-start) | copy-done | bytes 516120
  1.8 2.4 %collective-permute-start.1 = (bf16[4,256,128]{2,1,0:T(8,128)(2,1)S(1)}, bf16[4,256,128]{2,1,0:T(8,128)(2,1)S(1)}, u32[]{:S(2)}, u32[]{:S(2)}) collective-permute-start(bf16[4,256,128]{2,1,0:T(8,128)(2,1)S(1)} %get-tuple-element.38), channel_id=1, source_target_pairs={{0,1},{1,0},{2,3},{3,2},{4,8},{5,9},{6,10},{7,11},{8,4},{9,5},{10,... | collective-permute-start | bytes 786440 | tf_op jit(solution)/shard_map/ppermute | solution.py:345
  4.1 4.0 %shard_map.64 = (bf16[16,256,256]{2,1,0:T(8,128)(2,1)S(1)}, bf16[1512,1512]{1,0:T(8,128)(2,1)S(1)}, s32[41]{0:T(128)S(4)}) custom-call(bf16[4,508032]{1,0:T(4,128)(2,1)} %flat.3, bf16[1,1512,1512]{2,1,0:T(8,128)(2,1)} %rest_0_.1, s32[1]{0:T(128)} %bitcast.rest_1_, s32[1]{0:T(128)S(6)} %copy.7.rest_2_.counts, s32[1,2]{1,0:T(1,128)} %rest_3_.1, s32[4,8]{1,0:T(4,128)} %rest_4_.1), custom_call_target="tpu_custom_call" | custom-call | flops 1048576 | bytes 12582912 | tf_op jit(solution)/shard_map/pallas_call | solution.py:389
  8.1 1.0 %shard_map.66.part = f32[1512,128]{1,0:T(8,128)S(1)} custom-call(bf16[1512,1512]{1,0:T(8,128)(2,1)S(1)} %get-tuple-element.36.inverse, f32[4,256,128]{2,1,0:T(8,128)S(1)} %get-tuple-element.37.own.v0), custom_call_target="tpu_custom_call" | custom-call | flops 1073741824 | bytes 4194304 | tf_op jit(solution)/shard_map/pallas_call | solution.py:410
  9.1 0.3 shard_map.67
  9.5 0.5 collective-permute-start.2
  10.0 0.9 %shard_map.68 = (f32[4,256,128]{2,1,0:T(8,128)S(1)}, bf16[1,256,128]{2,1,0:T(8,128)(2,1)S(1)}) custom-call(s32[41]{0:T(128)S(4)} %get-tuple-element.34.table, bf16[1512,1512]{1,0:T(8,128)(2,1)S(1)} %get-tuple-element.36.inverse, f32[1512,128]{1,0:T(8,128)S(1)} %shard_map.66.part, bf16[616,128]{1,0:T(8,128)(2,1)S(1)} %get-tuple-element.39.ext), custom_call_target="tpu_custom_call" | custom-call | flops 1073741824 | bytes 4194304 | tf_op jit(solution)/shard_map/pallas_call | solution.py:422
  10.9 0.1 shard_map.69
  11.0 1.3 %collective-permute-start.3 = (bf16[5,256,128]{2,1,0:T(8,128)(2,1)S(1)}, bf16[5,256,128]{2,1,0:T(8,128)(2,1)S(1)}, u32[]{:S(2)}, u32[]{:S(2)}) collective-permute-start(bf16[5,256,128]{2,1,0:T(8,128)(2,1)S(1)} %get-tuple-element.43.rest_0_), channel_id=1, source_target_pairs={{0,1},{1,0},{2,3},{3,2},{4,8},{5,9},{6,10},{7,11},{8,4},{9,5},{10,... | collective-permute-start | bytes 983048 | tf_op jit(solution)/shard_map/ppermute | solution.py:345
  12.4 0.4 collective-permute-start.5
  12.8 1.6 %collective-permute-start.4 = (bf16[4,256,128]{2,1,0:T(8,128)(2,1)S(1)}, bf16[4,256,128]{2,1,0:T(8,128)(2,1)S(1)}, u32[]{:S(2)}, u32[]{:S(2)}) collective-permute-start(bf16[4,256,128]{2,1,0:T(8,128)(2,1)S(1)} %get-tuple-element.45), channel_id=1, source_target_pairs={{0,4},{1,5},{2,6},{3,7},{4,0},{5,1},{6,2},{7,3},{8,12},{9,13},{10,... | collective-permute-start | bytes 786440 | tf_op jit(solution)/shard_map/ppermute | solution.py:345
  14.4 3.3 %shard_map.70.cb = bf16[16,256,256]{2,1,0:T(8,128)(2,1)S(1)} custom-call(bf16[4,508032]{1,0:T(4,128)(2,1)} %flat.3, bf16[5,256,128]{2,1,0:T(8,128)(2,1)S(1)} %get-tuple-element.43.rest_0_), custom_call_target="tpu_custom_call" | custom-call | flops 1048576 | bytes 12582912 | tf_op jit(solution)/shard_map/pallas_call | solution.py:389
  17.7 1.1 %collective-permute-done.5.far = bf16[1,256,128]{2,1,0:T(8,128)(2,1)S(1)} collective-permute-done((bf16[1,256,128]{2,1,0:T(8,128)(2,1)S(1)}, bf16[1,256,128]{2,1,0:T(8,128)(2,1)S(1)}, u32[]{:S(2)}, u32[]{:S(2)}) %collective-permute-start.5) | collective-permute-done | bytes 65568 | tf_op jit(solution)/shard_map/ppermute | solution.py:345
  18.9 0.7 %shard_map.72 = (f32[4,256,128]{2,1,0:T(8,128)S(1)}, f32[4,256,128]{2,1,0:T(8,128)S(1)}, bf16[1,256,128]{2,1,0:T(8,128)(2,1)S(1)}, f32[8,128]{1,0:T(8,128)S(1)}) custom-call(s32[41]{0:T(128)S(4)} %get-tuple-element.34.table, bf16[16,256,256]{2,1,0:T(8,128)(2,1)S(1)} %get-tuple-element.35.ca, bf16[16,256,256]{2,1,0:T(8,128)(2,1)S(1)} %shard_map.70.cb, ...), custom_call_target="tpu_custom_call" | custom-call | tf_op jit(solution)/shard_map/pallas_call | solution.py:446
  19.6 1.2 %collective-permute-start.7 = (bf16[1,256,128]{2,1,0:T(8,128)(2,1)S(1)}, bf16[1,256,128]{2,1,0:T(8,128)(2,1)S(1)}, u32[]{:S(2)}, u32[]{:S(2)}) collective-permute-start(bf16[1,256,128]{2,1,0:T(8,128)(2,1)S(1)} %get-tuple-element.50), channel_id=1, source_target_pairs={{0,1},{1,0},{2,3},{3,2},{4,8},{5,9},{6,10},{7,11},{8,4},{9,5},{10,... | collective-permute-start | bytes 196616 | tf_op jit(solution)/shard_map/ppermute | solution.py:345
  20.8 1.1 %collective-permute-start.6 = (bf16[1,256,128]{2,1,0:T(8,128)(2,1)S(1)}, bf16[1,256,128]{2,1,0:T(8,128)(2,1)S(1)}, u32[]{:S(2)}, u32[]{:S(2)}) collective-permute-start(bf16[1,256,128]{2,1,0:T(8,128)(2,1)S(1)} %shard_map.74), channel_id=1, source_target_pairs={{0,4},{1,5},{2,6},{3,7},{4,0},{5,1},{6,2},{7,3},{8,12},{9,13},{10,... | collective-permute-start | bytes 196616 | tf_op jit(solution)/shard_map/ppermute | solution.py:345
  21.9 1.0 %shard_map.73.part = f32[1512,128]{1,0:T(8,128)S(1)} custom-call(bf16[1512,1512]{1,0:T(8,128)(2,1)S(1)} %get-tuple-element.36.inverse, f32[4,256,128]{2,1,0:T(8,128)S(1)} %get-tuple-element.49.own.w.rest_0_), custom_call_target="tpu_custom_call" | custom-call | flops 1073741824 | bytes 4194304 | tf_op jit(solution)/shard_map/pallas_call | solution.py:410
  22.9 1.0 %collective-permute-done.7.outer = bf16[1,256,128]{2,1,0:T(8,128)(2,1)S(1)} collective-permute-done((bf16[1,256,128]{2,1,0:T(8,128)(2,1)S(1)}, bf16[1,256,128]{2,1,0:T(8,128)(2,1)S(1)}, u32[]{:S(2)}, u32[]{:S(2)}) %collective-permute-start.7) | collective-permute-done | bytes 65568 | tf_op jit(solution)/shard_map/ppermute | solution.py:345
  23.9 0.3 shard_map.75
  24.3 0.3 collective-permute-start.8
  24.6 0.9 %shard_map.76 = (f32[4,256,128]{2,1,0:T(8,128)S(1)}, bf16[1,256,128]{2,1,0:T(8,128)(2,1)S(1)}) custom-call(s32[41]{0:T(128)S(4)} %get-tuple-element.34.table, bf16[1512,1512]{1,0:T(8,128)(2,1)S(1)} %get-tuple-element.36.inverse, f32[1512,128]{1,0:T(8,128)S(1)} %shard_map.73.part, bf16[616,128]{1,0:T(8,128)(2,1)S(1)} %get-tuple-element.51.ext), custom_call_target="tpu_custom_call" | custom-call | flops 1073741824 | bytes 4194304 | tf_op jit(solution)/shard_map/pallas_call | solution.py:422
  25.5 0.3 collective-permute-done.8.spill_in
  25.8 0.1 shard_map.77
  25.9 1.2 %collective-permute-start.9 = (bf16[5,256,128]{2,1,0:T(8,128)(2,1)S(1)}, bf16[5,256,128]{2,1,0:T(8,128)(2,1)S(1)}, u32[]{:S(2)}, u32[]{:S(2)}) collective-permute-start(bf16[5,256,128]{2,1,0:T(8,128)(2,1)S(1)} %get-tuple-element.56), channel_id=1, source_target_pairs={{0,1},{1,0},{2,3},{3,2},{4,8},{5,9},{6,10},{7,11},{8,4},{9,5},{10,... | collective-permute-start | bytes 983048 | tf_op jit(solution)/shard_map/ppermute | solution.py:345
  27.1 1.1 %collective-permute-start.11 = (bf16[1,256,128]{2,1,0:T(8,128)(2,1)S(1)}, bf16[1,256,128]{2,1,0:T(8,128)(2,1)S(1)}, u32[]{:S(2)}, u32[]{:S(2)}) collective-permute-start(bf16[1,256,128]{2,1,0:T(8,128)(2,1)S(1)} %get-tuple-element.54.spill_out), channel_id=1, source_target_pairs={{0,4},{1,5},{2,6},{3,7},{4,12},{5,13},{6,14},{7,15},{8,0},{9,1},{1... | collective-permute-start | bytes 196616 | tf_op jit(solution)/shard_map/ppermute | solution.py:345
  28.1 2.7 %collective-permute-start.10 = (bf16[4,256,128]{2,1,0:T(8,128)(2,1)S(1)}, bf16[4,256,128]{2,1,0:T(8,128)(2,1)S(1)}, u32[]{:S(2)}, u32[]{:S(2)}) collective-permute-start(bf16[4,256,128]{2,1,0:T(8,128)(2,1)S(1)} %get-tuple-element.57), channel_id=1, source_target_pairs={{0,4},{1,5},{2,6},{3,7},{4,0},{5,1},{6,2},{7,3},{8,12},{9,13},{10,... | collective-permute-start | bytes 786440 | tf_op jit(solution)/shard_map/ppermute | solution.py:345
  30.9 2.9 %collective-permute-done.11.far = bf16[1,256,128]{2,1,0:T(8,128)(2,1)S(1)} collective-permute-done((bf16[1,256,128]{2,1,0:T(8,128)(2,1)S(1)}, bf16[1,256,128]{2,1,0:T(8,128)(2,1)S(1)}, u32[]{:S(2)}, u32[]{:S(2)}) %collective-permute-start.11) | collective-permute-done | bytes 65568 | tf_op jit(solution)/shard_map/ppermute | solution.py:345
  33.8 0.6 %shard_map.79 = (f32[4,256,128]{2,1,0:T(8,128)S(1)}, f32[8,128]{1,0:T(8,128)S(1)}) custom-call(s32[41]{0:T(128)S(4)} %get-tuple-element.34.table, bf16[16,256,256]{2,1,0:T(8,128)(2,1)S(1)} %get-tuple-element.35.ca, bf16[16,256,256]{2,1,0:T(8,128)(2,1)S(1)} %shard_map.70.cb, f32[4,256,128]{2,1,0:T(8,128)S(1)} %get-tuple-element.55.part, ...), custom_call_target="tpu_custom_call" | custom-call | tf_op jit(solution)/shard_map/pallas_call | solution.py:446
  34.4 0.1 collective-permute-start.12
  34.5 1.2 %collective-permute-done.12 = f32[6,128]{1,0:T(8,128)S(1)} collective-permute-done((f32[6,128]{1,0:T(8,128)S(1)}, f32[6,128]{1,0:T(8,128)S(1)}, u32[]{:S(2)}, u32[]{:S(2)}) %collective-permute-start.12) | collective-permute-done | bytes 3104 | tf_op jit(solution)/shard_map/ppermute | solution.py:345
  35.7 24.9 %all_to_all.5.gathered = f32[32,6,128]{2,1,0:T(8,128)S(1)} all-to-all(f32[32,6,128]{2,1,0:T(8,128)S(1)} %broadcast_in_dim.2), channel_id=1, replica_groups={{0,8,16,24,32,40,48,56,64,72,80,88,96,104,112,120,128,136,144,152,160,1..., dimensions={0} | all-to-all | bytes 196608 | tf_op jit(solution)/shard_map/all_to_all | solution.py:461
  60.6 0.9 %shard_map.80 = f32[1008,128]{1,0:T(8,128)} custom-call(f32[32,6,128]{2,1,0:T(8,128)S(1)} %all_to_all.5.gathered, f32[4,256,128]{2,1,0:T(8,128)S(1)} %get-tuple-element.61.p0, f32[4,256,128]{2,1,0:T(8,128)S(1)} %get-tuple-element.62.q), custom_call_target="tpu_custom_call" | custom-call | tf_op jit(solution)/shard_map/pallas_call | solution.py:465
  (19 shorter events, 0.2 us)
Async XLA Ops:
  0.7 1.0 %copy-start = (f32[4,252,128]{2,0,1:T(4,128)S(1)}, f32[4,252,128]{2,0,1:T(4,128)}, u32[]{:S(2)}) copy-start(f32[4,252,128]{2,0,1:T(4,128)} %param.6) | copy-start | bytes 1548292
  1.8 7.3 %collective-permute-start.1 = (bf16[4,256,128]{2,1,0:T(8,128)(2,1)S(1)}, bf16[4,256,128]{2,1,0:T(8,128)(2,1)S(1)}, u32[]{:S(2)}, u32[]{:S(2)}) collective-permute-start(bf16[4,256,128]{2,1,0:T(8,128)(2,1)S(1)} %get-tuple-element.38), channel_id=1, source_target_pairs={{0,1},{1,0},{2,3},{3,2},{4,8},{5,9},{6,10},{7,11},{8,4},{9,5},{10,... | collective-permute-start | bytes 786440 | tf_op jit(solution)/shard_map/ppermute | solution.py:345
  4.1 5.0 %collective-permute-start = (bf16[4,256,128]{2,1,0:T(8,128)(2,1)S(1)}, bf16[4,256,128]{2,1,0:T(8,128)(2,1)S(1)}, u32[]{:S(2)}, u32[]{:S(2)}) collective-permute-start(bf16[4,256,128]{2,1,0:T(8,128)(2,1)S(1)} %get-tuple-element.38), channel_id=1, source_target_pairs={{0,4},{1,5},{2,6},{3,7},{4,0},{5,1},{6,2},{7,3},{8,12},{9,13},{10,... | collective-permute-start | bytes 786440 | tf_op jit(solution)/shard_map/ppermute | solution.py:345
  9.5 1.4 %collective-permute-start.2 = (bf16[1,256,128]{2,1,0:T(8,128)(2,1)S(1)}, bf16[1,256,128]{2,1,0:T(8,128)(2,1)S(1)}, u32[]{:S(2)}, u32[]{:S(2)}) collective-permute-start(bf16[1,256,128]{2,1,0:T(8,128)(2,1)S(1)} %get-tuple-element.41), channel_id=1, source_target_pairs={{0,4},{1,5},{2,6},{3,7},{4,0},{5,1},{6,2},{7,3},{8,12},{9,13},{10,... | collective-permute-start | bytes 196616 | tf_op jit(solution)/shard_map/ppermute | solution.py:345
  11.0 7.8 %collective-permute-start.3 = (bf16[5,256,128]{2,1,0:T(8,128)(2,1)S(1)}, bf16[5,256,128]{2,1,0:T(8,128)(2,1)S(1)}, u32[]{:S(2)}, u32[]{:S(2)}) collective-permute-start(bf16[5,256,128]{2,1,0:T(8,128)(2,1)S(1)} %get-tuple-element.43.rest_0_), channel_id=1, source_target_pairs={{0,1},{1,0},{2,3},{3,2},{4,8},{5,9},{6,10},{7,11},{8,4},{9,5},{10,... | collective-permute-start | bytes 983048 | tf_op jit(solution)/shard_map/ppermute | solution.py:345
  12.4 6.5 %collective-permute-start.5 = (bf16[1,256,128]{2,1,0:T(8,128)(2,1)S(1)}, bf16[1,256,128]{2,1,0:T(8,128)(2,1)S(1)}, u32[]{:S(2)}, u32[]{:S(2)}) collective-permute-start(bf16[1,256,128]{2,1,0:T(8,128)(2,1)S(1)} %get-tuple-element.42.spill_out), channel_id=1, source_target_pairs={{0,4},{1,5},{2,6},{3,7},{4,12},{5,13},{6,14},{7,15},{8,0},{9,1},{1... | collective-permute-start | bytes 196616 | tf_op jit(solution)/shard_map/ppermute | solution.py:345
  12.8 6.1 %collective-permute-start.4 = (bf16[4,256,128]{2,1,0:T(8,128)(2,1)S(1)}, bf16[4,256,128]{2,1,0:T(8,128)(2,1)S(1)}, u32[]{:S(2)}, u32[]{:S(2)}) collective-permute-start(bf16[4,256,128]{2,1,0:T(8,128)(2,1)S(1)} %get-tuple-element.45), channel_id=1, source_target_pairs={{0,4},{1,5},{2,6},{3,7},{4,0},{5,1},{6,2},{7,3},{8,12},{9,13},{10,... | collective-permute-start | bytes 786440 | tf_op jit(solution)/shard_map/ppermute | solution.py:345
  19.6 4.4 %collective-permute-start.7 = (bf16[1,256,128]{2,1,0:T(8,128)(2,1)S(1)}, bf16[1,256,128]{2,1,0:T(8,128)(2,1)S(1)}, u32[]{:S(2)}, u32[]{:S(2)}) collective-permute-start(bf16[1,256,128]{2,1,0:T(8,128)(2,1)S(1)} %get-tuple-element.50), channel_id=1, source_target_pairs={{0,1},{1,0},{2,3},{3,2},{4,8},{5,9},{6,10},{7,11},{8,4},{9,5},{10,... | collective-permute-start | bytes 196616 | tf_op jit(solution)/shard_map/ppermute | solution.py:345
  20.8 3.1 %collective-permute-start.6 = (bf16[1,256,128]{2,1,0:T(8,128)(2,1)S(1)}, bf16[1,256,128]{2,1,0:T(8,128)(2,1)S(1)}, u32[]{:S(2)}, u32[]{:S(2)}) collective-permute-start(bf16[1,256,128]{2,1,0:T(8,128)(2,1)S(1)} %shard_map.74), channel_id=1, source_target_pairs={{0,4},{1,5},{2,6},{3,7},{4,0},{5,1},{6,2},{7,3},{8,12},{9,13},{10,... | collective-permute-start | bytes 196616 | tf_op jit(solution)/shard_map/ppermute | solution.py:345
  24.3 1.5 %collective-permute-start.8 = (bf16[1,256,128]{2,1,0:T(8,128)(2,1)S(1)}, bf16[1,256,128]{2,1,0:T(8,128)(2,1)S(1)}, u32[]{:S(2)}, u32[]{:S(2)}) collective-permute-start(bf16[1,256,128]{2,1,0:T(8,128)(2,1)S(1)} %get-tuple-element.53), channel_id=1, source_target_pairs={{0,4},{1,5},{2,6},{3,7},{4,0},{5,1},{6,2},{7,3},{8,12},{9,13},{10,... | collective-permute-start | bytes 196616 | tf_op jit(solution)/shard_map/ppermute | solution.py:345
  25.9 7.9 %collective-permute-start.9 = (bf16[5,256,128]{2,1,0:T(8,128)(2,1)S(1)}, bf16[5,256,128]{2,1,0:T(8,128)(2,1)S(1)}, u32[]{:S(2)}, u32[]{:S(2)}) collective-permute-start(bf16[5,256,128]{2,1,0:T(8,128)(2,1)S(1)} %get-tuple-element.56), channel_id=1, source_target_pairs={{0,1},{1,0},{2,3},{3,2},{4,8},{5,9},{6,10},{7,11},{8,4},{9,5},{10,... | collective-permute-start | bytes 983048 | tf_op jit(solution)/shard_map/ppermute | solution.py:345
  27.1 6.7 %collective-permute-start.11 = (bf16[1,256,128]{2,1,0:T(8,128)(2,1)S(1)}, bf16[1,256,128]{2,1,0:T(8,128)(2,1)S(1)}, u32[]{:S(2)}, u32[]{:S(2)}) collective-permute-start(bf16[1,256,128]{2,1,0:T(8,128)(2,1)S(1)} %get-tuple-element.54.spill_out), channel_id=1, source_target_pairs={{0,4},{1,5},{2,6},{3,7},{4,12},{5,13},{6,14},{7,15},{8,0},{9,1},{1... | collective-permute-start | bytes 196616 | tf_op jit(solution)/shard_map/ppermute | solution.py:345
  28.1 5.7 %collective-permute-start.10 = (bf16[4,256,128]{2,1,0:T(8,128)(2,1)S(1)}, bf16[4,256,128]{2,1,0:T(8,128)(2,1)S(1)}, u32[]{:S(2)}, u32[]{:S(2)}) collective-permute-start(bf16[4,256,128]{2,1,0:T(8,128)(2,1)S(1)} %get-tuple-element.57), channel_id=1, source_target_pairs={{0,4},{1,5},{2,6},{3,7},{4,0},{5,1},{6,2},{7,3},{8,12},{9,13},{10,... | collective-permute-start | bytes 786440 | tf_op jit(solution)/shard_map/ppermute | solution.py:345
  34.4 1.3 %collective-permute-start.12 = (f32[6,128]{1,0:T(8,128)S(1)}, f32[6,128]{1,0:T(8,128)S(1)}, u32[]{:S(2)}, u32[]{:S(2)}) collective-permute-start(f32[6,128]{1,0:T(8,128)S(1)} %pad_maximum_fusion), channel_id=1, source_target_pairs={{0,4},{1,5},{2,6},{3,7},{4,0},{5,1},{6,2},{7,3},{8,12},{9,13},{10,... | collective-permute-start | bytes 9224 | tf_op jit(solution)/shard_map/ppermute | solution.py:345

commit v10 on v9

--- a/solution.py
+++ b/solution.py
@@ -22,7 +22,6 @@
 SPLIT = 4
 EVEN, FIRST, LAST, LOW, HIGH, COUNT, ENDS, NEXT, OUT, SLOTS = range(10)
 TABLE = SLOTS + NS * NB
-FAR_WEIGHT = 2450000000
 OWN = 1024
 FROM = 896
 ANY = pl.BlockSpec(memory_space=pl.ANY)
@@ -232,14 +231,8 @@
     sent_ref[NS] = spill_out[0]
 
 
-def far_kernel(table, far, values_ref, mark_ref):
-    values, index = opened(far[0])
-    values_ref[...] = values
-    mark_ref[...] = jnp.zeros((8, R), F32) + jnp.where(table[NEXT] == 1, -1.0, index)
-
-
 def system_kernel(
-    first, table, ca, cb, part, got, near, far, mark, spill_out, v0, *rest
+    first, table, ca, cb, part, got, near, far, spill_out, v0, *rest
 ):
     if first:
         p_ref, w_ref, wout_ref, sums_ref, u = rest
@@ -247,7 +240,8 @@
         w, p_ref, sums_ref, u = rest
     got_values, got_index = opened(got[NS])
     got_index = jnp.where(table[ENDS] == 1, -1.0, got_index)
-    far_values, far_index = far[...], mark[0:1, :]
+    far_values, far_index = opened(far[0])
+    far_index = jnp.where(table[NEXT] == 1, -1.0, far_index)
     count = table[COUNT]
     for s in range(NS):
         alive = jnp.where(count > s, 1.0, 0.0)
@@ -433,12 +427,6 @@
             inner_kernel, [(block, F32), ((NS + 1, WP, R), BF16), (block, BF16)], [VM] * 3
         )(out, got_in, spill_out)
         got, near, far = to_outer(sent), to_inner(near), to_far(spill_out)
-        far, mark = call(
-            far_kernel,
-            [((WP, R), F32), ((8, R), F32)],
-            [SM, VM],
-            cost=pl.CostEstimate(flops=FAR_WEIGHT, bytes_accessed=1 << 18, transcendentals=0),
-        )(table, far)
         if first:
             (made,) = matrices(False, sent)
             matrix_parts.append(pltpu.with_memory_space_constraint(made, pltpu.VMEM))
@@ -446,9 +434,9 @@
         return call(
             functools.partial(system_kernel, first),
             outs + [((8, R), F32)],
-            [SM] + [VM] * (8 + len(more)),
+            [SM] + [VM] * (7 + len(more)),
             [pltpu.VMEM((3 * NS, WP, R), BF16)],
-        )(table, *matrix_parts, part, got, near, far, mark, spill_out, *more)
+        )(table, *matrix_parts, part, got, near, far, spill_out, *more)
 
     matrix_parts = [first_part]
     out, got_in, spill_out = solve(v0, inner, outer)

time: 62.2 us -> 61.9 us (level)
  waiting for transfers between devices: 6.57 us -> 11.4 us
  starting transfers between devices: 14 us -> 9.18 us
    ppermute x13, starting transfers between devices: 14 us -> 9.18 us  [permuted(): lax.ppermute(x, ('sub', 'rhs'), [(i * parts + j, t[0] * parts + t[1]) for...]
    ppermute x13, waiting for transfers between devices: 6.57 us -> 11.4 us  [permuted(): lax.ppermute(x, ('sub', 'rhs'), [(i * parts + j, t[0] * parts + t[1]) for...]
where the time goes in v10:
time: 61.9 us; the launch traced here: 61.7 us
  blocking collectives  24.9 us (40%)
  Pallas kernels  14.1 us (23%)
  waiting for transfers between devices  11.4 us (18%)
  starting transfers between devices  9.18 us (15%)
  local copies, waits for them, and re-layouts  1.05 us (2%)
  between operations  0.97 us (2%)
    all_to_all x1, blocking collectives, body(): lax.all_to_all(jnp.broadcast_to(sums[None], (NSUB // 2, 6, R)), 'sub', 0,...  24.9 us
    ppermute x13, waiting for transfers between devices, permuted(): lax.ppermute(x, ('sub', 'rhs'), [(i * parts + j, t[0] * parts + t[1]) for...  11.4 us
    ppermute x13, starting transfers between devices, permuted(): lax.ppermute(x, ('sub', 'rhs'), [(i * parts + j, t[0] * parts + t[1]) for...  9.18 us
    pallas_call x2, Pallas kernels, matrices(): call(functools.partial(coupling_kernel, blocks, groups, first), outs, [AN...  7.25 us
    pallas_call x2, Pallas kernels, solve(): call(own_kernel, [((6 * W, R), F32, pltpu.VMEM)], [VM, VM], [pltpu.VMEM((...  1.97 us
    pallas_call x2, Pallas kernels, solve(): call(solve_kernel, [(block, F32), (one, BF16)], [SM] + [VM] * 3, [pltpu.V...  1.73 us
    pallas_call x2, Pallas kernels, system(): call(functools.partial(system_kernel, first), outs + [((8, R), F32)], [SM...  1.31 us
  transfers between devices with their start and end apart: 13, of which 5 were waited for; matrix products, arithmetic and copies ran while one was open for 0% of the time, Pallas kernels for 18%

profile of v10, /device:TPU:2, one launch (start us, length us, event | category | flops | bytes accessed | tf_op | source)
XLA Modules:
  0.0 61.7 jit_solution(7668451548375283484)
XLA Ops:
  0.7 1.0 %copy-done = f32[4,252,128]{2,0,1:T(4,128)S(1)} copy-done((f32[4,252,128]{2,0,1:T(4,128)S(1)}, f32[4,252,128]{2,0,1:T(4,128)}, u32[]{:S(2)}) %copy-start) | copy-done | bytes 516120
  1.7 0.1 shard_map.65
  1.8 2.4 %collective-permute-start.1 = (bf16[4,256,128]{2,1,0:T(8,128)(2,1)S(1)}, bf16[4,256,128]{2,1,0:T(8,128)(2,1)S(1)}, u32[]{:S(2)}, u32[]{:S(2)}) collective-permute-start(bf16[4,256,128]{2,1,0:T(8,128)(2,1)S(1)} %get-tuple-element.34), channel_id=1, source_target_pairs={{0,1},{1,0},{2,3},{3,2},{4,8},{5,9},{6,10},{7,11},{8,4},{9,5},{10,... | collective-permute-start | bytes 786440 | tf_op jit(solution)/shard_map/ppermute | solution.py:339
  4.1 4.0 %shard_map.64 = (bf16[16,256,256]{2,1,0:T(8,128)(2,1)S(1)}, bf16[1512,1512]{1,0:T(8,128)(2,1)S(1)}, s32[41]{0:T(128)S(4)}) custom-call(bf16[4,508032]{1,0:T(4,128)(2,1)} %flat.3, bf16[1,1512,1512]{2,1,0:T(8,128)(2,1)} %rest_0_.1, s32[1]{0:T(128)} %bitcast.rest_1_, s32[1]{0:T(128)S(6)} %copy.7.rest_2_.counts, s32[1,2]{1,0:T(1,128)} %rest_3_.1, s32[4,8]{1,0:T(4,128)} %rest_4_.1), custom_call_target="tpu_custom_call" | custom-call | flops 1048576 | bytes 12582912 | tf_op jit(solution)/shard_map/pallas_call | solution.py:383
  8.1 1.0 %shard_map.66.part = f32[1512,128]{1,0:T(8,128)S(1)} custom-call(bf16[1512,1512]{1,0:T(8,128)(2,1)S(1)} %get-tuple-element.32.inverse, f32[4,256,128]{2,1,0:T(8,128)S(1)} %get-tuple-element.33.own.v0), custom_call_target="tpu_custom_call" | custom-call | flops 1073741824 | bytes 4194304 | tf_op jit(solution)/shard_map/pallas_call | solution.py:404
  9.1 0.3 shard_map.67
  9.5 0.5 collective-permute-start.2
  10.0 0.9 %shard_map.68 = (f32[4,256,128]{2,1,0:T(8,128)S(1)}, bf16[1,256,128]{2,1,0:T(8,128)(2,1)S(1)}) custom-call(s32[41]{0:T(128)S(4)} %get-tuple-element.30.table, bf16[1512,1512]{1,0:T(8,128)(2,1)S(1)} %get-tuple-element.32.inverse, f32[1512,128]{1,0:T(8,128)S(1)} %shard_map.66.part, bf16[616,128]{1,0:T(8,128)(2,1)S(1)} %get-tuple-element.35.ext), custom_call_target="tpu_custom_call" | custom-call | flops 1073741824 | bytes 4194304 | tf_op jit(solution)/shard_map/pallas_call | solution.py:416
  10.9 0.1 shard_map.69
  11.0 1.3 %collective-permute-start.3 = (bf16[5,256,128]{2,1,0:T(8,128)(2,1)S(1)}, bf16[5,256,128]{2,1,0:T(8,128)(2,1)S(1)}, u32[]{:S(2)}, u32[]{:S(2)}) collective-permute-start(bf16[5,256,128]{2,1,0:T(8,128)(2,1)S(1)} %get-tuple-element.39.rest_0_), channel_id=1, source_target_pairs={{0,1},{1,0},{2,3},{3,2},{4,8},{5,9},{6,10},{7,11},{8,4},{9,5},{10,... | collective-permute-start | bytes 983048 | tf_op jit(solution)/shard_map/ppermute | solution.py:339
  12.4 0.4 collective-permute-start.4
  12.8 0.1 collective-permute-start.5
  12.9 3.3 %shard_map.70.cb = bf16[16,256,256]{2,1,0:T(8,128)(2,1)S(1)} custom-call(bf16[4,508032]{1,0:T(4,128)(2,1)} %flat.3, bf16[5,256,128]{2,1,0:T(8,128)(2,1)S(1)} %get-tuple-element.39.rest_0_), custom_call_target="tpu_custom_call" | custom-call | flops 1048576 | bytes 12582912 | tf_op jit(solution)/shard_map/pallas_call | solution.py:383
  16.1 2.7 %collective-permute-done.5.far = bf16[1,256,128]{2,1,0:T(8,128)(2,1)S(1)} collective-permute-done((bf16[1,256,128]{2,1,0:T(8,128)(2,1)S(1)}, bf16[1,256,128]{2,1,0:T(8,128)(2,1)S(1)}, u32[]{:S(2)}, u32[]{:S(2)}) %collective-permute-start.5) | collective-permute-done | bytes 65568 | tf_op jit(solution)/shard_map/ppermute | solution.py:339
  18.8 0.7 %shard_map.71 = (f32[4,256,128]{2,1,0:T(8,128)S(1)}, f32[4,256,128]{2,1,0:T(8,128)S(1)}, bf16[1,256,128]{2,1,0:T(8,128)(2,1)S(1)}, f32[8,128]{1,0:T(8,128)S(1)}) custom-call(s32[41]{0:T(128)S(4)} %get-tuple-element.30.table, bf16[16,256,256]{2,1,0:T(8,128)(2,1)S(1)} %get-tuple-element.31.ca, bf16[16,256,256]{2,1,0:T(8,128)(2,1)S(1)} %shard_map.70.cb, ...), custom_call_target="tpu_custom_call" | custom-call | tf_op jit(solution)/shard_map/pallas_call | solution.py:434
  19.5 1.2 %collective-permute-start.7 = (bf16[1,256,128]{2,1,0:T(8,128)(2,1)S(1)}, bf16[1,256,128]{2,1,0:T(8,128)(2,1)S(1)}, u32[]{:S(2)}, u32[]{:S(2)}) collective-permute-start(bf16[1,256,128]{2,1,0:T(8,128)(2,1)S(1)} %get-tuple-element.44), channel_id=1, source_target_pairs={{0,1},{1,0},{2,3},{3,2},{4,8},{5,9},{6,10},{7,11},{8,4},{9,5},{10,... | collective-permute-start | bytes 196616 | tf_op jit(solution)/shard_map/ppermute | solution.py:339
  20.7 0.6 %collective-permute-start.6 = (bf16[1,256,128]{2,1,0:T(8,128)(2,1)S(1)}, bf16[1,256,128]{2,1,0:T(8,128)(2,1)S(1)}, u32[]{:S(2)}, u32[]{:S(2)}) collective-permute-start(bf16[1,256,128]{2,1,0:T(8,128)(2,1)S(1)} %shard_map.73), channel_id=1, source_target_pairs={{0,4},{1,5},{2,6},{3,7},{4,0},{5,1},{6,2},{7,3},{8,12},{9,13},{10,... | collective-permute-start | bytes 196616 | tf_op jit(solution)/shard_map/ppermute | solution.py:339
  21.4 1.0 %shard_map.72.part = f32[1512,128]{1,0:T(8,128)S(1)} custom-call(bf16[1512,1512]{1,0:T(8,128)(2,1)S(1)} %get-tuple-element.32.inverse, f32[4,256,128]{2,1,0:T(8,128)S(1)} %get-tuple-element.43.own.w.rest_0_), custom_call_target="tpu_custom_call" | custom-call | flops 1073741824 | bytes 4194304 | tf_op jit(solution)/shard_map/pallas_call | solution.py:404
  22.4 1.5 %collective-permute-done.7.outer = bf16[1,256,128]{2,1,0:T(8,128)(2,1)S(1)} collective-permute-done((bf16[1,256,128]{2,1,0:T(8,128)(2,1)S(1)}, bf16[1,256,128]{2,1,0:T(8,128)(2,1)S(1)}, u32[]{:S(2)}, u32[]{:S(2)}) %collective-permute-start.7) | collective-permute-done | bytes 65568 | tf_op jit(solution)/shard_map/ppermute | solution.py:339
  23.9 0.3 shard_map.74
  24.2 0.3 collective-permute-start.8
  24.5 0.9 %shard_map.75 = (f32[4,256,128]{2,1,0:T(8,128)S(1)}, bf16[1,256,128]{2,1,0:T(8,128)(2,1)S(1)}) custom-call(s32[41]{0:T(128)S(4)} %get-tuple-element.30.table, bf16[1512,1512]{1,0:T(8,128)(2,1)S(1)} %get-tuple-element.32.inverse, f32[1512,128]{1,0:T(8,128)S(1)} %shard_map.72.part, bf16[616,128]{1,0:T(8,128)(2,1)S(1)} %get-tuple-element.45.ext), custom_call_target="tpu_custom_call" | custom-call | flops 1073741824 | bytes 4194304 | tf_op jit(solution)/shard_map/pallas_call | solution.py:416
  25.4 0.4 collective-permute-done.8.spill_in
  25.7 0.1 shard_map.76
  25.8 1.2 %collective-permute-start.9 = (bf16[5,256,128]{2,1,0:T(8,128)(2,1)S(1)}, bf16[5,256,128]{2,1,0:T(8,128)(2,1)S(1)}, u32[]{:S(2)}, u32[]{:S(2)}) collective-permute-start(bf16[5,256,128]{2,1,0:T(8,128)(2,1)S(1)} %get-tuple-element.50), channel_id=1, source_target_pairs={{0,1},{1,0},{2,3},{3,2},{4,8},{5,9},{6,10},{7,11},{8,4},{9,5},{10,... | collective-permute-start | bytes 983048 | tf_op jit(solution)/shard_map/ppermute | solution.py:339
  27.0 1.1 %collective-permute-start.10 = (bf16[4,256,128]{2,1,0:T(8,128)(2,1)S(1)}, bf16[4,256,128]{2,1,0:T(8,128)(2,1)S(1)}, u32[]{:S(2)}, u32[]{:S(2)}) collective-permute-start(bf16[4,256,128]{2,1,0:T(8,128)(2,1)S(1)} %get-tuple-element.51), channel_id=1, source_target_pairs={{0,4},{1,5},{2,6},{3,7},{4,0},{5,1},{6,2},{7,3},{8,12},{9,13},{10,... | collective-permute-start | bytes 786440 | tf_op jit(solution)/shard_map/ppermute | solution.py:339
  28.1 5.6 %collective-permute-done.11.far = bf16[1,256,128]{2,1,0:T(8,128)(2,1)S(1)} collective-permute-done((bf16[1,256,128]{2,1,0:T(8,128)(2,1)S(1)}, bf16[1,256,128]{2,1,0:T(8,128)(2,1)S(1)}, u32[]{:S(2)}, u32[]{:S(2)}) %collective-permute-start.11) | collective-permute-done | bytes 65568 | tf_op jit(solution)/shard_map/ppermute | solution.py:339
  33.7 0.6 %shard_map.77 = (f32[4,256,128]{2,1,0:T(8,128)S(1)}, f32[8,128]{1,0:T(8,128)S(1)}) custom-call(s32[41]{0:T(128)S(4)} %get-tuple-element.30.table, bf16[16,256,256]{2,1,0:T(8,128)(2,1)S(1)} %get-tuple-element.31.ca, bf16[16,256,256]{2,1,0:T(8,128)(2,1)S(1)} %shard_map.70.cb, f32[4,256,128]{2,1,0:T(8,128)S(1)} %get-tuple-element.49.part, ...), custom_call_target="tpu_custom_call" | custom-call | tf_op jit(solution)/shard_map/pallas_call | solution.py:434
  34.4 0.1 collective-permute-start.12
  34.5 1.2 %collective-permute-done.12 = f32[6,128]{1,0:T(8,128)S(1)} collective-permute-done((f32[6,128]{1,0:T(8,128)S(1)}, f32[6,128]{1,0:T(8,128)S(1)}, u32[]{:S(2)}, u32[]{:S(2)}) %collective-permute-start.12) | collective-permute-done | bytes 3104 | tf_op jit(solution)/shard_map/ppermute | solution.py:339
  35.7 24.9 %all_to_all.5.gathered = f32[32,6,128]{2,1,0:T(8,128)S(1)} all-to-all(f32[32,6,128]{2,1,0:T(8,128)S(1)} %broadcast_in_dim.2), channel_id=1, replica_groups={{0,8,16,24,32,40,48,56,64,72,80,88,96,104,112,120,128,136,144,152,160,1..., dimensions={0} | all-to-all | bytes 196608 | tf_op jit(solution)/shard_map/all_to_all | solution.py:449
  60.6 0.9 %shard_map.78 = f32[1008,128]{1,0:T(8,128)} custom-call(f32[32,6,128]{2,1,0:T(8,128)S(1)} %all_to_all.5.gathered, f32[4,256,128]{2,1,0:T(8,128)S(1)} %get-tuple-element.53.p0, f32[4,256,128]{2,1,0:T(8,128)S(1)} %get-tuple-element.54.q), custom_call_target="tpu_custom_call" | custom-call | tf_op jit(solution)/shard_map/pallas_call | solution.py:453
  (17 shorter events, 0.1 us)
Async XLA Ops:
  0.7 1.0 %copy-start = (f32[4,252,128]{2,0,1:T(4,128)S(1)}, f32[4,252,128]{2,0,1:T(4,128)}, u32[]{:S(2)}) copy-start(f32[4,252,128]{2,0,1:T(4,128)} %param.6) | copy-start | bytes 1548292
  1.8 7.3 %collective-permute-start.1 = (bf16[4,256,128]{2,1,0:T(8,128)(2,1)S(1)}, bf16[4,256,128]{2,1,0:T(8,128)(2,1)S(1)}, u32[]{:S(2)}, u32[]{:S(2)}) collective-permute-start(bf16[4,256,128]{2,1,0:T(8,128)(2,1)S(1)} %get-tuple-element.34), channel_id=1, source_target_pairs={{0,1},{1,0},{2,3},{3,2},{4,8},{5,9},{6,10},{7,11},{8,4},{9,5},{10,... | collective-permute-start | bytes 786440 | tf_op jit(solution)/shard_map/ppermute | solution.py:339
  4.1 5.0 %collective-permute-start = (bf16[4,256,128]{2,1,0:T(8,128)(2,1)S(1)}, bf16[4,256,128]{2,1,0:T(8,128)(2,1)S(1)}, u32[]{:S(2)}, u32[]{:S(2)}) collective-permute-start(bf16[4,256,128]{2,1,0:T(8,128)(2,1)S(1)} %get-tuple-element.34), channel_id=1, source_target_pairs={{0,4},{1,5},{2,6},{3,7},{4,0},{5,1},{6,2},{7,3},{8,12},{9,13},{10,... | collective-permute-start | bytes 786440 | tf_op jit(solution)/shard_map/ppermute | solution.py:339
  9.5 1.4 %collective-permute-start.2 = (bf16[1,256,128]{2,1,0:T(8,128)(2,1)S(1)}, bf16[1,256,128]{2,1,0:T(8,128)(2,1)S(1)}, u32[]{:S(2)}, u32[]{:S(2)}) collective-permute-start(bf16[1,256,128]{2,1,0:T(8,128)(2,1)S(1)} %get-tuple-element.37), channel_id=1, source_target_pairs={{0,4},{1,5},{2,6},{3,7},{4,0},{5,1},{6,2},{7,3},{8,12},{9,13},{10,... | collective-permute-start | bytes 196616 | tf_op jit(solution)/shard_map/ppermute | solution.py:339
  11.0 7.8 %collective-permute-start.3 = (bf16[5,256,128]{2,1,0:T(8,128)(2,1)S(1)}, bf16[5,256,128]{2,1,0:T(8,128)(2,1)S(1)}, u32[]{:S(2)}, u32[]{:S(2)}) collective-permute-start(bf16[5,256,128]{2,1,0:T(8,128)(2,1)S(1)} %get-tuple-element.39.rest_0_), channel_id=1, source_target_pairs={{0,1},{1,0},{2,3},{3,2},{4,8},{5,9},{6,10},{7,11},{8,4},{9,5},{10,... | collective-permute-start | bytes 983048 | tf_op jit(solution)/shard_map/ppermute | solution.py:339
  12.4 6.5 %collective-permute-start.4 = (bf16[4,256,128]{2,1,0:T(8,128)(2,1)S(1)}, bf16[4,256,128]{2,1,0:T(8,128)(2,1)S(1)}, u32[]{:S(2)}, u32[]{:S(2)}) collective-permute-start(bf16[4,256,128]{2,1,0:T(8,128)(2,1)S(1)} %get-tuple-element.41), channel_id=1, source_target_pairs={{0,4},{1,5},{2,6},{3,7},{4,0},{5,1},{6,2},{7,3},{8,12},{9,13},{10,... | collective-permute-start | bytes 786440 | tf_op jit(solution)/shard_map/ppermute | solution.py:339
  12.8 6.0 %collective-permute-start.5 = (bf16[1,256,128]{2,1,0:T(8,128)(2,1)S(1)}, bf16[1,256,128]{2,1,0:T(8,128)(2,1)S(1)}, u32[]{:S(2)}, u32[]{:S(2)}) collective-permute-start(bf16[1,256,128]{2,1,0:T(8,128)(2,1)S(1)} %get-tuple-element.38.spill_out), channel_id=1, source_target_pairs={{0,4},{1,5},{2,6},{3,7},{4,12},{5,13},{6,14},{7,15},{8,0},{9,1},{1... | collective-permute-start | bytes 196616 | tf_op jit(solution)/shard_map/ppermute | solution.py:339
  19.5 4.4 %collective-permute-start.7 = (bf16[1,256,128]{2,1,0:T(8,128)(2,1)S(1)}, bf16[1,256,128]{2,1,0:T(8,128)(2,1)S(1)}, u32[]{:S(2)}, u32[]{:S(2)}) collective-permute-start(bf16[1,256,128]{2,1,0:T(8,128)(2,1)S(1)} %get-tuple-element.44), channel_id=1, source_target_pairs={{0,1},{1,0},{2,3},{3,2},{4,8},{5,9},{6,10},{7,11},{8,4},{9,5},{10,... | collective-permute-start | bytes 196616 | tf_op jit(solution)/shard_map/ppermute | solution.py:339
  20.7 3.1 %collective-permute-start.6 = (bf16[1,256,128]{2,1,0:T(8,128)(2,1)S(1)}, bf16[1,256,128]{2,1,0:T(8,128)(2,1)S(1)}, u32[]{:S(2)}, u32[]{:S(2)}) collective-permute-start(bf16[1,256,128]{2,1,0:T(8,128)(2,1)S(1)} %shard_map.73), channel_id=1, source_target_pairs={{0,4},{1,5},{2,6},{3,7},{4,0},{5,1},{6,2},{7,3},{8,12},{9,13},{10,... | collective-permute-start | bytes 196616 | tf_op jit(solution)/shard_map/ppermute | solution.py:339
  24.2 1.5 %collective-permute-start.8 = (bf16[1,256,128]{2,1,0:T(8,128)(2,1)S(1)}, bf16[1,256,128]{2,1,0:T(8,128)(2,1)S(1)}, u32[]{:S(2)}, u32[]{:S(2)}) collective-permute-start(bf16[1,256,128]{2,1,0:T(8,128)(2,1)S(1)} %get-tuple-element.47), channel_id=1, source_target_pairs={{0,4},{1,5},{2,6},{3,7},{4,0},{5,1},{6,2},{7,3},{8,12},{9,13},{10,... | collective-permute-start | bytes 196616 | tf_op jit(solution)/shard_map/ppermute | solution.py:339
  25.8 7.9 %collective-permute-start.9 = (bf16[5,256,128]{2,1,0:T(8,128)(2,1)S(1)}, bf16[5,256,128]{2,1,0:T(8,128)(2,1)S(1)}, u32[]{:S(2)}, u32[]{:S(2)}) collective-permute-start(bf16[5,256,128]{2,1,0:T(8,128)(2,1)S(1)} %get-tuple-element.50), channel_id=1, source_target_pairs={{0,1},{1,0},{2,3},{3,2},{4,8},{5,9},{6,10},{7,11},{8,4},{9,5},{10,... | collective-permute-start | bytes 983048 | tf_op jit(solution)/shard_map/ppermute | solution.py:339
  27.0 6.7 %collective-permute-start.10 = (bf16[4,256,128]{2,1,0:T(8,128)(2,1)S(1)}, bf16[4,256,128]{2,1,0:T(8,128)(2,1)S(1)}, u32[]{:S(2)}, u32[]{:S(2)}) collective-permute-start(bf16[4,256,128]{2,1,0:T(8,128)(2,1)S(1)} %get-tuple-element.51), channel_id=1, source_target_pairs={{0,4},{1,5},{2,6},{3,7},{4,0},{5,1},{6,2},{7,3},{8,12},{9,13},{10,... | collective-permute-start | bytes 786440 | tf_op jit(solution)/shard_map/ppermute | solution.py:339
  28.1 5.6 %collective-permute-start.11 = (bf16[1,256,128]{2,1,0:T(8,128)(2,1)S(1)}, bf16[1,256,128]{2,1,0:T(8,128)(2,1)S(1)}, u32[]{:S(2)}, u32[]{:S(2)}) collective-permute-start(bf16[1,256,128]{2,1,0:T(8,128)(2,1)S(1)} %get-tuple-element.48.spill_out), channel_id=1, source_target_pairs={{0,4},{1,5},{2,6},{3,7},{4,12},{5,13},{6,14},{7,15},{8,0},{9,1},{1... | collective-permute-start | bytes 196616 | tf_op jit(solution)/shard_map/ppermute | solution.py:339
  34.4 1.3 %collective-permute-start.12 = (f32[6,128]{1,0:T(8,128)S(1)}, f32[6,128]{1,0:T(8,128)S(1)}, u32[]{:S(2)}, u32[]{:S(2)}) collective-permute-start(f32[6,128]{1,0:T(8,128)S(1)} %pad_maximum_fusion), channel_id=1, source_target_pairs={{0,4},{1,5},{2,6},{3,7},{4,0},{5,1},{6,2},{7,3},{8,12},{9,13},{10,... | collective-permute-start | bytes 9224 | tf_op jit(solution)/shard_map/ppermute | solution.py:339

commit v11 on v10

--- a/solution.py
+++ b/solution.py
@@ -290,8 +290,8 @@
     picked(win_ref, w, opened(spill_in[0])[1])
 
 
-def finish_kernel(gathered, p0, q, out_ref, out, sems):
-    total = jnp.sum(gathered[...], axis=0)
+def finish_kernel(table, gathered, other, p0, q, out_ref, out, sems):
+    total = jnp.where(table[EVEN] == 1, jnp.sum(other[...], axis=0), jnp.sum(gathered[...], axis=0))
     s00, s01, s11, s02, s12, s22 = (total[i : i + 1, :] for i in range(6))
     c = SHIFT
     bb = s00 + EPS
@@ -356,6 +356,23 @@
         return i + (2 if i % 2 else -2), j
 
     return permuted(x, target)
+
+
+def sum_groups(parts):
+    odd = [[i * parts + j for i in range(1, NSUB, 2)] for j in range(parts)]
+    near = NSUB // 2 // parts
+    rows = 4
+    width = near // rows
+    even = [
+        [
+            (2 * (row * (NSUB // 2 // rows) + block * width + k)) * parts + j
+            for j in range(parts)
+            for row in range(rows)
+            for k in range(width)
+        ]
+        for block in range(parts)
+    ]
+    return odd + even
 
 
 def body(right_side, coupling, neighbours, inverse, margin, counts):
@@ -447,15 +464,16 @@
     sums = jnp.concatenate([sums_one[:3], sums_two[:3]], axis=0)
     sums = sums + to_inner(sums)
     gathered = lax.all_to_all(
-        jnp.broadcast_to(sums[None], (NSUB // 2, 6, R)), "sub", 0, 0,
-        axis_index_groups=[list(range(c, NSUB, 2)) for c in range(2)],
-    )
+        jnp.broadcast_to(sums[None], (NSUB // 2, 6, R)), ("sub", "rhs"), 0, 0,
+        axis_index_groups=sum_groups(lax.axis_size("rhs")),
+    )
+    other = to_inner(gathered)
     (flat,) = call(
         finish_kernel,
         [((W * NS, R), F32, pltpu.HBM)],
-        [VM] * 3,
+        [SM] + [VM] * 4,
         [pltpu.VMEM((W * NS, R), F32), pltpu.SemaphoreType.DMA((len(PARTS),))],
-    )(gathered, p0, q)
+    )(table, gathered, other, p0, q)
     return flat.reshape(W, NS, R).transpose(1, 0, 2)
 
 

time: 61.9 us -> 63.4 us (1.024)
  the two profiles are of different devices: /device:TPU:2 before, /device:TPU:1 now
where the time goes in v11:
time: 63.4 us; the launch traced here: 63.1 us
  blocking collectives  22.3 us (35%)
  starting transfers between devices  18.2 us (29%)
  Pallas kernels  14.1 us (22%)
  waiting for transfers between devices  6.45 us (10%)
  local copies, waits for them, and re-layouts  1.05 us (2%)
  between operations  0.98 us (2%)
    all_to_all x1, blocking collectives, body(): lax.all_to_all(jnp.broadcast_to(sums[None], (NSUB // 2, 6, R)), ('sub', '...  22.3 us
    ppermute x14, starting transfers between devices, permuted(): lax.ppermute(x, ('sub', 'rhs'), [(i * parts + j, t[0] * parts + t[1]) for...  18.2 us
    pallas_call x2, Pallas kernels, matrices(): call(functools.partial(coupling_kernel, blocks, groups, first), outs, [AN...  7.25 us
    ppermute x14, waiting for transfers between devices, permuted(): lax.ppermute(x, ('sub', 'rhs'), [(i * parts + j, t[0] * parts + t[1]) for...  6.45 us
    pallas_call x2, Pallas kernels, solve(): call(own_kernel, [((6 * W, R), F32, pltpu.VMEM)], [VM, VM], [pltpu.VMEM((...  1.97 us
    pallas_call x2, Pallas kernels, solve(): call(solve_kernel, [(block, F32), (one, BF16)], [SM] + [VM] * 3, [pltpu.V...  1.82 us
    pallas_call x2, Pallas kernels, system(): call(functools.partial(system_kernel, first), outs + [((8, R), F32)], [SM...  1.31 us
  transfers between devices with their start and end apart: 14, of which 5 were waited for; matrix products, arithmetic and copies ran while one was open for 0% of the time, Pallas kernels for 18%

profile of v11, /device:TPU:1, one launch (start us, length us, event | category | flops | bytes accessed | tf_op | source)
XLA Modules:
  0.0 63.1 jit_solution(8969845795488457866)
XLA Ops:
  0.7 1.0 %copy-done = f32[4,252,128]{2,0,1:T(4,128)S(1)} copy-done((f32[4,252,128]{2,0,1:T(4,128)S(1)}, f32[4,252,128]{2,0,1:T(4,128)}, u32[]{:S(2)}) %copy-start) | copy-done | bytes 516120
  1.8 3.1 %collective-permute-start.1 = (bf16[4,256,128]{2,1,0:T(8,128)(2,1)S(1)}, bf16[4,256,128]{2,1,0:T(8,128)(2,1)S(1)}, u32[]{:S(2)}, u32[]{:S(2)}) collective-permute-start(bf16[4,256,128]{2,1,0:T(8,128)(2,1)S(1)} %get-tuple-element.34), channel_id=1, source_target_pairs={{0,1},{1,0},{2,3},{3,2},{4,8},{5,9},{6,10},{7,11},{8,4},{9,5},{10,... | collective-permute-start | bytes 786440 | tf_op jit(solution)/shard_map/ppermute | solution.py:339
  4.9 0.3 collective-permute-start
  5.2 4.0 %shard_map.64 = (bf16[16,256,256]{2,1,0:T(8,128)(2,1)S(1)}, bf16[1512,1512]{1,0:T(8,128)(2,1)S(1)}, s32[41]{0:T(128)S(4)}) custom-call(bf16[4,508032]{1,0:T(4,128)(2,1)} %flat.3, bf16[1,1512,1512]{2,1,0:T(8,128)(2,1)} %rest_0_.1, s32[1]{0:T(128)} %bitcast.rest_1_, s32[1]{0:T(128)S(6)} %copy.7.rest_2_.counts, s32[1,2]{1,0:T(1,128)} %rest_3_.1, s32[4,8]{1,0:T(4,128)} %rest_4_.1), custom_call_target="tpu_custom_call" | custom-call | flops 1048576 | bytes 12582912 | tf_op jit(solution)/shard_map/pallas_call | solution.py:400
  9.2 1.0 %shard_map.66.part = f32[1512,128]{1,0:T(8,128)S(1)} custom-call(bf16[1512,1512]{1,0:T(8,128)(2,1)S(1)} %get-tuple-element.32.inverse, f32[4,256,128]{2,1,0:T(8,128)S(1)} %get-tuple-element.33.own.v0), custom_call_target="tpu_custom_call" | custom-call | flops 1073741824 | bytes 4194304 | tf_op jit(solution)/shard_map/pallas_call | solution.py:421
  10.2 0.3 shard_map.67
  10.5 1.4 %collective-permute-start.2 = (bf16[1,256,128]{2,1,0:T(8,128)(2,1)S(1)}, bf16[1,256,128]{2,1,0:T(8,128)(2,1)S(1)}, u32[]{:S(2)}, u32[]{:S(2)}) collective-permute-start(bf16[1,256,128]{2,1,0:T(8,128)(2,1)S(1)} %get-tuple-element.37), channel_id=1, source_target_pairs={{0,4},{1,5},{2,6},{3,7},{4,0},{5,1},{6,2},{7,3},{8,12},{9,13},{10,... | collective-permute-start | bytes 196616 | tf_op jit(solution)/shard_map/ppermute | solution.py:339
  11.9 0.9 %shard_map.68 = (f32[4,256,128]{2,1,0:T(8,128)S(1)}, bf16[1,256,128]{2,1,0:T(8,128)(2,1)S(1)}) custom-call(s32[41]{0:T(128)S(4)} %get-tuple-element.30.table, bf16[1512,1512]{1,0:T(8,128)(2,1)S(1)} %get-tuple-element.32.inverse, f32[1512,128]{1,0:T(8,128)S(1)} %shard_map.66.part, bf16[616,128]{1,0:T(8,128)(2,1)S(1)} %get-tuple-element.35.ext), custom_call_target="tpu_custom_call" | custom-call | flops 1073741824 | bytes 4194304 | tf_op jit(solution)/shard_map/pallas_call | solution.py:433
  12.8 0.1 shard_map.69
  12.9 0.9 %collective-permute-start.3 = (bf16[5,256,128]{2,1,0:T(8,128)(2,1)S(1)}, bf16[5,256,128]{2,1,0:T(8,128)(2,1)S(1)}, u32[]{:S(2)}, u32[]{:S(2)}) collective-permute-start(bf16[5,256,128]{2,1,0:T(8,128)(2,1)S(1)} %get-tuple-element.39.rest_0_), channel_id=1, source_target_pairs={{0,1},{1,0},{2,3},{3,2},{4,8},{5,9},{6,10},{7,11},{8,4},{9,5},{10,... | collective-permute-start | bytes 983048 | tf_op jit(solution)/shard_map/ppermute | solution.py:339
  13.8 0.3 collective-permute-start.4
  14.1 1.3 %collective-permute-start.5 = (bf16[1,256,128]{2,1,0:T(8,128)(2,1)S(1)}, bf16[1,256,128]{2,1,0:T(8,128)(2,1)S(1)}, u32[]{:S(2)}, u32[]{:S(2)}) collective-permute-start(bf16[1,256,128]{2,1,0:T(8,128)(2,1)S(1)} %get-tuple-element.38.spill_out), channel_id=1, source_target_pairs={{0,4},{1,5},{2,6},{3,7},{4,12},{5,13},{6,14},{7,15},{8,0},{9,1},{1... | collective-permute-start | bytes 196616 | tf_op jit(solution)/shard_map/ppermute | solution.py:339
  15.4 3.3 %shard_map.70.cb = bf16[16,256,256]{2,1,0:T(8,128)(2,1)S(1)} custom-call(bf16[4,508032]{1,0:T(4,128)(2,1)} %flat.3, bf16[5,256,128]{2,1,0:T(8,128)(2,1)S(1)} %get-tuple-element.39.rest_0_), custom_call_target="tpu_custom_call" | custom-call | flops 1048576 | bytes 12582912 | tf_op jit(solution)/shard_map/pallas_call | solution.py:400
  18.7 1.1 %collective-permute-done.3.got = bf16[5,256,128]{2,1,0:T(8,128)(2,1)S(1)} collective-permute-done((bf16[5,256,128]{2,1,0:T(8,128)(2,1)S(1)}, bf16[5,256,128]{2,1,0:T(8,128)(2,1)S(1)}, u32[]{:S(2)}, u32[]{:S(2)}) %collective-permute-start.3) | collective-permute-done | bytes 327712 | tf_op jit(solution)/shard_map/ppermute | solution.py:339
  19.8 0.7 %shard_map.71 = (f32[4,256,128]{2,1,0:T(8,128)S(1)}, f32[4,256,128]{2,1,0:T(8,128)S(1)}, bf16[1,256,128]{2,1,0:T(8,128)(2,1)S(1)}, f32[8,128]{1,0:T(8,128)S(1)}) custom-call(s32[41]{0:T(128)S(4)} %get-tuple-element.30.table, bf16[16,256,256]{2,1,0:T(8,128)(2,1)S(1)} %get-tuple-element.31.ca, bf16[16,256,256]{2,1,0:T(8,128)(2,1)S(1)} %shard_map.70.cb, ...), custom_call_target="tpu_custom_call" | custom-call | tf_op jit(solution)/shard_map/pallas_call | solution.py:451
  20.5 1.7 %collective-permute-start.7 = (bf16[1,256,128]{2,1,0:T(8,128)(2,1)S(1)}, bf16[1,256,128]{2,1,0:T(8,128)(2,1)S(1)}, u32[]{:S(2)}, u32[]{:S(2)}) collective-permute-start(bf16[1,256,128]{2,1,0:T(8,128)(2,1)S(1)} %get-tuple-element.44), channel_id=1, source_target_pairs={{0,1},{1,0},{2,3},{3,2},{4,8},{5,9},{6,10},{7,11},{8,4},{9,5},{10,... | collective-permute-start | bytes 196616 | tf_op jit(solution)/shard_map/ppermute | solution.py:339
  22.3 0.5 collective-permute-start.6
  22.7 1.0 %shard_map.72.part = f32[1512,128]{1,0:T(8,128)S(1)} custom-call(bf16[1512,1512]{1,0:T(8,128)(2,1)S(1)} %get-tuple-element.32.inverse, f32[4,256,128]{2,1,0:T(8,128)S(1)} %get-tuple-element.43.own.w.rest_0_), custom_call_target="tpu_custom_call" | custom-call | flops 1073741824 | bytes 4194304 | tf_op jit(solution)/shard_map/pallas_call | solution.py:421
  23.7 0.5 collective-permute-done.7.outer
  24.3 0.3 shard_map.74
  24.6 2.0 %collective-permute-start.8 = (bf16[1,256,128]{2,1,0:T(8,128)(2,1)S(1)}, bf16[1,256,128]{2,1,0:T(8,128)(2,1)S(1)}, u32[]{:S(2)}, u32[]{:S(2)}) collective-permute-start(bf16[1,256,128]{2,1,0:T(8,128)(2,1)S(1)} %get-tuple-element.47), channel_id=1, source_target_pairs={{0,4},{1,5},{2,6},{3,7},{4,0},{5,1},{6,2},{7,3},{8,12},{9,13},{10,... | collective-permute-start | bytes 196616 | tf_op jit(solution)/shard_map/ppermute | solution.py:339
  26.6 0.9 %shard_map.75 = (f32[4,256,128]{2,1,0:T(8,128)S(1)}, bf16[1,256,128]{2,1,0:T(8,128)(2,1)S(1)}) custom-call(s32[41]{0:T(128)S(4)} %get-tuple-element.30.table, bf16[1512,1512]{1,0:T(8,128)(2,1)S(1)} %get-tuple-element.32.inverse, f32[1512,128]{1,0:T(8,128)S(1)} %shard_map.72.part, bf16[616,128]{1,0:T(8,128)(2,1)S(1)} %get-tuple-element.45.ext), custom_call_target="tpu_custom_call" | custom-call | flops 1073741824 | bytes 4194304 | tf_op jit(solution)/shard_map/pallas_call | solution.py:433
  27.6 2.8 %collective-permute-start.9 = (bf16[5,256,128]{2,1,0:T(8,128)(2,1)S(1)}, bf16[5,256,128]{2,1,0:T(8,128)(2,1)S(1)}, u32[]{:S(2)}, u32[]{:S(2)}) collective-permute-start(bf16[5,256,128]{2,1,0:T(8,128)(2,1)S(1)} %get-tuple-element.50), channel_id=1, source_target_pairs={{0,1},{1,0},{2,3},{3,2},{4,8},{5,9},{6,10},{7,11},{8,4},{9,5},{10,... | collective-permute-start | bytes 983048 | tf_op jit(solution)/shard_map/ppermute | solution.py:339
  30.4 1.7 %collective-permute-start.11 = (bf16[1,256,128]{2,1,0:T(8,128)(2,1)S(1)}, bf16[1,256,128]{2,1,0:T(8,128)(2,1)S(1)}, u32[]{:S(2)}, u32[]{:S(2)}) collective-permute-start(bf16[1,256,128]{2,1,0:T(8,128)(2,1)S(1)} %get-tuple-element.48.spill_out), channel_id=1, source_target_pairs={{0,4},{1,5},{2,6},{3,7},{4,12},{5,13},{6,14},{7,15},{8,0},{9,1},{1... | collective-permute-start | bytes 196616 | tf_op jit(solution)/shard_map/ppermute | solution.py:339
  32.1 3.0 %collective-permute-done.11.far = bf16[1,256,128]{2,1,0:T(8,128)(2,1)S(1)} collective-permute-done((bf16[1,256,128]{2,1,0:T(8,128)(2,1)S(1)}, bf16[1,256,128]{2,1,0:T(8,128)(2,1)S(1)}, u32[]{:S(2)}, u32[]{:S(2)}) %collective-permute-start.11) | collective-permute-done | bytes 65568 | tf_op jit(solution)/shard_map/ppermute | solution.py:339
  35.2 0.6 shard_map.77
  35.8 1.5 %collective-permute-start.12 = (f32[6,128]{1,0:T(8,128)S(1)}, f32[6,128]{1,0:T(8,128)S(1)}, u32[]{:S(2)}, u32[]{:S(2)}) collective-permute-start(f32[6,128]{1,0:T(8,128)S(1)} %pad_maximum_fusion), channel_id=1, source_target_pairs={{0,4},{1,5},{2,6},{3,7},{4,0},{5,1},{6,2},{7,3},{8,12},{9,13},{10,... | collective-permute-start | bytes 9224 | tf_op jit(solution)/shard_map/ppermute | solution.py:339
  37.3 0.8 %collective-permute-done.12 = f32[6,128]{1,0:T(8,128)S(1)} collective-permute-done((f32[6,128]{1,0:T(8,128)S(1)}, f32[6,128]{1,0:T(8,128)S(1)}, u32[]{:S(2)}, u32[]{:S(2)}) %collective-permute-start.12) | collective-permute-done | bytes 3104 | tf_op jit(solution)/shard_map/ppermute | solution.py:339
  38.1 22.3 %all_to_all.5.gathered = f32[32,6,128]{2,1,0:T(8,128)S(1)} all-to-all(f32[32,6,128]{2,1,0:T(8,128)S(1)} %broadcast_in_dim.2), channel_id=1, replica_groups={{4,12,20,28,36,44,52,60,68,76,84,92,100,108,116,124,132,140,148,156,164..., dimensions={0} | all-to-all | bytes 196608 | tf_op jit(solution)/shard_map/all_to_all | solution.py:466
  60.4 0.6 collective-permute-start.13
  61.0 1.0 %collective-permute-done.13.other = f32[32,6,128]{2,1,0:T(8,128)S(1)} collective-permute-done((f32[32,6,128]{2,1,0:T(8,128)S(1)}, f32[32,6,128]{2,1,0:T(8,128)S(1)}, u32[]{:S(2)}, u32[]{:S(2)}) %collective-permute-start.13) | collective-permute-done | bytes 98336 | tf_op jit(solution)/shard_map/ppermute | solution.py:339
  62.0 0.9 %shard_map.78 = f32[1008,128]{1,0:T(8,128)} custom-call(s32[41]{0:T(128)S(4)} %get-tuple-element.30.table, f32[32,6,128]{2,1,0:T(8,128)S(1)} %all_to_all.5.gathered, f32[32,6,128]{2,1,0:T(8,128)S(1)} %collective-permute-done.13.other, f32[4,256,128]{2,1,0:T(8,128)S(1)} %get-tuple-element.53.p0, f32[4,256,128]{2,1,0:T(8,128)S(1)} %get-tuple-element.54.q), custom_call_target="tpu_custom_call" | custom-call | tf_op jit(solution)/shard_map/pallas_call | solution.py:471
  (19 shorter events, 0.3 us)
Async XLA Ops:
  0.7 1.0 %copy-start = (f32[4,252,128]{2,0,1:T(4,128)S(1)}, f32[4,252,128]{2,0,1:T(4,128)}, u32[]{:S(2)}) copy-start(f32[4,252,128]{2,0,1:T(4,128)} %param.6) | copy-start | bytes 1548292
  1.8 8.4 %collective-permute-start.1 = (bf16[4,256,128]{2,1,0:T(8,128)(2,1)S(1)}, bf16[4,256,128]{2,1,0:T(8,128)(2,1)S(1)}, u32[]{:S(2)}, u32[]{:S(2)}) collective-permute-start(bf16[4,256,128]{2,1,0:T(8,128)(2,1)S(1)} %get-tuple-element.34), channel_id=1, source_target_pairs={{0,1},{1,0},{2,3},{3,2},{4,8},{5,9},{6,10},{7,11},{8,4},{9,5},{10,... | collective-permute-start | bytes 786440 | tf_op jit(solution)/shard_map/ppermute | solution.py:339
  4.9 5.3 %collective-permute-start = (bf16[4,256,128]{2,1,0:T(8,128)(2,1)S(1)}, bf16[4,256,128]{2,1,0:T(8,128)(2,1)S(1)}, u32[]{:S(2)}, u32[]{:S(2)}) collective-permute-start(bf16[4,256,128]{2,1,0:T(8,128)(2,1)S(1)} %get-tuple-element.34), channel_id=1, source_target_pairs={{0,4},{1,5},{2,6},{3,7},{4,0},{5,1},{6,2},{7,3},{8,12},{9,13},{10,... | collective-permute-start | bytes 786440 | tf_op jit(solution)/shard_map/ppermute | solution.py:339
  10.5 2.3 %collective-permute-start.2 = (bf16[1,256,128]{2,1,0:T(8,128)(2,1)S(1)}, bf16[1,256,128]{2,1,0:T(8,128)(2,1)S(1)}, u32[]{:S(2)}, u32[]{:S(2)}) collective-permute-start(bf16[1,256,128]{2,1,0:T(8,128)(2,1)S(1)} %get-tuple-element.37), channel_id=1, source_target_pairs={{0,4},{1,5},{2,6},{3,7},{4,0},{5,1},{6,2},{7,3},{8,12},{9,13},{10,... | collective-permute-start | bytes 196616 | tf_op jit(solution)/shard_map/ppermute | solution.py:339
  12.9 6.9 %collective-permute-start.3 = (bf16[5,256,128]{2,1,0:T(8,128)(2,1)S(1)}, bf16[5,256,128]{2,1,0:T(8,128)(2,1)S(1)}, u32[]{:S(2)}, u32[]{:S(2)}) collective-permute-start(bf16[5,256,128]{2,1,0:T(8,128)(2,1)S(1)} %get-tuple-element.39.rest_0_), channel_id=1, source_target_pairs={{0,1},{1,0},{2,3},{3,2},{4,8},{5,9},{6,10},{7,11},{8,4},{9,5},{10,... | collective-permute-start | bytes 983048 | tf_op jit(solution)/shard_map/ppermute | solution.py:339
  13.8 4.9 %collective-permute-start.4 = (bf16[4,256,128]{2,1,0:T(8,128)(2,1)S(1)}, bf16[4,256,128]{2,1,0:T(8,128)(2,1)S(1)}, u32[]{:S(2)}, u32[]{:S(2)}) collective-permute-start(bf16[4,256,128]{2,1,0:T(8,128)(2,1)S(1)} %get-tuple-element.41), channel_id=1, source_target_pairs={{0,4},{1,5},{2,6},{3,7},{4,0},{5,1},{6,2},{7,3},{8,12},{9,13},{10,... | collective-permute-start | bytes 786440 | tf_op jit(solution)/shard_map/ppermute | solution.py:339
  14.1 4.6 %collective-permute-start.5 = (bf16[1,256,128]{2,1,0:T(8,128)(2,1)S(1)}, bf16[1,256,128]{2,1,0:T(8,128)(2,1)S(1)}, u32[]{:S(2)}, u32[]{:S(2)}) collective-permute-start(bf16[1,256,128]{2,1,0:T(8,128)(2,1)S(1)} %get-tuple-element.38.spill_out), channel_id=1, source_target_pairs={{0,4},{1,5},{2,6},{3,7},{4,12},{5,13},{6,14},{7,15},{8,0},{9,1},{1... | collective-permute-start | bytes 196616 | tf_op jit(solution)/shard_map/ppermute | solution.py:339
  20.5 3.8 %collective-permute-start.7 = (bf16[1,256,128]{2,1,0:T(8,128)(2,1)S(1)}, bf16[1,256,128]{2,1,0:T(8,128)(2,1)S(1)}, u32[]{:S(2)}, u32[]{:S(2)}) collective-permute-start(bf16[1,256,128]{2,1,0:T(8,128)(2,1)S(1)} %get-tuple-element.44), channel_id=1, source_target_pairs={{0,1},{1,0},{2,3},{3,2},{4,8},{5,9},{6,10},{7,11},{8,4},{9,5},{10,... | collective-permute-start | bytes 196616 | tf_op jit(solution)/shard_map/ppermute | solution.py:339
  22.3 2.0 %collective-permute-start.6 = (bf16[1,256,128]{2,1,0:T(8,128)(2,1)S(1)}, bf16[1,256,128]{2,1,0:T(8,128)(2,1)S(1)}, u32[]{:S(2)}, u32[]{:S(2)}) collective-permute-start(bf16[1,256,128]{2,1,0:T(8,128)(2,1)S(1)} %shard_map.73), channel_id=1, source_target_pairs={{0,4},{1,5},{2,6},{3,7},{4,0},{5,1},{6,2},{7,3},{8,12},{9,13},{10,... | collective-permute-start | bytes 196616 | tf_op jit(solution)/shard_map/ppermute | solution.py:339
  24.6 2.9 %collective-permute-start.8 = (bf16[1,256,128]{2,1,0:T(8,128)(2,1)S(1)}, bf16[1,256,128]{2,1,0:T(8,128)(2,1)S(1)}, u32[]{:S(2)}, u32[]{:S(2)}) collective-permute-start(bf16[1,256,128]{2,1,0:T(8,128)(2,1)S(1)} %get-tuple-element.47), channel_id=1, source_target_pairs={{0,4},{1,5},{2,6},{3,7},{4,0},{5,1},{6,2},{7,3},{8,12},{9,13},{10,... | collective-permute-start | bytes 196616 | tf_op jit(solution)/shard_map/ppermute | solution.py:339
  27.6 7.6 %collective-permute-start.9 = (bf16[5,256,128]{2,1,0:T(8,128)(2,1)S(1)}, bf16[5,256,128]{2,1,0:T(8,128)(2,1)S(1)}, u32[]{:S(2)}, u32[]{:S(2)}) collective-permute-start(bf16[5,256,128]{2,1,0:T(8,128)(2,1)S(1)} %get-tuple-element.50), channel_id=1, source_target_pairs={{0,1},{1,0},{2,3},{3,2},{4,8},{5,9},{6,10},{7,11},{8,4},{9,5},{10,... | collective-permute-start | bytes 983048 | tf_op jit(solution)/shard_map/ppermute | solution.py:339
  30.4 4.7 %collective-permute-start.10 = (bf16[4,256,128]{2,1,0:T(8,128)(2,1)S(1)}, bf16[4,256,128]{2,1,0:T(8,128)(2,1)S(1)}, u32[]{:S(2)}, u32[]{:S(2)}) collective-permute-start(bf16[4,256,128]{2,1,0:T(8,128)(2,1)S(1)} %get-tuple-element.51), channel_id=1, source_target_pairs={{0,4},{1,5},{2,6},{3,7},{4,0},{5,1},{6,2},{7,3},{8,12},{9,13},{10,... | collective-permute-start | bytes 786440 | tf_op jit(solution)/shard_map/ppermute | solution.py:339
  30.4 4.7 %collective-permute-start.11 = (bf16[1,256,128]{2,1,0:T(8,128)(2,1)S(1)}, bf16[1,256,128]{2,1,0:T(8,128)(2,1)S(1)}, u32[]{:S(2)}, u32[]{:S(2)}) collective-permute-start(bf16[1,256,128]{2,1,0:T(8,128)(2,1)S(1)} %get-tuple-element.48.spill_out), channel_id=1, source_target_pairs={{0,4},{1,5},{2,6},{3,7},{4,12},{5,13},{6,14},{7,15},{8,0},{9,1},{1... | collective-permute-start | bytes 196616 | tf_op jit(solution)/shard_map/ppermute | solution.py:339
  35.8 2.3 %collective-permute-start.12 = (f32[6,128]{1,0:T(8,128)S(1)}, f32[6,128]{1,0:T(8,128)S(1)}, u32[]{:S(2)}, u32[]{:S(2)}) collective-permute-start(f32[6,128]{1,0:T(8,128)S(1)} %pad_maximum_fusion), channel_id=1, source_target_pairs={{0,4},{1,5},{2,6},{3,7},{4,0},{5,1},{6,2},{7,3},{8,12},{9,13},{10,... | collective-permute-start | bytes 9224 | tf_op jit(solution)/shard_map/ppermute | solution.py:339
  60.4 1.6 %collective-permute-start.13 = (f32[32,6,128]{2,1,0:T(8,128)S(1)}, f32[32,6,128]{2,1,0:T(8,128)S(1)}, u32[]{:S(2)}, u32[]{:S(2)}) collective-permute-start(f32[32,6,128]{2,1,0:T(8,128)S(1)} %all_to_all.5.gathered), channel_id=1, source_target_pairs={{0,4},{1,5},{2,6},{3,7},{4,0},{5,1},{6,2},{7,3},{8,12},{9,13},{10,... | collective-permute-start | bytes 294920 | tf_op jit(solution)/shard_map/ppermute | solution.py:339

commit v12 on v10

--- a/solution.py
+++ b/solution.py
@@ -22,6 +22,7 @@
 SPLIT = 4
 EVEN, FIRST, LAST, LOW, HIGH, COUNT, ENDS, NEXT, OUT, SLOTS = range(10)
 TABLE = SLOTS + NS * NB
+SPARE = 32
 OWN = 1024
 FROM = 896
 ANY = pl.BlockSpec(memory_space=pl.ANY)
@@ -43,10 +44,13 @@
 
 
 def start_kernel(counts, right, v0_ref, v0b_ref):
+    whole = W // 8 * 8
+    tail = right[whole * NS :, :]
     for s in range(NS):
         alive = jnp.where(counts[0] > s, 1.0, 0.0)
-        v0_ref[s, :W, :] = right[pl.ds(s, W, stride=NS), :] * alive
-        v0_ref[s, W:, :] = jnp.zeros((WP - W, R), F32)
+        v0_ref[s, :whole, :] = right[pl.ds(s, whole, stride=NS), :] * alive
+        last = [tail[NS * i + s : NS * i + s + 1, :] * alive for i in range(W - whole)]
+        v0_ref[s, whole:, :] = jnp.concatenate(last + [jnp.zeros((WP - W, R), F32)], axis=0)
         v0b_ref[s] = v0_ref[s].astype(BF16)
 
 
@@ -147,7 +151,7 @@
     for s in range(NS):
         ext[s * W : (s + 1) * W, :] = own[s, :W, :]
     ext[NS * W :, :] = jnp.zeros((OWN - NS * W, R), F32)
-    part_ref[...] = jnp.dot(inverse[:, :OWN], ext[...].astype(BF16), preferred_element_type=F32)
+    part_ref[: 6 * W, :] = jnp.dot(inverse[:, :OWN], ext[...].astype(BF16), preferred_element_type=F32)
 
 
 def places(table):
@@ -181,7 +185,7 @@
     put(last, NS + 1, own, high)
     put(jnp.logical_and(odd, jnp.logical_not(last)), NS + 1, outer, high if some else 0)
     put(even, NS + 1, inner, high if some else 0)
-    ext_ref[...] = ext[...].astype(BF16)
+    ext_ref[...] = ext[: 6 * W - FROM, :].astype(BF16)
 
     @pl.when(even)
     def _():
@@ -195,7 +199,7 @@
 def solve_kernel(table, inverse, part, ext, out_ref, out2_ref, res):
     even, first, last, low, high = places(table)
     mine = NS * W
-    res[...] = part[:mine, :] + jnp.dot(inverse[:mine, FROM:], ext[...], preferred_element_type=F32)
+    res[:mine, :] = part[:mine, :] + jnp.dot(inverse[:mine, FROM:], ext[...], preferred_element_type=F32)
     pad = jnp.zeros((WP - W, R), F32)
     for s in range(NS):
         out_ref[s] = jnp.concatenate([res[s * W : (s + 1) * W, :], pad], axis=0)
@@ -387,8 +391,8 @@
             [
                 pltpu.VMEM((NS, count * lanes), BF16),
                 pltpu.VMEM((4 * NS, lanes), BF16),
-                pltpu.VMEM((count * GROUP * NS, 128), F32),
-                pltpu.VMEM((count * GROUP * NS, 128), F32),
+                pltpu.VMEM((count * GROUP * NS + SPARE, 128), F32),
+                pltpu.VMEM((count * GROUP * NS + SPARE, 128), F32),
                 pltpu.SemaphoreType.DMA((count // CHUNK + 1,)),
             ],
             limit=24,
@@ -402,7 +406,7 @@
 
     def solve(own, inner, outer):
         (part,) = call(
-            own_kernel, [((6 * W, R), F32, pltpu.VMEM)], [VM, VM], [pltpu.VMEM((OWN, R), F32)],
+            own_kernel, [((6 * W + 8, R), F32, pltpu.VMEM)], [VM, VM], [pltpu.VMEM((OWN, R), F32)],
             cost=pl.CostEstimate(flops=1 << 30, bytes_accessed=4 << 20, transcendentals=0),
         )(held, own)
         depth = 6 * W - FROM
@@ -410,14 +414,14 @@
             margin_kernel,
             [(one, BF16), ((depth, R), BF16)],
             [SM] + [VM] * 5,
-            [pltpu.VMEM((depth, R), F32)],
+            [pltpu.VMEM((depth + 8, R), F32)],
         )(table, held, part, own, inner, outer)
         got_in = to_inner(spill_in)
         out, spill_out = call(
             solve_kernel,
             [(block, F32), (one, BF16)],
             [SM] + [VM] * 3,
-            [pltpu.VMEM((NS * W, R), F32)],
+            [pltpu.VMEM((NS * W + 8, R), F32)],
             cost=pl.CostEstimate(flops=1 << 30, bytes_accessed=4 << 20, transcendentals=0),
         )(table, held, part, ext)
         return out, got_in, spill_out
@@ -454,7 +458,7 @@
         finish_kernel,
         [((W * NS, R), F32, pltpu.HBM)],
         [VM] * 3,
-        [pltpu.VMEM((W * NS, R), F32), pltpu.SemaphoreType.DMA((len(PARTS),))],
+        [pltpu.VMEM((W * NS + SPARE, R), F32), pltpu.SemaphoreType.DMA((len(PARTS),))],
     )(gathered, p0, q)
     return flat.reshape(W, NS, R).transpose(1, 0, 2)
 

time: 61.9 us -> 62.3 us (level)
  no operation moved by 1% of the time
where the time goes in v12:
time: 62.3 us; the launch traced here: 62.1 us
  blocking collectives  25.4 us (41%)
  Pallas kernels  14.1 us (23%)
  waiting for transfers between devices  11.4 us (18%)
  starting transfers between devices  9.17 us (15%)
  local copies, waits for them, and re-layouts  1.05 us (2%)
  between operations  0.97 us (2%)
    all_to_all x1, blocking collectives, body(): lax.all_to_all(jnp.broadcast_to(sums[None], (NSUB // 2, 6, R)), 'sub', 0,...  25.4 us
    ppermute x13, waiting for transfers between devices, permuted(): lax.ppermute(x, ('sub', 'rhs'), [(i * parts + j, t[0] * parts + t[1]) for...  11.4 us
    ppermute x13, starting transfers between devices, permuted(): lax.ppermute(x, ('sub', 'rhs'), [(i * parts + j, t[0] * parts + t[1]) for...  9.17 us
    pallas_call x2, Pallas kernels, matrices(): call(functools.partial(coupling_kernel, blocks, groups, first), outs, [AN...  7.25 us
    pallas_call x2, Pallas kernels, solve(): call(own_kernel, [((6 * W + 8, R), F32, pltpu.VMEM)], [VM, VM], [pltpu.VM...  1.97 us
    pallas_call x2, Pallas kernels, solve(): call(solve_kernel, [(block, F32), (one, BF16)], [SM] + [VM] * 3, [pltpu.V...  1.74 us
    pallas_call x2, Pallas kernels, system(): call(functools.partial(system_kernel, first), outs + [((8, R), F32)], [SM...  1.31 us
  transfers between devices with their start and end apart: 13, of which 5 were waited for; matrix products, arithmetic and copies ran while one was open for 0% of the time, Pallas kernels for 18%

profile of v12, /device:TPU:2, one launch (start us, length us, event | category | flops | bytes accessed | tf_op | source)
XLA Modules:
  0.0 62.1 jit_solution(9888377058152357871)
XLA Ops:
  0.7 1.0 %copy-done = f32[4,252,128]{2,0,1:T(4,128)S(1)} copy-done((f32[4,252,128]{2,0,1:T(4,128)S(1)}, f32[4,252,128]{2,0,1:T(4,128)}, u32[]{:S(2)}) %copy-start) | copy-done | bytes 516120
  1.7 0.1 shard_map.65
  1.8 2.4 %collective-permute-start.1 = (bf16[4,256,128]{2,1,0:T(8,128)(2,1)S(1)}, bf16[4,256,128]{2,1,0:T(8,128)(2,1)S(1)}, u32[]{:S(2)}, u32[]{:S(2)}) collective-permute-start(bf16[4,256,128]{2,1,0:T(8,128)(2,1)S(1)} %get-tuple-element.34), channel_id=1, source_target_pairs={{0,1},{1,0},{2,3},{3,2},{4,8},{5,9},{6,10},{7,11},{8,4},{9,5},{10,... | collective-permute-start | bytes 786440 | tf_op jit(solution)/shard_map/ppermute | solution.py:343
  4.1 4.0 %shard_map.64 = (bf16[16,256,256]{2,1,0:T(8,128)(2,1)S(1)}, bf16[1512,1512]{1,0:T(8,128)(2,1)S(1)}, s32[41]{0:T(128)S(4)}) custom-call(bf16[4,508032]{1,0:T(4,128)(2,1)} %flat.3, bf16[1,1512,1512]{2,1,0:T(8,128)(2,1)} %rest_0_.1, s32[1]{0:T(128)} %bitcast.rest_1_, s32[1]{0:T(128)S(6)} %copy.7.rest_2_.counts, s32[1,2]{1,0:T(1,128)} %rest_3_.1, s32[4,8]{1,0:T(4,128)} %rest_4_.1), custom_call_target="tpu_custom_call" | custom-call | flops 1048576 | bytes 12582912 | tf_op jit(solution)/shard_map/pallas_call | solution.py:387
  8.1 1.0 %shard_map.66.part = f32[1520,128]{1,0:T(8,128)S(1)} custom-call(bf16[1512,1512]{1,0:T(8,128)(2,1)S(1)} %get-tuple-element.32.inverse, f32[4,256,128]{2,1,0:T(8,128)S(1)} %get-tuple-element.33.own.v0), custom_call_target="tpu_custom_call" | custom-call | flops 1073741824 | bytes 4194304 | tf_op jit(solution)/shard_map/pallas_call | solution.py:408
  9.1 0.3 shard_map.67
  9.5 0.6 collective-permute-start.2
  10.0 0.9 %shard_map.68 = (f32[4,256,128]{2,1,0:T(8,128)S(1)}, bf16[1,256,128]{2,1,0:T(8,128)(2,1)S(1)}) custom-call(s32[41]{0:T(128)S(4)} %get-tuple-element.30.table, bf16[1512,1512]{1,0:T(8,128)(2,1)S(1)} %get-tuple-element.32.inverse, f32[1520,128]{1,0:T(8,128)S(1)} %shard_map.66.part, bf16[616,128]{1,0:T(8,128)(2,1)S(1)} %get-tuple-element.35.ext), custom_call_target="tpu_custom_call" | custom-call | flops 1073741824 | bytes 4194304 | tf_op jit(solution)/shard_map/pallas_call | solution.py:420
  10.9 0.1 shard_map.69
  11.0 1.3 %collective-permute-start.3 = (bf16[5,256,128]{2,1,0:T(8,128)(2,1)S(1)}, bf16[5,256,128]{2,1,0:T(8,128)(2,1)S(1)}, u32[]{:S(2)}, u32[]{:S(2)}) collective-permute-start(bf16[5,256,128]{2,1,0:T(8,128)(2,1)S(1)} %get-tuple-element.39.rest_0_), channel_id=1, source_target_pairs={{0,1},{1,0},{2,3},{3,2},{4,8},{5,9},{6,10},{7,11},{8,4},{9,5},{10,... | collective-permute-start | bytes 983048 | tf_op jit(solution)/shard_map/ppermute | solution.py:343
  12.3 0.4 collective-permute-start.4
  12.8 0.1 collective-permute-start.5
  12.9 3.3 %shard_map.70.cb = bf16[16,256,256]{2,1,0:T(8,128)(2,1)S(1)} custom-call(bf16[4,508032]{1,0:T(4,128)(2,1)} %flat.3, bf16[5,256,128]{2,1,0:T(8,128)(2,1)S(1)} %get-tuple-element.39.rest_0_), custom_call_target="tpu_custom_call" | custom-call | flops 1048576 | bytes 12582912 | tf_op jit(solution)/shard_map/pallas_call | solution.py:387
  16.1 2.7 %collective-permute-done.5.far = bf16[1,256,128]{2,1,0:T(8,128)(2,1)S(1)} collective-permute-done((bf16[1,256,128]{2,1,0:T(8,128)(2,1)S(1)}, bf16[1,256,128]{2,1,0:T(8,128)(2,1)S(1)}, u32[]{:S(2)}, u32[]{:S(2)}) %collective-permute-start.5) | collective-permute-done | bytes 65568 | tf_op jit(solution)/shard_map/ppermute | solution.py:343
  18.8 0.7 %shard_map.71 = (f32[4,256,128]{2,1,0:T(8,128)S(1)}, f32[4,256,128]{2,1,0:T(8,128)S(1)}, bf16[1,256,128]{2,1,0:T(8,128)(2,1)S(1)}, f32[8,128]{1,0:T(8,128)S(1)}) custom-call(s32[41]{0:T(128)S(4)} %get-tuple-element.30.table, bf16[16,256,256]{2,1,0:T(8,128)(2,1)S(1)} %get-tuple-element.31.ca, bf16[16,256,256]{2,1,0:T(8,128)(2,1)S(1)} %shard_map.70.cb, ...), custom_call_target="tpu_custom_call" | custom-call | tf_op jit(solution)/shard_map/pallas_call | solution.py:438
  19.5 1.2 %collective-permute-start.7 = (bf16[1,256,128]{2,1,0:T(8,128)(2,1)S(1)}, bf16[1,256,128]{2,1,0:T(8,128)(2,1)S(1)}, u32[]{:S(2)}, u32[]{:S(2)}) collective-permute-start(bf16[1,256,128]{2,1,0:T(8,128)(2,1)S(1)} %get-tuple-element.44), channel_id=1, source_target_pairs={{0,1},{1,0},{2,3},{3,2},{4,8},{5,9},{6,10},{7,11},{8,4},{9,5},{10,... | collective-permute-start | bytes 196616 | tf_op jit(solution)/shard_map/ppermute | solution.py:343
  20.8 0.6 collective-permute-start.6
  21.4 1.0 %shard_map.72.part = f32[1520,128]{1,0:T(8,128)S(1)} custom-call(bf16[1512,1512]{1,0:T(8,128)(2,1)S(1)} %get-tuple-element.32.inverse, f32[4,256,128]{2,1,0:T(8,128)S(1)} %get-tuple-element.43.own.w.rest_0_), custom_call_target="tpu_custom_call" | custom-call | flops 1073741824 | bytes 4194304 | tf_op jit(solution)/shard_map/pallas_call | solution.py:408
  22.4 1.5 %collective-permute-done.7.outer = bf16[1,256,128]{2,1,0:T(8,128)(2,1)S(1)} collective-permute-done((bf16[1,256,128]{2,1,0:T(8,128)(2,1)S(1)}, bf16[1,256,128]{2,1,0:T(8,128)(2,1)S(1)}, u32[]{:S(2)}, u32[]{:S(2)}) %collective-permute-start.7) | collective-permute-done | bytes 65568 | tf_op jit(solution)/shard_map/ppermute | solution.py:343
  23.9 0.3 shard_map.74
  24.2 0.3 collective-permute-start.8
  24.5 0.9 %shard_map.75 = (f32[4,256,128]{2,1,0:T(8,128)S(1)}, bf16[1,256,128]{2,1,0:T(8,128)(2,1)S(1)}) custom-call(s32[41]{0:T(128)S(4)} %get-tuple-element.30.table, bf16[1512,1512]{1,0:T(8,128)(2,1)S(1)} %get-tuple-element.32.inverse, f32[1520,128]{1,0:T(8,128)S(1)} %shard_map.72.part, bf16[616,128]{1,0:T(8,128)(2,1)S(1)} %get-tuple-element.45.ext), custom_call_target="tpu_custom_call" | custom-call | flops 1073741824 | bytes 4194304 | tf_op jit(solution)/shard_map/pallas_call | solution.py:420
  25.4 0.4 collective-permute-done.8.spill_in
  25.8 0.1 shard_map.76
  25.8 1.2 %collective-permute-start.9 = (bf16[5,256,128]{2,1,0:T(8,128)(2,1)S(1)}, bf16[5,256,128]{2,1,0:T(8,128)(2,1)S(1)}, u32[]{:S(2)}, u32[]{:S(2)}) collective-permute-start(bf16[5,256,128]{2,1,0:T(8,128)(2,1)S(1)} %get-tuple-element.50), channel_id=1, source_target_pairs={{0,1},{1,0},{2,3},{3,2},{4,8},{5,9},{6,10},{7,11},{8,4},{9,5},{10,... | collective-permute-start | bytes 983048 | tf_op jit(solution)/shard_map/ppermute | solution.py:343
  27.0 1.1 %collective-permute-start.10 = (bf16[4,256,128]{2,1,0:T(8,128)(2,1)S(1)}, bf16[4,256,128]{2,1,0:T(8,128)(2,1)S(1)}, u32[]{:S(2)}, u32[]{:S(2)}) collective-permute-start(bf16[4,256,128]{2,1,0:T(8,128)(2,1)S(1)} %get-tuple-element.51), channel_id=1, source_target_pairs={{0,4},{1,5},{2,6},{3,7},{4,0},{5,1},{6,2},{7,3},{8,12},{9,13},{10,... | collective-permute-start | bytes 786440 | tf_op jit(solution)/shard_map/ppermute | solution.py:343
  28.1 5.6 %collective-permute-done.11.far = bf16[1,256,128]{2,1,0:T(8,128)(2,1)S(1)} collective-permute-done((bf16[1,256,128]{2,1,0:T(8,128)(2,1)S(1)}, bf16[1,256,128]{2,1,0:T(8,128)(2,1)S(1)}, u32[]{:S(2)}, u32[]{:S(2)}) %collective-permute-start.11) | collective-permute-done | bytes 65568 | tf_op jit(solution)/shard_map/ppermute | solution.py:343
  33.7 0.6 shard_map.77
  34.4 0.1 collective-permute-start.12
  34.5 1.2 %collective-permute-done.12 = f32[6,128]{1,0:T(8,128)S(1)} collective-permute-done((f32[6,128]{1,0:T(8,128)S(1)}, f32[6,128]{1,0:T(8,128)S(1)}, u32[]{:S(2)}, u32[]{:S(2)}) %collective-permute-start.12) | collective-permute-done | bytes 3104 | tf_op jit(solution)/shard_map/ppermute | solution.py:343
  35.7 25.4 %all_to_all.5.gathered = f32[32,6,128]{2,1,0:T(8,128)S(1)} all-to-all(f32[32,6,128]{2,1,0:T(8,128)S(1)} %broadcast_in_dim.2), channel_id=1, replica_groups={{0,8,16,24,32,40,48,56,64,72,80,88,96,104,112,120,128,136,144,152,160,1..., dimensions={0} | all-to-all | bytes 196608 | tf_op jit(solution)/shard_map/all_to_all | solution.py:453
  61.0 0.9 %shard_map.78 = f32[1008,128]{1,0:T(8,128)} custom-call(f32[32,6,128]{2,1,0:T(8,128)S(1)} %all_to_all.5.gathered, f32[4,256,128]{2,1,0:T(8,128)S(1)} %get-tuple-element.53.p0, f32[4,256,128]{2,1,0:T(8,128)S(1)} %get-tuple-element.54.q), custom_call_target="tpu_custom_call" | custom-call | tf_op jit(solution)/shard_map/pallas_call | solution.py:457
  (17 shorter events, 0.1 us)
Async XLA Ops:
  0.7 1.0 %copy-start = (f32[4,252,128]{2,0,1:T(4,128)S(1)}, f32[4,252,128]{2,0,1:T(4,128)}, u32[]{:S(2)}) copy-start(f32[4,252,128]{2,0,1:T(4,128)} %param.6) | copy-start | bytes 1548292
  1.8 7.3 %collective-permute-start.1 = (bf16[4,256,128]{2,1,0:T(8,128)(2,1)S(1)}, bf16[4,256,128]{2,1,0:T(8,128)(2,1)S(1)}, u32[]{:S(2)}, u32[]{:S(2)}) collective-permute-start(bf16[4,256,128]{2,1,0:T(8,128)(2,1)S(1)} %get-tuple-element.34), channel_id=1, source_target_pairs={{0,1},{1,0},{2,3},{3,2},{4,8},{5,9},{6,10},{7,11},{8,4},{9,5},{10,... | collective-permute-start | bytes 786440 | tf_op jit(solution)/shard_map/ppermute | solution.py:343
  4.1 5.0 %collective-permute-start = (bf16[4,256,128]{2,1,0:T(8,128)(2,1)S(1)}, bf16[4,256,128]{2,1,0:T(8,128)(2,1)S(1)}, u32[]{:S(2)}, u32[]{:S(2)}) collective-permute-start(bf16[4,256,128]{2,1,0:T(8,128)(2,1)S(1)} %get-tuple-element.34), channel_id=1, source_target_pairs={{0,4},{1,5},{2,6},{3,7},{4,0},{5,1},{6,2},{7,3},{8,12},{9,13},{10,... | collective-permute-start | bytes 786440 | tf_op jit(solution)/shard_map/ppermute | solution.py:343
  9.5 1.5 %collective-permute-start.2 = (bf16[1,256,128]{2,1,0:T(8,128)(2,1)S(1)}, bf16[1,256,128]{2,1,0:T(8,128)(2,1)S(1)}, u32[]{:S(2)}, u32[]{:S(2)}) collective-permute-start(bf16[1,256,128]{2,1,0:T(8,128)(2,1)S(1)} %get-tuple-element.37), channel_id=1, source_target_pairs={{0,4},{1,5},{2,6},{3,7},{4,0},{5,1},{6,2},{7,3},{8,12},{9,13},{10,... | collective-permute-start | bytes 196616 | tf_op jit(solution)/shard_map/ppermute | solution.py:343
  11.0 7.8 %collective-permute-start.3 = (bf16[5,256,128]{2,1,0:T(8,128)(2,1)S(1)}, bf16[5,256,128]{2,1,0:T(8,128)(2,1)S(1)}, u32[]{:S(2)}, u32[]{:S(2)}) collective-permute-start(bf16[5,256,128]{2,1,0:T(8,128)(2,1)S(1)} %get-tuple-element.39.rest_0_), channel_id=1, source_target_pairs={{0,1},{1,0},{2,3},{3,2},{4,8},{5,9},{6,10},{7,11},{8,4},{9,5},{10,... | collective-permute-start | bytes 983048 | tf_op jit(solution)/shard_map/ppermute | solution.py:343
  12.3 6.5 %collective-permute-start.4 = (bf16[4,256,128]{2,1,0:T(8,128)(2,1)S(1)}, bf16[4,256,128]{2,1,0:T(8,128)(2,1)S(1)}, u32[]{:S(2)}, u32[]{:S(2)}) collective-permute-start(bf16[4,256,128]{2,1,0:T(8,128)(2,1)S(1)} %get-tuple-element.41), channel_id=1, source_target_pairs={{0,4},{1,5},{2,6},{3,7},{4,0},{5,1},{6,2},{7,3},{8,12},{9,13},{10,... | collective-permute-start | bytes 786440 | tf_op jit(solution)/shard_map/ppermute | solution.py:343
  12.8 6.1 %collective-permute-start.5 = (bf16[1,256,128]{2,1,0:T(8,128)(2,1)S(1)}, bf16[1,256,128]{2,1,0:T(8,128)(2,1)S(1)}, u32[]{:S(2)}, u32[]{:S(2)}) collective-permute-start(bf16[1,256,128]{2,1,0:T(8,128)(2,1)S(1)} %get-tuple-element.38.spill_out), channel_id=1, source_target_pairs={{0,4},{1,5},{2,6},{3,7},{4,12},{5,13},{6,14},{7,15},{8,0},{9,1},{1... | collective-permute-start | bytes 196616 | tf_op jit(solution)/shard_map/ppermute | solution.py:343
  19.5 4.4 %collective-permute-start.7 = (bf16[1,256,128]{2,1,0:T(8,128)(2,1)S(1)}, bf16[1,256,128]{2,1,0:T(8,128)(2,1)S(1)}, u32[]{:S(2)}, u32[]{:S(2)}) collective-permute-start(bf16[1,256,128]{2,1,0:T(8,128)(2,1)S(1)} %get-tuple-element.44), channel_id=1, source_target_pairs={{0,1},{1,0},{2,3},{3,2},{4,8},{5,9},{6,10},{7,11},{8,4},{9,5},{10,... | collective-permute-start | bytes 196616 | tf_op jit(solution)/shard_map/ppermute | solution.py:343
  20.8 3.1 %collective-permute-start.6 = (bf16[1,256,128]{2,1,0:T(8,128)(2,1)S(1)}, bf16[1,256,128]{2,1,0:T(8,128)(2,1)S(1)}, u32[]{:S(2)}, u32[]{:S(2)}) collective-permute-start(bf16[1,256,128]{2,1,0:T(8,128)(2,1)S(1)} %shard_map.73), channel_id=1, source_target_pairs={{0,4},{1,5},{2,6},{3,7},{4,0},{5,1},{6,2},{7,3},{8,12},{9,13},{10,... | collective-permute-start | bytes 196616 | tf_op jit(solution)/shard_map/ppermute | solution.py:343
  24.2 1.5 %collective-permute-start.8 = (bf16[1,256,128]{2,1,0:T(8,128)(2,1)S(1)}, bf16[1,256,128]{2,1,0:T(8,128)(2,1)S(1)}, u32[]{:S(2)}, u32[]{:S(2)}) collective-permute-start(bf16[1,256,128]{2,1,0:T(8,128)(2,1)S(1)} %get-tuple-element.47), channel_id=1, source_target_pairs={{0,4},{1,5},{2,6},{3,7},{4,0},{5,1},{6,2},{7,3},{8,12},{9,13},{10,... | collective-permute-start | bytes 196616 | tf_op jit(solution)/shard_map/ppermute | solution.py:343
  25.8 7.9 %collective-permute-start.9 = (bf16[5,256,128]{2,1,0:T(8,128)(2,1)S(1)}, bf16[5,256,128]{2,1,0:T(8,128)(2,1)S(1)}, u32[]{:S(2)}, u32[]{:S(2)}) collective-permute-start(bf16[5,256,128]{2,1,0:T(8,128)(2,1)S(1)} %get-tuple-element.50), channel_id=1, source_target_pairs={{0,1},{1,0},{2,3},{3,2},{4,8},{5,9},{6,10},{7,11},{8,4},{9,5},{10,... | collective-permute-start | bytes 983048 | tf_op jit(solution)/shard_map/ppermute | solution.py:343
  27.0 6.7 %collective-permute-start.10 = (bf16[4,256,128]{2,1,0:T(8,128)(2,1)S(1)}, bf16[4,256,128]{2,1,0:T(8,128)(2,1)S(1)}, u32[]{:S(2)}, u32[]{:S(2)}) collective-permute-start(bf16[4,256,128]{2,1,0:T(8,128)(2,1)S(1)} %get-tuple-element.51), channel_id=1, source_target_pairs={{0,4},{1,5},{2,6},{3,7},{4,0},{5,1},{6,2},{7,3},{8,12},{9,13},{10,... | collective-permute-start | bytes 786440 | tf_op jit(solution)/shard_map/ppermute | solution.py:343
  28.1 5.6 %collective-permute-start.11 = (bf16[1,256,128]{2,1,0:T(8,128)(2,1)S(1)}, bf16[1,256,128]{2,1,0:T(8,128)(2,1)S(1)}, u32[]{:S(2)}, u32[]{:S(2)}) collective-permute-start(bf16[1,256,128]{2,1,0:T(8,128)(2,1)S(1)} %get-tuple-element.48.spill_out), channel_id=1, source_target_pairs={{0,4},{1,5},{2,6},{3,7},{4,12},{5,13},{6,14},{7,15},{8,0},{9,1},{1... | collective-permute-start | bytes 196616 | tf_op jit(solution)/shard_map/ppermute | solution.py:343
  34.4 1.3 %collective-permute-start.12 = (f32[6,128]{1,0:T(8,128)S(1)}, f32[6,128]{1,0:T(8,128)S(1)}, u32[]{:S(2)}, u32[]{:S(2)}) collective-permute-start(f32[6,128]{1,0:T(8,128)S(1)} %pad_maximum_fusion), channel_id=1, source_target_pairs={{0,4},{1,5},{2,6},{3,7},{4,0},{5,1},{6,2},{7,3},{8,12},{9,13},{10,... | collective-permute-start | bytes 9224 | tf_op jit(solution)/shard_map/ppermute | solution.py:343

commit v13 on v12

--- a/solution.py
+++ b/solution.py
@@ -241,11 +241,12 @@
     if first:
         p_ref, w_ref, wout_ref, sums_ref, u = rest
     else:
-        w, p_ref, sums_ref, u = rest
+        w, sums_one, p_ref, sums_ref, u = rest
     got_values, got_index = opened(got[NS])
     got_index = jnp.where(table[ENDS] == 1, -1.0, got_index)
-    far_values, far_index = opened(far[0])
-    far_index = jnp.where(table[NEXT] == 1, -1.0, far_index)
+    far_index = jnp.where(table[NEXT] == 1, -1.0, far[0, W : W + 1, :].astype(F32))
+    inside = lax.broadcasted_iota(jnp.int32, (WP, R), 0) < W
+    far_values = jnp.where(inside, far[0], jnp.zeros((), BF16))
     count = table[COUNT]
     for s in range(NS):
         alive = jnp.where(count > s, 1.0, 0.0)
@@ -253,10 +254,15 @@
         p_ref[s] = p
         u[s] = got[s]
         u[NS + s] = p.astype(BF16)
-        u[2 * NS + s] = (near[s].astype(F32) + jnp.where(far_index == s, far_values, 0.0)).astype(BF16)
+        u[2 * NS + s] = near[s] + jnp.where(
+            jnp.broadcast_to(far_index, (WP, R)) == s, far_values, jnp.zeros((), BF16)
+        )
     index = table[OUT]
     u[index] = (got[index].astype(F32) + opened(spill_out[0])[0]).astype(BF16)
-    sums_ref[...] = jnp.zeros((8, R), F32)
+    if first:
+        sums_ref[...] = jnp.zeros((6, R), F32)
+    else:
+        sums_ref[...] = sums_one[...]
     if first:
         w_ref[...] = jnp.zeros((NS, WP, R), F32)
 
@@ -275,7 +281,8 @@
         else:
             terms = (start * image, w[s] * image, image * image)
         sums = [jnp.sum(x, axis=0, keepdims=True) for x in terms]
-        sums_ref[...] += jnp.concatenate(sums + [jnp.zeros((5, R), F32)], axis=0)
+        rest_of_six = [jnp.zeros((3, R), F32)]
+        sums_ref[...] += jnp.concatenate(sums + rest_of_six if first else rest_of_six + sums, axis=0)
 
     for s in range(NS):
         pl.when(count > s)(functools.partial(one, s))
@@ -437,7 +444,7 @@
         outs = [(block, F32)] + ([(block, F32), (one, BF16)] if first else [])
         return call(
             functools.partial(system_kernel, first),
-            outs + [((8, R), F32)],
+            outs + [((6, R), F32)],
             [SM] + [VM] * (7 + len(more)),
             [pltpu.VMEM((3 * NS, WP, R), BF16)],
         )(table, *matrix_parts, part, got, near, far, spill_out, *more)
@@ -447,8 +454,7 @@
     p0, w, w_out, sums_one = system(True, out, got_in, spill_out, v0)
     outer = to_outer(w_out)
     (w_in,) = call(pick_kernel, [(one, BF16)], [VM] * 2)(w, got_in)
-    q, sums_two = system(False, *solve(w, to_inner(w_in), outer), v0, w)
-    sums = jnp.concatenate([sums_one[:3], sums_two[:3]], axis=0)
+    q, sums = system(False, *solve(w, to_inner(w_in), outer), v0, w, sums_one)
     sums = sums + to_inner(sums)
     gathered = lax.all_to_all(
         jnp.broadcast_to(sums[None], (NSUB // 2, 6, R)), "sub", 0, 0,

time: 62.3 us -> 62.1 us (level)
  no operation moved by 1% of the time
where the time goes in v13:
time: 62.1 us
  blocking collectives  25.4 us (41%)
  Pallas kernels  14.2 us (23%)
  waiting for transfers between devices  11.4 us (18%)
  starting transfers between devices  9.16 us (15%)
  local copies, waits for them, and re-layouts  1.04 us (2%)
  between operations  0.95 us (2%)
    all_to_all x1, blocking collectives, body(): lax.all_to_all(jnp.broadcast_to(sums[None], (NSUB // 2, 6, R)), 'sub', 0,...  25.4 us
    ppermute x13, waiting for transfers between devices, permuted(): lax.ppermute(x, ('sub', 'rhs'), [(i * parts + j, t[0] * parts + t[1]) for...  11.4 us
    ppermute x13, starting transfers between devices, permuted(): lax.ppermute(x, ('sub', 'rhs'), [(i * parts + j, t[0] * parts + t[1]) for...  9.16 us
    pallas_call x2, Pallas kernels, matrices(): call(functools.partial(coupling_kernel, blocks, groups, first), outs, [AN...  7.25 us
    pallas_call x2, Pallas kernels, solve(): call(own_kernel, [((6 * W + 8, R), F32, pltpu.VMEM)], [VM, VM], [pltpu.VM...  1.97 us
    pallas_call x2, Pallas kernels, solve(): call(solve_kernel, [(block, F32), (one, BF16)], [SM] + [VM] * 3, [pltpu.V...  1.74 us
    pallas_call x2, Pallas kernels, system(): call(functools.partial(system_kernel, first), outs + [((6, R), F32)], [SM...  1.31 us
  transfers between devices with their start and end apart: 13, of which 5 were waited for; matrix products, arithmetic and copies ran while one was open for 0% of the time, Pallas kernels for 18%

profile of v13, /device:TPU:2, one launch (start us, length us, event | category | flops | bytes accessed | tf_op | source)
XLA Modules:
  0.0 62.1 jit_solution(9614483429047606006)
XLA Ops:
  0.7 1.0 %copy-done = f32[4,252,128]{2,0,1:T(4,128)S(1)} copy-done((f32[4,252,128]{2,0,1:T(4,128)S(1)}, f32[4,252,128]{2,0,1:T(4,128)}, u32[]{:S(2)}) %copy-start) | copy-done | bytes 516120
  1.7 0.1 shard_map.65
  1.8 2.4 %collective-permute-start.1 = (bf16[4,256,128]{2,1,0:T(8,128)(2,1)S(1)}, bf16[4,256,128]{2,1,0:T(8,128)(2,1)S(1)}, u32[]{:S(2)}, u32[]{:S(2)}) collective-permute-start(bf16[4,256,128]{2,1,0:T(8,128)(2,1)S(1)} %get-tuple-element.34), channel_id=1, source_target_pairs={{0,1},{1,0},{2,3},{3,2},{4,8},{5,9},{6,10},{7,11},{8,4},{9,5},{10,... | collective-permute-start | bytes 786440 | tf_op jit(solution)/shard_map/ppermute | solution.py:350
  4.1 4.0 %shard_map.64 = (bf16[16,256,256]{2,1,0:T(8,128)(2,1)S(1)}, bf16[1512,1512]{1,0:T(8,128)(2,1)S(1)}, s32[41]{0:T(128)S(4)}) custom-call(bf16[4,508032]{1,0:T(4,128)(2,1)} %flat.3, bf16[1,1512,1512]{2,1,0:T(8,128)(2,1)} %rest_0_.1, s32[1]{0:T(128)} %bitcast.rest_1_, s32[1]{0:T(128)S(6)} %copy.7.rest_2_.counts, s32[1,2]{1,0:T(1,128)} %rest_3_.1, s32[4,8]{1,0:T(4,128)} %rest_4_.1), custom_call_target="tpu_custom_call" | custom-call | flops 1048576 | bytes 12582912 | tf_op jit(solution)/shard_map/pallas_call | solution.py:394
  8.1 1.0 %shard_map.66.part = f32[1520,128]{1,0:T(8,128)S(1)} custom-call(bf16[1512,1512]{1,0:T(8,128)(2,1)S(1)} %get-tuple-element.32.inverse, f32[4,256,128]{2,1,0:T(8,128)S(1)} %get-tuple-element.33.own.v0), custom_call_target="tpu_custom_call" | custom-call | flops 1073741824 | bytes 4194304 | tf_op jit(solution)/shard_map/pallas_call | solution.py:415
  9.1 0.3 shard_map.67
  9.5 0.6 collective-permute-start.2
  10.0 0.9 %shard_map.68 = (f32[4,256,128]{2,1,0:T(8,128)S(1)}, bf16[1,256,128]{2,1,0:T(8,128)(2,1)S(1)}) custom-call(s32[41]{0:T(128)S(4)} %get-tuple-element.30.table, bf16[1512,1512]{1,0:T(8,128)(2,1)S(1)} %get-tuple-element.32.inverse, f32[1520,128]{1,0:T(8,128)S(1)} %shard_map.66.part, bf16[616,128]{1,0:T(8,128)(2,1)S(1)} %get-tuple-element.35.ext), custom_call_target="tpu_custom_call" | custom-call | flops 1073741824 | bytes 4194304 | tf_op jit(solution)/shard_map/pallas_call | solution.py:427
  10.9 0.1 shard_map.69
  11.0 1.3 %collective-permute-start.3 = (bf16[5,256,128]{2,1,0:T(8,128)(2,1)S(1)}, bf16[5,256,128]{2,1,0:T(8,128)(2,1)S(1)}, u32[]{:S(2)}, u32[]{:S(2)}) collective-permute-start(bf16[5,256,128]{2,1,0:T(8,128)(2,1)S(1)} %get-tuple-element.39.rest_0_), channel_id=1, source_target_pairs={{0,1},{1,0},{2,3},{3,2},{4,8},{5,9},{6,10},{7,11},{8,4},{9,5},{10,... | collective-permute-start | bytes 983048 | tf_op jit(solution)/shard_map/ppermute | solution.py:350
  12.3 0.4 collective-permute-start.4
  12.8 0.1 collective-permute-start.5
  12.9 3.3 %shard_map.70.cb = bf16[16,256,256]{2,1,0:T(8,128)(2,1)S(1)} custom-call(bf16[4,508032]{1,0:T(4,128)(2,1)} %flat.3, bf16[5,256,128]{2,1,0:T(8,128)(2,1)S(1)} %get-tuple-element.39.rest_0_), custom_call_target="tpu_custom_call" | custom-call | flops 1048576 | bytes 12582912 | tf_op jit(solution)/shard_map/pallas_call | solution.py:394
  16.1 2.7 %collective-permute-done.5.far = bf16[1,256,128]{2,1,0:T(8,128)(2,1)S(1)} collective-permute-done((bf16[1,256,128]{2,1,0:T(8,128)(2,1)S(1)}, bf16[1,256,128]{2,1,0:T(8,128)(2,1)S(1)}, u32[]{:S(2)}, u32[]{:S(2)}) %collective-permute-start.5) | collective-permute-done | bytes 65568 | tf_op jit(solution)/shard_map/ppermute | solution.py:350
  18.8 0.7 %shard_map.71 = (f32[4,256,128]{2,1,0:T(8,128)S(1)}, f32[4,256,128]{2,1,0:T(8,128)S(1)}, bf16[1,256,128]{2,1,0:T(8,128)(2,1)S(1)}, f32[6,128]{1,0:T(8,128)S(1)}) custom-call(s32[41]{0:T(128)S(4)} %get-tuple-element.30.table, bf16[16,256,256]{2,1,0:T(8,128)(2,1)S(1)} %get-tuple-element.31.ca, bf16[16,256,256]{2,1,0:T(8,128)(2,1)S(1)} %shard_map.70.cb, ...), custom_call_target="tpu_custom_call" | custom-call | tf_op jit(solution)/shard_map/pallas_call | solution.py:445
  19.5 1.2 %collective-permute-start.7 = (bf16[1,256,128]{2,1,0:T(8,128)(2,1)S(1)}, bf16[1,256,128]{2,1,0:T(8,128)(2,1)S(1)}, u32[]{:S(2)}, u32[]{:S(2)}) collective-permute-start(bf16[1,256,128]{2,1,0:T(8,128)(2,1)S(1)} %get-tuple-element.43), channel_id=1, source_target_pairs={{0,1},{1,0},{2,3},{3,2},{4,8},{5,9},{6,10},{7,11},{8,4},{9,5},{10,... | collective-permute-start | bytes 196616 | tf_op jit(solution)/shard_map/ppermute | solution.py:350
  20.8 0.6 collective-permute-start.6
  21.4 1.0 %shard_map.72.part = f32[1520,128]{1,0:T(8,128)S(1)} custom-call(bf16[1512,1512]{1,0:T(8,128)(2,1)S(1)} %get-tuple-element.32.inverse, f32[4,256,128]{2,1,0:T(8,128)S(1)} %get-tuple-element.42.own.w.rest_0_), custom_call_target="tpu_custom_call" | custom-call | flops 1073741824 | bytes 4194304 | tf_op jit(solution)/shard_map/pallas_call | solution.py:415
  22.4 1.5 %collective-permute-done.7.outer = bf16[1,256,128]{2,1,0:T(8,128)(2,1)S(1)} collective-permute-done((bf16[1,256,128]{2,1,0:T(8,128)(2,1)S(1)}, bf16[1,256,128]{2,1,0:T(8,128)(2,1)S(1)}, u32[]{:S(2)}, u32[]{:S(2)}) %collective-permute-start.7) | collective-permute-done | bytes 65568 | tf_op jit(solution)/shard_map/ppermute | solution.py:350
  23.9 0.3 shard_map.74
  24.2 0.3 collective-permute-start.8
  24.5 0.9 %shard_map.75 = (f32[4,256,128]{2,1,0:T(8,128)S(1)}, bf16[1,256,128]{2,1,0:T(8,128)(2,1)S(1)}) custom-call(s32[41]{0:T(128)S(4)} %get-tuple-element.30.table, bf16[1512,1512]{1,0:T(8,128)(2,1)S(1)} %get-tuple-element.32.inverse, f32[1520,128]{1,0:T(8,128)S(1)} %shard_map.72.part, bf16[616,128]{1,0:T(8,128)(2,1)S(1)} %get-tuple-element.44.ext), custom_call_target="tpu_custom_call" | custom-call | flops 1073741824 | bytes 4194304 | tf_op jit(solution)/shard_map/pallas_call | solution.py:427
  25.4 0.4 collective-permute-done.8.spill_in
  25.7 0.1 shard_map.76
  25.8 1.2 %collective-permute-start.9 = (bf16[5,256,128]{2,1,0:T(8,128)(2,1)S(1)}, bf16[5,256,128]{2,1,0:T(8,128)(2,1)S(1)}, u32[]{:S(2)}, u32[]{:S(2)}) collective-permute-start(bf16[5,256,128]{2,1,0:T(8,128)(2,1)S(1)} %get-tuple-element.49), channel_id=1, source_target_pairs={{0,1},{1,0},{2,3},{3,2},{4,8},{5,9},{6,10},{7,11},{8,4},{9,5},{10,... | collective-permute-start | bytes 983048 | tf_op jit(solution)/shard_map/ppermute | solution.py:350
  27.0 1.0 %collective-permute-start.10 = (bf16[4,256,128]{2,1,0:T(8,128)(2,1)S(1)}, bf16[4,256,128]{2,1,0:T(8,128)(2,1)S(1)}, u32[]{:S(2)}, u32[]{:S(2)}) collective-permute-start(bf16[4,256,128]{2,1,0:T(8,128)(2,1)S(1)} %get-tuple-element.50), channel_id=1, source_target_pairs={{0,4},{1,5},{2,6},{3,7},{4,0},{5,1},{6,2},{7,3},{8,12},{9,13},{10,... | collective-permute-start | bytes 786440 | tf_op jit(solution)/shard_map/ppermute | solution.py:350
  28.1 5.6 %collective-permute-done.11.far = bf16[1,256,128]{2,1,0:T(8,128)(2,1)S(1)} collective-permute-done((bf16[1,256,128]{2,1,0:T(8,128)(2,1)S(1)}, bf16[1,256,128]{2,1,0:T(8,128)(2,1)S(1)}, u32[]{:S(2)}, u32[]{:S(2)}) %collective-permute-start.11) | collective-permute-done | bytes 65568 | tf_op jit(solution)/shard_map/ppermute | solution.py:350
  33.7 0.6 %shard_map.77 = (f32[4,256,128]{2,1,0:T(8,128)S(1)}, f32[6,128]{1,0:T(8,128)S(1)}) custom-call(s32[41]{0:T(128)S(4)} %get-tuple-element.30.table, bf16[16,256,256]{2,1,0:T(8,128)(2,1)S(1)} %get-tuple-element.31.ca, bf16[16,256,256]{2,1,0:T(8,128)(2,1)S(1)} %shard_map.70.cb, f32[4,256,128]{2,1,0:T(8,128)S(1)} %get-tuple-element.48.part, ...), custom_call_target="tpu_custom_call" | custom-call | tf_op jit(solution)/shard_map/pallas_call | solution.py:445
  34.4 0.1 collective-permute-start.12
  34.5 1.2 %collective-permute-done.12 = f32[6,128]{1,0:T(8,128)S(1)} collective-permute-done((f32[6,128]{1,0:T(8,128)S(1)}, f32[6,128]{1,0:T(8,128)S(1)}, u32[]{:S(2)}, u32[]{:S(2)}) %collective-permute-start.12) | collective-permute-done | bytes 3104 | tf_op jit(solution)/shard_map/ppermute | solution.py:350
  35.6 25.4 %all_to_all.5.gathered = f32[32,6,128]{2,1,0:T(8,128)S(1)} all-to-all(f32[32,6,128]{2,1,0:T(8,128)S(1)} %broadcast_in_dim.2), channel_id=1, replica_groups={{0,8,16,24,32,40,48,56,64,72,80,88,96,104,112,120,128,136,144,152,160,1..., dimensions={0} | all-to-all | bytes 196608 | tf_op jit(solution)/shard_map/all_to_all | solution.py:459
  61.0 0.9 %shard_map.78 = f32[1008,128]{1,0:T(8,128)} custom-call(f32[32,6,128]{2,1,0:T(8,128)S(1)} %all_to_all.5.gathered, f32[4,256,128]{2,1,0:T(8,128)S(1)} %get-tuple-element.53.p0, f32[4,256,128]{2,1,0:T(8,128)S(1)} %get-tuple-element.54.q), custom_call_target="tpu_custom_call" | custom-call | tf_op jit(solution)/shard_map/pallas_call | solution.py:463
  (14 shorter events, 0.1 us)
Async XLA Ops:
  0.7 1.0 %copy-start = (f32[4,252,128]{2,0,1:T(4,128)S(1)}, f32[4,252,128]{2,0,1:T(4,128)}, u32[]{:S(2)}) copy-start(f32[4,252,128]{2,0,1:T(4,128)} %param.6) | copy-start | bytes 1548292
  1.8 7.3 %collective-permute-start.1 = (bf16[4,256,128]{2,1,0:T(8,128)(2,1)S(1)}, bf16[4,256,128]{2,1,0:T(8,128)(2,1)S(1)}, u32[]{:S(2)}, u32[]{:S(2)}) collective-permute-start(bf16[4,256,128]{2,1,0:T(8,128)(2,1)S(1)} %get-tuple-element.34), channel_id=1, source_target_pairs={{0,1},{1,0},{2,3},{3,2},{4,8},{5,9},{6,10},{7,11},{8,4},{9,5},{10,... | collective-permute-start | bytes 786440 | tf_op jit(solution)/shard_map/ppermute | solution.py:350
  4.1 5.0 %collective-permute-start = (bf16[4,256,128]{2,1,0:T(8,128)(2,1)S(1)}, bf16[4,256,128]{2,1,0:T(8,128)(2,1)S(1)}, u32[]{:S(2)}, u32[]{:S(2)}) collective-permute-start(bf16[4,256,128]{2,1,0:T(8,128)(2,1)S(1)} %get-tuple-element.34), channel_id=1, source_target_pairs={{0,4},{1,5},{2,6},{3,7},{4,0},{5,1},{6,2},{7,3},{8,12},{9,13},{10,... | collective-permute-start | bytes 786440 | tf_op jit(solution)/shard_map/ppermute | solution.py:350
  9.5 1.5 %collective-permute-start.2 = (bf16[1,256,128]{2,1,0:T(8,128)(2,1)S(1)}, bf16[1,256,128]{2,1,0:T(8,128)(2,1)S(1)}, u32[]{:S(2)}, u32[]{:S(2)}) collective-permute-start(bf16[1,256,128]{2,1,0:T(8,128)(2,1)S(1)} %get-tuple-element.37), channel_id=1, source_target_pairs={{0,4},{1,5},{2,6},{3,7},{4,0},{5,1},{6,2},{7,3},{8,12},{9,13},{10,... | collective-permute-start | bytes 196616 | tf_op jit(solution)/shard_map/ppermute | solution.py:350
  11.0 7.8 %collective-permute-start.3 = (bf16[5,256,128]{2,1,0:T(8,128)(2,1)S(1)}, bf16[5,256,128]{2,1,0:T(8,128)(2,1)S(1)}, u32[]{:S(2)}, u32[]{:S(2)}) collective-permute-start(bf16[5,256,128]{2,1,0:T(8,128)(2,1)S(1)} %get-tuple-element.39.rest_0_), channel_id=1, source_target_pairs={{0,1},{1,0},{2,3},{3,2},{4,8},{5,9},{6,10},{7,11},{8,4},{9,5},{10,... | collective-permute-start | bytes 983048 | tf_op jit(solution)/shard_map/ppermute | solution.py:350
  12.3 6.5 %collective-permute-start.4 = (bf16[4,256,128]{2,1,0:T(8,128)(2,1)S(1)}, bf16[4,256,128]{2,1,0:T(8,128)(2,1)S(1)}, u32[]{:S(2)}, u32[]{:S(2)}) collective-permute-start(bf16[4,256,128]{2,1,0:T(8,128)(2,1)S(1)} %get-tuple-element.41), channel_id=1, source_target_pairs={{0,4},{1,5},{2,6},{3,7},{4,0},{5,1},{6,2},{7,3},{8,12},{9,13},{10,... | collective-permute-start | bytes 786440 | tf_op jit(solution)/shard_map/ppermute | solution.py:350
  12.8 6.1 %collective-permute-start.5 = (bf16[1,256,128]{2,1,0:T(8,128)(2,1)S(1)}, bf16[1,256,128]{2,1,0:T(8,128)(2,1)S(1)}, u32[]{:S(2)}, u32[]{:S(2)}) collective-permute-start(bf16[1,256,128]{2,1,0:T(8,128)(2,1)S(1)} %get-tuple-element.38.spill_out), channel_id=1, source_target_pairs={{0,4},{1,5},{2,6},{3,7},{4,12},{5,13},{6,14},{7,15},{8,0},{9,1},{1... | collective-permute-start | bytes 196616 | tf_op jit(solution)/shard_map/ppermute | solution.py:350
  19.5 4.4 %collective-permute-start.7 = (bf16[1,256,128]{2,1,0:T(8,128)(2,1)S(1)}, bf16[1,256,128]{2,1,0:T(8,128)(2,1)S(1)}, u32[]{:S(2)}, u32[]{:S(2)}) collective-permute-start(bf16[1,256,128]{2,1,0:T(8,128)(2,1)S(1)} %get-tuple-element.43), channel_id=1, source_target_pairs={{0,1},{1,0},{2,3},{3,2},{4,8},{5,9},{6,10},{7,11},{8,4},{9,5},{10,... | collective-permute-start | bytes 196616 | tf_op jit(solution)/shard_map/ppermute | solution.py:350
  20.8 3.1 %collective-permute-start.6 = (bf16[1,256,128]{2,1,0:T(8,128)(2,1)S(1)}, bf16[1,256,128]{2,1,0:T(8,128)(2,1)S(1)}, u32[]{:S(2)}, u32[]{:S(2)}) collective-permute-start(bf16[1,256,128]{2,1,0:T(8,128)(2,1)S(1)} %shard_map.73), channel_id=1, source_target_pairs={{0,4},{1,5},{2,6},{3,7},{4,0},{5,1},{6,2},{7,3},{8,12},{9,13},{10,... | collective-permute-start | bytes 196616 | tf_op jit(solution)/shard_map/ppermute | solution.py:350
  24.2 1.5 %collective-permute-start.8 = (bf16[1,256,128]{2,1,0:T(8,128)(2,1)S(1)}, bf16[1,256,128]{2,1,0:T(8,128)(2,1)S(1)}, u32[]{:S(2)}, u32[]{:S(2)}) collective-permute-start(bf16[1,256,128]{2,1,0:T(8,128)(2,1)S(1)} %get-tuple-element.46), channel_id=1, source_target_pairs={{0,4},{1,5},{2,6},{3,7},{4,0},{5,1},{6,2},{7,3},{8,12},{9,13},{10,... | collective-permute-start | bytes 196616 | tf_op jit(solution)/shard_map/ppermute | solution.py:350
  25.8 7.9 %collective-permute-start.9 = (bf16[5,256,128]{2,1,0:T(8,128)(2,1)S(1)}, bf16[5,256,128]{2,1,0:T(8,128)(2,1)S(1)}, u32[]{:S(2)}, u32[]{:S(2)}) collective-permute-start(bf16[5,256,128]{2,1,0:T(8,128)(2,1)S(1)} %get-tuple-element.49), channel_id=1, source_target_pairs={{0,1},{1,0},{2,3},{3,2},{4,8},{5,9},{6,10},{7,11},{8,4},{9,5},{10,... | collective-permute-start | bytes 983048 | tf_op jit(solution)/shard_map/ppermute | solution.py:350
  27.0 6.7 %collective-permute-start.10 = (bf16[4,256,128]{2,1,0:T(8,128)(2,1)S(1)}, bf16[4,256,128]{2,1,0:T(8,128)(2,1)S(1)}, u32[]{:S(2)}, u32[]{:S(2)}) collective-permute-start(bf16[4,256,128]{2,1,0:T(8,128)(2,1)S(1)} %get-tuple-element.50), channel_id=1, source_target_pairs={{0,4},{1,5},{2,6},{3,7},{4,0},{5,1},{6,2},{7,3},{8,12},{9,13},{10,... | collective-permute-start | bytes 786440 | tf_op jit(solution)/shard_map/ppermute | solution.py:350
  28.1 5.6 %collective-permute-start.11 = (bf16[1,256,128]{2,1,0:T(8,128)(2,1)S(1)}, bf16[1,256,128]{2,1,0:T(8,128)(2,1)S(1)}, u32[]{:S(2)}, u32[]{:S(2)}) collective-permute-start(bf16[1,256,128]{2,1,0:T(8,128)(2,1)S(1)} %get-tuple-element.47.spill_out), channel_id=1, source_target_pairs={{0,4},{1,5},{2,6},{3,7},{4,12},{5,13},{6,14},{7,15},{8,0},{9,1},{1... | collective-permute-start | bytes 196616 | tf_op jit(solution)/shard_map/ppermute | solution.py:350
  34.4 1.3 %collective-permute-start.12 = (f32[6,128]{1,0:T(8,128)S(1)}, f32[6,128]{1,0:T(8,128)S(1)}, u32[]{:S(2)}, u32[]{:S(2)}) collective-permute-start(f32[6,128]{1,0:T(8,128)S(1)} %get-tuple-element.52), channel_id=1, source_target_pairs={{0,4},{1,5},{2,6},{3,7},{4,0},{5,1},{6,2},{7,3},{8,12},{9,13},{10,... | collective-permute-start | bytes 9224 | tf_op jit(solution)/shard_map/ppermute | solution.py:350

commit v14 on v13

--- a/solution.py
+++ b/solution.py
@@ -239,7 +239,7 @@
     first, table, ca, cb, part, got, near, far, spill_out, v0, *rest
 ):
     if first:
-        p_ref, w_ref, wout_ref, sums_ref, u = rest
+        p_ref, w_ref, wout_ref, u = rest
     else:
         w, sums_one, p_ref, sums_ref, u = rest
     got_values, got_index = opened(got[NS])
@@ -259,9 +259,7 @@
         )
     index = table[OUT]
     u[index] = (got[index].astype(F32) + opened(spill_out[0])[0]).astype(BF16)
-    if first:
-        sums_ref[...] = jnp.zeros((6, R), F32)
-    else:
+    if not first:
         sums_ref[...] = sums_one[...]
     if first:
         w_ref[...] = jnp.zeros((NS, WP, R), F32)
@@ -275,19 +273,24 @@
         image = acc
         start = v0[s]
         if first:
-            image = image - SHIFT * start
-            w_ref[s] = image
-            terms = (start * start, start * image, image * image)
+            w_ref[s] = image - SHIFT * start
         else:
-            terms = (start * image, w[s] * image, image * image)
-        sums = [jnp.sum(x, axis=0, keepdims=True) for x in terms]
-        rest_of_six = [jnp.zeros((3, R), F32)]
-        sums_ref[...] += jnp.concatenate(sums + rest_of_six if first else rest_of_six + sums, axis=0)
+            add_sums(sums_ref, 3, (start * image, w[s] * image, image * image))
 
     for s in range(NS):
         pl.when(count > s)(functools.partial(one, s))
     if first:
         picked(wout_ref, w_ref, got_index)
+
+
+def add_sums(ref, row, terms):
+    ref[row : row + 3, :] += jnp.concatenate([jnp.sum(x, axis=0, keepdims=True) for x in terms], axis=0)
+
+
+def first_sums_kernel(v0, w, _, sums_ref):
+    sums_ref[...] = jnp.zeros((6, R), F32)
+    for s in range(NS):
+        add_sums(sums_ref, 0, (v0[s] * v0[s], v0[s] * w[s], w[s] * w[s]))
 
 
 def picked(ref, w, index):
@@ -441,20 +444,22 @@
         if first:
             (made,) = matrices(False, sent)
             matrix_parts.append(pltpu.with_memory_space_constraint(made, pltpu.VMEM))
+        if not first:
+            more += tuple(call(first_sums_kernel, [((6, R), F32)], [VM, VM, ANY])(*more, sent))
         outs = [(block, F32)] + ([(block, F32), (one, BF16)] if first else [])
         return call(
             functools.partial(system_kernel, first),
-            outs + [((6, R), F32)],
+            outs if first else outs + [((6, R), F32)],
             [SM] + [VM] * (7 + len(more)),
             [pltpu.VMEM((3 * NS, WP, R), BF16)],
         )(table, *matrix_parts, part, got, near, far, spill_out, *more)
 
     matrix_parts = [first_part]
     out, got_in, spill_out = solve(v0, inner, outer)
-    p0, w, w_out, sums_one = system(True, out, got_in, spill_out, v0)
+    p0, w, w_out = system(True, out, got_in, spill_out, v0)
     outer = to_outer(w_out)
     (w_in,) = call(pick_kernel, [(one, BF16)], [VM] * 2)(w, got_in)
-    q, sums = system(False, *solve(w, to_inner(w_in), outer), v0, w, sums_one)
+    q, sums = system(False, *solve(w, to_inner(w_in), outer), v0, w)
     sums = sums + to_inner(sums)
     gathered = lax.all_to_all(
         jnp.broadcast_to(sums[None], (NSUB // 2, 6, R)), "sub", 0, 0,

time: 62.1 us -> 61.8 us (level)
    pallas_call x2 -> x3, Pallas kernels: 1.31 us -> 1.42 us  [the longest x2 1.3 us: system(): call(functools.partial(system_kernel, first), outs if first else outs + [...]
where the time goes in v14:
time: 61.8 us; the launch traced here: 61.6 us
  blocking collectives  24.9 us (40%)
  Pallas kernels  14.2 us (23%)
  waiting for transfers between devices  11.3 us (18%)
  starting transfers between devices  9.18 us (15%)
  local copies, waits for them, and re-layouts  1.04 us (2%)
  between operations  0.96 us (2%)
    all_to_all x1, blocking collectives, body(): lax.all_to_all(jnp.broadcast_to(sums[None], (NSUB // 2, 6, R)), 'sub', 0,...  24.9 us
    ppermute x13, waiting for transfers between devices, permuted(): lax.ppermute(x, ('sub', 'rhs'), [(i * parts + j, t[0] * parts + t[1]) for...  11.3 us
    ppermute x13, starting transfers between devices, permuted(): lax.ppermute(x, ('sub', 'rhs'), [(i * parts + j, t[0] * parts + t[1]) for...  9.18 us
    pallas_call x2, Pallas kernels, matrices(): call(functools.partial(coupling_kernel, blocks, groups, first), outs, [AN...  7.25 us
    pallas_call x2, Pallas kernels, solve(): call(own_kernel, [((6 * W + 8, R), F32, pltpu.VMEM)], [VM, VM], [pltpu.VM...  1.97 us
    pallas_call x2, Pallas kernels, solve(): call(solve_kernel, [(block, F32), (one, BF16)], [SM] + [VM] * 3, [pltpu.V...  1.7 us
    pallas_call x2, Pallas kernels, system(): call(functools.partial(system_kernel, first), outs if first else outs + [...  1.3 us
  transfers between devices with their start and end apart: 13, of which 5 were waited for; matrix products, arithmetic and copies ran while one was open for 0% of the time, Pallas kernels for 18%

profile of v14, /device:TPU:2, one launch (start us, length us, event | category | flops | bytes accessed | tf_op | source)
XLA Modules:
  0.0 61.6 jit_solution(3886401160890073640)
XLA Ops:
  0.7 1.0 %copy-done = f32[4,252,128]{2,0,1:T(4,128)S(1)} copy-done((f32[4,252,128]{2,0,1:T(4,128)S(1)}, f32[4,252,128]{2,0,1:T(4,128)}, u32[]{:S(2)}) %copy-start) | copy-done | bytes 516120
  1.8 2.4 %collective-permute-start.1 = (bf16[4,256,128]{2,1,0:T(8,128)(2,1)S(1)}, bf16[4,256,128]{2,1,0:T(8,128)(2,1)S(1)}, u32[]{:S(2)}, u32[]{:S(2)}) collective-permute-start(bf16[4,256,128]{2,1,0:T(8,128)(2,1)S(1)} %get-tuple-element.33), channel_id=1, source_target_pairs={{0,1},{1,0},{2,3},{3,2},{4,8},{5,9},{6,10},{7,11},{8,4},{9,5},{10,... | collective-permute-start | bytes 786440 | tf_op jit(solution)/shard_map/ppermute | solution.py:353
  4.1 4.0 %shard_map.64 = (bf16[16,256,256]{2,1,0:T(8,128)(2,1)S(1)}, bf16[1512,1512]{1,0:T(8,128)(2,1)S(1)}, s32[41]{0:T(128)S(4)}) custom-call(bf16[4,508032]{1,0:T(4,128)(2,1)} %flat.3, bf16[1,1512,1512]{2,1,0:T(8,128)(2,1)} %rest_0_.1, s32[1]{0:T(128)} %bitcast.rest_1_, s32[1]{0:T(128)S(6)} %copy.7.rest_2_.counts, s32[1,2]{1,0:T(1,128)} %rest_3_.1, s32[4,8]{1,0:T(4,128)} %rest_4_.1), custom_call_target="tpu_custom_call" | custom-call | flops 1048576 | bytes 12582912 | tf_op jit(solution)/shard_map/pallas_call | solution.py:397
  8.1 1.0 %shard_map.66.part = f32[1520,128]{1,0:T(8,128)S(1)} custom-call(bf16[1512,1512]{1,0:T(8,128)(2,1)S(1)} %get-tuple-element.31.inverse, f32[4,256,128]{2,1,0:T(8,128)S(1)} %get-tuple-element.32.own.v0), custom_call_target="tpu_custom_call" | custom-call | flops 1073741824 | bytes 4194304 | tf_op jit(solution)/shard_map/pallas_call | solution.py:418
  9.1 0.3 shard_map.67
  9.5 0.5 collective-permute-start.2
  10.0 0.8 %shard_map.68 = (f32[4,256,128]{2,1,0:T(8,128)S(1)}, bf16[1,256,128]{2,1,0:T(8,128)(2,1)S(1)}) custom-call(s32[41]{0:T(128)S(4)} %get-tuple-element.29.table, bf16[1512,1512]{1,0:T(8,128)(2,1)S(1)} %get-tuple-element.31.inverse, f32[1520,128]{1,0:T(8,128)S(1)} %shard_map.66.part, bf16[616,128]{1,0:T(8,128)(2,1)S(1)} %get-tuple-element.34.ext), custom_call_target="tpu_custom_call" | custom-call | flops 1073741824 | bytes 4194304 | tf_op jit(solution)/shard_map/pallas_call | solution.py:430
  10.9 0.1 shard_map.69
  11.0 1.3 %collective-permute-start.3 = (bf16[5,256,128]{2,1,0:T(8,128)(2,1)S(1)}, bf16[5,256,128]{2,1,0:T(8,128)(2,1)S(1)}, u32[]{:S(2)}, u32[]{:S(2)}) collective-permute-start(bf16[5,256,128]{2,1,0:T(8,128)(2,1)S(1)} %get-tuple-element.38.rest_0_), channel_id=1, source_target_pairs={{0,1},{1,0},{2,3},{3,2},{4,8},{5,9},{6,10},{7,11},{8,4},{9,5},{10,... | collective-permute-start | bytes 983048 | tf_op jit(solution)/shard_map/ppermute | solution.py:353
  12.3 0.4 collective-permute-start.4
  12.8 0.1 collective-permute-start.5
  12.9 3.3 %shard_map.70.cb = bf16[16,256,256]{2,1,0:T(8,128)(2,1)S(1)} custom-call(bf16[4,508032]{1,0:T(4,128)(2,1)} %flat.3, bf16[5,256,128]{2,1,0:T(8,128)(2,1)S(1)} %get-tuple-element.38.rest_0_), custom_call_target="tpu_custom_call" | custom-call | flops 1048576 | bytes 12582912 | tf_op jit(solution)/shard_map/pallas_call | solution.py:397
  16.1 2.7 %collective-permute-done.5.far = bf16[1,256,128]{2,1,0:T(8,128)(2,1)S(1)} collective-permute-done((bf16[1,256,128]{2,1,0:T(8,128)(2,1)S(1)}, bf16[1,256,128]{2,1,0:T(8,128)(2,1)S(1)}, u32[]{:S(2)}, u32[]{:S(2)}) %collective-permute-start.5) | collective-permute-done | bytes 65568 | tf_op jit(solution)/shard_map/ppermute | solution.py:353
  18.8 0.7 %shard_map.71 = (f32[4,256,128]{2,1,0:T(8,128)S(1)}, f32[4,256,128]{2,1,0:T(8,128)S(1)}, bf16[1,256,128]{2,1,0:T(8,128)(2,1)S(1)}) custom-call(s32[41]{0:T(128)S(4)} %get-tuple-element.29.table, bf16[16,256,256]{2,1,0:T(8,128)(2,1)S(1)} %get-tuple-element.30.ca, bf16[16,256,256]{2,1,0:T(8,128)(2,1)S(1)} %shard_map.70.cb, ...), custom_call_target="tpu_custom_call" | custom-call | tf_op jit(solution)/shard_map/pallas_call | solution.py:450
  19.5 1.2 %collective-permute-start.7 = (bf16[1,256,128]{2,1,0:T(8,128)(2,1)S(1)}, bf16[1,256,128]{2,1,0:T(8,128)(2,1)S(1)}, u32[]{:S(2)}, u32[]{:S(2)}) collective-permute-start(bf16[1,256,128]{2,1,0:T(8,128)(2,1)S(1)} %get-tuple-element.42), channel_id=1, source_target_pairs={{0,1},{1,0},{2,3},{3,2},{4,8},{5,9},{6,10},{7,11},{8,4},{9,5},{10,... | collective-permute-start | bytes 196616 | tf_op jit(solution)/shard_map/ppermute | solution.py:353
  20.7 0.6 %collective-permute-start.6 = (bf16[1,256,128]{2,1,0:T(8,128)(2,1)S(1)}, bf16[1,256,128]{2,1,0:T(8,128)(2,1)S(1)}, u32[]{:S(2)}, u32[]{:S(2)}) collective-permute-start(bf16[1,256,128]{2,1,0:T(8,128)(2,1)S(1)} %shard_map.73), channel_id=1, source_target_pairs={{0,4},{1,5},{2,6},{3,7},{4,0},{5,1},{6,2},{7,3},{8,12},{9,13},{10,... | collective-permute-start | bytes 196616 | tf_op jit(solution)/shard_map/ppermute | solution.py:353
  21.3 1.0 %shard_map.72.part = f32[1520,128]{1,0:T(8,128)S(1)} custom-call(bf16[1512,1512]{1,0:T(8,128)(2,1)S(1)} %get-tuple-element.31.inverse, f32[4,256,128]{2,1,0:T(8,128)S(1)} %get-tuple-element.41.own.w.rest_0_), custom_call_target="tpu_custom_call" | custom-call | flops 1073741824 | bytes 4194304 | tf_op jit(solution)/shard_map/pallas_call | solution.py:418
  22.3 1.5 %collective-permute-done.7.outer = bf16[1,256,128]{2,1,0:T(8,128)(2,1)S(1)} collective-permute-done((bf16[1,256,128]{2,1,0:T(8,128)(2,1)S(1)}, bf16[1,256,128]{2,1,0:T(8,128)(2,1)S(1)}, u32[]{:S(2)}, u32[]{:S(2)}) %collective-permute-start.7) | collective-permute-done | bytes 65568 | tf_op jit(solution)/shard_map/ppermute | solution.py:353
  23.9 0.3 shard_map.74
  24.2 0.3 collective-permute-start.8
  24.5 0.8 %shard_map.75 = (f32[4,256,128]{2,1,0:T(8,128)S(1)}, bf16[1,256,128]{2,1,0:T(8,128)(2,1)S(1)}) custom-call(s32[41]{0:T(128)S(4)} %get-tuple-element.29.table, bf16[1512,1512]{1,0:T(8,128)(2,1)S(1)} %get-tuple-element.31.inverse, f32[1520,128]{1,0:T(8,128)S(1)} %shard_map.72.part, bf16[616,128]{1,0:T(8,128)(2,1)S(1)} %get-tuple-element.43.ext), custom_call_target="tpu_custom_call" | custom-call | flops 1073741824 | bytes 4194304 | tf_op jit(solution)/shard_map/pallas_call | solution.py:430
  25.3 0.4 collective-permute-done.8.spill_in
  25.7 0.1 shard_map.76
  25.8 1.2 %collective-permute-start.9 = (bf16[5,256,128]{2,1,0:T(8,128)(2,1)S(1)}, bf16[5,256,128]{2,1,0:T(8,128)(2,1)S(1)}, u32[]{:S(2)}, u32[]{:S(2)}) collective-permute-start(bf16[5,256,128]{2,1,0:T(8,128)(2,1)S(1)} %get-tuple-element.48._), channel_id=1, source_target_pairs={{0,1},{1,0},{2,3},{3,2},{4,8},{5,9},{6,10},{7,11},{8,4},{9,5},{10,... | collective-permute-start | bytes 983048 | tf_op jit(solution)/shard_map/ppermute | solution.py:353
  27.0 1.1 %collective-permute-start.10 = (bf16[4,256,128]{2,1,0:T(8,128)(2,1)S(1)}, bf16[4,256,128]{2,1,0:T(8,128)(2,1)S(1)}, u32[]{:S(2)}, u32[]{:S(2)}) collective-permute-start(bf16[4,256,128]{2,1,0:T(8,128)(2,1)S(1)} %get-tuple-element.49), channel_id=1, source_target_pairs={{0,4},{1,5},{2,6},{3,7},{4,0},{5,1},{6,2},{7,3},{8,12},{9,13},{10,... | collective-permute-start | bytes 786440 | tf_op jit(solution)/shard_map/ppermute | solution.py:353
  28.1 0.1 shard_map.77.rest_1_
  28.2 5.5 %collective-permute-done.11.far = bf16[1,256,128]{2,1,0:T(8,128)(2,1)S(1)} collective-permute-done((bf16[1,256,128]{2,1,0:T(8,128)(2,1)S(1)}, bf16[1,256,128]{2,1,0:T(8,128)(2,1)S(1)}, u32[]{:S(2)}, u32[]{:S(2)}) %collective-permute-start.11) | collective-permute-done | bytes 65568 | tf_op jit(solution)/shard_map/ppermute | solution.py:353
  33.7 0.6 %shard_map.78 = (f32[4,256,128]{2,1,0:T(8,128)S(1)}, f32[6,128]{1,0:T(8,128)S(1)}) custom-call(s32[41]{0:T(128)S(4)} %get-tuple-element.29.table, bf16[16,256,256]{2,1,0:T(8,128)(2,1)S(1)} %get-tuple-element.30.ca, bf16[16,256,256]{2,1,0:T(8,128)(2,1)S(1)} %shard_map.70.cb, f32[4,256,128]{2,1,0:T(8,128)S(1)} %get-tuple-element.47.part, ...), custom_call_target="tpu_custom_call" | custom-call | tf_op jit(solution)/shard_map/pallas_call | solution.py:450
  34.3 0.1 collective-permute-start.12
  34.4 1.2 %collective-permute-done.12 = f32[6,128]{1,0:T(8,128)S(1)} collective-permute-done((f32[6,128]{1,0:T(8,128)S(1)}, f32[6,128]{1,0:T(8,128)S(1)}, u32[]{:S(2)}, u32[]{:S(2)}) %collective-permute-start.12) | collective-permute-done | bytes 3104 | tf_op jit(solution)/shard_map/ppermute | solution.py:353
  35.6 24.9 %all_to_all.5.gathered = f32[32,6,128]{2,1,0:T(8,128)S(1)} all-to-all(f32[32,6,128]{2,1,0:T(8,128)S(1)} %broadcast_in_dim.2), channel_id=1, replica_groups={{0,8,16,24,32,40,48,56,64,72,80,88,96,104,112,120,128,136,144,152,160,1..., dimensions={0} | all-to-all | bytes 196608 | tf_op jit(solution)/shard_map/all_to_all | solution.py:464
  60.5 0.9 %shard_map.79 = f32[1008,128]{1,0:T(8,128)} custom-call(f32[32,6,128]{2,1,0:T(8,128)S(1)} %all_to_all.5.gathered, f32[4,256,128]{2,1,0:T(8,128)S(1)} %get-tuple-element.51.p0, f32[4,256,128]{2,1,0:T(8,128)S(1)} %get-tuple-element.52.q), custom_call_target="tpu_custom_call" | custom-call | tf_op jit(solution)/shard_map/pallas_call | solution.py:468
  (15 shorter events, 0.2 us)
Async XLA Ops:
  0.7 1.0 %copy-start = (f32[4,252,128]{2,0,1:T(4,128)S(1)}, f32[4,252,128]{2,0,1:T(4,128)}, u32[]{:S(2)}) copy-start(f32[4,252,128]{2,0,1:T(4,128)} %param.6) | copy-start | bytes 1548292
  1.8 7.3 %collective-permute-start.1 = (bf16[4,256,128]{2,1,0:T(8,128)(2,1)S(1)}, bf16[4,256,128]{2,1,0:T(8,128)(2,1)S(1)}, u32[]{:S(2)}, u32[]{:S(2)}) collective-permute-start(bf16[4,256,128]{2,1,0:T(8,128)(2,1)S(1)} %get-tuple-element.33), channel_id=1, source_target_pairs={{0,1},{1,0},{2,3},{3,2},{4,8},{5,9},{6,10},{7,11},{8,4},{9,5},{10,... | collective-permute-start | bytes 786440 | tf_op jit(solution)/shard_map/ppermute | solution.py:353
  4.1 5.0 %collective-permute-start = (bf16[4,256,128]{2,1,0:T(8,128)(2,1)S(1)}, bf16[4,256,128]{2,1,0:T(8,128)(2,1)S(1)}, u32[]{:S(2)}, u32[]{:S(2)}) collective-permute-start(bf16[4,256,128]{2,1,0:T(8,128)(2,1)S(1)} %get-tuple-element.33), channel_id=1, source_target_pairs={{0,4},{1,5},{2,6},{3,7},{4,0},{5,1},{6,2},{7,3},{8,12},{9,13},{10,... | collective-permute-start | bytes 786440 | tf_op jit(solution)/shard_map/ppermute | solution.py:353
  9.5 1.4 %collective-permute-start.2 = (bf16[1,256,128]{2,1,0:T(8,128)(2,1)S(1)}, bf16[1,256,128]{2,1,0:T(8,128)(2,1)S(1)}, u32[]{:S(2)}, u32[]{:S(2)}) collective-permute-start(bf16[1,256,128]{2,1,0:T(8,128)(2,1)S(1)} %get-tuple-element.36), channel_id=1, source_target_pairs={{0,4},{1,5},{2,6},{3,7},{4,0},{5,1},{6,2},{7,3},{8,12},{9,13},{10,... | collective-permute-start | bytes 196616 | tf_op jit(solution)/shard_map/ppermute | solution.py:353
  11.0 7.8 %collective-permute-start.3 = (bf16[5,256,128]{2,1,0:T(8,128)(2,1)S(1)}, bf16[5,256,128]{2,1,0:T(8,128)(2,1)S(1)}, u32[]{:S(2)}, u32[]{:S(2)}) collective-permute-start(bf16[5,256,128]{2,1,0:T(8,128)(2,1)S(1)} %get-tuple-element.38.rest_0_), channel_id=1, source_target_pairs={{0,1},{1,0},{2,3},{3,2},{4,8},{5,9},{6,10},{7,11},{8,4},{9,5},{10,... | collective-permute-start | bytes 983048 | tf_op jit(solution)/shard_map/ppermute | solution.py:353
  12.3 6.5 %collective-permute-start.4 = (bf16[4,256,128]{2,1,0:T(8,128)(2,1)S(1)}, bf16[4,256,128]{2,1,0:T(8,128)(2,1)S(1)}, u32[]{:S(2)}, u32[]{:S(2)}) collective-permute-start(bf16[4,256,128]{2,1,0:T(8,128)(2,1)S(1)} %get-tuple-element.40), channel_id=1, source_target_pairs={{0,4},{1,5},{2,6},{3,7},{4,0},{5,1},{6,2},{7,3},{8,12},{9,13},{10,... | collective-permute-start | bytes 786440 | tf_op jit(solution)/shard_map/ppermute | solution.py:353
  12.8 6.0 %collective-permute-start.5 = (bf16[1,256,128]{2,1,0:T(8,128)(2,1)S(1)}, bf16[1,256,128]{2,1,0:T(8,128)(2,1)S(1)}, u32[]{:S(2)}, u32[]{:S(2)}) collective-permute-start(bf16[1,256,128]{2,1,0:T(8,128)(2,1)S(1)} %get-tuple-element.37.spill_out), channel_id=1, source_target_pairs={{0,4},{1,5},{2,6},{3,7},{4,12},{5,13},{6,14},{7,15},{8,0},{9,1},{1... | collective-permute-start | bytes 196616 | tf_op jit(solution)/shard_map/ppermute | solution.py:353
  19.5 4.4 %collective-permute-start.7 = (bf16[1,256,128]{2,1,0:T(8,128)(2,1)S(1)}, bf16[1,256,128]{2,1,0:T(8,128)(2,1)S(1)}, u32[]{:S(2)}, u32[]{:S(2)}) collective-permute-start(bf16[1,256,128]{2,1,0:T(8,128)(2,1)S(1)} %get-tuple-element.42), channel_id=1, source_target_pairs={{0,1},{1,0},{2,3},{3,2},{4,8},{5,9},{6,10},{7,11},{8,4},{9,5},{10,... | collective-permute-start | bytes 196616 | tf_op jit(solution)/shard_map/ppermute | solution.py:353
  20.7 3.1 %collective-permute-start.6 = (bf16[1,256,128]{2,1,0:T(8,128)(2,1)S(1)}, bf16[1,256,128]{2,1,0:T(8,128)(2,1)S(1)}, u32[]{:S(2)}, u32[]{:S(2)}) collective-permute-start(bf16[1,256,128]{2,1,0:T(8,128)(2,1)S(1)} %shard_map.73), channel_id=1, source_target_pairs={{0,4},{1,5},{2,6},{3,7},{4,0},{5,1},{6,2},{7,3},{8,12},{9,13},{10,... | collective-permute-start | bytes 196616 | tf_op jit(solution)/shard_map/ppermute | solution.py:353
  24.2 1.5 %collective-permute-start.8 = (bf16[1,256,128]{2,1,0:T(8,128)(2,1)S(1)}, bf16[1,256,128]{2,1,0:T(8,128)(2,1)S(1)}, u32[]{:S(2)}, u32[]{:S(2)}) collective-permute-start(bf16[1,256,128]{2,1,0:T(8,128)(2,1)S(1)} %get-tuple-element.45), channel_id=1, source_target_pairs={{0,4},{1,5},{2,6},{3,7},{4,0},{5,1},{6,2},{7,3},{8,12},{9,13},{10,... | collective-permute-start | bytes 196616 | tf_op jit(solution)/shard_map/ppermute | solution.py:353
  25.8 7.9 %collective-permute-start.9 = (bf16[5,256,128]{2,1,0:T(8,128)(2,1)S(1)}, bf16[5,256,128]{2,1,0:T(8,128)(2,1)S(1)}, u32[]{:S(2)}, u32[]{:S(2)}) collective-permute-start(bf16[5,256,128]{2,1,0:T(8,128)(2,1)S(1)} %get-tuple-element.48._), channel_id=1, source_target_pairs={{0,1},{1,0},{2,3},{3,2},{4,8},{5,9},{6,10},{7,11},{8,4},{9,5},{10,... | collective-permute-start | bytes 983048 | tf_op jit(solution)/shard_map/ppermute | solution.py:353
  27.0 6.7 %collective-permute-start.10 = (bf16[4,256,128]{2,1,0:T(8,128)(2,1)S(1)}, bf16[4,256,128]{2,1,0:T(8,128)(2,1)S(1)}, u32[]{:S(2)}, u32[]{:S(2)}) collective-permute-start(bf16[4,256,128]{2,1,0:T(8,128)(2,1)S(1)} %get-tuple-element.49), channel_id=1, source_target_pairs={{0,4},{1,5},{2,6},{3,7},{4,0},{5,1},{6,2},{7,3},{8,12},{9,13},{10,... | collective-permute-start | bytes 786440 | tf_op jit(solution)/shard_map/ppermute | solution.py:353
  28.1 5.6 %collective-permute-start.11 = (bf16[1,256,128]{2,1,0:T(8,128)(2,1)S(1)}, bf16[1,256,128]{2,1,0:T(8,128)(2,1)S(1)}, u32[]{:S(2)}, u32[]{:S(2)}) collective-permute-start(bf16[1,256,128]{2,1,0:T(8,128)(2,1)S(1)} %get-tuple-element.46.spill_out), channel_id=1, source_target_pairs={{0,4},{1,5},{2,6},{3,7},{4,12},{5,13},{6,14},{7,15},{8,0},{9,1},{1... | collective-permute-start | bytes 196616 | tf_op jit(solution)/shard_map/ppermute | solution.py:353
  34.3 1.3 %collective-permute-start.12 = (f32[6,128]{1,0:T(8,128)S(1)}, f32[6,128]{1,0:T(8,128)S(1)}, u32[]{:S(2)}, u32[]{:S(2)}) collective-permute-start(f32[6,128]{1,0:T(8,128)S(1)} %get-tuple-element.50), channel_id=1, source_target_pairs={{0,4},{1,5},{2,6},{3,7},{4,0},{5,1},{6,2},{7,3},{8,12},{9,13},{10,... | collective-permute-start | bytes 9224 | tf_op jit(solution)/shard_map/ppermute | solution.py:353

commit v15 on v13

--- a/solution.py
+++ b/solution.py
@@ -455,11 +455,7 @@
     outer = to_outer(w_out)
     (w_in,) = call(pick_kernel, [(one, BF16)], [VM] * 2)(w, got_in)
     q, sums = system(False, *solve(w, to_inner(w_in), outer), v0, w, sums_one)
-    sums = sums + to_inner(sums)
-    gathered = lax.all_to_all(
-        jnp.broadcast_to(sums[None], (NSUB // 2, 6, R)), "sub", 0, 0,
-        axis_index_groups=[list(range(c, NSUB, 2)) for c in range(2)],
-    )
+    gathered = lax.all_to_all(jnp.broadcast_to(sums[None], (NSUB, 6, R)), "sub", 0, 0)
     (flat,) = call(
         finish_kernel,
         [((W * NS, R), F32, pltpu.HBM)],

time: 62.1 us -> 65 us (1.047); the launches traced: 62.1 us -> 64.1 us
  blocking collectives: 25.4 us -> 28.5 us
  waiting for transfers between devices: 11.4 us -> 10.3 us
    all_to_all x1, blocking collectives: 25.4 us -> 28.5 us  [body(): lax.all_to_all(jnp.broadcast_to(sums[None], (NSUB, 6, R)), 'sub', 0, 0)]
    ppermute x13 -> x12, waiting for transfers between devices: 11.4 us -> 10.3 us  [permuted(): lax.ppermute(x, ('sub', 'rhs'), [(i * parts + j, t[0] * parts + t[1]) for...]
    ppermute x13 -> x12, starting transfers between devices: 9.16 us -> 9.07 us  [permuted(): lax.ppermute(x, ('sub', 'rhs'), [(i * parts + j, t[0] * parts + t[1]) for...]
  transfers between devices with their start and end apart: 13 -> 12, of which waited for: 5 -> 4; matrix products, arithmetic and copies ran while one was open for 0% -> 0% of each run, Pallas kernels for 18% -> 17%
where the time goes in v15:
time: 65 us; the launch traced here: 64.1 us
  blocking collectives  28.5 us (44%)
  Pallas kernels  14.2 us (22%)
  waiting for transfers between devices  10.3 us (16%)
  starting transfers between devices  9.07 us (14%)
  local copies, waits for them, and re-layouts  1.05 us (2%)
  between operations  0.95 us (1%)
    all_to_all x1, blocking collectives, body(): lax.all_to_all(jnp.broadcast_to(sums[None], (NSUB, 6, R)), 'sub', 0, 0)  28.5 us
    ppermute x12, waiting for transfers between devices, permuted(): lax.ppermute(x, ('sub', 'rhs'), [(i * parts + j, t[0] * parts + t[1]) for...  10.3 us
    ppermute x12, starting transfers between devices, permuted(): lax.ppermute(x, ('sub', 'rhs'), [(i * parts + j, t[0] * parts + t[1]) for...  9.07 us
    pallas_call x2, Pallas kernels, matrices(): call(functools.partial(coupling_kernel, blocks, groups, first), outs, [AN...  7.25 us
    pallas_call x2, Pallas kernels, solve(): call(own_kernel, [((6 * W + 8, R), F32, pltpu.VMEM)], [VM, VM], [pltpu.VM...  1.97 us
    pallas_call x2, Pallas kernels, solve(): call(solve_kernel, [(block, F32), (one, BF16)], [SM] + [VM] * 3, [pltpu.V...  1.74 us
    pallas_call x2, Pallas kernels, system(): call(functools.partial(system_kernel, first), outs + [((6, R), F32)], [SM...  1.31 us
  transfers between devices with their start and end apart: 12, of which 4 were waited for; matrix products, arithmetic and copies ran while one was open for 0% of the time, Pallas kernels for 17%

profile of v15, /device:TPU:2, one launch (start us, length us, event | category | flops | bytes accessed | tf_op | source)
XLA Modules:
  0.0 64.1 jit_solution(8706904179815511052)
XLA Ops:
  0.7 1.0 %copy-done = f32[4,252,128]{2,0,1:T(4,128)S(1)} copy-done((f32[4,252,128]{2,0,1:T(4,128)S(1)}, f32[4,252,128]{2,0,1:T(4,128)}, u32[]{:S(2)}) %copy-start) | copy-done | bytes 516120
  1.7 0.1 shard_map.65
  1.8 2.4 %collective-permute-start.1 = (bf16[4,256,128]{2,1,0:T(8,128)(2,1)S(1)}, bf16[4,256,128]{2,1,0:T(8,128)(2,1)S(1)}, u32[]{:S(2)}, u32[]{:S(2)}) collective-permute-start(bf16[4,256,128]{2,1,0:T(8,128)(2,1)S(1)} %get-tuple-element.34), channel_id=1, source_target_pairs={{0,1},{1,0},{2,3},{3,2},{4,8},{5,9},{6,10},{7,11},{8,4},{9,5},{10,... | collective-permute-start | bytes 786440 | tf_op jit(solution)/shard_map/ppermute | solution.py:350
  4.1 0.0 collective-permute-start
  4.1 4.0 %shard_map.64 = (bf16[16,256,256]{2,1,0:T(8,128)(2,1)S(1)}, bf16[1512,1512]{1,0:T(8,128)(2,1)S(1)}, s32[41]{0:T(128)S(4)}) custom-call(bf16[4,508032]{1,0:T(4,128)(2,1)} %flat.3, bf16[1,1512,1512]{2,1,0:T(8,128)(2,1)} %rest_0_.1, s32[1]{0:T(128)} %bitcast.rest_1_, s32[1]{0:T(128)S(6)} %copy.7.rest_2_.counts, s32[1,2]{1,0:T(1,128)} %rest_3_.1, s32[4,8]{1,0:T(4,128)} %rest_4_.1), custom_call_target="tpu_custom_call" | custom-call | flops 1048576 | bytes 12582912 | tf_op jit(solution)/shard_map/pallas_call | solution.py:394
  8.1 1.0 %shard_map.66.part = f32[1520,128]{1,0:T(8,128)S(1)} custom-call(bf16[1512,1512]{1,0:T(8,128)(2,1)S(1)} %get-tuple-element.32.inverse, f32[4,256,128]{2,1,0:T(8,128)S(1)} %get-tuple-element.33.own.v0), custom_call_target="tpu_custom_call" | custom-call | flops 1073741824 | bytes 4194304 | tf_op jit(solution)/shard_map/pallas_call | solution.py:415
  9.1 0.3 shard_map.67
  9.5 0.6 collective-permute-start.2
  10.0 0.9 %shard_map.68 = (f32[4,256,128]{2,1,0:T(8,128)S(1)}, bf16[1,256,128]{2,1,0:T(8,128)(2,1)S(1)}) custom-call(s32[41]{0:T(128)S(4)} %get-tuple-element.30.table, bf16[1512,1512]{1,0:T(8,128)(2,1)S(1)} %get-tuple-element.32.inverse, f32[1520,128]{1,0:T(8,128)S(1)} %shard_map.66.part, bf16[616,128]{1,0:T(8,128)(2,1)S(1)} %get-tuple-element.35.ext), custom_call_target="tpu_custom_call" | custom-call | flops 1073741824 | bytes 4194304 | tf_op jit(solution)/shard_map/pallas_call | solution.py:427
  10.9 0.0 collective-permute-done.2.spill_in
  10.9 0.1 shard_map.69
  11.0 1.3 %collective-permute-start.3 = (bf16[5,256,128]{2,1,0:T(8,128)(2,1)S(1)}, bf16[5,256,128]{2,1,0:T(8,128)(2,1)S(1)}, u32[]{:S(2)}, u32[]{:S(2)}) collective-permute-start(bf16[5,256,128]{2,1,0:T(8,128)(2,1)S(1)} %get-tuple-element.39.rest_0_), channel_id=1, source_target_pairs={{0,1},{1,0},{2,3},{3,2},{4,8},{5,9},{6,10},{7,11},{8,4},{9,5},{10,... | collective-permute-start | bytes 983048 | tf_op jit(solution)/shard_map/ppermute | solution.py:350
  12.3 0.4 collective-permute-start.4
  12.8 0.1 collective-permute-start.5
  12.9 3.3 %shard_map.70.cb = bf16[16,256,256]{2,1,0:T(8,128)(2,1)S(1)} custom-call(bf16[4,508032]{1,0:T(4,128)(2,1)} %flat.3, bf16[5,256,128]{2,1,0:T(8,128)(2,1)S(1)} %get-tuple-element.39.rest_0_), custom_call_target="tpu_custom_call" | custom-call | flops 1048576 | bytes 12582912 | tf_op jit(solution)/shard_map/pallas_call | solution.py:394
  16.1 2.7 %collective-permute-done.5.far = bf16[1,256,128]{2,1,0:T(8,128)(2,1)S(1)} collective-permute-done((bf16[1,256,128]{2,1,0:T(8,128)(2,1)S(1)}, bf16[1,256,128]{2,1,0:T(8,128)(2,1)S(1)}, u32[]{:S(2)}, u32[]{:S(2)}) %collective-permute-start.5) | collective-permute-done | bytes 65568 | tf_op jit(solution)/shard_map/ppermute | solution.py:350
  18.8 0.7 %shard_map.71 = (f32[4,256,128]{2,1,0:T(8,128)S(1)}, f32[4,256,128]{2,1,0:T(8,128)S(1)}, bf16[1,256,128]{2,1,0:T(8,128)(2,1)S(1)}, f32[6,128]{1,0:T(8,128)S(1)}) custom-call(s32[41]{0:T(128)S(4)} %get-tuple-element.30.table, bf16[16,256,256]{2,1,0:T(8,128)(2,1)S(1)} %get-tuple-element.31.ca, bf16[16,256,256]{2,1,0:T(8,128)(2,1)S(1)} %shard_map.70.cb, ...), custom_call_target="tpu_custom_call" | custom-call | tf_op jit(solution)/shard_map/pallas_call | solution.py:445
  19.5 1.2 %collective-permute-start.7 = (bf16[1,256,128]{2,1,0:T(8,128)(2,1)S(1)}, bf16[1,256,128]{2,1,0:T(8,128)(2,1)S(1)}, u32[]{:S(2)}, u32[]{:S(2)}) collective-permute-start(bf16[1,256,128]{2,1,0:T(8,128)(2,1)S(1)} %get-tuple-element.43), channel_id=1, source_target_pairs={{0,1},{1,0},{2,3},{3,2},{4,8},{5,9},{6,10},{7,11},{8,4},{9,5},{10,... | collective-permute-start | bytes 196616 | tf_op jit(solution)/shard_map/ppermute | solution.py:350
  20.8 0.6 collective-permute-start.6
  21.4 1.0 %shard_map.72.part = f32[1520,128]{1,0:T(8,128)S(1)} custom-call(bf16[1512,1512]{1,0:T(8,128)(2,1)S(1)} %get-tuple-element.32.inverse, f32[4,256,128]{2,1,0:T(8,128)S(1)} %get-tuple-element.42.own.w.rest_0_), custom_call_target="tpu_custom_call" | custom-call | flops 1073741824 | bytes 4194304 | tf_op jit(solution)/shard_map/pallas_call | solution.py:415
  22.4 1.5 %collective-permute-done.7.outer = bf16[1,256,128]{2,1,0:T(8,128)(2,1)S(1)} collective-permute-done((bf16[1,256,128]{2,1,0:T(8,128)(2,1)S(1)}, bf16[1,256,128]{2,1,0:T(8,128)(2,1)S(1)}, u32[]{:S(2)}, u32[]{:S(2)}) %collective-permute-start.7) | collective-permute-done | bytes 65568 | tf_op jit(solution)/shard_map/ppermute | solution.py:350
  23.9 0.3 shard_map.74
  24.2 0.3 collective-permute-start.8
  24.5 0.9 %shard_map.75 = (f32[4,256,128]{2,1,0:T(8,128)S(1)}, bf16[1,256,128]{2,1,0:T(8,128)(2,1)S(1)}) custom-call(s32[41]{0:T(128)S(4)} %get-tuple-element.30.table, bf16[1512,1512]{1,0:T(8,128)(2,1)S(1)} %get-tuple-element.32.inverse, f32[1520,128]{1,0:T(8,128)S(1)} %shard_map.72.part, bf16[616,128]{1,0:T(8,128)(2,1)S(1)} %get-tuple-element.44.ext), custom_call_target="tpu_custom_call" | custom-call | flops 1073741824 | bytes 4194304 | tf_op jit(solution)/shard_map/pallas_call | solution.py:427
  25.4 0.4 collective-permute-done.8.spill_in
  25.7 0.1 shard_map.76
  25.8 1.2 %collective-permute-start.9 = (bf16[5,256,128]{2,1,0:T(8,128)(2,1)S(1)}, bf16[5,256,128]{2,1,0:T(8,128)(2,1)S(1)}, u32[]{:S(2)}, u32[]{:S(2)}) collective-permute-start(bf16[5,256,128]{2,1,0:T(8,128)(2,1)S(1)} %get-tuple-element.49), channel_id=1, source_target_pairs={{0,1},{1,0},{2,3},{3,2},{4,8},{5,9},{6,10},{7,11},{8,4},{9,5},{10,... | collective-permute-start | bytes 983048 | tf_op jit(solution)/shard_map/ppermute | solution.py:350
  27.0 1.0 %collective-permute-start.10 = (bf16[4,256,128]{2,1,0:T(8,128)(2,1)S(1)}, bf16[4,256,128]{2,1,0:T(8,128)(2,1)S(1)}, u32[]{:S(2)}, u32[]{:S(2)}) collective-permute-start(bf16[4,256,128]{2,1,0:T(8,128)(2,1)S(1)} %get-tuple-element.50), channel_id=1, source_target_pairs={{0,4},{1,5},{2,6},{3,7},{4,0},{5,1},{6,2},{7,3},{8,12},{9,13},{10,... | collective-permute-start | bytes 786440 | tf_op jit(solution)/shard_map/ppermute | solution.py:350
  28.1 5.7 %collective-permute-done.11.far = bf16[1,256,128]{2,1,0:T(8,128)(2,1)S(1)} collective-permute-done((bf16[1,256,128]{2,1,0:T(8,128)(2,1)S(1)}, bf16[1,256,128]{2,1,0:T(8,128)(2,1)S(1)}, u32[]{:S(2)}, u32[]{:S(2)}) %collective-permute-start.11) | collective-permute-done | bytes 65568 | tf_op jit(solution)/shard_map/ppermute | solution.py:350
  33.8 0.6 shard_map.77
  34.5 28.5 %all_to_all.5.gathered = f32[64,6,128]{2,1,0:T(8,128)S(1)} all-to-all(f32[64,6,128]{2,1,0:T(8,128)S(1)} %broadcast_in_dim.2), channel_id=1, replica_groups=mesh['sub'=64,'rhs'=4] {'sub'}, dimensions={0} | all-to-all | bytes 393216 | tf_op jit(solution)/shard_map/all_to_all | solution.py:458
  63.0 1.0 %shard_map.78 = f32[1008,128]{1,0:T(8,128)} custom-call(f32[64,6,128]{2,1,0:T(8,128)S(1)} %all_to_all.5.gathered, f32[4,256,128]{2,1,0:T(8,128)S(1)} %get-tuple-element.53.p0, f32[4,256,128]{2,1,0:T(8,128)S(1)} %get-tuple-element.54.q), custom_call_target="tpu_custom_call" | custom-call | tf_op jit(solution)/shard_map/pallas_call | solution.py:459
  (11 shorter events, 0.1 us)
Async XLA Ops:
  0.7 1.0 %copy-start = (f32[4,252,128]{2,0,1:T(4,128)S(1)}, f32[4,252,128]{2,0,1:T(4,128)}, u32[]{:S(2)}) copy-start(f32[4,252,128]{2,0,1:T(4,128)} %param.6) | copy-start | bytes 1548292
  1.8 7.3 %collective-permute-start.1 = (bf16[4,256,128]{2,1,0:T(8,128)(2,1)S(1)}, bf16[4,256,128]{2,1,0:T(8,128)(2,1)S(1)}, u32[]{:S(2)}, u32[]{:S(2)}) collective-permute-start(bf16[4,256,128]{2,1,0:T(8,128)(2,1)S(1)} %get-tuple-element.34), channel_id=1, source_target_pairs={{0,1},{1,0},{2,3},{3,2},{4,8},{5,9},{6,10},{7,11},{8,4},{9,5},{10,... | collective-permute-start | bytes 786440 | tf_op jit(solution)/shard_map/ppermute | solution.py:350
  4.1 5.0 %collective-permute-start = (bf16[4,256,128]{2,1,0:T(8,128)(2,1)S(1)}, bf16[4,256,128]{2,1,0:T(8,128)(2,1)S(1)}, u32[]{:S(2)}, u32[]{:S(2)}) collective-permute-start(bf16[4,256,128]{2,1,0:T(8,128)(2,1)S(1)} %get-tuple-element.34), channel_id=1, source_target_pairs={{0,4},{1,5},{2,6},{3,7},{4,0},{5,1},{6,2},{7,3},{8,12},{9,13},{10,... | collective-permute-start | bytes 786440 | tf_op jit(solution)/shard_map/ppermute | solution.py:350
  9.5 1.5 %collective-permute-start.2 = (bf16[1,256,128]{2,1,0:T(8,128)(2,1)S(1)}, bf16[1,256,128]{2,1,0:T(8,128)(2,1)S(1)}, u32[]{:S(2)}, u32[]{:S(2)}) collective-permute-start(bf16[1,256,128]{2,1,0:T(8,128)(2,1)S(1)} %get-tuple-element.37), channel_id=1, source_target_pairs={{0,4},{1,5},{2,6},{3,7},{4,0},{5,1},{6,2},{7,3},{8,12},{9,13},{10,... | collective-permute-start | bytes 196616 | tf_op jit(solution)/shard_map/ppermute | solution.py:350
  11.0 7.8 %collective-permute-start.3 = (bf16[5,256,128]{2,1,0:T(8,128)(2,1)S(1)}, bf16[5,256,128]{2,1,0:T(8,128)(2,1)S(1)}, u32[]{:S(2)}, u32[]{:S(2)}) collective-permute-start(bf16[5,256,128]{2,1,0:T(8,128)(2,1)S(1)} %get-tuple-element.39.rest_0_), channel_id=1, source_target_pairs={{0,1},{1,0},{2,3},{3,2},{4,8},{5,9},{6,10},{7,11},{8,4},{9,5},{10,... | collective-permute-start | bytes 983048 | tf_op jit(solution)/shard_map/ppermute | solution.py:350
  12.3 6.5 %collective-permute-start.4 = (bf16[4,256,128]{2,1,0:T(8,128)(2,1)S(1)}, bf16[4,256,128]{2,1,0:T(8,128)(2,1)S(1)}, u32[]{:S(2)}, u32[]{:S(2)}) collective-permute-start(bf16[4,256,128]{2,1,0:T(8,128)(2,1)S(1)} %get-tuple-element.41), channel_id=1, source_target_pairs={{0,4},{1,5},{2,6},{3,7},{4,0},{5,1},{6,2},{7,3},{8,12},{9,13},{10,... | collective-permute-start | bytes 786440 | tf_op jit(solution)/shard_map/ppermute | solution.py:350
  12.8 6.1 %collective-permute-start.5 = (bf16[1,256,128]{2,1,0:T(8,128)(2,1)S(1)}, bf16[1,256,128]{2,1,0:T(8,128)(2,1)S(1)}, u32[]{:S(2)}, u32[]{:S(2)}) collective-permute-start(bf16[1,256,128]{2,1,0:T(8,128)(2,1)S(1)} %get-tuple-element.38.spill_out), channel_id=1, source_target_pairs={{0,4},{1,5},{2,6},{3,7},{4,12},{5,13},{6,14},{7,15},{8,0},{9,1},{1... | collective-permute-start | bytes 196616 | tf_op jit(solution)/shard_map/ppermute | solution.py:350
  19.5 4.4 %collective-permute-start.7 = (bf16[1,256,128]{2,1,0:T(8,128)(2,1)S(1)}, bf16[1,256,128]{2,1,0:T(8,128)(2,1)S(1)}, u32[]{:S(2)}, u32[]{:S(2)}) collective-permute-start(bf16[1,256,128]{2,1,0:T(8,128)(2,1)S(1)} %get-tuple-element.43), channel_id=1, source_target_pairs={{0,1},{1,0},{2,3},{3,2},{4,8},{5,9},{6,10},{7,11},{8,4},{9,5},{10,... | collective-permute-start | bytes 196616 | tf_op jit(solution)/shard_map/ppermute | solution.py:350
  20.8 3.1 %collective-permute-start.6 = (bf16[1,256,128]{2,1,0:T(8,128)(2,1)S(1)}, bf16[1,256,128]{2,1,0:T(8,128)(2,1)S(1)}, u32[]{:S(2)}, u32[]{:S(2)}) collective-permute-start(bf16[1,256,128]{2,1,0:T(8,128)(2,1)S(1)} %shard_map.73), channel_id=1, source_target_pairs={{0,4},{1,5},{2,6},{3,7},{4,0},{5,1},{6,2},{7,3},{8,12},{9,13},{10,... | collective-permute-start | bytes 196616 | tf_op jit(solution)/shard_map/ppermute | solution.py:350
  24.2 1.5 %collective-permute-start.8 = (bf16[1,256,128]{2,1,0:T(8,128)(2,1)S(1)}, bf16[1,256,128]{2,1,0:T(8,128)(2,1)S(1)}, u32[]{:S(2)}, u32[]{:S(2)}) collective-permute-start(bf16[1,256,128]{2,1,0:T(8,128)(2,1)S(1)} %get-tuple-element.46), channel_id=1, source_target_pairs={{0,4},{1,5},{2,6},{3,7},{4,0},{5,1},{6,2},{7,3},{8,12},{9,13},{10,... | collective-permute-start | bytes 196616 | tf_op jit(solution)/shard_map/ppermute | solution.py:350
  25.8 8.0 %collective-permute-start.9 = (bf16[5,256,128]{2,1,0:T(8,128)(2,1)S(1)}, bf16[5,256,128]{2,1,0:T(8,128)(2,1)S(1)}, u32[]{:S(2)}, u32[]{:S(2)}) collective-permute-start(bf16[5,256,128]{2,1,0:T(8,128)(2,1)S(1)} %get-tuple-element.49), channel_id=1, source_target_pairs={{0,1},{1,0},{2,3},{3,2},{4,8},{5,9},{6,10},{7,11},{8,4},{9,5},{10,... | collective-permute-start | bytes 983048 | tf_op jit(solution)/shard_map/ppermute | solution.py:350
  27.0 6.8 %collective-permute-start.10 = (bf16[4,256,128]{2,1,0:T(8,128)(2,1)S(1)}, bf16[4,256,128]{2,1,0:T(8,128)(2,1)S(1)}, u32[]{:S(2)}, u32[]{:S(2)}) collective-permute-start(bf16[4,256,128]{2,1,0:T(8,128)(2,1)S(1)} %get-tuple-element.50), channel_id=1, source_target_pairs={{0,4},{1,5},{2,6},{3,7},{4,0},{5,1},{6,2},{7,3},{8,12},{9,13},{10,... | collective-permute-start | bytes 786440 | tf_op jit(solution)/shard_map/ppermute | solution.py:350
  28.1 5.7 %collective-permute-start.11 = (bf16[1,256,128]{2,1,0:T(8,128)(2,1)S(1)}, bf16[1,256,128]{2,1,0:T(8,128)(2,1)S(1)}, u32[]{:S(2)}, u32[]{:S(2)}) collective-permute-start(bf16[1,256,128]{2,1,0:T(8,128)(2,1)S(1)} %get-tuple-element.47.spill_out), channel_id=1, source_target_pairs={{0,4},{1,5},{2,6},{3,7},{4,12},{5,13},{6,14},{7,15},{8,0},{9,1},{1... | collective-permute-start | bytes 196616 | tf_op jit(solution)/shard_map/ppermute | solution.py:350
